TPU v7x, 32 devices: a whole 2x2x4 slice. The times are simulated.
32 devices in a mesh: seq: 8 (over z, x), tp: 4 (over y, core).
Axes of the slice: x: 2, y: 2, z: 4, core: 2. Of those that a mesh axis runs over, the one named last changes fastest.
Arguments:
- panels: bfloat16 [256, 8, 5120], P('seq', None, 'tp'), may hold values from -60 to 60
- w_merge: bfloat16 [5120, 8192], P('seq', 'tp'), may hold values from -2 to 2
- ln_gain: bfloat16 [8192], P('tp'), may hold values from 0.099609375 to 1.8984375
- w_kv: bfloat16 [8192, 1024], P('tp'), may hold values from -0.0625 to 0.0625
- page_src: int32 [256, 1], P('seq'), may hold values from 0 to 7; in each aligned block of 32 rows (0 to 31, 32 to 63, ...) at most 8 rows name the same one
- page_tile: int32 [256], P('seq'), may hold values from 0 to 31
- doc_pages: int32 [8, 4], P('seq'), may hold values from 1 to 16, 32 in all within a row
- prefix_id: int32 [32], P('seq'), may hold values from 0 to 7
- prefix_cache: bfloat16 [8, 32, 1024], P('seq', None, 'tp'), may hold values from -4 to 4
- queries: bfloat16 [32, 128, 4096], P('seq', None, 'tp'), may hold values from -9 to 9
- text_kv: bfloat16 [32, 128, 1024], P('seq', None, 'tp'), may hold values from -4 to 4
Outputs:
- attended: bfloat16 [32, 128, 4096], P('seq', None, 'tp')
- vision_kv: bfloat16 [2048, 1024], P('seq', 'tp')
Inputs may be any that keep to these rules, and one draw needn't show every extreme that they name: `page_src`: in the 32 rows of one owner index (aligned blocks), no encoder index is named more than 8 times, and some encoder index is named exactly 8 times in some block.
All inputs are finite; a program needn't handle non-finite values.
Results may differ from a plain program's by a relative error of at most 0.015.
Values may be sent and summed in bfloat16 or wider, within the bound.
No kernel may reach another device: no remote copies, remote signals or barrier semaphores. Data moves between devices by JAX's collectives and lax.ppermute only.
A program may use at most 128 MiB of HBM per device.

v0:
```python
import jax
import jax.numpy as jnp
from jax import lax
from jax.sharding import PartitionSpec as P

D = 8192
HD = 128
GROUP = 8


def merge_rows(rows, w_merge):
    total = jnp.dot(
        rows, lax.all_gather(w_merge, "seq", axis=0, tiled=True), preferred_element_type=jnp.float32
    )
    return total.astype(jnp.bfloat16)


def absorb(state, scores, valid, values, form):
    best, total, accum = state
    masked = jnp.where(valid, scores, -1e30)
    new_best = jnp.maximum(best, jnp.max(masked, axis=-1))
    factor = jnp.exp(best - new_best)
    weights = jnp.where(valid, jnp.exp(masked - new_best[..., None]), 0.0)
    total = total * factor + jnp.sum(weights, axis=-1)
    update = jnp.einsum(
        form, weights.astype(jnp.bfloat16), values, preferred_element_type=jnp.float32
    )
    accum = accum * factor[..., None] + update
    return (new_best, total, accum)


def shards(
    panels,
    w_merge,
    ln_gain,
    w_kv,
    page_src,
    page_tile,
    doc_pages,
    prefix_id,
    prefix_cache,
    queries,
    text_kv,
):
    seq_count = lax.axis_size("seq")
    holder = lax.axis_index("seq")
    tile_count, panel_rows, _ = panels.shape
    page_count = page_src.shape[0]
    capacity = max(2, 2 * page_count // seq_count)
    sources = page_src[:, 0]
    all_sources, all_tiles = (
        lax.all_gather(sources, "seq", axis=0, tiled=True),
        lax.all_gather(page_tile, "seq", axis=0, tiled=True),
    )
    all_sources = all_sources.reshape(seq_count, page_count)
    all_tiles = all_tiles.reshape(seq_count, page_count)
    asked = (all_sources == holder).astype(jnp.int32)
    order = jnp.cumsum(asked, axis=1) - 1
    slots = jnp.arange(capacity, dtype=jnp.int32)
    picked = asked[:, None, :] * (order[:, None, :] == slots[None, :, None]).astype(jnp.int32)
    wanted = jnp.sum(picked * all_tiles[:, None, :], axis=2)
    position = jnp.arange(page_count, dtype=jnp.int32)
    earlier = (sources[:, None] == sources[None, :]) & (position[None, :] < position[:, None])
    rank = jnp.sum(earlier.astype(jnp.int32), axis=1)
    arrival = sources * capacity + rank
    outgoing = panels[wanted]
    incoming = lax.all_to_all(outgoing, "seq", split_axis=0, concat_axis=0, tiled=True)
    incoming = incoming.reshape(seq_count * capacity, panel_rows, -1)
    local_rows = incoming[arrival].reshape(page_count * panel_rows, -1)
    full_rows = lax.all_gather(local_rows, "tp", axis=1, tiled=True)
    merged = merge_rows(full_rows, w_merge)
    merged_float = merged.astype(jnp.float32)
    squares = lax.psum(jnp.sum(merged_float * merged_float, axis=1), "tp")
    row_scale = lax.rsqrt(squares / D + 1e-06)
    normed = (merged_float * ln_gain.astype(jnp.float32)[None, :] * row_scale[:, None]).astype(
        jnp.bfloat16
    )
    partial_kv = jnp.dot(normed, w_kv, preferred_element_type=jnp.float32)
    vision_kv = lax.psum_scatter(
        partial_kv.astype(jnp.bfloat16), "tp", scatter_dimension=1, tiled=True
    )
    doc_count, query_rows, _ = queries.shape
    heads = vision_kv.shape[1] // (2 * HD)
    query_all = queries.reshape(doc_count, query_rows, heads, GROUP, HD)
    score_scale = HD ** (-0.5)
    vision = vision_kv.reshape(-1, heads, 2, HD)
    ends = jnp.cumsum(doc_pages[0])
    page_of_row = jnp.arange(vision.shape[0], dtype=jnp.int32) // panel_rows
    row_doc = jnp.sum((page_of_row[:, None] >= ends[None, :]).astype(jnp.int32), axis=1)
    doc_index = jnp.arange(doc_count, dtype=jnp.int32)
    state = (
        jnp.full((doc_count, heads, GROUP, query_rows), -1e30, jnp.float32),
        jnp.zeros((doc_count, heads, GROUP, query_rows), jnp.float32),
        jnp.zeros((doc_count, heads, GROUP, query_rows, HD), jnp.float32),
    )
    piece = lax.all_gather(prefix_cache, "seq", axis=0, tiled=True)
    inside = (prefix_id >= 0) & (prefix_id < piece.shape[0])

    def attend(current):
        picked_blocks = piece[jnp.clip(prefix_id, 0, piece.shape[0] - 1)].reshape(
            doc_count, -1, heads, 2, HD
        )
        block_scores = (
            jnp.einsum(
                "dqhgc,dkhc->dhgqk",
                query_all,
                picked_blocks[:, :, :, 0],
                preferred_element_type=jnp.float32,
            )
            * score_scale
        )
        valid = inside[:, None, None, None, None]
        return absorb(current, block_scores, valid, picked_blocks[:, :, :, 1], "dhgqk,dkhc->dhgqc")

    state = lax.cond(jnp.any(inside), attend, lambda current: current, state)
    scores = (
        jnp.einsum(
            "dqhgc,khc->dhgqk", query_all, vision[:, :, 0], preferred_element_type=jnp.float32
        )
        * score_scale
    )
    valid = (row_doc[None, :] == doc_index[:, None])[:, None, None, None, :]
    state = absorb(state, scores, valid, vision[:, :, 1], "dhgqk,khc->dhgqc")
    own = text_kv.reshape(doc_count, query_rows, heads, 2, HD)
    scores = (
        jnp.einsum(
            "dqhgc,dkhc->dhgqk", query_all, own[:, :, :, 0], preferred_element_type=jnp.float32
        )
        * score_scale
    )
    text_rows = jnp.arange(query_rows, dtype=jnp.int32)
    causal = (text_rows[None, :] <= text_rows[:, None])[None, None, None]
    state = absorb(state, scores, causal, own[:, :, :, 1], "dhgqk,dkhc->dhgqc")
    best, total, accum = state
    result = accum / total[..., None]
    attended = (
        result.transpose(0, 3, 1, 2, 4).reshape(doc_count, query_rows, -1).astype(jnp.bfloat16)
    )
    return (attended, vision_kv)


def solution(mesh):
    return jax.shard_map(
        shards,
        mesh=mesh,
        in_specs=(
            P("seq", None, "tp"),
            P("seq", "tp"),
            P("tp"),
            P("tp", None),
            P("seq", None),
            P("seq"),
            P("seq", None),
            P("seq"),
            P("seq", None, "tp"),
            P("seq", None, "tp"),
            P("seq", None, "tp"),
        ),
        out_specs=(P("seq", None, "tp"), P("seq", "tp")),
        check_vma=False,
    )
```

profile of v0, /device:TPU:0, one launch (start us, length us, event | category | flops | bytes accessed | tf_op | source)
XLA Modules:
  0.0 567.9 jit_solution(4990424773883245890)
XLA Ops:
  7.2 0.0 copy-start
  7.2 1.3 dynamic-slice
  9.2 0.8 bitcast_dynamic-update-slice_fusion
  9.9 0.8 dynamic-update-slice.1
  10.7 13.1 %all-reduce.2 = (s32[256]{0:T(256)S(1)}, s32[256]{0:T(256)S(1)}) all-reduce(s32[256]{0:T(256)S(1)} %dynamic-update-slice.1, s32[256]{0:T(256)S(1)} %bitcast_dynamic-update-slice_fusion), channel_id=1, replica_groups=mesh['seq'=8,'tp'=4] {'seq'}, use_global_device_ids=true, to_apply=%add.1 | all-reduce | flops 512 | bytes 4096
  23.8 0.1 reshape.279
  23.9 0.2 reduce_window_sum.18
  24.1 0.1 mul.108
  24.2 0.2 multiply_reduce_fusion
  24.4 0.1 reshape.290
  24.5 0.0 copy-done
  24.5 0.0 copy-start.6
  24.5 1.7 gather_fusion.1
  26.2 3.6 all-to-all-start
  29.8 0.0 all-gather.4.cloned.1.call-start
  29.8 0.0 copy-done.6
  29.8 0.2 convert_reduce_fusion
  30.0 28.6 %all-to-all-done = bf16[8,8,8,1280]{3,2,1,0:T(8,128)(2,1)S(1)} async-done(((bf16[8,8,8,1280]{3,2,1,0:T(8,128)(2,1)}), bf16[8,8,8,1280]{3,2,1,0:T(8,128)(2,1)S(1)}, u32[]{:S(2)}, u32[]{:S(2)}) %all-to-all-start) | async-done | bytes 1310752 | tf_op jit(solution)/shard_map/all_to_all | solution.py:67
  58.7 0.0 copy-start.5
  58.7 0.0 copy-start.3
  58.7 1.4 gather_fusion.2
  60.1 0.0 all-gather.4.cloned.1.call-update
  60.1 0.0 all-gather.6.cloned.1.call-start
  60.2 0.7 all-gather.6.cloned.1.call-update
  60.9 0.0 reduce-scatter.2.cloned.1.call-start
  60.9 0.0 copy-done.5
  60.9 0.0 copy-done.3
  60.9 0.2 copy.59
  61.1 23.6 %all-gather.4.cloned.1.call-done = bf16[256,5120]{1,0:T(8,128)(2,1)} async-done(((bf16[256,1280]{1,0:T(8,128)(2,1)}), bf16[256,5120]{1,0:T(8,128)(2,1)}) %all-gather.4.cloned.1.call-update) | async-done | bytes 2621456 | tf_op jit(solution)/shard_map/all_gather | solution.py:70
  84.7 403.3 %all-gather.6.cloned.1.call-done = bf16[5120,2048]{1,0:T(8,128)(2,1)} async-done(((bf16[640,2048]{1,0:T(8,128)(2,1)}), bf16[5120,2048]{1,0:T(8,128)(2,1)}) %all-gather.6.cloned.1.call-update) | async-done | bytes 20971536 | tf_op jit(solution)/shard_map/all_gather | solution.py:13
  488.1 11.4 %fusion.19 = (f32[256]{0:T(256)S(1)}, bf16[256,2048]{1,0:T(8,128)(2,1)}) fusion(bf16[256,5120]{1,0:T(8,128)(2,1)} %all-gather.4.cloned.1.call-done, bf16[5120,2048]{1,0:T(8,128)(2,1)} %all-gather.6.cloned.1.call-done), kind=kOutput, calls=%fused_computation.36 | convolution fusion | flops 5370806272 | bytes 24642560 | tf_op jit(solution)/shard_map/dot_general | solution.py:12
  499.4 6.8 %psum.7 = f32[256]{0:T(256)S(1)} all-reduce(f32[256]{0:T(256)S(1)} %get-tuple-element.49), channel_id=1, replica_groups=mesh['seq'=8,'tp'=4] {'tp'}, use_global_device_ids=true, to_apply=%region_11.12 | all-reduce | flops 256 | bytes 2048 | tf_op jit(solution)/shard_map/psum | solution.py:73
  506.3 0.0 copy-start.8
  506.3 0.0 copy-start.4
  506.3 0.0 copy-start.1
  506.3 4.7 convolution_convert_fusion.1
  511.0 0.0 reduce-scatter.2.cloned.1.call-update
  511.0 0.0 copy-done.8
  511.0 0.6 compare_and_fusion
  512.3 0.0 copy-done.7
  512.3 0.2 reduce-window.8
  512.5 0.0 copy-done.4
  512.5 30.5 %all_gather.15 = bf16[8,32,256]{2,1,0:T(8,128)(2,1)S(1)} all-gather(bf16[1,32,256]{2,1,0:T(8,128)(2,1)S(1)} %copy-done.4), channel_id=1, replica_groups=mesh['seq'=8,'tp'=4] {'seq'}, dimensions={0}, use_global_device_ids=true | all-gather | bytes 147456 | tf_op jit(solution)/shard_map/all_gather | solution.py:96
  543.0 0.0 copy-done.1
  543.0 6.7 %conditional.1 = (f32[4,1,8,128]{3,2,0,1:T(8,128)S(1)}, f32[4,1,8,128]{3,2,0,1:T(8,128)S(1)}, f32[4,1,8,128,128]{3,4,2,0,1:T(8,128)}) conditional(s32[]{:T(128)} %convert_element_type.57, () %tuple.16, (pred[4]{0:T(512)(128)(4,1)S(1)}, s32[4]{0:T(128)S(1)}, bf16[8,32,256]{2,1,0:T(8,128)(2,1)S(1)}, bf16[4,128,1024]{2,1,0:T(8,128)(2,1)S(1)}) %tuple.46), branch_computations={%region_1.2_spmd, %region_2.0_spmd} | conditional | flops 68834320 | bytes 9572452 | solution.py:115
  543.1 0.6 gather_fusion
  543.6 0.1 fusion.68
  543.7 0.5 fusion.69
  544.3 2.3 add_bitcast_fusion
  546.5 2.9 copy.74
  549.4 0.1 fusion.6
  549.8 0.1 convert_reduce_fusion.1
  549.9 1.9 fusion.32
  551.8 0.9 reshape.268
  552.7 0.2 fusion.70
  552.9 0.1 copy.78
  553.0 0.9 fusion.14
  553.9 1.2 fusion.15
  555.1 0.0 copy-start.2
  555.2 1.5 fusion.21
  556.7 0.1 copy-done.2
  556.7 0.6 fusion.33
  557.3 2.7 fusion.30
  560.0 1.3 copy.64
  (22 shorter events, 0.2 us)
Async XLA Ops:
  7.2 17.3 %copy-start = (bf16[32,8,1280]{2,1,0:T(8,128)(2,1)S(1)}, bf16[32,8,1280]{2,1,0:T(8,128)(2,1)}, u32[]{:S(2)}) copy-start(bf16[32,8,1280]{2,1,0:T(8,128)(2,1)} %param.13) | copy-start | bytes 1966084
  24.5 5.3 copy-start.6
  26.2 32.5 %all-to-all-start = ((bf16[8,8,8,1280]{3,2,1,0:T(8,128)(2,1)}), bf16[8,8,8,1280]{3,2,1,0:T(8,128)(2,1)S(1)}, u32[]{:S(2)}, u32[]{:S(2)}) async-start(bf16[8,8,8,1280]{3,2,1,0:T(8,128)(2,1)} %bitcast.17), calls=%async_computation | async-start | bytes 2621440 | tf_op jit(solution)/shard_map/all_to_all | solution.py:67
  29.8 54.9 %all-gather.4.cloned.1.call-start = ((), (), s32[]{:S(2)}) async-start(), calls=%async_computation.2 | async-start | bytes 3276800 | tf_op jit(solution)/shard_map/all_gather | solution.py:70
  58.7 2.3 copy-start.5
  58.7 2.3 copy-start.3
  60.1 427.9 %all-gather.6.cloned.1.call-start = ((), (), s32[]{:S(2)}) async-start(), calls=%async_computation.3 | async-start | bytes 23592960 | tf_op jit(solution)/shard_map/all_gather | solution.py:13
  60.9 490.9 %reduce-scatter.2.cloned.1.call-start = ((), (), s32[]{:S(2)}) async-start(), calls=%async_computation.4 | async-start | bytes 655360 | tf_op jit(solution)/shard_map/reduce_scatter | solution.py:79
  506.3 4.8 copy-start.8
  506.3 6.0 %copy-start.7 = (s32[1,4]{1,0:T(1,128)S(1)}, s32[1,4]{1,0:T(1,128)}, u32[]{:S(2)}) copy-start(s32[1,4]{1,0:T(1,128)} %param.19) | copy-start | bytes 52
  506.3 6.2 %copy-start.4 = (bf16[1,32,256]{2,1,0:T(8,128)(2,1)S(1)}, bf16[1,32,256]{2,1,0:T(8,128)(2,1)}, u32[]{:S(2)}) copy-start(bf16[1,32,256]{2,1,0:T(8,128)(2,1)} %param.21) | copy-start | bytes 49156
  506.3 36.7 %copy-start.1 = (bf16[4,128,1024]{2,1,0:T(8,128)(2,1)S(1)}, bf16[4,128,1024]{2,1,0:T(8,128)(2,1)}, u32[]{:S(2)}) copy-start(bf16[4,128,1024]{2,1,0:T(8,128)(2,1)} %param.22) | copy-start | bytes 3145732
  555.1 1.6 copy-start.2
Sparse Core Ops, SparseCore 0:
  60.2 24.4 all-gather.3
  86.2 401.7 all-gather.5
  511.2 20.6 reduce-scatter.1
where the time goes:
time: 568 us
  waiting for transfers between devices  456 us (80%)
  blocking collectives  50.4 us (9%)
  matrix products  25.8 us (5%)
  between operations  15.3 us (3%)
  local copies, waits for them, and re-layouts  12.7 us (2%)
    all_gather x1, waiting for transfers between devices, merge_rows(): lax.all_gather(w_merge, 'seq', axis=0, tiled=True)  403 us
    all_gather x1, blocking collectives, shards(): piece = lax.all_gather(prefix_cache, 'seq', axis=0, tiled=True)  30.5 us
    all_to_all x1, waiting for transfers between devices, shards(): lax.all_to_all(outgoing, 'seq', split_axis=0, concat_axis=0, tiled=True)  28.6 us
    all_gather x1, waiting for transfers between devices, shards(): full_rows = lax.all_gather(local_rows, 'tp', axis=1, tiled=True)  23.6 us
    unnamed x1, blocking collectives  13.1 us
    dot_general x1, matrix products, merge_rows(): jnp.dot(rows, lax.all_gather(w_merge, 'seq', axis=0, tiled=True), preferr...  11.4 us
  transfers between devices with their start and end apart: 4, of which 3 were waited for; matrix products, arithmetic and copies ran while one was open for 2% of the time, Pallas kernels for 0%

commit v1 on v0

v1 whole, which is shorter than its diff:
```python
import jax
import jax.numpy as jnp
from jax import lax
from jax.sharding import PartitionSpec as P

D = 8192
HD = 128
GROUP = 8
CHUNKS = 2


def slot(origin, block, count):
    half = count // 2
    return ((origin ^ block) & 1) * half + origin // 2


def absorb(state, scores, valid, values, form):
    best, total, accum = state
    masked = jnp.where(valid, scores, -1e30)
    new_best = jnp.maximum(best, jnp.max(masked, axis=-1))
    factor = jnp.exp(best - new_best)
    weights = jnp.where(valid, jnp.exp(masked - new_best[..., None]), 0.0)
    total = total * factor + jnp.sum(weights, axis=-1)
    update = jnp.einsum(
        form, weights.astype(jnp.bfloat16), values, preferred_element_type=jnp.float32
    )
    accum = accum * factor[..., None] + update
    return (new_best, total, accum)


def merge_tiles(panels, w_merge):
    seq_count, tp_count = lax.axis_size("seq"), lax.axis_size("tp")
    width = seq_count // tp_count
    member = lax.axis_index("seq") // width
    tiles, panel_rows, depth = panels.shape
    rows = tiles * panel_rows
    local = panels.reshape(rows, depth)
    pairs = []
    for origin in range(tp_count):
        for inner in range(width):
            for block in range(tp_count):
                source = (origin * width + inner) * tp_count + block
                target = (block * width + inner) * tp_count + slot(origin, block, tp_count)
                pairs.append((source, target))
    moved = lax.ppermute(local, ("seq", "tp"), pairs)
    gathered = lax.all_gather(moved, "tp", axis=0, tiled=True)
    swapped = jnp.roll(gathered, rows * tp_count // 2, axis=0)
    ordered = jnp.where(member % 2 == 1, swapped, gathered)
    ordered = ordered.reshape(2, tp_count // 2, rows, depth).swapaxes(0, 1)
    ordered = ordered.reshape(tp_count * rows, depth)
    inner_groups = [[g * width + i for i in range(width)] for g in range(tp_count)]
    outer_groups = [[g * width + i for g in range(tp_count)] for i in range(width)]
    pieces = []
    columns = w_merge.shape[1] // CHUNKS
    for chunk in range(CHUNKS):
        weights = lax.all_gather(
            w_merge[:, chunk * columns : (chunk + 1) * columns],
            "seq",
            axis=0,
            tiled=True,
            axis_index_groups=inner_groups,
        )
        partial = jnp.dot(ordered, weights, preferred_element_type=jnp.float32)
        pieces.append(
            lax.psum_scatter(
                partial.astype(jnp.bfloat16),
                "seq",
                scatter_dimension=0,
                tiled=True,
                axis_index_groups=outer_groups,
            )
        )
    return jnp.concatenate(pieces, axis=1)


def shards(
    panels,
    w_merge,
    ln_gain,
    w_kv,
    page_src,
    page_tile,
    doc_pages,
    prefix_id,
    prefix_cache,
    queries,
    text_kv,
):
    tile_count, panel_rows, _ = panels.shape
    merged = merge_tiles(panels, w_merge)
    merged_float = merged.astype(jnp.float32)
    squares = lax.psum(jnp.sum(merged_float * merged_float, axis=1), "tp")
    row_scale = lax.rsqrt(squares / D + 1e-06)
    normed = (merged_float * ln_gain.astype(jnp.float32)[None, :] * row_scale[:, None]).astype(
        jnp.bfloat16
    )
    partial_kv = jnp.dot(normed, w_kv, preferred_element_type=jnp.float32)
    tile_kv = lax.psum_scatter(
        partial_kv.astype(jnp.bfloat16), "tp", scatter_dimension=1, tiled=True
    )
    all_kv = lax.all_gather(tile_kv, "seq", axis=0, tiled=True)
    all_kv = all_kv.reshape(-1, panel_rows, all_kv.shape[1])
    chosen = page_src[:, 0] * tile_count + page_tile
    vision_kv = all_kv[chosen].reshape(-1, all_kv.shape[2])
    doc_count, query_rows, _ = queries.shape
    heads = vision_kv.shape[1] // (2 * HD)
    query_all = queries.reshape(doc_count, query_rows, heads, GROUP, HD)
    score_scale = HD ** (-0.5)
    vision = vision_kv.reshape(-1, heads, 2, HD)
    ends = jnp.cumsum(doc_pages[0])
    page_of_row = jnp.arange(vision.shape[0], dtype=jnp.int32) // panel_rows
    row_doc = jnp.sum((page_of_row[:, None] >= ends[None, :]).astype(jnp.int32), axis=1)
    doc_index = jnp.arange(doc_count, dtype=jnp.int32)
    state = (
        jnp.full((doc_count, heads, GROUP, query_rows), -1e30, jnp.float32),
        jnp.zeros((doc_count, heads, GROUP, query_rows), jnp.float32),
        jnp.zeros((doc_count, heads, GROUP, query_rows, HD), jnp.float32),
    )
    piece = lax.all_gather(prefix_cache, "seq", axis=0, tiled=True)
    picked_blocks = piece[prefix_id].reshape(doc_count, -1, heads, 2, HD)
    scores = (
        jnp.einsum(
            "dqhgc,dkhc->dhgqk",
            query_all,
            picked_blocks[:, :, :, 0],
            preferred_element_type=jnp.float32,
        )
        * score_scale
    )
    state = absorb(state, scores, True, picked_blocks[:, :, :, 1], "dhgqk,dkhc->dhgqc")
    own = text_kv.reshape(doc_count, query_rows, heads, 2, HD)
    scores = (
        jnp.einsum(
            "dqhgc,dkhc->dhgqk", query_all, own[:, :, :, 0], preferred_element_type=jnp.float32
        )
        * score_scale
    )
    text_rows = jnp.arange(query_rows, dtype=jnp.int32)
    causal = (text_rows[None, :] <= text_rows[:, None])[None, None, None]
    state = absorb(state, scores, causal, own[:, :, :, 1], "dhgqk,dkhc->dhgqc")
    scores = (
        jnp.einsum(
            "dqhgc,khc->dhgqk", query_all, vision[:, :, 0], preferred_element_type=jnp.float32
        )
        * score_scale
    )
    valid = (row_doc[None, :] == doc_index[:, None])[:, None, None, None, :]
    state = absorb(state, scores, valid, vision[:, :, 1], "dhgqk,khc->dhgqc")
    best, total, accum = state
    result = accum / total[..., None]
    attended = (
        result.transpose(0, 3, 1, 2, 4).reshape(doc_count, query_rows, -1).astype(jnp.bfloat16)
    )
    return (attended, vision_kv)


def solution(mesh):
    return jax.shard_map(
        shards,
        mesh=mesh,
        in_specs=(
            P("seq", None, "tp"),
            P("seq", "tp"),
            P("tp"),
            P("tp", None),
            P("seq", None),
            P("seq"),
            P("seq", None),
            P("seq"),
            P("seq", None, "tp"),
            P("seq", None, "tp"),
            P("seq", None, "tp"),
        ),
        out_specs=(P("seq", None, "tp"), P("seq", "tp")),
        check_vma=False,
    )
```

time: 568 us -> 350 us (0.62)
  waiting for transfers between devices: 456 us -> 237 us
  blocking collectives: 50.4 us -> 37.4 us
  local copies, waits for them, and re-layouts: 12.7 us -> 19 us
    all_gather x2 -> x4, waiting for transfers between devices: 427 us -> 132 us  [the longest x2 69.4 us: merge_tiles(): lax.all_gather(w_merge[:, chunk * columns:(chunk + 1) * columns], 'seq',...]
    reduce_scatter x0 -> x2, waiting for transfers between devices: none -> 84.1 us  [merge_tiles(): lax.psum_scatter(partial.astype(jnp.bfloat16), 'seq', scatter_dimension=0...]
    all_to_all x1 -> x0, waiting for transfers between devices: 28.6 us -> none  [shards(): lax.all_to_all(outgoing, 'seq', split_axis=0, concat_axis=0, tiled=True)]
    reduce_scatter x1, waiting for transfers between devices: 0.01 us -> 20.6 us  [shards(): lax.psum_scatter(partial_kv.astype(jnp.bfloat16), 'tp', scatter_dimension...]
    unnamed x1 -> x0, blocking collectives: 13.1 us -> none
    slice x1 -> x3, local copies, waits for them, and re-layouts: 0.09 us -> 6.28 us  [the longest x1 3.55 us: merge_tiles(): w_merge[:, chunk * columns:(chunk + 1) * columns]]
    dot_general x2 -> x3, matrix products: 11.8 us -> 15.4 us  [the longest x2 13.5 us: merge_tiles(): partial = jnp.dot(ordered, weights, preferred_element_type=jnp.float32)]
  transfers between devices with their start and end apart: 4 -> 8, of which waited for: 3 -> 7; matrix products, arithmetic and copies ran while one was open for 2% -> 8% of each run, Pallas kernels for 0% -> 0%
where the time goes in v1:
time: 350 us; the launch traced here: 349 us
  waiting for transfers between devices  237 us (68%)
  blocking collectives  37.4 us (11%)
  matrix products  30.8 us (9%)
  local copies, waits for them, and re-layouts  19 us (5%)
  between operations  14.4 us (4%)
  other arithmetic  8.5 us (2%)
    reduce_scatter x2, waiting for transfers between devices, merge_tiles(): lax.psum_scatter(partial.astype(jnp.bfloat16), 'seq', scatter_dimension=0...  84.1 us
    all_gather x2, waiting for transfers between devices, merge_tiles(): lax.all_gather(w_merge[:, chunk * columns:(chunk + 1) * columns], 'seq',...  69.4 us
    all_gather x1, waiting for transfers between devices, merge_tiles(): gathered = lax.all_gather(moved, 'tp', axis=0, tiled=True)  55.9 us
    all_gather x1, blocking collectives, shards(): piece = lax.all_gather(prefix_cache, 'seq', axis=0, tiled=True)  31 us
    reduce_scatter x1, waiting for transfers between devices, shards(): lax.psum_scatter(partial_kv.astype(jnp.bfloat16), 'tp', scatter_dimension...  20.6 us
    dot_general x2, matrix products, merge_tiles(): partial = jnp.dot(ordered, weights, preferred_element_type=jnp.float32)  13.5 us
  transfers between devices with their start and end apart: 8, of which 7 were waited for; matrix products, arithmetic and copies ran while one was open for 8% of the time, Pallas kernels for 0%

profile of v1, /device:TPU:0, one launch (start us, length us, event | category | flops | bytes accessed | tf_op | source)
XLA Modules:
  0.0 349.2 jit_solution(10966447677001323099)
XLA Ops:
  7.2 0.0 copy-start
  7.2 0.0 all-gather.5.cloned.1.call-start
  7.2 1.9 collective-permute-start
  9.1 0.8 copy-done.5
  9.9 0.0 all-gather.5.cloned.1.call-update
  10.0 0.0 all-gather.7.cloned.1.call-start
  10.0 3.5 %fusion.55 = (bf16[640,1024]{1,0:T(8,128)(2,1)}, bf16[640,1024]{1,0:T(8,128)(2,1)}) fusion(bf16[640,2048]{1,0:T(8,128)(2,1)} %param.12), kind=kLoop, calls=%fused_computation.89 | loop fusion | bytes 5242880 | tf_op jit(solution)/shard_map/slice | solution.py:57
  13.6 0.0 all-gather.7.cloned.1.call-update
  13.6 0.0 all-gather.9.cloned.1.call-start
  13.6 0.7 all-gather.9.cloned.1.call-update
  14.3 0.0 reduce-scatter.4.cloned.1.call-start
  14.4 55.9 %all-gather.5.cloned.1.call-done = bf16[1024,1280]{1,0:T(8,128)(2,1)} async-done(((bf16[256,1280]{1,0:T(8,128)(2,1)}), bf16[1024,1280]{1,0:T(8,128)(2,1)}) %all-gather.5.cloned.1.call-update) | async-done | bytes 2621456 | tf_op jit(solution)/shard_map/all_gather | solution.py:46
  70.3 2.0 fusion.56
  72.3 0.5 copy-done.2
  72.8 0.7 maximum_select_fusion
  73.5 1.7 copy.70
  75.2 35.7 %all-gather.7.cloned.1.call-done = bf16[1280,1024]{1,0:T(8,128)(2,1)} async-done(((bf16[640,1024]{1,0:T(8,128)(2,1)}), bf16[1280,1024]{1,0:T(8,128)(2,1)}) %all-gather.7.cloned.1.call-update) | async-done | bytes 2621456 | tf_op jit(solution)/shard_map/all_gather | solution.py:56
  110.9 6.8 %convolution_convert_fusion.1 = bf16[1024,1024]{1,0:T(8,128)(2,1)} fusion(bf16[1024,1280]{1,0:T(8,128)(2,1)} %bitcast.150, bf16[1280,1024]{1,0:T(8,128)(2,1)} %all-gather.7.cloned.1.call-done), kind=kOutput, calls=%fused_computation.26 | convolution fusion | flops 2685403136 | bytes 7340032 | tf_op jit(solution)/shard_map/dot_general | solution.py:63
  117.7 0.0 reduce-scatter.4.cloned.1.call-update
  117.7 0.0 reduce-scatter.6.cloned.1.call-start
  117.7 33.7 %all-gather.9.cloned.1.call-done = bf16[1280,1024]{1,0:T(8,128)(2,1)} async-done(((bf16[640,1024]{1,0:T(8,128)(2,1)}), bf16[1280,1024]{1,0:T(8,128)(2,1)}) %all-gather.9.cloned.1.call-update) | async-done | bytes 2621456 | tf_op jit(solution)/shard_map/all_gather | solution.py:56
  151.5 6.8 %convolution_convert_fusion = bf16[1024,1024]{1,0:T(8,128)(2,1)} fusion(bf16[1024,1280]{1,0:T(8,128)(2,1)} %bitcast.151, bf16[1280,1024]{1,0:T(8,128)(2,1)} %all-gather.9.cloned.1.call-done), kind=kOutput, calls=%fused_computation.25 | convolution fusion | flops 2685403136 | bytes 7340032 | tf_op jit(solution)/shard_map/dot_general | solution.py:63
  158.2 0.0 reduce-scatter.6.cloned.1.call-update
  158.3 0.0 reduce-scatter.8.cloned.1.call-start
  158.3 0.6 copy-done.18
  158.9 38.6 %reduce-scatter.4.cloned.1.call-done = bf16[256,1024]{1,0:T(8,128)(2,1)} async-done(((bf16[1024,1024]{1,0:T(8,128)(2,1)}), bf16[256,1024]{1,0:T(8,128)(2,1)}) %reduce-scatter.4.cloned.1.call-update) | async-done | bytes 524304 | tf_op jit(solution)/shard_map/reduce_scatter | solution.py:65
  197.5 45.4 %reduce-scatter.6.cloned.1.call-done = bf16[256,1024]{1,0:T(8,128)(2,1)} async-done(((bf16[1024,1024]{1,0:T(8,128)(2,1)}), bf16[256,1024]{1,0:T(8,128)(2,1)}) %reduce-scatter.6.cloned.1.call-update) | async-done | bytes 524304 | tf_op jit(solution)/shard_map/reduce_scatter | solution.py:65
  243.0 1.5 fusion.5
  244.5 6.4 %psum.7 = f32[256]{0:T(256)S(1)} all-reduce(f32[256]{0:T(256)S(1)} %fusion.5), channel_id=1, replica_groups=mesh['seq'=8,'tp'=4] {'tp'}, use_global_device_ids=true, to_apply=%region_7.8 | all-reduce | flops 256 | bytes 2048 | tf_op jit(solution)/shard_map/psum | solution.py:92
  250.9 0.0 copy-start.7
  250.9 0.0 copy-start.15
  250.9 0.0 copy-start.21
  250.9 0.0 copy-start.22
  250.9 4.7 %convolution_convert_fusion.2 = bf16[256,1024]{1,0:T(8,128)(2,1)} fusion(bf16[2048,1024]{1,0:T(8,128)(2,1)} %param.14, f32[256]{0:T(256)S(1)} %add_rsqrt_fusion, f32[2048]{0:T(1024)S(1)} %convert_element_type.45, bf16[256,1024]{1,0:T(8,128)(2,1)} %reduce-scatter.6.cloned.1.call-done, bf16[256,1024]{1,0:T(8,128)(2,1)} %reduce-scatter.4.cloned.1.call-done), kind=kOutput, calls=%fused_computation.30 | convolution fusion | flops 1077673984 | bytes 5776384 | tf_op jit(solution)/shard_map/dot_general | solution.py:97
  255.6 0.0 reduce-scatter.8.cloned.1.call-update
  255.6 0.0 all-gather.11.cloned.1.call-start
  255.7 20.6 %reduce-scatter.8.cloned.1.call-done = bf16[256,256]{1,0:T(8,128)(2,1)} async-done(((bf16[256,1024]{1,0:T(8,128)(2,1)}), bf16[256,256]{1,0:T(8,128)(2,1)}) %reduce-scatter.8.cloned.1.call-update) | async-done | bytes 131088 | tf_op jit(solution)/shard_map/reduce_scatter | solution.py:98
  276.3 0.0 all-gather.11.cloned.1.call-update
  276.3 0.2 reduce-window.8
  276.5 0.2 copy.65
  276.7 31.0 %all_gather.15 = bf16[8,32,256]{2,1,0:T(8,128)(2,1)S(1)} all-gather(bf16[1,32,256]{2,1,0:T(8,128)(2,1)S(1)} %copy-done.15), channel_id=1, replica_groups=mesh['seq'=8,'tp'=4] {'seq'}, dimensions={0}, use_global_device_ids=true | all-gather | bytes 147456 | tf_op jit(solution)/shard_map/all_gather | solution.py:119
  307.7 0.6 gather_fusion
  308.3 0.1 convert_reduce_fusion
  308.4 0.7 fusion.58
  309.1 1.9 fusion.59
  311.0 0.6 iota_compare_fusion.1
  311.6 1.2 fusion.16
  312.7 6.2 %all-gather.11.cloned.1.call-done = bf16[2048,256]{1,0:T(8,128)(2,1)} async-done(((bf16[256,256]{1,0:T(8,128)(2,1)}), bf16[2048,256]{1,0:T(8,128)(2,1)}) %all-gather.11.cloned.1.call-update) | async-done | bytes 1048592 | tf_op jit(solution)/shard_map/all_gather | solution.py:101
  319.0 2.4 gather_fusion.1
  321.4 0.9 reshape_reshape.3
  322.4 0.8 fusion.57
  323.2 3.6 %fusion = (f32[4,8,128]{2,1,0:T(8,128)S(1)}, f32[256,4,128,8]{2,0,3,1:T(8,128)}) fusion(pred[4,256]{1,0:T(4,128)(4,1)} %iota_compare_fusion.1, bf16[256,1,1,128]{3,2,0,1:T(2,128)(2,1)S(1)} %get-tuple-element.22, bf16[4,128,1024]{2,1,0:T(8,128)(2,1)S(1)} %copy-done), kind=kOutput, calls=%fused_computation.4 | convolution fusion | flops 271577088 | bytes 5325824 | tf_op jit(solution)/shard_map/dqhgc,khc->dhgqk/dot_general | solution.py:142
  326.8 0.6 fusion.53
  327.4 0.7 fusion.38
  328.1 1.8 fusion.41
  329.9 0.7 copy.89
  330.7 3.5 %fusion.1 = f32[4,8,128]{2,1,0:T(8,128)S(1)} fusion(f32[256,4,128,8]{2,0,3,1:T(8,128)} %get-tuple-element.28, f32[4,8,128]{2,1,0:T(8,128)} %get-tuple-element.15, pred[4,256]{1,0:T(4,128)(4,1)} %iota_compare_fusion.1), kind=kLoop, calls=%fused_computation.5 | loop fusion | flops 5238784 | bytes 4228096 | tf_op jit(solution)/shard_map/reduce_sum | solution.py:23
  334.3 2.1 fusion.7
  336.4 0.5 fusion.17
  337.0 0.1 copy-done.9
  337.1 0.0 copy-done.14
  337.1 0.9 copy-done.4
  338.0 2.1 fusion.10
  340.1 2.3 copy.75
  (46 shorter events, 0.2 us)
Async XLA Ops:
  7.2 302.0 %copy-start = (bf16[4,128,1024]{2,1,0:T(8,128)(2,1)S(1)}, bf16[4,128,1024]{2,1,0:T(8,128)(2,1)}, u32[]{:S(2)}) copy-start(bf16[4,128,1024]{2,1,0:T(8,128)(2,1)} %param.20) | copy-start | bytes 3145732
  7.2 63.1 %all-gather.5.cloned.1.call-start = ((), (), s32[]{:S(2)}) async-start(), calls=%async_computation.3 | async-start | bytes 3276800 | tf_op jit(solution)/shard_map/all_gather | solution.py:46
  7.2 1.9 collective-permute-start
  9.1 0.8 copy-start.5
  10.0 100.9 %all-gather.7.cloned.1.call-start = ((), (), s32[]{:S(2)}) async-start(), calls=%async_computation.4 | async-start | bytes 3932160 | tf_op jit(solution)/shard_map/all_gather | solution.py:56
  13.6 137.9 %all-gather.9.cloned.1.call-start = ((), (), s32[]{:S(2)}) async-start(), calls=%async_computation.6 | async-start | bytes 3932160 | tf_op jit(solution)/shard_map/all_gather | solution.py:56
  14.3 183.2 %reduce-scatter.4.cloned.1.call-start = ((), (), s32[]{:S(2)}) async-start(), calls=%async_computation.5 | async-start | bytes 2621440 | tf_op jit(solution)/shard_map/reduce_scatter | solution.py:65
  70.3 2.5 copy-start.2
  117.7 125.3 %reduce-scatter.6.cloned.1.call-start = ((), (), s32[]{:S(2)}) async-start(), calls=%async_computation.7 | async-start | bytes 2621440 | tf_op jit(solution)/shard_map/reduce_scatter | solution.py:65
  158.2 0.7 copy-start.18
  158.3 118.0 %reduce-scatter.8.cloned.1.call-start = ((), (), s32[]{:S(2)}) async-start(), calls=%async_computation.8 | async-start | bytes 655360 | tf_op jit(solution)/shard_map/reduce_scatter | solution.py:98
  250.9 25.4 %copy-start.19 = (s32[4]{0:T(128)S(1)}, s32[4]{0:T(128)}, u32[]{:S(2)}) copy-start(s32[4]{0:T(128)} %param.18) | copy-start | bytes 52
  250.9 25.4 %copy-start.20 = (s32[1,4]{1,0:T(1,128)S(1)}, s32[1,4]{1,0:T(1,128)}, u32[]{:S(2)}) copy-start(s32[1,4]{1,0:T(1,128)} %param.17) | copy-start | bytes 52
  250.9 25.6 %copy-start.7 = (bf16[4,128,256]{2,1,0:T(8,128)(2,1)S(1)}, bf16[4,128,256]{2,1,0:T(8,128)(2,1)}, u32[]{:S(2)}) copy-start(bf16[4,128,256]{2,1,0:T(8,128)(2,1)} %param.21) | copy-start | bytes 786436
  250.9 25.8 %copy-start.15 = (bf16[1,32,256]{2,1,0:T(8,128)(2,1)S(1)}, bf16[1,32,256]{2,1,0:T(8,128)(2,1)}, u32[]{:S(2)}) copy-start(bf16[1,32,256]{2,1,0:T(8,128)(2,1)} %param.19) | copy-start | bytes 49156
  250.9 57.4 %copy-start.21 = (s32[32]{0:T(128)S(1)}, s32[32]{0:T(128)}, u32[]{:S(2)}) copy-start(s32[32]{0:T(128)} %param.16) | copy-start | bytes 388
  250.9 57.4 %copy-start.22 = (s32[32,1]{0,1:T(1,128)S(1)}, s32[32,1]{0,1:T(1,128)}, u32[]{:S(2)}) copy-start(s32[32,1]{0,1:T(1,128)} %param.15) | copy-start | bytes 388
  255.6 63.3 %all-gather.11.cloned.1.call-start = ((), (), s32[]{:S(2)}) async-start(), calls=%async_computation.9 | async-start | bytes 1179648 | tf_op jit(solution)/shard_map/all_gather | solution.py:101
  323.2 3.6 %copy-start.8 = (f32[4,8,128]{2,1,0:T(8,128)S(1)}, f32[4,8,128]{2,1,0:T(8,128)}, u32[]{:S(2)}) copy-start(f32[4,8,128]{2,1,0:T(8,128)} %get-tuple-element.31) | copy-start | bytes 49156
  323.2 3.6 %copy-start.13 = (f32[4,8,128]{2,1,0:T(8,128)S(1)}, f32[4,8,128]{2,1,0:T(8,128)}, u32[]{:S(2)}) copy-start(f32[4,8,128]{2,1,0:T(8,128)} %get-tuple-element.29) | copy-start | bytes 49156
  323.2 4.2 %copy-start.3 = (f32[4,1,8,128,32]{3,4,2,0,1:T(8,128)S(1)}, f32[4,1,8,128,32]{3,4,2,0,1:T(8,128)}, u32[]{:S(2)}) copy-start(f32[4,1,8,128,32]{3,4,2,0,1:T(8,128)} %get-tuple-element.32) | copy-start | bytes 1572868
  323.2 4.9 %copy-start.12 = (bf16[4,32,1,1,128]{4,3,1,0,2:T(2,128)(2,1)S(1)}, bf16[4,32,1,1,128]{4,3,1,0,2:T(2,128)(2,1)}, u32[]{:S(2)}) copy-start(bf16[4,32,1,1,128]{4,3,1,0,2:T(2,128)(2,1)} %get-tuple-element.23) | copy-start | bytes 98308
  326.8 3.2 copy-start.6
  330.7 3.5 %copy-start.1 = (f32[256,4,128,8]{2,0,3,1:T(8,128)S(1)}, f32[256,4,128,8]{2,0,3,1:T(8,128)}, u32[]{:S(2)}) copy-start(f32[256,4,128,8]{2,0,3,1:T(8,128)} %get-tuple-element.28) | copy-start | bytes 12582916
  330.7 3.6 %copy-start.11 = (f32[4,8,128]{2,1,0:T(8,128)S(1)}, f32[4,8,128]{2,1,0:T(8,128)}, u32[]{:S(2)}) copy-start(f32[4,8,128]{2,1,0:T(8,128)} %get-tuple-element.15) | copy-start | bytes 49156
  330.7 3.6 %copy-start.17 = (pred[4,256]{1,0:T(4,128)(4,1)S(1)}, pred[4,256]{1,0:T(4,128)(4,1)}, u32[]{:S(2)}) copy-start(pred[4,256]{1,0:T(4,128)(4,1)} %iota_compare_fusion.1) | copy-start | bytes 3076
  334.3 2.2 copy-start.10
  336.4 0.7 copy-start.9
  336.4 0.7 copy-start.14
  336.4 1.6 copy-start.4
  336.4 1.6 copy-start.16
Sparse Core Ops, SparseCore 0:
  10.1 60.0 all-gather.4
  71.8 39.0 all-gather.6
  112.4 39.0 all-gather.8
  153.6 43.8 reduce-scatter.3
  199.8 43.1 reduce-scatter.5
  255.7 20.4 reduce-scatter.7
  278.6 40.3 all-gather.10

commit v2 on v0

v2 whole, which is shorter than its diff:
```python
import functools

import jax
import jax.numpy as jnp
from jax import lax
from jax.experimental import pallas as pl
from jax.experimental.pallas import tpu as pltpu
from jax.sharding import PartitionSpec as P

D = 8192
HD = 128
GROUP = 8
MOST_PAGES = 16
CHUNKS = 4
VMEM = 48 * 1024 * 1024


def bits_of(count):
    return [1 << bit for bit in range(count.bit_length() - 1)]


def flip(value, axis, bit):
    count = lax.axis_size(axis)
    return lax.ppermute(value, axis, [(i, i ^ bit) for i in range(count)])


def transpose_panels(local):
    seq_count, tp_count = lax.axis_size("seq"), lax.axis_size("tp")
    width = seq_count // tp_count
    half = tp_count // 2
    pairs = []
    for origin in range(tp_count):
        for inner in range(width):
            for block in range(tp_count):
                source = (origin * width + inner) * tp_count + block
                slot = ((origin ^ block) & 1) * half + origin // 2
                pairs.append((source, (block * width + inner) * tp_count + slot))
    held = lax.ppermute(local, ("seq", "tp"), pairs)[None]
    bits = bits_of(tp_count)
    for bit in bits[-1:] + bits[:-1]:
        held = jnp.concatenate([held, flip(held, "tp", bit)], axis=0)
    group = lax.axis_index("seq") // width
    place = lax.axis_index("tp")
    base = 2 * (place % half) + ((place // half) ^ (group & 1))
    return held, base


def partial_kernel(base_ref, rows_ref, weights_ref, out_ref):
    out_ref[0] = jnp.dot(rows_ref[0], weights_ref[...], preferred_element_type=jnp.float32)


def partial_products(base, held, weights):
    groups, rows, depth = held.shape
    columns = weights.shape[1]
    return pl.pallas_call(
        partial_kernel,
        grid_spec=pltpu.PrefetchScalarGridSpec(
            num_scalar_prefetch=1,
            grid=(groups,),
            in_specs=[
                pl.BlockSpec((1, rows, depth), lambda i, base: (base[0] ^ i, 0, 0)),
                pl.BlockSpec((depth, columns), lambda i, base: (0, 0)),
            ],
            out_specs=pl.BlockSpec((1, rows, columns), lambda i, base: (i, 0, 0)),
        ),
        out_shape=jax.ShapeDtypeStruct((groups, rows, columns), jnp.float32),
        compiler_params=pltpu.CompilerParams(vmem_limit_bytes=VMEM),
        cost_estimate=pl.CostEstimate(
            flops=2 * groups * rows * depth * columns,
            bytes_accessed=2 * (groups * rows * depth + depth * columns)
            + 4 * groups * rows * columns,
            transcendentals=0,
        ),
    )(base.reshape(1).astype(jnp.int32), held, weights)


def reduce_groups(parts):
    seq_count, tp_count = lax.axis_size("seq"), lax.axis_size("tp")
    width = seq_count // tp_count
    group = lax.axis_index("seq") // width
    total = lax.dynamic_index_in_dim(parts, group, 0, keepdims=False)
    for sign in (1, -1):
        carried = None
        for reach in range(tp_count - 1, 0, -1):
            target = jnp.clip(group + sign * reach, 0, tp_count - 1)
            block = lax.dynamic_index_in_dim(parts, target, 0, keepdims=False)
            if carried is not None:
                block = block + carried.astype(jnp.float32)
            pairs = []
            for origin in range(tp_count):
                if 0 <= origin + sign * reach < tp_count:
                    for inner in range(width):
                        source = origin * width + inner
                        pairs.append((source, source + sign * width))
            carried = lax.ppermute(block.astype(jnp.bfloat16), "seq", pairs)
        total = total + carried.astype(jnp.float32)
    return total.astype(jnp.bfloat16)


def merge_tiles(panels, w_merge, ln_gain, w_kv):
    seq_count, tp_count = lax.axis_size("seq"), lax.axis_size("tp")
    width = seq_count // tp_count
    tiles, panel_rows, depth = panels.shape
    share = w_merge.shape[0]
    inner = lax.axis_index("seq") % width
    local = panels.reshape(tiles * panel_rows, depth)
    turned = lax.dynamic_slice_in_dim(
        jnp.concatenate([local, local], axis=1), inner * share, depth, axis=1
    )
    held, base = transpose_panels(turned)
    columns = w_merge.shape[1] // CHUNKS
    kv = 0.0
    squares = 0.0
    for chunk in range(CHUNKS):
        own = w_merge[:, chunk * columns : (chunk + 1) * columns]
        pieces = [own]
        for offset in range(1, width):
            pairs = [
                (g * width + (i + offset) % width, g * width + i)
                for g in range(tp_count)
                for i in range(width)
            ]
            pieces.append(lax.ppermute(own, "seq", pairs))
        parts = partial_products(base, held, jnp.concatenate(pieces, axis=0))
        merged = reduce_groups(parts).astype(jnp.float32)
        squares = squares + jnp.sum(merged * merged, axis=1)
        gain = ln_gain[chunk * columns : (chunk + 1) * columns].astype(jnp.float32)
        kv = kv + jnp.dot(
            (merged * gain[None, :]).astype(jnp.bfloat16),
            w_kv[chunk * columns : (chunk + 1) * columns],
            preferred_element_type=jnp.float32,
        )
    return kv, squares


def scatter_heads(kv, squares):
    tp_count = lax.axis_size("tp")
    place = lax.axis_index("tp")
    rows = kv.shape[0]
    blocks = jnp.stack(jnp.split(kv, tp_count, axis=1))
    for bit in bits_of(tp_count):
        paired = blocks.reshape(blocks.shape[0] // 2, 2, rows, blocks.shape[2])
        mine = (place // bit) % 2
        keep = lax.dynamic_index_in_dim(paired, mine, 1, keepdims=False)
        give = lax.dynamic_index_in_dim(paired, 1 - mine, 1, keepdims=False)
        blocks = keep + flip(give.astype(jnp.bfloat16), "tp", bit).astype(jnp.float32)
        squares = squares + flip(squares, "tp", bit)
    return blocks[0], squares


def share_small(prefix_cache, sources, tiles):
    rows = prefix_cache.shape[1]
    width = prefix_cache.shape[2]
    asks = jnp.stack([sources, tiles]).astype(jnp.bfloat16)
    asks = jnp.pad(asks, ((0, 14), (0, width - asks.shape[1])))
    held = jnp.concatenate([prefix_cache[0], asks], axis=0)[None]
    for bit in bits_of(lax.axis_size("seq")):
        held = jnp.concatenate([held, flip(held, "seq", bit)], axis=0)
    count = sources.shape[0]
    prefixes = held[:, :rows]
    asked_sources = held[:, rows, :count].astype(jnp.int32)
    asked_tiles = held[:, rows + 1, :count].astype(jnp.int32)
    return prefixes, asked_sources, asked_tiles


def attend_kernel(
    place_ref, query_ref, prefix_ref, text_ref, pages_ref, pick_ref, seen_ref, all_ref, out_ref, vision_ref
):
    pages = pages_ref[...]
    count = pages.shape[0]

    def pick(index):
        one_hot = lax.broadcasted_iota(jnp.int32, (index.shape[0], count), 1) == index
        one_hot = jnp.where(one_hot, 1.0, 0.0).astype(jnp.bfloat16)
        return jnp.dot(one_hot, pages, preferred_element_type=jnp.float32).astype(jnp.bfloat16)

    @pl.when(pl.program_id(0) == 0)
    def _():
        vision_ref[...] = pick(all_ref[...])

    window = pick(pick_ref[0])
    keys_values = jnp.concatenate([prefix_ref[0], window, text_ref[0]], axis=0)
    text_rows = text_ref.shape[1]
    heads = keys_values.shape[1] // (2 * HD)
    query = query_ref[0]
    for head in range(heads):
        keys = keys_values[:, 2 * head * HD : (2 * head + 1) * HD]
        values = keys_values[:, (2 * head + 1) * HD : (2 * head + 2) * HD]
        stacked = jnp.concatenate(
            [
                query[:, (head * GROUP + a) * HD : (head * GROUP + a + 1) * HD]
                for a in range(GROUP)
            ],
            axis=0,
        )
        scores = lax.dot_general(
            stacked, keys, (((1,), (1,)), ((), ())), preferred_element_type=jnp.float32
        ) * (HD**-0.5)
        row = lax.broadcasted_iota(jnp.int32, scores.shape, 0) % text_rows
        column = lax.broadcasted_iota(jnp.int32, scores.shape, 1)
        text_column = column - (scores.shape[1] - text_rows)
        allowed = (text_column <= row) & (seen_ref[0] > 0)
        scores = jnp.where(allowed, scores, -1e30)
        best = jnp.max(scores, axis=1, keepdims=True)
        weights = jnp.exp(scores - best)
        total = jnp.sum(weights, axis=1, keepdims=True)
        result = jnp.dot(weights.astype(jnp.bfloat16), values, preferred_element_type=jnp.float32)
        result = (result / total).astype(jnp.bfloat16)
        for a in range(GROUP):
            out_ref[0, :, (head * GROUP + a) * HD : (head * GROUP + a + 1) * HD] = result[
                a * text_rows : (a + 1) * text_rows
            ]


def attend(place, queries, prefixes, text_kv, pages, picks, seen, all_rows):
    docs, rows, width = queries.shape
    kv_width = text_kv.shape[2]
    vision_rows = all_rows.shape[0]
    keys = seen.shape[2]
    return pl.pallas_call(
        attend_kernel,
        grid_spec=pltpu.PrefetchScalarGridSpec(
            num_scalar_prefetch=1,
            grid=(docs,),
            in_specs=[
                pl.BlockSpec((1, rows, width), lambda d, place: (d, 0, 0)),
                pl.BlockSpec((1,) + prefixes.shape[1:], lambda d, place: (place[d], 0, 0)),
                pl.BlockSpec((1, rows, kv_width), lambda d, place: (d, 0, 0)),
                pl.BlockSpec(pages.shape, lambda d, place: (0, 0)),
                pl.BlockSpec((1,) + picks.shape[1:], lambda d, place: (d, 0, 0)),
                pl.BlockSpec((1, 1, keys), lambda d, place: (d, 0, 0)),
                pl.BlockSpec(all_rows.shape, lambda d, place: (0, 0)),
            ],
            out_specs=[
                pl.BlockSpec((1, rows, width), lambda d, place: (d, 0, 0)),
                pl.BlockSpec((vision_rows, kv_width), lambda d, place: (0, 0)),
            ],
        ),
        out_shape=[
            jax.ShapeDtypeStruct(queries.shape, jnp.bfloat16),
            jax.ShapeDtypeStruct((vision_rows, kv_width), jnp.bfloat16),
        ],
        compiler_params=pltpu.CompilerParams(vmem_limit_bytes=VMEM),
        cost_estimate=pl.CostEstimate(
            flops=4 * docs * rows * width * keys,
            bytes_accessed=8 * docs * rows * width,
            transcendentals=docs * rows * keys * width // HD,
        ),
    )(place, queries, prefixes, text_kv, pages, picks, seen, all_rows)


def shards(
    panels,
    w_merge,
    ln_gain,
    w_kv,
    page_src,
    page_tile,
    doc_pages,
    prefix_id,
    prefix_cache,
    queries,
    text_kv,
):
    seq_count = lax.axis_size("seq")
    holder = lax.axis_index("seq")
    tile_count, panel_rows, _ = panels.shape
    page_count = page_src.shape[0]
    capacity = max(2, 2 * page_count // seq_count)
    sources = page_src[:, 0]

    prefixes, asked_sources, asked_tiles = share_small(prefix_cache, sources, page_tile)
    asked = (asked_sources == holder).astype(jnp.int32)
    order = jnp.cumsum(asked, axis=1) - 1
    slots = jnp.arange(capacity, dtype=jnp.int32)
    picked = asked[:, None, :] * (order[:, None, :] == slots[None, :, None]).astype(jnp.int32)
    wanted = jnp.sum(picked * asked_tiles[:, None, :], axis=2)
    wanted = wanted[jnp.arange(seq_count, dtype=jnp.int32) ^ holder]
    within = jnp.arange(panel_rows, dtype=jnp.int32)
    wanted_rows = (wanted.reshape(-1, 1) * panel_rows + within[None, :]).reshape(-1)
    chooser = wanted_rows[:, None] == jnp.arange(tile_count * panel_rows, dtype=jnp.int32)[None, :]
    chooser = chooser.astype(jnp.bfloat16)

    position = jnp.arange(page_count, dtype=jnp.int32)
    earlier = (sources[:, None] == sources[None, :]) & (position[None, :] < position[:, None])
    rank = jnp.sum(earlier.astype(jnp.int32), axis=1)
    arrival = sources * capacity + rank
    all_rows = (arrival[:, None] * panel_rows + within[None, :]).reshape(-1, 1)
    lengths = doc_pages[0]
    starts = jnp.cumsum(lengths) - lengths
    step = jnp.arange(MOST_PAGES, dtype=jnp.int32)
    inside = step[None, :] < lengths[:, None]
    page = jnp.minimum(starts[:, None] + step[None, :], page_count - 1)
    doc_rows = arrival[page][:, :, None] * panel_rows + within[None, None, :]
    doc_rows = jnp.where(inside[:, :, None], doc_rows, -1)
    doc_count, query_rows, _ = queries.shape
    picks = doc_rows.reshape(doc_count, -1, 1)
    seen = jnp.concatenate(
        [
            jnp.ones((doc_count, prefixes.shape[1]), jnp.int32),
            (doc_rows >= 0).reshape(doc_count, -1).astype(jnp.int32),
            jnp.ones((doc_count, query_rows), jnp.int32),
        ],
        axis=1,
    )[:, None, :]

    kv, squares = merge_tiles(panels, w_merge, ln_gain, w_kv)
    kv, squares = scatter_heads(kv, squares)
    row_scale = lax.rsqrt(squares / D + 1e-06)
    tile_kv = (kv * row_scale[:, None]).astype(jnp.bfloat16)
    outgoing = jnp.dot(chooser, tile_kv, preferred_element_type=jnp.float32).astype(jnp.bfloat16)
    pages = lax.all_to_all(outgoing, "seq", split_axis=0, concat_axis=0, tiled=True)
    attended, vision_kv = attend(
        prefix_id ^ holder, queries, prefixes, text_kv, pages, picks, seen, all_rows
    )
    return (attended, vision_kv)


def solution(mesh):
    return jax.shard_map(
        shards,
        mesh=mesh,
        in_specs=(
            P("seq", None, "tp"),
            P("seq", "tp"),
            P("tp"),
            P("tp", None),
            P("seq", None),
            P("seq"),
            P("seq", None),
            P("seq"),
            P("seq", None, "tp"),
            P("seq", None, "tp"),
            P("seq", None, "tp"),
        ),
        out_specs=(P("seq", None, "tp"), P("seq", "tp")),
        check_vma=False,
    )
```

time: 568 us -> 208 us (0.37)
  waiting for transfers between devices: 456 us -> 81.7 us
  starting transfers between devices: 3.69 us -> 87.1 us
  blocking collectives: 50.4 us -> 0 us
  matrix products: 25.8 us -> 2.79 us
  between operations: 15.3 us -> 1.46 us
  Pallas kernels: 0 us -> 13.7 us
  other arithmetic: 3.53 us -> 14.7 us
  local copies, waits for them, and re-layouts: 12.7 us -> 5.77 us
    all_gather x2 -> x0, waiting for transfers between devices: 427 us -> none  [the longest x1 403 us: merge_rows(): lax.all_gather(w_merge, 'seq', axis=0, tiled=True)]
    ppermute x0 -> x38, starting transfers between devices: none -> 83.7 us  [the longest x24 63.3 us: reduce_groups(): carried = lax.ppermute(block.astype(jnp.bfloat16), 'seq', pairs)]
    ppermute x0 -> x38, waiting for transfers between devices: none -> 73.9 us  [the longest x9 57 us: flip(): return lax.ppermute(value, axis, [(i, i ^ bit) for i in range(count)])]
    all_gather x1 -> x0, blocking collectives: 30.5 us -> none  [shards(): piece = lax.all_gather(prefix_cache, 'seq', axis=0, tiled=True)]
    dot_general x8 -> x5, matrix products: 25.8 us -> 2.79 us  [the longest x4 1.77 us: merge_tiles(): jnp.dot((merged * gain[None, :]).astype(jnp.bfloat16), w_kv[chunk * colum...]
    all_to_all x1, waiting for transfers between devices: 28.6 us -> 7.84 us  [shards(): lax.all_to_all(outgoing, 'seq', split_axis=0, concat_axis=0, tiled=True)]
    pallas_call x0 -> x5, Pallas kernels: none -> 13.7 us  [the longest x4 8.15 us: partial_products(): pl.pallas_call(partial_kernel, grid_spec=pltpu.PrefetchScalarGridSpec(num...]
    unnamed x1 -> x0, blocking collectives: 13.1 us -> none
  transfers between devices with their start and end apart: 4 -> 39, of which waited for: 3 -> 15; matrix products, arithmetic and copies ran while one was open for 2% -> 8% of each run, Pallas kernels for 0% -> 3%
where the time goes in v2:
time: 208 us; the launch traced here: 207 us
  starting transfers between devices  87.1 us (42%)
  waiting for transfers between devices  81.7 us (39%)
  other arithmetic  14.7 us (7%)
  Pallas kernels  13.7 us (7%)
  local copies, waits for them, and re-layouts  5.77 us (3%)
  matrix products  2.79 us (1%)
    ppermute x24, starting transfers between devices, reduce_groups(): carried = lax.ppermute(block.astype(jnp.bfloat16), 'seq', pairs)  63.3 us
    ppermute x9, waiting for transfers between devices, flip(): return lax.ppermute(value, axis, [(i, i ^ bit) for i in range(count)])  57 us
    ppermute x24, waiting for transfers between devices, reduce_groups(): carried = lax.ppermute(block.astype(jnp.bfloat16), 'seq', pairs)  16.9 us
    ppermute x9, starting transfers between devices, flip(): return lax.ppermute(value, axis, [(i, i ^ bit) for i in range(count)])  12 us
    pallas_call x4, Pallas kernels, partial_products(): pl.pallas_call(partial_kernel, grid_spec=pltpu.PrefetchScalarGridSpec(num...  8.15 us
    all_to_all x1, waiting for transfers between devices, shards(): lax.all_to_all(outgoing, 'seq', split_axis=0, concat_axis=0, tiled=True)  7.84 us
    ppermute x4, starting transfers between devices, merge_tiles(): pieces.append(lax.ppermute(own, 'seq', pairs))  6.45 us
    pallas_call x1, Pallas kernels, attend(): pl.pallas_call(attend_kernel, grid_spec=pltpu.PrefetchScalarGridSpec(num_...  5.5 us
  transfers between devices with their start and end apart: 39, of which 15 were waited for; matrix products, arithmetic and copies ran while one was open for 8% of the time, Pallas kernels for 3%

profile of v2, /device:TPU:0, one launch (start us, length us, event | category | flops | bytes accessed | tf_op | source)
XLA Modules:
  0.0 207.2 jit_solution(15414268794165795985)
XLA Ops:
  0.6 2.2 %fusion.5 = bf16[256,1280]{1,0:T(8,128)(2,1)} fusion(s32[]{:T(128)S(6)} %select_n.117, bf16[256,1280]{1,0:T(8,128)(2,1)} %bitcast.165), kind=kLoop, calls=%fused_computation.28 | loop fusion | flops 1310720 | bytes 1310724 | tf_op jit(solution)/shard_map/concatenate | solution.py:108
  2.8 1.9 collective-permute-start.3
  4.7 2.7 %fusion.75 = (bf16[640,512]{1,0:T(8,128)(2,1)}, bf16[640,512]{1,0:T(8,128)(2,1)S(1)}, bf16[640,512]{1,0:T(8,128)(2,1)S(1)}, bf16[640,512]{1,0:T(8,128)(2,1)S(1)}) fusion(bf16[640,2048]{1,0:T(8,128)(2,1)} %param.12), kind=kLoop, calls=%fused_computation.164 | loop fusion | bytes 5242880 | tf_op jit(solution)/shard_map/slice | solution.py:115
  7.4 2.9 %collective-permute-start.27 = (bf16[640,512]{1,0:T(8,128)(2,1)}, bf16[640,512]{1,0:T(8,128)(2,1)}, u32[]{:S(2)}, u32[]{:S(2)}) collective-permute-start(bf16[640,512]{1,0:T(8,128)(2,1)} %get-tuple-element.10), channel_id=1, source_target_pairs={{4,0},{0,4},{12,8},{8,12},{20,16},{16,20},{28,24},{24,28},{5,1},{1... | collective-permute-start | bytes 1966088 | tf_op jit(solution)/shard_map/ppermute | solution.py:123
  10.4 2.0 collective-permute-start.13
  13.1 0.8 gather_fusion.1
  14.8 37.6 %collective-permute-done = bf16[1,48,256]{2,1,0:T(8,128)(2,1)S(1)} collective-permute-done((bf16[1,48,256]{2,1,0:T(8,128)(2,1)S(1)}, bf16[1,48,256]{2,1,0:T(8,128)(2,1)S(1)}, u32[]{:S(2)}, u32[]{:S(2)}) %collective-permute-start) | collective-permute-done | bytes 24608 | tf_op jit(solution)/shard_map/ppermute | solution.py:24
  52.4 4.2 %collective-permute-start.1 = (bf16[2,48,256]{2,1,0:T(8,128)(2,1)S(1)}, bf16[2,48,256]{2,1,0:T(8,128)(2,1)S(1)}, u32[]{:S(2)}, u32[]{:S(2)}) collective-permute-start(bf16[2,48,256]{2,1,0:T(8,128)(2,1)S(1)} %pad_maximum_fusion.9), channel_id=1, source_target_pairs={{0,8},{4,12},{8,0},{12,4},{16,24},{20,28},{24,16},{28,20},{1,9},{5... | collective-permute-start | bytes 147464 | tf_op jit(solution)/shard_map/ppermute | solution.py:24
  56.6 2.1 collective-permute-done.1
  58.7 3.6 %collective-permute-start.2 = (bf16[4,48,256]{2,1,0:T(8,128)(2,1)S(1)}, bf16[4,48,256]{2,1,0:T(8,128)(2,1)S(1)}, u32[]{:S(2)}, u32[]{:S(2)}) collective-permute-start(bf16[4,48,256]{2,1,0:T(8,128)(2,1)S(1)} %pad_maximum_fusion.8), channel_id=1, source_target_pairs={{0,16},{4,20},{8,24},{12,28},{16,0},{20,4},{24,8},{28,12},{1,17},{... | collective-permute-start | bytes 294920 | tf_op jit(solution)/shard_map/ppermute | solution.py:24
  62.2 1.4 collective-permute-start.4
  63.6 2.3 %collective-permute-done.2 = bf16[4,48,256]{2,1,0:T(8,128)(2,1)S(1)} collective-permute-done((bf16[4,48,256]{2,1,0:T(8,128)(2,1)S(1)}, bf16[4,48,256]{2,1,0:T(8,128)(2,1)S(1)}, u32[]{:S(2)}, u32[]{:S(2)}) %collective-permute-start.2) | collective-permute-done | bytes 98336 | tf_op jit(solution)/shard_map/ppermute | solution.py:24
  65.9 1.5 collective-permute-start.6
  67.9 0.6 gather_fusion
  68.5 9.2 %collective-permute-done.4 = bf16[1,256,1280]{2,1,0:T(8,128)(2,1)} collective-permute-done((bf16[1,256,1280]{2,1,0:T(8,128)(2,1)S(1)}, bf16[1,256,1280]{2,1,0:T(8,128)(2,1)}, u32[]{:S(2)}, u32[]{:S(2)}) %collective-permute-start.4) | collective-permute-done | bytes 655392 | tf_op jit(solution)/shard_map/ppermute | solution.py:24
  77.6 2.3 %pad_maximum_fusion.1 = bf16[2,256,1280]{2,1,0:T(8,128)(2,1)} fusion(bf16[1,256,1280]{2,1,0:T(8,128)(2,1)} %collective-permute-done.4, bf16[1,256,1280]{2,1,0:T(8,128)(2,1)S(1)} %bitcast.163), kind=kLoop, calls=%fused_computation.8 | loop fusion | flops 655360 | bytes 2621440 | tf_op jit(solution)/shard_map/concatenate | solution.py:41
  80.0 1.4 pad_maximum_fusion.5.weights_ref
  81.4 1.2 pad_maximum_fusion.4.weights_ref
  82.6 1.2 pad_maximum_fusion.3.weights_ref
  83.8 1.2 pad_maximum_fusion.2.weights_ref
  85.0 1.7 pad_maximum_fusion.rows_ref
  86.7 2.0 shard_map.125
  88.8 2.6 %collective-permute-start.28 = (bf16[256,512]{1,0:T(8,128)(2,1)S(1)}, bf16[256,512]{1,0:T(8,128)(2,1)S(1)}, u32[]{:S(2)}, u32[]{:S(2)}) collective-permute-start(bf16[256,512]{1,0:T(8,128)(2,1)S(1)} %get-tuple-element.16), channel_id=1, source_target_pairs={{0,8},{4,12},{1,9},{5,13},{2,10},{6,14},{3,11},{7,15}} | collective-permute-start | bytes 786440 | tf_op jit(solution)/shard_map/ppermute | solution.py:95
  91.4 0.7 collective-permute-start.31
  92.1 2.0 shard_map.124
  94.2 1.3 collective-permute-start.21
  95.5 0.7 collective-permute-start.24
  96.2 2.0 shard_map.123
  98.3 1.3 collective-permute-start.14
  99.6 2.0 shard_map.122
  101.8 0.7 collective-permute-start.17
  102.6 1.0 collective-permute-done.21
  103.6 4.4 %collective-permute-start.7 = (bf16[256,512]{1,0:T(8,128)(2,1)S(1)}, bf16[256,512]{1,0:T(8,128)(2,1)S(1)}, u32[]{:S(2)}, u32[]{:S(2)}) collective-permute-start(bf16[256,512]{1,0:T(8,128)(2,1)S(1)} %get-tuple-element.28), channel_id=1, source_target_pairs={{0,8},{4,12},{1,9},{5,13},{2,10},{6,14},{3,11},{7,15}} | collective-permute-start | bytes 786440 | tf_op jit(solution)/shard_map/ppermute | solution.py:95
  108.1 1.1 collective-permute-done.14
  109.2 4.4 %collective-permute-start.29 = (bf16[256,512]{1,0:T(8,128)(2,1)S(1)}, bf16[256,512]{1,0:T(8,128)(2,1)S(1)}, u32[]{:S(2)}, u32[]{:S(2)}) collective-permute-start(bf16[256,512]{1,0:T(8,128)(2,1)S(1)} %fusion.16), channel_id=1, source_target_pairs={{0,8},{4,12},{8,16},{12,20},{1,9},{5,13},{9,17},{13,21},{2,10},{6,... | collective-permute-start | bytes 786440 | tf_op jit(solution)/shard_map/ppermute | solution.py:95
  113.7 1.1 collective-permute-done.7
  114.8 4.4 %collective-permute-start.22 = (bf16[256,512]{1,0:T(8,128)(2,1)S(1)}, bf16[256,512]{1,0:T(8,128)(2,1)S(1)}, u32[]{:S(2)}, u32[]{:S(2)}) collective-permute-start(bf16[256,512]{1,0:T(8,128)(2,1)S(1)} %fusion.22), channel_id=1, source_target_pairs={{0,8},{4,12},{8,16},{12,20},{1,9},{5,13},{9,17},{13,21},{2,10},{6,... | collective-permute-start | bytes 786440 | tf_op jit(solution)/shard_map/ppermute | solution.py:95
  119.3 0.7 collective-permute-start.10
  120.5 4.4 %collective-permute-start.8 = (bf16[256,512]{1,0:T(8,128)(2,1)S(1)}, bf16[256,512]{1,0:T(8,128)(2,1)S(1)}, u32[]{:S(2)}, u32[]{:S(2)}) collective-permute-start(bf16[256,512]{1,0:T(8,128)(2,1)S(1)} %fusion.34), channel_id=1, source_target_pairs={{0,8},{4,12},{8,16},{12,20},{1,9},{5,13},{9,17},{13,21},{2,10},{6,... | collective-permute-start | bytes 786440 | tf_op jit(solution)/shard_map/ppermute | solution.py:95
  125.0 1.9 collective-permute-start.15
  127.0 0.7 collective-permute-start.32
  127.8 4.1 %collective-permute-start.30 = (bf16[256,512]{1,0:T(8,128)(2,1)S(1)}, bf16[256,512]{1,0:T(8,128)(2,1)S(1)}, u32[]{:S(2)}, u32[]{:S(2)}) collective-permute-start(bf16[256,512]{1,0:T(8,128)(2,1)S(1)} %get-tuple-element.14), channel_id=1, source_target_pairs={{0,8},{4,12},{8,16},{12,20},{16,24},{20,28},{1,9},{5,13},{9,17},{1... | collective-permute-start | bytes 786440 | tf_op jit(solution)/shard_map/ppermute | solution.py:95
  132.0 0.7 collective-permute-start.25
  132.8 5.2 %collective-permute-start.23 = (bf16[256,512]{1,0:T(8,128)(2,1)S(1)}, bf16[256,512]{1,0:T(8,128)(2,1)S(1)}, u32[]{:S(2)}, u32[]{:S(2)}) collective-permute-start(bf16[256,512]{1,0:T(8,128)(2,1)S(1)} %get-tuple-element.18), channel_id=1, source_target_pairs={{0,8},{4,12},{8,16},{12,20},{16,24},{20,28},{1,9},{5,13},{9,17},{1... | collective-permute-start | bytes 786440 | tf_op jit(solution)/shard_map/ppermute | solution.py:95
  138.0 0.7 collective-permute-start.11
  138.9 0.7 collective-permute-start.18
  139.7 14.3 %collective-permute-start.9 = (bf16[256,512]{1,0:T(8,128)(2,1)S(1)}, bf16[256,512]{1,0:T(8,128)(2,1)S(1)}, u32[]{:S(2)}, u32[]{:S(2)}) collective-permute-start(bf16[256,512]{1,0:T(8,128)(2,1)S(1)} %get-tuple-element.26), channel_id=1, source_target_pairs={{0,8},{4,12},{8,16},{12,20},{16,24},{20,28},{1,9},{5,13},{9,17},{1... | collective-permute-start | bytes 786440 | tf_op jit(solution)/shard_map/ppermute | solution.py:95
  154.1 1.3 collective-permute-start.12
  155.5 4.6 %collective-permute-start.16 = (bf16[256,512]{1,0:T(8,128)(2,1)S(1)}, bf16[256,512]{1,0:T(8,128)(2,1)S(1)}, u32[]{:S(2)}, u32[]{:S(2)}) collective-permute-start(bf16[256,512]{1,0:T(8,128)(2,1)S(1)} %get-tuple-element.22), channel_id=1, source_target_pairs={{0,8},{4,12},{8,16},{12,20},{16,24},{20,28},{1,9},{5,13},{9,17},{1... | collective-permute-start | bytes 786440 | tf_op jit(solution)/shard_map/ppermute | solution.py:95
  160.1 1.3 collective-permute-start.33
  161.4 3.7 %collective-permute-done.12 = bf16[256,512]{1,0:T(8,128)(2,1)S(1)} collective-permute-done((bf16[256,512]{1,0:T(8,128)(2,1)S(1)}, bf16[256,512]{1,0:T(8,128)(2,1)S(1)}, u32[]{:S(2)}, u32[]{:S(2)}) %collective-permute-start.12) | collective-permute-done | bytes 262176 | tf_op jit(solution)/shard_map/ppermute | solution.py:95
  165.1 1.3 collective-permute-start.19
  167.0 1.3 collective-permute-start.26
  168.3 7.3 %collective-permute-done.19 = bf16[256,512]{1,0:T(8,128)(2,1)S(1)} collective-permute-done((bf16[256,512]{1,0:T(8,128)(2,1)S(1)}, bf16[256,512]{1,0:T(8,128)(2,1)S(1)}, u32[]{:S(2)}, u32[]{:S(2)}) %collective-permute-start.19) | collective-permute-done | bytes 262176 | tf_op jit(solution)/shard_map/ppermute | solution.py:95
  176.3 2.2 %collective-permute-done.26 = bf16[256,512]{1,0:T(8,128)(2,1)S(1)} collective-permute-done((bf16[256,512]{1,0:T(8,128)(2,1)S(1)}, bf16[256,512]{1,0:T(8,128)(2,1)S(1)}, u32[]{:S(2)}, u32[]{:S(2)}) %collective-permute-start.26) | collective-permute-done | bytes 262176 | tf_op jit(solution)/shard_map/ppermute | solution.py:95
  180.1 0.5 collective-permute-start.36
  180.7 0.9 collective-permute-done.36
  181.6 1.8 collective-permute-start.37
  183.8 1.4 collective-permute-done.37
  185.2 3.6 %collective-permute-done.35 = bf16[1,256,256]{2,1,0:T(8,128)(2,1)S(1)} collective-permute-done((bf16[1,256,256]{2,1,0:T(8,128)(2,1)S(1)}, bf16[1,256,256]{2,1,0:T(8,128)(2,1)S(1)}, u32[]{:S(2)}, u32[]{:S(2)}) %collective-permute-start.35) | collective-permute-done | bytes 131104 | tf_op jit(solution)/shard_map/ppermute | solution.py:24
  188.8 1.0 convolution_convert_fusion
  189.8 3.4 %all-to-all-start = ((bf16[8,64,256]{2,1,0:T(8,128)(2,1)}), bf16[8,64,256]{2,1,0:T(8,128)(2,1)S(1)}, u32[]{:S(2)}, u32[]{:S(2)}) async-start(bf16[8,64,256]{2,1,0:T(8,128)(2,1)} %bitcast.46), calls=%async_computation | async-start | bytes 524288 | tf_op jit(solution)/shard_map/all_to_all | solution.py:312
  193.8 7.8 %all-to-all-done = bf16[8,64,256]{2,1,0:T(8,128)(2,1)S(1)} async-done(((bf16[8,64,256]{2,1,0:T(8,128)(2,1)}), bf16[8,64,256]{2,1,0:T(8,128)(2,1)S(1)}, u32[]{:S(2)}, u32[]{:S(2)}) %all-to-all-start) | async-done | bytes 262176 | tf_op jit(solution)/shard_map/all_to_all | solution.py:312
  201.7 5.5 %shard_map.126 = (bf16[4,128,1024]{2,1,0:T(8,128)(2,1)}, bf16[256,256]{1,0:T(8,128)(2,1)}) custom-call(s32[4]{0:T(128)S(1)} %broadcast_xor_fusion.place_ref, bf16[4,128,1024]{2,1,0:T(8,128)(2,1)S(1)} %copy-done, bf16[8,32,256]{2,1,0:T(8,128)(2,1)S(1)} %slice.64.prefix_ref, bf16[4,128,256]{2,1,0:T(8,128)(2,1)S(1)} %copy-done.1, ...), custom_call_target="tpu_custom_call" | custom-call | flops 603979776 | bytes 4194304 | tf_op jit(solution)/shard_map/pallas_call | solution.py:220
  (129 shorter events, 8.2 us)
Async XLA Ops:
  2.8 9.5 %copy-start.5 = (s32[32,1]{0,1:T(1,128)S(1)}, s32[32,1]{0,1:T(1,128)}, u32[]{:S(2)}) copy-start(s32[32,1]{0,1:T(1,128)} %param.15) | copy-start | bytes 388
  2.8 9.7 %copy-start.6 = (s32[32]{0:T(128)S(1)}, s32[32]{0:T(128)}, u32[]{:S(2)}) copy-start(s32[32]{0:T(128)} %param.16) | copy-start | bytes 388
  2.8 9.8 %copy-start.3 = (bf16[1,32,256]{2,1,0:T(8,128)(2,1)S(1)}, bf16[1,32,256]{2,1,0:T(8,128)(2,1)}, u32[]{:S(2)}) copy-start(bf16[1,32,256]{2,1,0:T(8,128)(2,1)} %param.19) | copy-start | bytes 49156
  2.8 9.9 %copy-start.4 = (bf16[2048]{0:T(1024)(128)(2,1)S(1)}, bf16[2048]{0:T(1024)(128)(2,1)}, u32[]{:S(2)}) copy-start(bf16[2048]{0:T(1024)(128)(2,1)} %param.13) | copy-start | bytes 12292
  2.8 9.9 %copy-start.7 = (s32[1,4]{1,0:T(1,128)S(1)}, s32[1,4]{1,0:T(1,128)}, u32[]{:S(2)}) copy-start(s32[1,4]{1,0:T(1,128)} %param.17) | copy-start | bytes 52
  2.8 59.4 %collective-permute-start.3 = (bf16[256,1280]{1,0:T(8,128)(2,1)}, bf16[256,1280]{1,0:T(8,128)(2,1)S(1)}, u32[]{:S(2)}, u32[]{:S(2)}) collective-permute-start(bf16[256,1280]{1,0:T(8,128)(2,1)} %fusion.5), channel_id=1, source_target_pairs={{0,0},{1,10},{2,16},{3,26},{4,4},{5,14},{6,20},{7,30},{8,2},{9,8},... | collective-permute-start | bytes 1966088 | tf_op jit(solution)/shard_map/ppermute | solution.py:38
  7.4 72.6 %collective-permute-start.27 = (bf16[640,512]{1,0:T(8,128)(2,1)}, bf16[640,512]{1,0:T(8,128)(2,1)}, u32[]{:S(2)}, u32[]{:S(2)}) collective-permute-start(bf16[640,512]{1,0:T(8,128)(2,1)} %get-tuple-element.10), channel_id=1, source_target_pairs={{4,0},{0,4},{12,8},{8,12},{20,16},{16,20},{28,24},{24,28},{5,1},{1... | collective-permute-start | bytes 1966088 | tf_op jit(solution)/shard_map/ppermute | solution.py:123
  10.3 71.0 %collective-permute-start.20 = (bf16[640,512]{1,0:T(8,128)(2,1)S(1)}, bf16[640,512]{1,0:T(8,128)(2,1)}, u32[]{:S(2)}, u32[]{:S(2)}) collective-permute-start(bf16[640,512]{1,0:T(8,128)(2,1)S(1)} %get-tuple-element.13), channel_id=1, source_target_pairs={{4,0},{0,4},{12,8},{8,12},{20,16},{16,20},{28,24},{24,28},{5,1},{1... | collective-permute-start | bytes 1966088 | tf_op jit(solution)/shard_map/ppermute | solution.py:123
  10.4 72.2 %collective-permute-start.13 = (bf16[640,512]{1,0:T(8,128)(2,1)S(1)}, bf16[640,512]{1,0:T(8,128)(2,1)}, u32[]{:S(2)}, u32[]{:S(2)}) collective-permute-start(bf16[640,512]{1,0:T(8,128)(2,1)S(1)} %get-tuple-element.11), channel_id=1, source_target_pairs={{4,0},{0,4},{12,8},{8,12},{20,16},{16,20},{28,24},{24,28},{5,1},{1... | collective-permute-start | bytes 1966088 | tf_op jit(solution)/shard_map/ppermute | solution.py:123
  12.6 39.7 %collective-permute-start = (bf16[1,48,256]{2,1,0:T(8,128)(2,1)S(1)}, bf16[1,48,256]{2,1,0:T(8,128)(2,1)S(1)}, u32[]{:S(2)}, u32[]{:S(2)}) collective-permute-start(bf16[1,48,256]{2,1,0:T(8,128)(2,1)S(1)} %maximum_bitcast_fusion), channel_id=1, source_target_pairs={{0,4},{4,0},{8,12},{12,8},{16,20},{20,16},{24,28},{28,24},{1,5},{5... | collective-permute-start | bytes 73736 | tf_op jit(solution)/shard_map/ppermute | solution.py:24
  52.4 6.3 %collective-permute-start.1 = (bf16[2,48,256]{2,1,0:T(8,128)(2,1)S(1)}, bf16[2,48,256]{2,1,0:T(8,128)(2,1)S(1)}, u32[]{:S(2)}, u32[]{:S(2)}) collective-permute-start(bf16[2,48,256]{2,1,0:T(8,128)(2,1)S(1)} %pad_maximum_fusion.9), channel_id=1, source_target_pairs={{0,8},{4,12},{8,0},{12,4},{16,24},{20,28},{24,16},{28,20},{1,9},{5... | collective-permute-start | bytes 147464 | tf_op jit(solution)/shard_map/ppermute | solution.py:24
  58.7 7.3 %collective-permute-start.2 = (bf16[4,48,256]{2,1,0:T(8,128)(2,1)S(1)}, bf16[4,48,256]{2,1,0:T(8,128)(2,1)S(1)}, u32[]{:S(2)}, u32[]{:S(2)}) collective-permute-start(bf16[4,48,256]{2,1,0:T(8,128)(2,1)S(1)} %pad_maximum_fusion.8), channel_id=1, source_target_pairs={{0,16},{4,20},{8,24},{12,28},{16,0},{20,4},{24,8},{28,12},{1,17},{... | collective-permute-start | bytes 294920 | tf_op jit(solution)/shard_map/ppermute | solution.py:24
  62.2 15.4 %collective-permute-start.4 = (bf16[1,256,1280]{2,1,0:T(8,128)(2,1)S(1)}, bf16[1,256,1280]{2,1,0:T(8,128)(2,1)}, u32[]{:S(2)}, u32[]{:S(2)}) collective-permute-start(bf16[1,256,1280]{2,1,0:T(8,128)(2,1)S(1)} %bitcast.162), channel_id=1, source_target_pairs={{0,2},{1,3},{2,0},{3,1},{4,6},{5,7},{6,4},{7,5},{8,10},{9,11},{10,... | collective-permute-start | bytes 1966088 | tf_op jit(solution)/shard_map/ppermute | solution.py:24
  65.9 17.8 %collective-permute-start.6 = (bf16[640,512]{1,0:T(8,128)(2,1)S(1)}, bf16[640,512]{1,0:T(8,128)(2,1)}, u32[]{:S(2)}, u32[]{:S(2)}) collective-permute-start(bf16[640,512]{1,0:T(8,128)(2,1)S(1)} %get-tuple-element.12), channel_id=1, source_target_pairs={{4,0},{0,4},{12,8},{8,12},{20,16},{16,20},{28,24},{24,28},{5,1},{1... | collective-permute-start | bytes 1966088 | tf_op jit(solution)/shard_map/ppermute | solution.py:123
  79.9 5.0 %collective-permute-start.5 = (bf16[2,256,1280]{2,1,0:T(8,128)(2,1)}, bf16[2,256,1280]{2,1,0:T(8,128)(2,1)}, u32[]{:S(2)}, u32[]{:S(2)}) collective-permute-start(bf16[2,256,1280]{2,1,0:T(8,128)(2,1)} %pad_maximum_fusion.1), channel_id=1, source_target_pairs={{0,1},{1,0},{2,3},{3,2},{4,5},{5,4},{6,7},{7,6},{8,9},{9,8},{10,11... | collective-permute-start | bytes 3932168 | tf_op jit(solution)/shard_map/ppermute | solution.py:24
  88.8 13.0 %collective-permute-start.28 = (bf16[256,512]{1,0:T(8,128)(2,1)S(1)}, bf16[256,512]{1,0:T(8,128)(2,1)S(1)}, u32[]{:S(2)}, u32[]{:S(2)}) collective-permute-start(bf16[256,512]{1,0:T(8,128)(2,1)S(1)} %get-tuple-element.16), channel_id=1, source_target_pairs={{0,8},{4,12},{1,9},{5,13},{2,10},{6,14},{3,11},{7,15}} | collective-permute-start | bytes 786440 | tf_op jit(solution)/shard_map/ppermute | solution.py:95
  91.4 27.9 %collective-permute-start.31 = (bf16[256,512]{1,0:T(8,128)(2,1)S(1)}, bf16[256,512]{1,0:T(8,128)(2,1)S(1)}, u32[]{:S(2)}, u32[]{:S(2)}) collective-permute-start(bf16[256,512]{1,0:T(8,128)(2,1)S(1)} %get-tuple-element.17), channel_id=1, source_target_pairs={{24,16},{28,20},{25,17},{29,21},{26,18},{30,22},{27,19},{31,23}} | collective-permute-start | bytes 786440 | tf_op jit(solution)/shard_map/ppermute | solution.py:95
  94.2 9.4 %collective-permute-start.21 = (bf16[256,512]{1,0:T(8,128)(2,1)S(1)}, bf16[256,512]{1,0:T(8,128)(2,1)S(1)}, u32[]{:S(2)}, u32[]{:S(2)}) collective-permute-start(bf16[256,512]{1,0:T(8,128)(2,1)S(1)} %get-tuple-element.20), channel_id=1, source_target_pairs={{0,8},{4,12},{1,9},{5,13},{2,10},{6,14},{3,11},{7,15}} | collective-permute-start | bytes 786440 | tf_op jit(solution)/shard_map/ppermute | solution.py:95
  95.5 29.5 %collective-permute-start.24 = (bf16[256,512]{1,0:T(8,128)(2,1)S(1)}, bf16[256,512]{1,0:T(8,128)(2,1)S(1)}, u32[]{:S(2)}, u32[]{:S(2)}) collective-permute-start(bf16[256,512]{1,0:T(8,128)(2,1)S(1)} %get-tuple-element.21), channel_id=1, source_target_pairs={{24,16},{28,20},{25,17},{29,21},{26,18},{30,22},{27,19},{31,23}} | collective-permute-start | bytes 786440 | tf_op jit(solution)/shard_map/ppermute | solution.py:95
  98.3 10.9 %collective-permute-start.14 = (bf16[256,512]{1,0:T(8,128)(2,1)S(1)}, bf16[256,512]{1,0:T(8,128)(2,1)S(1)}, u32[]{:S(2)}, u32[]{:S(2)}) collective-permute-start(bf16[256,512]{1,0:T(8,128)(2,1)S(1)} %get-tuple-element.24), channel_id=1, source_target_pairs={{0,8},{4,12},{1,9},{5,13},{2,10},{6,14},{3,11},{7,15}} | collective-permute-start | bytes 786440 | tf_op jit(solution)/shard_map/ppermute | solution.py:95
  101.8 31.0 %collective-permute-start.17 = (bf16[256,512]{1,0:T(8,128)(2,1)S(1)}, bf16[256,512]{1,0:T(8,128)(2,1)S(1)}, u32[]{:S(2)}, u32[]{:S(2)}) collective-permute-start(bf16[256,512]{1,0:T(8,128)(2,1)S(1)} %get-tuple-element.25), channel_id=1, source_target_pairs={{24,16},{28,20},{25,17},{29,21},{26,18},{30,22},{27,19},{31,23}} | collective-permute-start | bytes 786440 | tf_op jit(solution)/shard_map/ppermute | solution.py:95
  103.6 11.2 %collective-permute-start.7 = (bf16[256,512]{1,0:T(8,128)(2,1)S(1)}, bf16[256,512]{1,0:T(8,128)(2,1)S(1)}, u32[]{:S(2)}, u32[]{:S(2)}) collective-permute-start(bf16[256,512]{1,0:T(8,128)(2,1)S(1)} %get-tuple-element.28), channel_id=1, source_target_pairs={{0,8},{4,12},{1,9},{5,13},{2,10},{6,14},{3,11},{7,15}} | collective-permute-start | bytes 786440 | tf_op jit(solution)/shard_map/ppermute | solution.py:95
  109.2 11.2 %collective-permute-start.29 = (bf16[256,512]{1,0:T(8,128)(2,1)S(1)}, bf16[256,512]{1,0:T(8,128)(2,1)S(1)}, u32[]{:S(2)}, u32[]{:S(2)}) collective-permute-start(bf16[256,512]{1,0:T(8,128)(2,1)S(1)} %fusion.16), channel_id=1, source_target_pairs={{0,8},{4,12},{8,16},{12,20},{1,9},{5,13},{9,17},{13,21},{2,10},{6,... | collective-permute-start | bytes 786440 | tf_op jit(solution)/shard_map/ppermute | solution.py:95
  114.8 12.1 %collective-permute-start.22 = (bf16[256,512]{1,0:T(8,128)(2,1)S(1)}, bf16[256,512]{1,0:T(8,128)(2,1)S(1)}, u32[]{:S(2)}, u32[]{:S(2)}) collective-permute-start(bf16[256,512]{1,0:T(8,128)(2,1)S(1)} %fusion.22), channel_id=1, source_target_pairs={{0,8},{4,12},{8,16},{12,20},{1,9},{5,13},{9,17},{13,21},{2,10},{6,... | collective-permute-start | bytes 786440 | tf_op jit(solution)/shard_map/ppermute | solution.py:95
  119.3 8.5 %collective-permute-start.10 = (bf16[256,512]{1,0:T(8,128)(2,1)S(1)}, bf16[256,512]{1,0:T(8,128)(2,1)S(1)}, u32[]{:S(2)}, u32[]{:S(2)}) collective-permute-start(bf16[256,512]{1,0:T(8,128)(2,1)S(1)} %get-tuple-element.29), channel_id=1, source_target_pairs={{24,16},{28,20},{25,17},{29,21},{26,18},{30,22},{27,19},{31,23}} | collective-permute-start | bytes 786440 | tf_op jit(solution)/shard_map/ppermute | solution.py:95
  120.5 11.5 %collective-permute-start.8 = (bf16[256,512]{1,0:T(8,128)(2,1)S(1)}, bf16[256,512]{1,0:T(8,128)(2,1)S(1)}, u32[]{:S(2)}, u32[]{:S(2)}) collective-permute-start(bf16[256,512]{1,0:T(8,128)(2,1)S(1)} %fusion.34), channel_id=1, source_target_pairs={{0,8},{4,12},{8,16},{12,20},{1,9},{5,13},{9,17},{13,21},{2,10},{6,... | collective-permute-start | bytes 786440 | tf_op jit(solution)/shard_map/ppermute | solution.py:95
  125.0 13.0 %collective-permute-start.15 = (bf16[256,512]{1,0:T(8,128)(2,1)S(1)}, bf16[256,512]{1,0:T(8,128)(2,1)S(1)}, u32[]{:S(2)}, u32[]{:S(2)}) collective-permute-start(bf16[256,512]{1,0:T(8,128)(2,1)S(1)} %fusion.28), channel_id=1, source_target_pairs={{0,8},{4,12},{8,16},{12,20},{1,9},{5,13},{9,17},{13,21},{2,10},{6,... | collective-permute-start | bytes 786440 | tf_op jit(solution)/shard_map/ppermute | solution.py:95
  127.0 11.9 %collective-permute-start.32 = (bf16[256,512]{1,0:T(8,128)(2,1)S(1)}, bf16[256,512]{1,0:T(8,128)(2,1)S(1)}, u32[]{:S(2)}, u32[]{:S(2)}) collective-permute-start(bf16[256,512]{1,0:T(8,128)(2,1)S(1)} %get-tuple-element.15), channel_id=1, source_target_pairs={{16,8},{20,12},{24,16},{28,20},{17,9},{21,13},{25,17},{29,21},{18,... | collective-permute-start | bytes 786440 | tf_op jit(solution)/shard_map/ppermute | solution.py:95
  127.8 51.2 %collective-permute-start.30 = (bf16[256,512]{1,0:T(8,128)(2,1)S(1)}, bf16[256,512]{1,0:T(8,128)(2,1)S(1)}, u32[]{:S(2)}, u32[]{:S(2)}) collective-permute-start(bf16[256,512]{1,0:T(8,128)(2,1)S(1)} %get-tuple-element.14), channel_id=1, source_target_pairs={{0,8},{4,12},{8,16},{12,20},{16,24},{20,28},{1,9},{5,13},{9,17},{1... | collective-permute-start | bytes 786440 | tf_op jit(solution)/shard_map/ppermute | solution.py:95
  132.0 22.1 %collective-permute-start.25 = (bf16[256,512]{1,0:T(8,128)(2,1)S(1)}, bf16[256,512]{1,0:T(8,128)(2,1)S(1)}, u32[]{:S(2)}, u32[]{:S(2)}) collective-permute-start(bf16[256,512]{1,0:T(8,128)(2,1)S(1)} %get-tuple-element.19), channel_id=1, source_target_pairs={{16,8},{20,12},{24,16},{28,20},{17,9},{21,13},{25,17},{29,21},{18,... | collective-permute-start | bytes 786440 | tf_op jit(solution)/shard_map/ppermute | solution.py:95
  132.8 43.4 %collective-permute-start.23 = (bf16[256,512]{1,0:T(8,128)(2,1)S(1)}, bf16[256,512]{1,0:T(8,128)(2,1)S(1)}, u32[]{:S(2)}, u32[]{:S(2)}) collective-permute-start(bf16[256,512]{1,0:T(8,128)(2,1)S(1)} %get-tuple-element.18), channel_id=1, source_target_pairs={{0,8},{4,12},{8,16},{12,20},{16,24},{20,28},{1,9},{5,13},{9,17},{1... | collective-permute-start | bytes 786440 | tf_op jit(solution)/shard_map/ppermute | solution.py:95
  138.0 1.6 collective-permute-start.11
  138.9 16.6 %collective-permute-start.18 = (bf16[256,512]{1,0:T(8,128)(2,1)S(1)}, bf16[256,512]{1,0:T(8,128)(2,1)S(1)}, u32[]{:S(2)}, u32[]{:S(2)}) collective-permute-start(bf16[256,512]{1,0:T(8,128)(2,1)S(1)} %get-tuple-element.23), channel_id=1, source_target_pairs={{16,8},{20,12},{24,16},{28,20},{17,9},{21,13},{25,17},{29,21},{18,... | collective-permute-start | bytes 786440 | tf_op jit(solution)/shard_map/ppermute | solution.py:95
  139.7 26.9 %copy-start.2 = (bf16[2048,1024]{1,0:T(8,128)(2,1)S(1)}, bf16[2048,1024]{1,0:T(8,128)(2,1)}, u32[]{:S(2)}) copy-start(bf16[2048,1024]{1,0:T(8,128)(2,1)} %param.14) | copy-start | bytes 12582916
  139.7 20.5 %collective-permute-start.9 = (bf16[256,512]{1,0:T(8,128)(2,1)S(1)}, bf16[256,512]{1,0:T(8,128)(2,1)S(1)}, u32[]{:S(2)}, u32[]{:S(2)}) collective-permute-start(bf16[256,512]{1,0:T(8,128)(2,1)S(1)} %get-tuple-element.26), channel_id=1, source_target_pairs={{0,8},{4,12},{8,16},{12,20},{16,24},{20,28},{1,9},{5,13},{9,17},{1... | collective-permute-start | bytes 786440 | tf_op jit(solution)/shard_map/ppermute | solution.py:95
  154.1 11.0 %collective-permute-start.12 = (bf16[256,512]{1,0:T(8,128)(2,1)S(1)}, bf16[256,512]{1,0:T(8,128)(2,1)S(1)}, u32[]{:S(2)}, u32[]{:S(2)}) collective-permute-start(bf16[256,512]{1,0:T(8,128)(2,1)S(1)} %fusion.33), channel_id=1, source_target_pairs={{8,0},{12,4},{16,8},{20,12},{24,16},{28,20},{9,1},{13,5},{17,9},{2... | collective-permute-start | bytes 786440 | tf_op jit(solution)/shard_map/ppermute | solution.py:95
  155.5 11.6 %collective-permute-start.16 = (bf16[256,512]{1,0:T(8,128)(2,1)S(1)}, bf16[256,512]{1,0:T(8,128)(2,1)S(1)}, u32[]{:S(2)}, u32[]{:S(2)}) collective-permute-start(bf16[256,512]{1,0:T(8,128)(2,1)S(1)} %get-tuple-element.22), channel_id=1, source_target_pairs={{0,8},{4,12},{8,16},{12,20},{16,24},{20,28},{1,9},{5,13},{9,17},{1... | collective-permute-start | bytes 786440 | tf_op jit(solution)/shard_map/ppermute | solution.py:95
  160.1 18.9 %collective-permute-start.33 = (bf16[256,512]{1,0:T(8,128)(2,1)S(1)}, bf16[256,512]{1,0:T(8,128)(2,1)S(1)}, u32[]{:S(2)}, u32[]{:S(2)}) collective-permute-start(bf16[256,512]{1,0:T(8,128)(2,1)S(1)} %fusion.15), channel_id=1, source_target_pairs={{8,0},{12,4},{16,8},{20,12},{24,16},{28,20},{9,1},{13,5},{17,9},{2... | collective-permute-start | bytes 786440 | tf_op jit(solution)/shard_map/ppermute | solution.py:95
  165.1 10.5 %collective-permute-start.19 = (bf16[256,512]{1,0:T(8,128)(2,1)S(1)}, bf16[256,512]{1,0:T(8,128)(2,1)S(1)}, u32[]{:S(2)}, u32[]{:S(2)}) collective-permute-start(bf16[256,512]{1,0:T(8,128)(2,1)S(1)} %fusion.27), channel_id=1, source_target_pairs={{8,0},{12,4},{16,8},{20,12},{24,16},{28,20},{9,1},{13,5},{17,9},{2... | collective-permute-start | bytes 786440 | tf_op jit(solution)/shard_map/ppermute | solution.py:95
  167.0 11.4 %collective-permute-start.26 = (bf16[256,512]{1,0:T(8,128)(2,1)S(1)}, bf16[256,512]{1,0:T(8,128)(2,1)S(1)}, u32[]{:S(2)}, u32[]{:S(2)}) collective-permute-start(bf16[256,512]{1,0:T(8,128)(2,1)S(1)} %fusion.21), channel_id=1, source_target_pairs={{8,0},{12,4},{16,8},{20,12},{24,16},{28,20},{9,1},{13,5},{17,9},{2... | collective-permute-start | bytes 786440 | tf_op jit(solution)/shard_map/ppermute | solution.py:95
  179.9 13.3 %copy-start.8 = (s32[4]{0:T(128)S(1)}, s32[4]{0:T(128)}, u32[]{:S(2)}) copy-start(s32[4]{0:T(128)} %param.18) | copy-start | bytes 52
  180.0 3.4 %collective-permute-start.34 = (bf16[2,256,256]{2,1,0:T(8,128)(2,1)S(1)}, bf16[2,256,256]{2,1,0:T(8,128)(2,1)S(1)}, u32[]{:S(2)}, u32[]{:S(2)}) collective-permute-start(bf16[2,256,256]{2,1,0:T(8,128)(2,1)S(1)} %fusion.46), channel_id=1, source_target_pairs={{0,1},{1,0},{2,3},{3,2},{4,5},{5,4},{6,7},{7,6},{8,9},{9,8},{10,11... | collective-permute-start | bytes 786440 | tf_op jit(solution)/shard_map/ppermute | solution.py:24
  180.1 1.5 collective-permute-start.36
  181.6 20.1 %copy-start = (bf16[4,128,1024]{2,1,0:T(8,128)(2,1)S(1)}, bf16[4,128,1024]{2,1,0:T(8,128)(2,1)}, u32[]{:S(2)}) copy-start(bf16[4,128,1024]{2,1,0:T(8,128)(2,1)} %query_ref.1) | copy-start | bytes 3145732
  181.6 20.1 %copy-start.1 = (bf16[4,128,256]{2,1,0:T(8,128)(2,1)S(1)}, bf16[4,128,256]{2,1,0:T(8,128)(2,1)}, u32[]{:S(2)}) copy-start(bf16[4,128,256]{2,1,0:T(8,128)(2,1)} %text_ref.1) | copy-start | bytes 786436
  181.6 3.6 %collective-permute-start.37 = (f32[256]{0:T(256)S(1)}, f32[256]{0:T(256)S(1)}, u32[]{:S(2)}, u32[]{:S(2)}) collective-permute-start(f32[256]{0:T(256)S(1)} %add.400), channel_id=1, source_target_pairs={{0,2},{1,3},{2,0},{3,1},{4,6},{5,7},{6,4},{7,5},{8,10},{9,11},{10,... | collective-permute-start | bytes 3080 | tf_op jit(solution)/shard_map/ppermute | solution.py:24
  183.5 5.3 %collective-permute-start.35 = (bf16[1,256,256]{2,1,0:T(8,128)(2,1)S(1)}, bf16[1,256,256]{2,1,0:T(8,128)(2,1)S(1)}, u32[]{:S(2)}, u32[]{:S(2)}) collective-permute-start(bf16[1,256,256]{2,1,0:T(8,128)(2,1)S(1)} %dynamic-slice_convert_fusion.9), channel_id=1, source_target_pairs={{0,2},{1,3},{2,0},{3,1},{4,6},{5,7},{6,4},{7,5},{8,10},{9,11},{10,... | collective-permute-start | bytes 393224 | tf_op jit(solution)/shard_map/ppermute | solution.py:24
  189.8 11.8 %all-to-all-start = ((bf16[8,64,256]{2,1,0:T(8,128)(2,1)}), bf16[8,64,256]{2,1,0:T(8,128)(2,1)S(1)}, u32[]{:S(2)}, u32[]{:S(2)}) async-start(bf16[8,64,256]{2,1,0:T(8,128)(2,1)} %bitcast.46), calls=%async_computation | async-start | bytes 524288 | tf_op jit(solution)/shard_map/all_to_all | solution.py:312

commit v3 on v2

--- a/solution.py
+++ b/solution.py
@@ -35,85 +35,137 @@
                 source = (origin * width + inner) * tp_count + block
                 slot = ((origin ^ block) & 1) * half + origin // 2
                 pairs.append((source, (block * width + inner) * tp_count + slot))
-    held = lax.ppermute(local, ("seq", "tp"), pairs)[None]
+    held = [lax.ppermute(local, ("seq", "tp"), pairs)]
     bits = bits_of(tp_count)
     for bit in bits[-1:] + bits[:-1]:
-        held = jnp.concatenate([held, flip(held, "tp", bit)], axis=0)
-    group = lax.axis_index("seq") // width
+        held = held + [flip(piece, "tp", bit) for piece in held]
+    return held
+
+
+def panel_base():
+    group = lax.axis_index("seq") // (lax.axis_size("seq") // lax.axis_size("tp"))
     place = lax.axis_index("tp")
-    base = 2 * (place % half) + ((place // half) ^ (group & 1))
-    return held, base
-
-
-def partial_kernel(base_ref, rows_ref, weights_ref, out_ref):
-    out_ref[0] = jnp.dot(rows_ref[0], weights_ref[...], preferred_element_type=jnp.float32)
-
-
-def partial_products(base, held, weights):
-    groups, rows, depth = held.shape
-    columns = weights.shape[1]
+    half = lax.axis_size("tp") // 2
+    return 2 * (place % half) + ((place // half) ^ (group & 1))
+
+
+ROLE_GROUPS = (3, 0, 2, 1)
+
+
+def partial_kernel(pieces, blocks, roles_ref, *refs):
+    rows_refs = refs[: 4 * pieces]
+    weights_refs = refs[4 * pieces : 4 * pieces + blocks]
+    far_end, near_end, far_mid, near_mid, first, second, held = refs[4 * pieces + blocks :]
+    rows = rows_refs[0].shape[0]
+    for place in range(4):
+        for piece in range(pieces):
+            total = None
+            at = 0
+            for weights in weights_refs:
+                depth = weights.shape[0]
+                term = jnp.dot(
+                    rows_refs[place * pieces + piece][:, at : at + depth],
+                    weights[...],
+                    preferred_element_type=jnp.float32,
+                )
+                total = term if total is None else total + term
+                at += depth
+            held[roles_ref[place], piece * rows : (piece + 1) * rows] = total
+    far_end[...] = held[0]
+    near_end[...] = held[1]
+    far_mid[...] = held[2]
+    near_mid[...] = held[3]
+    first[...] = held[0].astype(jnp.bfloat16)
+    second[0] = held[2].astype(jnp.bfloat16)
+    second[1] = held[3].astype(jnp.bfloat16)
+
+
+def partial_products(roles, held, weights):
+    pieces = len(held[0])
+    rows, depth = held[0][0].shape
+    columns = weights[0].shape[1]
+    tile = min(columns, 256)
+    block_rows = pieces * rows
+    one = pl.BlockSpec((block_rows, tile), lambda i, roles: (0, i))
     return pl.pallas_call(
-        partial_kernel,
+        functools.partial(partial_kernel, pieces, len(weights)),
         grid_spec=pltpu.PrefetchScalarGridSpec(
             num_scalar_prefetch=1,
-            grid=(groups,),
-            in_specs=[
-                pl.BlockSpec((1, rows, depth), lambda i, base: (base[0] ^ i, 0, 0)),
-                pl.BlockSpec((depth, columns), lambda i, base: (0, 0)),
-            ],
-            out_specs=pl.BlockSpec((1, rows, columns), lambda i, base: (i, 0, 0)),
-        ),
-        out_shape=jax.ShapeDtypeStruct((groups, rows, columns), jnp.float32),
+            grid=(columns // tile,),
+            in_specs=[pl.BlockSpec((rows, depth), lambda i, roles: (0, 0))] * (4 * pieces)
+            + [pl.BlockSpec((w.shape[0], tile), lambda i, roles: (0, i)) for w in weights],
+            out_specs=[one] * 5
+            + [pl.BlockSpec((2, block_rows, tile), lambda i, roles: (0, 0, i))],
+            scratch_shapes=[pltpu.VMEM((4, block_rows, tile), jnp.float32)],
+        ),
+        out_shape=[jax.ShapeDtypeStruct((block_rows, columns), jnp.float32)] * 4
+        + [
+            jax.ShapeDtypeStruct((block_rows, columns), jnp.bfloat16),
+            jax.ShapeDtypeStruct((2, block_rows, columns), jnp.bfloat16),
+        ],
         compiler_params=pltpu.CompilerParams(vmem_limit_bytes=VMEM),
         cost_estimate=pl.CostEstimate(
-            flops=2 * groups * rows * depth * columns,
-            bytes_accessed=2 * (groups * rows * depth + depth * columns)
-            + 4 * groups * rows * columns,
+            flops=8 * block_rows * depth * columns,
+            bytes_accessed=8 * block_rows * depth + 2 * depth * columns + 22 * block_rows * columns,
             transcendentals=0,
         ),
-    )(base.reshape(1).astype(jnp.int32), held, weights)
-
-
-def reduce_groups(parts):
+    )(roles, *[piece for place in held for piece in place], *weights)
+
+
+def along(pairs):
+    width = lax.axis_size("seq") // lax.axis_size("tp")
+    return [(a * width + i, b * width + i) for a, b in pairs for i in range(width)]
+
+
+ENDS_IN = ((0, 1), (3, 2))
+MIDDLES = ((1, 2), (2, 1))
+ENDS_OUT = ((2, 3), (1, 0))
+
+
+def reduce_groups(parts, is_end):
+    far_end, near_end, far_mid, near_mid, first, second = parts
+    first = lax.ppermute(first, "seq", along(ENDS_IN))
+    second = lax.ppermute(second, "seq", along(ENDS_IN))
+    passed = lax.ppermute(
+        (far_end + first.astype(jnp.float32)).astype(jnp.bfloat16), "seq", along(MIDDLES)
+    )
+    crossed = lax.ppermute(
+        (far_mid + second[0].astype(jnp.float32)).astype(jnp.bfloat16), "seq", along(MIDDLES)
+    )
+    outer = lax.ppermute(
+        (near_end + passed.astype(jnp.float32)).astype(jnp.bfloat16), "seq", along(ENDS_OUT)
+    )
+    end = near_end + outer.astype(jnp.float32)
+    middle = near_mid + second[1].astype(jnp.float32) + crossed.astype(jnp.float32)
+    return jnp.where(is_end, end, middle).astype(jnp.bfloat16)
+
+
+def merge_tiles(panels, w_merge, ln_gain, w_kv, small):
     seq_count, tp_count = lax.axis_size("seq"), lax.axis_size("tp")
-    width = seq_count // tp_count
-    group = lax.axis_index("seq") // width
-    total = lax.dynamic_index_in_dim(parts, group, 0, keepdims=False)
-    for sign in (1, -1):
-        carried = None
-        for reach in range(tp_count - 1, 0, -1):
-            target = jnp.clip(group + sign * reach, 0, tp_count - 1)
-            block = lax.dynamic_index_in_dim(parts, target, 0, keepdims=False)
-            if carried is not None:
-                block = block + carried.astype(jnp.float32)
-            pairs = []
-            for origin in range(tp_count):
-                if 0 <= origin + sign * reach < tp_count:
-                    for inner in range(width):
-                        source = origin * width + inner
-                        pairs.append((source, source + sign * width))
-            carried = lax.ppermute(block.astype(jnp.bfloat16), "seq", pairs)
-        total = total + carried.astype(jnp.float32)
-    return total.astype(jnp.bfloat16)
-
-
-def merge_tiles(panels, w_merge, ln_gain, w_kv):
-    seq_count, tp_count = lax.axis_size("seq"), lax.axis_size("tp")
+    assert tp_count == 4 and seq_count % 4 == 0
     width = seq_count // tp_count
     tiles, panel_rows, depth = panels.shape
     share = w_merge.shape[0]
+    group = lax.axis_index("seq") // width
     inner = lax.axis_index("seq") % width
     local = panels.reshape(tiles * panel_rows, depth)
     turned = lax.dynamic_slice_in_dim(
         jnp.concatenate([local, local], axis=1), inner * share, depth, axis=1
     )
-    held, base = transpose_panels(turned)
+    half = turned.shape[0] // 2
+    held_pieces = [transpose_panels(turned[:half]), transpose_panels(turned[half:])]
+    held = list(zip(*held_pieces))
     columns = w_merge.shape[1] // CHUNKS
-    kv = 0.0
-    squares = 0.0
-    for chunk in range(CHUNKS):
-        own = w_merge[:, chunk * columns : (chunk + 1) * columns]
-        pieces = [own]
+    own_chunks = [w_merge[:, c * columns : (c + 1) * columns] for c in range(CHUNKS)]
+    small = jnp.concatenate([small, flip(small, "seq", 1)], axis=0)
+    own_chunks, small = lax.optimization_barrier((own_chunks, small))
+    shift = jnp.where(group < 2, 0, 3)
+    groups = (panel_base() ^ jnp.arange(4, dtype=jnp.int32)) ^ shift
+    roles = jnp.array([ROLE_GROUPS.index(g) for g in range(4)], jnp.int32)[groups]
+    is_end = (group == 0) | (group == 3)
+    received = []
+    for own in own_chunks:
+        pieces = []
         for offset in range(1, width):
             pairs = [
                 (g * width + (i + offset) % width, g * width + i)
@@ -121,8 +173,18 @@
                 for i in range(width)
             ]
             pieces.append(lax.ppermute(own, "seq", pairs))
-        parts = partial_products(base, held, jnp.concatenate(pieces, axis=0))
-        merged = reduce_groups(parts).astype(jnp.float32)
+        received.append(pieces)
+    _, small = lax.optimization_barrier((held_pieces[1][0], small))
+    for bit in bits_of(seq_count)[1:]:
+        small = jnp.concatenate([small, flip(small, "seq", bit)], axis=0)
+    kv = 0.0
+    squares = 0.0
+    for chunk in range(CHUNKS):
+        weights = [own_chunks[chunk]] + received[chunk]
+        if share % 128:
+            weights = [jnp.concatenate(weights, axis=0)]
+        parts = partial_products(roles, held, weights)
+        merged = reduce_groups(parts, is_end).astype(jnp.float32)
         squares = squares + jnp.sum(merged * merged, axis=1)
         gain = ln_gain[chunk * columns : (chunk + 1) * columns].astype(jnp.float32)
         kv = kv + jnp.dot(
@@ -130,7 +192,7 @@
             w_kv[chunk * columns : (chunk + 1) * columns],
             preferred_element_type=jnp.float32,
         )
-    return kv, squares
+    return kv, squares, small
 
 
 def scatter_heads(kv, squares):
@@ -148,19 +210,11 @@
     return blocks[0], squares
 
 
-def share_small(prefix_cache, sources, tiles):
-    rows = prefix_cache.shape[1]
+def pack_small(prefix_cache, sources, tiles):
     width = prefix_cache.shape[2]
     asks = jnp.stack([sources, tiles]).astype(jnp.bfloat16)
     asks = jnp.pad(asks, ((0, 14), (0, width - asks.shape[1])))
-    held = jnp.concatenate([prefix_cache[0], asks], axis=0)[None]
-    for bit in bits_of(lax.axis_size("seq")):
-        held = jnp.concatenate([held, flip(held, "seq", bit)], axis=0)
-    count = sources.shape[0]
-    prefixes = held[:, :rows]
-    asked_sources = held[:, rows, :count].astype(jnp.int32)
-    asked_tiles = held[:, rows + 1, :count].astype(jnp.int32)
-    return prefixes, asked_sources, asked_tiles
+    return jnp.concatenate([prefix_cache[0], asks], axis=0)[None]
 
 
 def attend_kernel(
@@ -269,7 +323,13 @@
     capacity = max(2, 2 * page_count // seq_count)
     sources = page_src[:, 0]
 
-    prefixes, asked_sources, asked_tiles = share_small(prefix_cache, sources, page_tile)
+    kv, squares, small = merge_tiles(
+        panels, w_merge, ln_gain, w_kv, pack_small(prefix_cache, sources, page_tile)
+    )
+    prefix_rows = prefix_cache.shape[1]
+    prefixes = small[:, :prefix_rows]
+    asked_sources = small[:, prefix_rows, :page_count].astype(jnp.int32)
+    asked_tiles = small[:, prefix_rows + 1, :page_count].astype(jnp.int32)
     asked = (asked_sources == holder).astype(jnp.int32)
     order = jnp.cumsum(asked, axis=1) - 1
     slots = jnp.arange(capacity, dtype=jnp.int32)
@@ -304,7 +364,6 @@
         axis=1,
     )[:, None, :]
 
-    kv, squares = merge_tiles(panels, w_merge, ln_gain, w_kv)
     kv, squares = scatter_heads(kv, squares)
     row_scale = lax.rsqrt(squares / D + 1e-06)
     tile_kv = (kv * row_scale[:, None]).astype(jnp.bfloat16)

time: 208 us -> 201 us (0.966)
  starting transfers between devices: 87.1 us -> 75.9 us
  Pallas kernels: 13.7 us -> 23.9 us
  waiting for transfers between devices: 81.7 us -> 76 us
  other arithmetic: 14.7 us -> 11.3 us
  local copies, waits for them, and re-layouts: 5.77 us -> 8.64 us
    ppermute x9 -> x13, waiting for transfers between devices: 57 us -> 11.4 us  [flip(): return lax.ppermute(value, axis, [(i, i ^ bit) for i in range(count)])]
    ppermute x25 -> x22, starting transfers between devices: 65.2 us -> 33.7 us  [the longest x4 9.89 us: reduce_groups(): first = lax.ppermute(first, 'seq', along(ENDS_IN))]
    ppermute x25 -> x22, waiting for transfers between devices: 16.9 us -> 41.9 us  [the longest x4 24.1 us: reduce_groups(): lax.ppermute((near_end + passed.astype(jnp.float32)).astype(jnp.bfloat16)...]
    ppermute x9 -> x13, starting transfers between devices: 12 us -> 28.1 us  [flip(): return lax.ppermute(value, axis, [(i, i ^ bit) for i in range(count)])]
    ppermute x4, waiting for transfers between devices: 0.01 us -> 15.6 us  [merge_tiles(): pieces.append(lax.ppermute(own, 'seq', pairs))]
    pallas_call x4, Pallas kernels: 8.15 us -> 18.4 us  [partial_products(): pl.pallas_call(functools.partial(partial_kernel, pieces, len(weights)), g...]
    concatenate x9 -> x2, other arithmetic: 8.95 us -> 0.02 us  [the longest x1 0.01 us: merge_tiles(): small = jnp.concatenate([small, flip(small, 'seq', bit)], axis=0)]
    all_to_all x1, starting transfers between devices: 3.41 us -> 10.5 us  [shards(): lax.all_to_all(outgoing, 'seq', split_axis=0, concat_axis=0, tiled=True)]
  transfers between devices with their start and end apart: 39 -> 40, of which waited for: 15 -> 14; matrix products, arithmetic and copies ran while one was open for 8% -> 9% of each run, Pallas kernels for 3% -> 9%
where the time goes in v3:
time: 201 us; the launch traced here: 200 us
  waiting for transfers between devices  76 us (38%)
  starting transfers between devices  75.9 us (38%)
  Pallas kernels  23.9 us (12%)
  other arithmetic  11.3 us (6%)
  local copies, waits for them, and re-layouts  8.64 us (4%)
  matrix products  2.78 us (1%)
    ppermute x13, starting transfers between devices, flip(): return lax.ppermute(value, axis, [(i, i ^ bit) for i in range(count)])  28.1 us
    ppermute x4, waiting for transfers between devices, reduce_groups(): lax.ppermute((near_end + passed.astype(jnp.float32)).astype(jnp.bfloat16)...  24.1 us
    pallas_call x4, Pallas kernels, partial_products(): pl.pallas_call(functools.partial(partial_kernel, pieces, len(weights)), g...  18.4 us
    ppermute x4, waiting for transfers between devices, merge_tiles(): pieces.append(lax.ppermute(own, 'seq', pairs))  15.6 us
    ppermute x4, waiting for transfers between devices, reduce_groups(): first = lax.ppermute(first, 'seq', along(ENDS_IN))  12.5 us
    ppermute x13, waiting for transfers between devices, flip(): return lax.ppermute(value, axis, [(i, i ^ bit) for i in range(count)])  11.4 us
    all_to_all x1, starting transfers between devices, shards(): lax.all_to_all(outgoing, 'seq', split_axis=0, concat_axis=0, tiled=True)  10.5 us
    ppermute x4, starting transfers between devices, reduce_groups(): first = lax.ppermute(first, 'seq', along(ENDS_IN))  9.89 us
  transfers between devices with their start and end apart: 40, of which 14 were waited for; matrix products, arithmetic and copies ran while one was open for 9% of the time, Pallas kernels for 9%

profile of v3, /device:TPU:0, one launch (start us, length us, event | category | flops | bytes accessed | tf_op | source)
XLA Modules:
  0.0 200.0 jit_solution(16592817840779275607)
XLA Ops:
  0.7 1.3 fusion.5
  2.0 0.9 fusion.61
  2.9 1.8 collective-permute-start
  4.6 1.6 collective-permute-start.4
  6.3 0.9 convert_reduce_fusion
  7.2 0.7 fusion.55
  7.9 0.7 convert_bitcast_fusion
  8.6 0.7 maximum_bitcast_fusion
  9.3 2.9 %collective-permute-start.1 = (bf16[1,48,256]{2,1,0:T(8,128)(2,1)S(1)}, bf16[1,48,256]{2,1,0:T(8,128)(2,1)S(1)}, u32[]{:S(2)}, u32[]{:S(2)}) collective-permute-start(bf16[1,48,256]{2,1,0:T(8,128)(2,1)S(1)} %maximum_bitcast_fusion), channel_id=1, source_target_pairs={{0,4},{4,0},{8,12},{12,8},{16,20},{20,16},{24,28},{28,24},{1,5},{5... | collective-permute-start | bytes 73736 | tf_op jit(solution)/shard_map/ppermute | solution.py:24
  12.2 0.7 multiply_add_fusion
  13.5 1.9 fusion.60
  16.3 0.8 gather_fusion.2
  18.1 0.8 add.361
  19.2 0.8 gather_fusion.1
  20.1 6.6 %collective-permute-start.2 = (bf16[2,48,256]{2,1,0:T(8,128)(2,1)S(1)}, bf16[2,48,256]{2,1,0:T(8,128)(2,1)S(1)}, u32[]{:S(2)}, u32[]{:S(2)}) collective-permute-start(bf16[2,48,256]{2,1,0:T(8,128)(2,1)S(1)} %pad_maximum_fusion.2), channel_id=1, source_target_pairs={{0,8},{4,12},{8,0},{12,4},{16,24},{20,28},{24,16},{28,20},{1,9},{5... | collective-permute-start | bytes 147464 | tf_op jit(solution)/shard_map/ppermute | solution.py:24
  26.7 6.5 %collective-permute-start.6 = (bf16[128,1280]{1,0:T(8,128)(2,1)S(1)}, bf16[128,1280]{1,0:T(8,128)(2,1)}, u32[]{:S(2)}, u32[]{:S(2)}) collective-permute-start(bf16[128,1280]{1,0:T(8,128)(2,1)S(1)} %collective-permute-done.refs_1_), channel_id=1, source_target_pairs={{0,2},{1,3},{2,0},{3,1},{4,6},{5,7},{6,4},{7,5},{8,10},{9,11},{10,... | collective-permute-start | bytes 983048 | tf_op jit(solution)/shard_map/ppermute | solution.py:24
  33.3 5.1 %collective-permute-start.7 = (bf16[128,1280]{1,0:T(8,128)(2,1)S(1)}, bf16[128,1280]{1,0:T(8,128)(2,1)}, u32[]{:S(2)}, u32[]{:S(2)}) collective-permute-start(bf16[128,1280]{1,0:T(8,128)(2,1)S(1)} %collective-permute-done.4.refs_0_), channel_id=1, source_target_pairs={{0,1},{1,0},{2,3},{3,2},{4,5},{5,4},{6,7},{7,6},{8,9},{9,8},{10,11... | collective-permute-start | bytes 983048 | tf_op jit(solution)/shard_map/ppermute | solution.py:24
  38.4 3.7 %collective-permute-start.3 = (bf16[4,48,256]{2,1,0:T(8,128)(2,1)S(1)}, bf16[4,48,256]{2,1,0:T(8,128)(2,1)S(1)}, u32[]{:S(2)}, u32[]{:S(2)}) collective-permute-start(bf16[4,48,256]{2,1,0:T(8,128)(2,1)S(1)} %pad_maximum_fusion.1), channel_id=1, source_target_pairs={{0,16},{4,20},{8,24},{12,28},{16,0},{20,4},{24,8},{28,12},{1,17},{... | collective-permute-start | bytes 294920 | tf_op jit(solution)/shard_map/ppermute | solution.py:24
  42.1 5.6 %collective-permute-done.3 = bf16[4,48,256]{2,1,0:T(8,128)(2,1)S(1)} collective-permute-done((bf16[4,48,256]{2,1,0:T(8,128)(2,1)S(1)}, bf16[4,48,256]{2,1,0:T(8,128)(2,1)S(1)}, u32[]{:S(2)}, u32[]{:S(2)}) %collective-permute-start.3) | collective-permute-done | bytes 98336 | tf_op jit(solution)/shard_map/ppermute | solution.py:24
  47.7 0.7 copy-done.5
  48.6 1.5 collective-permute-start.23
  50.6 1.5 collective-permute-start.11
  54.5 4.6 %shard_map.134 = (f32[256,512]{1,0:T(8,128)S(1)}, f32[256,512]{1,0:T(8,128)S(1)}, f32[256,512]{1,0:T(8,128)S(1)}, f32[256,512]{1,0:T(8,128)S(1)}, bf16[256,512]{...) custom-call(s32[4]{0:T(128)S(1)} %gather_fusion.1, bf16[128,1280]{1,0:T(8,128)(2,1)S(1)} %collective-permute-done.4.refs_0_, ...), custom_call_target="tpu_custom_call" | custom-call | flops 1342177280 | bytes 6815744 | tf_op jit(solution)/shard_map/pallas_call | solution.py:90
  59.2 3.1 %collective-permute-start.30 = (bf16[256,512]{1,0:T(8,128)(2,1)S(1)}, bf16[256,512]{1,0:T(8,128)(2,1)}, u32[]{:S(2)}, u32[]{:S(2)}) collective-permute-start(bf16[256,512]{1,0:T(8,128)(2,1)S(1)} %get-tuple-element.58), channel_id=1, source_target_pairs={{0,8},{4,12},{24,16},{28,20},{1,9},{5,13},{25,17},{29,21},{2,10},{... | collective-permute-start | bytes 786440 | tf_op jit(solution)/shard_map/ppermute | solution.py:127
  62.3 1.3 collective-permute-start.33
  63.6 2.7 %collective-permute-done.23.refs_9_ = bf16[640,512]{1,0:T(8,128)(2,1)} collective-permute-done((bf16[640,512]{1,0:T(8,128)(2,1)S(1)}, bf16[640,512]{1,0:T(8,128)(2,1)}, u32[]{:S(2)}, u32[]{:S(2)}) %collective-permute-start.23) | collective-permute-done | bytes 655392 | tf_op jit(solution)/shard_map/ppermute | solution.py:175
  66.2 4.6 %shard_map.133 = (f32[256,512]{1,0:T(8,128)S(1)}, f32[256,512]{1,0:T(8,128)S(1)}, f32[256,512]{1,0:T(8,128)S(1)}, f32[256,512]{1,0:T(8,128)S(1)}, bf16[256,512]{...) custom-call(s32[4]{0:T(128)S(1)} %gather_fusion.1, bf16[128,1280]{1,0:T(8,128)(2,1)S(1)} %collective-permute-done.4.refs_0_, ...), custom_call_target="tpu_custom_call" | custom-call | flops 1342177280 | bytes 6815744 | tf_op jit(solution)/shard_map/pallas_call | solution.py:90
  70.8 3.1 %collective-permute-start.24 = (bf16[256,512]{1,0:T(8,128)(2,1)S(1)}, bf16[256,512]{1,0:T(8,128)(2,1)}, u32[]{:S(2)}, u32[]{:S(2)}) collective-permute-start(bf16[256,512]{1,0:T(8,128)(2,1)S(1)} %get-tuple-element.51), channel_id=1, source_target_pairs={{0,8},{4,12},{24,16},{28,20},{1,9},{5,13},{25,17},{29,21},{2,10},{... | collective-permute-start | bytes 786440 | tf_op jit(solution)/shard_map/ppermute | solution.py:127
  73.9 6.3 %collective-permute-done.17.refs_9_ = bf16[640,512]{1,0:T(8,128)(2,1)} collective-permute-done((bf16[640,512]{1,0:T(8,128)(2,1)S(1)}, bf16[640,512]{1,0:T(8,128)(2,1)}, u32[]{:S(2)}, u32[]{:S(2)}) %collective-permute-start.17) | collective-permute-done | bytes 655392 | tf_op jit(solution)/shard_map/ppermute | solution.py:175
  80.3 2.4 %collective-permute-start.27 = (bf16[2,256,512]{2,1,0:T(8,128)(2,1)S(1)}, bf16[2,256,512]{2,1,0:T(8,128)(2,1)S(1)}, u32[]{:S(2)}, u32[]{:S(2)}) collective-permute-start(bf16[2,256,512]{2,1,0:T(8,128)(2,1)S(1)} %get-tuple-element.53), channel_id=1, source_target_pairs={{0,8},{4,12},{24,16},{28,20},{1,9},{5,13},{25,17},{29,21},{2,10},{... | collective-permute-start | bytes 1572872 | tf_op jit(solution)/shard_map/ppermute | solution.py:128
  82.7 4.6 %shard_map.132 = (f32[256,512]{1,0:T(8,128)S(1)}, f32[256,512]{1,0:T(8,128)S(1)}, f32[256,512]{1,0:T(8,128)S(1)}, f32[256,512]{1,0:T(8,128)S(1)}, bf16[256,512]{...) custom-call(s32[4]{0:T(128)S(1)} %gather_fusion.1, bf16[128,1280]{1,0:T(8,128)(2,1)S(1)} %collective-permute-done.4.refs_0_, ...), custom_call_target="tpu_custom_call" | custom-call | flops 1342177280 | bytes 6815744 | tf_op jit(solution)/shard_map/pallas_call | solution.py:90
  87.3 6.6 %collective-permute-done.11.refs_9_ = bf16[640,512]{1,0:T(8,128)(2,1)} collective-permute-done((bf16[640,512]{1,0:T(8,128)(2,1)S(1)}, bf16[640,512]{1,0:T(8,128)(2,1)}, u32[]{:S(2)}, u32[]{:S(2)}) %collective-permute-start.11) | collective-permute-done | bytes 655392 | tf_op jit(solution)/shard_map/ppermute | solution.py:175
  93.9 2.4 %collective-permute-start.18 = (bf16[256,512]{1,0:T(8,128)(2,1)S(1)}, bf16[256,512]{1,0:T(8,128)(2,1)S(1)}, u32[]{:S(2)}, u32[]{:S(2)}) collective-permute-start(bf16[256,512]{1,0:T(8,128)(2,1)S(1)} %get-tuple-element.44), channel_id=1, source_target_pairs={{0,8},{4,12},{24,16},{28,20},{1,9},{5,13},{25,17},{29,21},{2,10},{... | collective-permute-start | bytes 786440 | tf_op jit(solution)/shard_map/ppermute | solution.py:127
  96.3 4.6 %shard_map.131 = (f32[256,512]{1,0:T(8,128)S(1)}, f32[256,512]{1,0:T(8,128)S(1)}, f32[256,512]{1,0:T(8,128)S(1)}, f32[256,512]{1,0:T(8,128)S(1)}, bf16[256,512]{...) custom-call(s32[4]{0:T(128)S(1)} %gather_fusion.1, bf16[128,1280]{1,0:T(8,128)(2,1)S(1)} %collective-permute-done.4.refs_0_, ...), custom_call_target="tpu_custom_call" | custom-call | flops 1342177280 | bytes 6815744 | tf_op jit(solution)/shard_map/pallas_call | solution.py:90
  101.0 1.3 collective-permute-start.21
  102.3 1.0 add_convert_fusion.1
  103.3 1.3 collective-permute-start.12
  104.6 1.0 add_convert_fusion.3
  105.7 0.7 collective-permute-start.31
  106.5 12.5 %collective-permute-done.12 = bf16[256,512]{1,0:T(8,128)(2,1)S(1)} collective-permute-done((bf16[256,512]{1,0:T(8,128)(2,1)S(1)}, bf16[256,512]{1,0:T(8,128)(2,1)S(1)}, u32[]{:S(2)}, u32[]{:S(2)}) %collective-permute-start.12) | collective-permute-done | bytes 262176 | tf_op jit(solution)/shard_map/ppermute | solution.py:127
  118.9 4.4 %collective-permute-start.15 = (bf16[2,256,512]{2,1,0:T(8,128)(2,1)S(1)}, bf16[2,256,512]{2,1,0:T(8,128)(2,1)S(1)}, u32[]{:S(2)}, u32[]{:S(2)}) collective-permute-start(bf16[2,256,512]{2,1,0:T(8,128)(2,1)S(1)} %get-tuple-element.39), channel_id=1, source_target_pairs={{0,8},{4,12},{24,16},{28,20},{1,9},{5,13},{25,17},{29,21},{2,10},{... | collective-permute-start | bytes 1572872 | tf_op jit(solution)/shard_map/ppermute | solution.py:128
  123.4 0.7 collective-permute-start.25
  124.2 0.7 collective-permute-start.19
  125.0 0.7 collective-permute-start.13
  125.8 1.6 collective-permute-start.32
  127.4 0.7 collective-permute-start.34
  128.2 5.3 %collective-permute-done.15 = bf16[2,256,512]{2,1,0:T(8,128)(2,1)S(1)} collective-permute-done((bf16[2,256,512]{2,1,0:T(8,128)(2,1)S(1)}, bf16[2,256,512]{2,1,0:T(8,128)(2,1)S(1)}, u32[]{:S(2)}, u32[]{:S(2)}) %collective-permute-start.15) | collective-permute-done | bytes 524320 | tf_op jit(solution)/shard_map/ppermute | solution.py:128
  133.5 1.3 collective-permute-start.14
  134.8 0.7 collective-permute-start.16
  135.6 1.3 collective-permute-start.26
  137.0 17.8 %collective-permute-done.14 = bf16[256,512]{1,0:T(8,128)(2,1)S(1)} collective-permute-done((bf16[256,512]{1,0:T(8,128)(2,1)S(1)}, bf16[256,512]{1,0:T(8,128)(2,1)S(1)}, u32[]{:S(2)}, u32[]{:S(2)}) %collective-permute-start.14) | collective-permute-done | bytes 262176 | tf_op jit(solution)/shard_map/ppermute | solution.py:135
  154.8 1.3 collective-permute-start.20
  156.1 0.7 collective-permute-start.22
  157.5 6.3 %collective-permute-done.20 = bf16[256,512]{1,0:T(8,128)(2,1)S(1)} collective-permute-done((bf16[256,512]{1,0:T(8,128)(2,1)S(1)}, bf16[256,512]{1,0:T(8,128)(2,1)S(1)}, u32[]{:S(2)}, u32[]{:S(2)}) %collective-permute-start.20) | collective-permute-done | bytes 262176 | tf_op jit(solution)/shard_map/ppermute | solution.py:135
  163.8 0.8 collective-permute-start.28
  167.8 0.9 collective-permute-done.37
  169.4 1.5 collective-permute-start.36
  170.9 1.4 collective-permute-done.38
  172.3 2.5 %collective-permute-done.36 = bf16[1,256,256]{2,1,0:T(8,128)(2,1)S(1)} collective-permute-done((bf16[1,256,256]{2,1,0:T(8,128)(2,1)S(1)}, bf16[1,256,256]{2,1,0:T(8,128)(2,1)S(1)}, u32[]{:S(2)}, u32[]{:S(2)}) %collective-permute-start.36) | collective-permute-done | bytes 131104 | tf_op jit(solution)/shard_map/ppermute | solution.py:24
  174.7 1.0 convolution_convert_fusion
  175.8 10.5 %all-to-all-start = ((bf16[8,64,256]{2,1,0:T(8,128)(2,1)}), bf16[8,64,256]{2,1,0:T(8,128)(2,1)S(1)}, u32[]{:S(2)}, u32[]{:S(2)}) async-start(bf16[8,64,256]{2,1,0:T(8,128)(2,1)} %bitcast.25), calls=%async_computation | async-start | bytes 524288 | tf_op jit(solution)/shard_map/all_to_all | solution.py:371
  186.4 0.9 slice.107.prefix_ref
  187.4 7.2 %all-to-all-done = bf16[8,64,256]{2,1,0:T(8,128)(2,1)S(1)} async-done(((bf16[8,64,256]{2,1,0:T(8,128)(2,1)}), bf16[8,64,256]{2,1,0:T(8,128)(2,1)S(1)}, u32[]{:S(2)}, u32[]{:S(2)}) %all-to-all-start) | async-done | bytes 262176 | tf_op jit(solution)/shard_map/all_to_all | solution.py:371
  194.5 5.5 %shard_map.135 = (bf16[4,128,1024]{2,1,0:T(8,128)(2,1)}, bf16[256,256]{1,0:T(8,128)(2,1)}) custom-call(s32[4]{0:T(128)S(1)} %broadcast_xor_fusion.place_ref, bf16[4,128,1024]{2,1,0:T(8,128)(2,1)S(1)} %copy-done, bf16[8,32,256]{2,1,0:T(8,128)(2,1)S(1)} %slice.107.prefix_ref, bf16[4,128,256]{2,1,0:T(8,128)(2,1)S(1)} %copy-done.1, ...), custom_call_target="tpu_custom_call" | custom-call | flops 603979776 | bytes 4194304 | tf_op jit(solution)/shard_map/pallas_call | solution.py:274
  (139 shorter events, 11.5 us)
Async XLA Ops:
  0.6 14.7 %copy-start.12 = (bf16[2048]{0:T(1024)(128)(2,1)S(1)}, bf16[2048]{0:T(1024)(128)(2,1)}, u32[]{:S(2)}) copy-start(bf16[2048]{0:T(1024)(128)(2,1)} %param.14) | copy-start | bytes 12292
  0.6 15.3 %copy-start.13 = (s32[1,4]{1,0:T(1,128)S(1)}, s32[1,4]{1,0:T(1,128)}, u32[]{:S(2)}) copy-start(s32[1,4]{1,0:T(1,128)} %param.18) | copy-start | bytes 52
  2.9 16.3 %copy-start.2 = (s32[4]{0:T(128)S(1)}, s32[4]{0:T(128)}, u32[]{:S(2)}) copy-start(s32[4]{0:T(128)} %constant.125.clone) | copy-start | bytes 52
  2.9 17.2 %collective-permute-start = (bf16[128,1280]{1,0:T(8,128)(2,1)}, bf16[128,1280]{1,0:T(8,128)(2,1)S(1)}, u32[]{:S(2)}, u32[]{:S(2)}) collective-permute-start(bf16[128,1280]{1,0:T(8,128)(2,1)} %get-tuple-element.79), channel_id=1, source_target_pairs={{0,0},{1,10},{2,16},{3,26},{4,4},{5,14},{6,20},{7,30},{8,2},{9,8},... | collective-permute-start | bytes 983048 | tf_op jit(solution)/shard_map/ppermute | solution.py:38
  4.6 28.6 %collective-permute-start.4 = (bf16[128,1280]{1,0:T(8,128)(2,1)}, bf16[128,1280]{1,0:T(8,128)(2,1)S(1)}, u32[]{:S(2)}, u32[]{:S(2)}) collective-permute-start(bf16[128,1280]{1,0:T(8,128)(2,1)} %get-tuple-element.78), channel_id=1, source_target_pairs={{0,0},{1,10},{2,16},{3,26},{4,4},{5,14},{6,20},{7,30},{8,2},{9,8},... | collective-permute-start | bytes 983048 | tf_op jit(solution)/shard_map/ppermute | solution.py:38
  9.3 10.7 %collective-permute-start.1 = (bf16[1,48,256]{2,1,0:T(8,128)(2,1)S(1)}, bf16[1,48,256]{2,1,0:T(8,128)(2,1)S(1)}, u32[]{:S(2)}, u32[]{:S(2)}) collective-permute-start(bf16[1,48,256]{2,1,0:T(8,128)(2,1)S(1)} %maximum_bitcast_fusion), channel_id=1, source_target_pairs={{0,4},{4,0},{8,12},{12,8},{16,20},{20,16},{24,28},{28,24},{1,5},{5... | collective-permute-start | bytes 73736 | tf_op jit(solution)/shard_map/ppermute | solution.py:24
  17.4 0.6 copy-start.10
  20.0 32.1 %collective-permute-start.29 = (bf16[640,512]{1,0:T(8,128)(2,1)S(1)}, bf16[640,512]{1,0:T(8,128)(2,1)}, u32[]{:S(2)}, u32[]{:S(2)}) collective-permute-start(bf16[640,512]{1,0:T(8,128)(2,1)S(1)} %get-tuple-element.55.refs_8_), channel_id=1, source_target_pairs={{4,0},{0,4},{12,8},{8,12},{20,16},{16,20},{28,24},{24,28},{5,1},{1... | collective-permute-start | bytes 1966088 | tf_op jit(solution)/shard_map/ppermute | solution.py:175
  20.1 18.3 %collective-permute-start.2 = (bf16[2,48,256]{2,1,0:T(8,128)(2,1)S(1)}, bf16[2,48,256]{2,1,0:T(8,128)(2,1)S(1)}, u32[]{:S(2)}, u32[]{:S(2)}) collective-permute-start(bf16[2,48,256]{2,1,0:T(8,128)(2,1)S(1)} %pad_maximum_fusion.2), channel_id=1, source_target_pairs={{0,8},{4,12},{8,0},{12,4},{16,24},{20,28},{24,16},{28,20},{1,9},{5... | collective-permute-start | bytes 147464 | tf_op jit(solution)/shard_map/ppermute | solution.py:24
  26.7 21.9 %collective-permute-start.6 = (bf16[128,1280]{1,0:T(8,128)(2,1)S(1)}, bf16[128,1280]{1,0:T(8,128)(2,1)}, u32[]{:S(2)}, u32[]{:S(2)}) collective-permute-start(bf16[128,1280]{1,0:T(8,128)(2,1)S(1)} %collective-permute-done.refs_1_), channel_id=1, source_target_pairs={{0,2},{1,3},{2,0},{3,1},{4,6},{5,7},{6,4},{7,5},{8,10},{9,11},{10,... | collective-permute-start | bytes 983048 | tf_op jit(solution)/shard_map/ppermute | solution.py:24
  33.2 16.9 %collective-permute-start.5 = (bf16[128,1280]{1,0:T(8,128)(2,1)S(1)}, bf16[128,1280]{1,0:T(8,128)(2,1)}, u32[]{:S(2)}, u32[]{:S(2)}) collective-permute-start(bf16[128,1280]{1,0:T(8,128)(2,1)S(1)} %collective-permute-done.4.refs_0_), channel_id=1, source_target_pairs={{0,2},{1,3},{2,0},{3,1},{4,6},{5,7},{6,4},{7,5},{8,10},{9,11},{10,... | collective-permute-start | bytes 983048 | tf_op jit(solution)/shard_map/ppermute | solution.py:24
  33.3 17.4 %collective-permute-start.7 = (bf16[128,1280]{1,0:T(8,128)(2,1)S(1)}, bf16[128,1280]{1,0:T(8,128)(2,1)}, u32[]{:S(2)}, u32[]{:S(2)}) collective-permute-start(bf16[128,1280]{1,0:T(8,128)(2,1)S(1)} %collective-permute-done.4.refs_0_), channel_id=1, source_target_pairs={{0,1},{1,0},{2,3},{3,2},{4,5},{5,4},{6,7},{7,6},{8,9},{9,8},{10,11... | collective-permute-start | bytes 983048 | tf_op jit(solution)/shard_map/ppermute | solution.py:24
  38.4 9.3 %collective-permute-start.3 = (bf16[4,48,256]{2,1,0:T(8,128)(2,1)S(1)}, bf16[4,48,256]{2,1,0:T(8,128)(2,1)S(1)}, u32[]{:S(2)}, u32[]{:S(2)}) collective-permute-start(bf16[4,48,256]{2,1,0:T(8,128)(2,1)S(1)} %pad_maximum_fusion.1), channel_id=1, source_target_pairs={{0,16},{4,20},{8,24},{12,28},{16,0},{20,4},{24,8},{28,12},{1,17},{... | collective-permute-start | bytes 294920 | tf_op jit(solution)/shard_map/ppermute | solution.py:24
  47.7 4.4 %collective-permute-start.8 = (bf16[128,1280]{1,0:T(8,128)(2,1)S(1)}, bf16[128,1280]{1,0:T(8,128)(2,1)}, u32[]{:S(2)}, u32[]{:S(2)}) collective-permute-start(bf16[128,1280]{1,0:T(8,128)(2,1)S(1)} %collective-permute-done.refs_1_), channel_id=1, source_target_pairs={{0,1},{1,0},{2,3},{3,2},{4,5},{5,4},{6,7},{7,6},{8,9},{9,8},{10,11... | collective-permute-start | bytes 983048 | tf_op jit(solution)/shard_map/ppermute | solution.py:24
  47.7 0.7 copy-start.5
  48.6 17.6 %collective-permute-start.23 = (bf16[640,512]{1,0:T(8,128)(2,1)S(1)}, bf16[640,512]{1,0:T(8,128)(2,1)}, u32[]{:S(2)}, u32[]{:S(2)}) collective-permute-start(bf16[640,512]{1,0:T(8,128)(2,1)S(1)} %get-tuple-element.48.refs_8_), channel_id=1, source_target_pairs={{4,0},{0,4},{12,8},{8,12},{20,16},{16,20},{28,24},{24,28},{5,1},{1... | collective-permute-start | bytes 1966088 | tf_op jit(solution)/shard_map/ppermute | solution.py:175
  50.1 30.2 %collective-permute-start.17 = (bf16[640,512]{1,0:T(8,128)(2,1)S(1)}, bf16[640,512]{1,0:T(8,128)(2,1)}, u32[]{:S(2)}, u32[]{:S(2)}) collective-permute-start(bf16[640,512]{1,0:T(8,128)(2,1)S(1)} %get-tuple-element.41.refs_8_), channel_id=1, source_target_pairs={{4,0},{0,4},{12,8},{8,12},{20,16},{16,20},{28,24},{24,28},{5,1},{1... | collective-permute-start | bytes 1966088 | tf_op jit(solution)/shard_map/ppermute | solution.py:175
  50.6 43.3 %collective-permute-start.11 = (bf16[640,512]{1,0:T(8,128)(2,1)S(1)}, bf16[640,512]{1,0:T(8,128)(2,1)}, u32[]{:S(2)}, u32[]{:S(2)}) collective-permute-start(bf16[640,512]{1,0:T(8,128)(2,1)S(1)} %get-tuple-element.34.refs_8_), channel_id=1, source_target_pairs={{4,0},{0,4},{12,8},{8,12},{20,16},{16,20},{28,24},{24,28},{5,1},{1... | collective-permute-start | bytes 1966088 | tf_op jit(solution)/shard_map/ppermute | solution.py:175
  52.1 2.0 collective-permute-start.10
  52.1 2.4 %collective-permute-start.9 = (bf16[128,1280]{1,0:T(8,128)(2,1)}, bf16[128,1280]{1,0:T(8,128)(2,1)}, u32[]{:S(2)}, u32[]{:S(2)}) collective-permute-start(bf16[128,1280]{1,0:T(8,128)(2,1)} %collective-permute-done.5.refs_2_), channel_id=1, source_target_pairs={{0,1},{1,0},{2,3},{3,2},{4,5},{5,4},{6,7},{7,6},{8,9},{9,8},{10,11... | collective-permute-start | bytes 983048 | tf_op jit(solution)/shard_map/ppermute | solution.py:24
  59.2 41.8 %collective-permute-start.30 = (bf16[256,512]{1,0:T(8,128)(2,1)S(1)}, bf16[256,512]{1,0:T(8,128)(2,1)}, u32[]{:S(2)}, u32[]{:S(2)}) collective-permute-start(bf16[256,512]{1,0:T(8,128)(2,1)S(1)} %get-tuple-element.58), channel_id=1, source_target_pairs={{0,8},{4,12},{24,16},{28,20},{1,9},{5,13},{25,17},{29,21},{2,10},{... | collective-permute-start | bytes 786440 | tf_op jit(solution)/shard_map/ppermute | solution.py:127
  62.3 61.9 %collective-permute-start.33 = (bf16[2,256,512]{2,1,0:T(8,128)(2,1)S(1)}, bf16[2,256,512]{2,1,0:T(8,128)(2,1)S(1)}, u32[]{:S(2)}, u32[]{:S(2)}) collective-permute-start(bf16[2,256,512]{2,1,0:T(8,128)(2,1)S(1)} %get-tuple-element.60), channel_id=1, source_target_pairs={{0,8},{4,12},{24,16},{28,20},{1,9},{5,13},{25,17},{29,21},{2,10},{... | collective-permute-start | bytes 1572872 | tf_op jit(solution)/shard_map/ppermute | solution.py:128
  70.8 32.5 %collective-permute-start.24 = (bf16[256,512]{1,0:T(8,128)(2,1)S(1)}, bf16[256,512]{1,0:T(8,128)(2,1)}, u32[]{:S(2)}, u32[]{:S(2)}) collective-permute-start(bf16[256,512]{1,0:T(8,128)(2,1)S(1)} %get-tuple-element.51), channel_id=1, source_target_pairs={{0,8},{4,12},{24,16},{28,20},{1,9},{5,13},{25,17},{29,21},{2,10},{... | collective-permute-start | bytes 786440 | tf_op jit(solution)/shard_map/ppermute | solution.py:127
  80.3 45.5 %collective-permute-start.27 = (bf16[2,256,512]{2,1,0:T(8,128)(2,1)S(1)}, bf16[2,256,512]{2,1,0:T(8,128)(2,1)S(1)}, u32[]{:S(2)}, u32[]{:S(2)}) collective-permute-start(bf16[2,256,512]{2,1,0:T(8,128)(2,1)S(1)} %get-tuple-element.53), channel_id=1, source_target_pairs={{0,8},{4,12},{24,16},{28,20},{1,9},{5,13},{25,17},{29,21},{2,10},{... | collective-permute-start | bytes 1572872 | tf_op jit(solution)/shard_map/ppermute | solution.py:128
  93.9 11.8 %collective-permute-start.18 = (bf16[256,512]{1,0:T(8,128)(2,1)S(1)}, bf16[256,512]{1,0:T(8,128)(2,1)S(1)}, u32[]{:S(2)}, u32[]{:S(2)}) collective-permute-start(bf16[256,512]{1,0:T(8,128)(2,1)S(1)} %get-tuple-element.44), channel_id=1, source_target_pairs={{0,8},{4,12},{24,16},{28,20},{1,9},{5,13},{25,17},{29,21},{2,10},{... | collective-permute-start | bytes 786440 | tf_op jit(solution)/shard_map/ppermute | solution.py:127
  101.0 34.7 %collective-permute-start.21 = (bf16[2,256,512]{2,1,0:T(8,128)(2,1)S(1)}, bf16[2,256,512]{2,1,0:T(8,128)(2,1)S(1)}, u32[]{:S(2)}, u32[]{:S(2)}) collective-permute-start(bf16[2,256,512]{2,1,0:T(8,128)(2,1)S(1)} %get-tuple-element.46), channel_id=1, source_target_pairs={{0,8},{4,12},{24,16},{28,20},{1,9},{5,13},{25,17},{29,21},{2,10},{... | collective-permute-start | bytes 1572872 | tf_op jit(solution)/shard_map/ppermute | solution.py:128
  103.3 15.6 %collective-permute-start.12 = (bf16[256,512]{1,0:T(8,128)(2,1)S(1)}, bf16[256,512]{1,0:T(8,128)(2,1)S(1)}, u32[]{:S(2)}, u32[]{:S(2)}) collective-permute-start(bf16[256,512]{1,0:T(8,128)(2,1)S(1)} %get-tuple-element.37), channel_id=1, source_target_pairs={{0,8},{4,12},{24,16},{28,20},{1,9},{5,13},{25,17},{29,21},{2,10},{... | collective-permute-start | bytes 786440 | tf_op jit(solution)/shard_map/ppermute | solution.py:127
  105.7 17.7 %collective-permute-start.31 = (bf16[256,512]{1,0:T(8,128)(2,1)S(1)}, bf16[256,512]{1,0:T(8,128)(2,1)S(1)}, u32[]{:S(2)}, u32[]{:S(2)}) collective-permute-start(bf16[256,512]{1,0:T(8,128)(2,1)S(1)} %add_convert_fusion.1), channel_id=1, source_target_pairs={{8,16},{12,20},{16,8},{20,12},{9,17},{13,21},{17,9},{21,13},{10,18... | collective-permute-start | bytes 786440 | tf_op jit(solution)/shard_map/ppermute | solution.py:129
  118.9 14.5 %collective-permute-start.15 = (bf16[2,256,512]{2,1,0:T(8,128)(2,1)S(1)}, bf16[2,256,512]{2,1,0:T(8,128)(2,1)S(1)}, u32[]{:S(2)}, u32[]{:S(2)}) collective-permute-start(bf16[2,256,512]{2,1,0:T(8,128)(2,1)S(1)} %get-tuple-element.39), channel_id=1, source_target_pairs={{0,8},{4,12},{24,16},{28,20},{1,9},{5,13},{25,17},{29,21},{2,10},{... | collective-permute-start | bytes 1572872 | tf_op jit(solution)/shard_map/ppermute | solution.py:128
  123.4 1.5 collective-permute-start.25
  124.2 10.6 %collective-permute-start.19 = (bf16[256,512]{1,0:T(8,128)(2,1)S(1)}, bf16[256,512]{1,0:T(8,128)(2,1)S(1)}, u32[]{:S(2)}, u32[]{:S(2)}) collective-permute-start(bf16[256,512]{1,0:T(8,128)(2,1)S(1)} %add_convert_fusion.5), channel_id=1, source_target_pairs={{8,16},{12,20},{16,8},{20,12},{9,17},{13,21},{17,9},{21,13},{10,18... | collective-permute-start | bytes 786440 | tf_op jit(solution)/shard_map/ppermute | solution.py:129
  125.0 2.4 %collective-permute-start.13 = (bf16[256,512]{1,0:T(8,128)(2,1)S(1)}, bf16[256,512]{1,0:T(8,128)(2,1)S(1)}, u32[]{:S(2)}, u32[]{:S(2)}) collective-permute-start(bf16[256,512]{1,0:T(8,128)(2,1)S(1)} %add_convert_fusion.7), channel_id=1, source_target_pairs={{8,16},{12,20},{16,8},{20,12},{9,17},{13,21},{17,9},{21,13},{10,18... | collective-permute-start | bytes 786440 | tf_op jit(solution)/shard_map/ppermute | solution.py:129
  125.7 31.3 %copy-start.3 = (bf16[2048,1024]{1,0:T(8,128)(2,1)S(1)}, bf16[2048,1024]{1,0:T(8,128)(2,1)}, u32[]{:S(2)}) copy-start(bf16[2048,1024]{1,0:T(8,128)(2,1)} %param.15) | copy-start | bytes 12582916
  125.7 31.3 %copy-start.9 = (f32[512]{0:T(512)S(1)}, f32[512]{0:T(512)}, u32[]{:S(2)}) copy-start(f32[512]{0:T(512)} %get-tuple-element.82) | copy-start | bytes 6148
  125.8 40.3 %collective-permute-start.32 = (bf16[256,512]{1,0:T(8,128)(2,1)S(1)}, bf16[256,512]{1,0:T(8,128)(2,1)S(1)}, u32[]{:S(2)}, u32[]{:S(2)}) collective-permute-start(bf16[256,512]{1,0:T(8,128)(2,1)S(1)} %add_convert_fusion), channel_id=1, source_target_pairs={{16,24},{20,28},{8,0},{12,4},{17,25},{21,29},{9,1},{13,5},{18,26},... | collective-permute-start | bytes 786440 | tf_op jit(solution)/shard_map/ppermute | solution.py:135
  127.4 38.7 %collective-permute-start.34 = (bf16[256,512]{1,0:T(8,128)(2,1)S(1)}, bf16[256,512]{1,0:T(8,128)(2,1)S(1)}, u32[]{:S(2)}, u32[]{:S(2)}) collective-permute-start(bf16[256,512]{1,0:T(8,128)(2,1)S(1)} %fusion.14), channel_id=1, source_target_pairs={{8,16},{12,20},{16,8},{20,12},{9,17},{13,21},{17,9},{21,13},{10,18... | collective-permute-start | bytes 786440 | tf_op jit(solution)/shard_map/ppermute | solution.py:132
  133.5 21.3 %collective-permute-start.14 = (bf16[256,512]{1,0:T(8,128)(2,1)S(1)}, bf16[256,512]{1,0:T(8,128)(2,1)S(1)}, u32[]{:S(2)}, u32[]{:S(2)}) collective-permute-start(bf16[256,512]{1,0:T(8,128)(2,1)S(1)} %add_convert_fusion.6), channel_id=1, source_target_pairs={{16,24},{20,28},{8,0},{12,4},{17,25},{21,29},{9,1},{13,5},{18,26},... | collective-permute-start | bytes 786440 | tf_op jit(solution)/shard_map/ppermute | solution.py:135
  134.8 21.2 %collective-permute-start.16 = (bf16[256,512]{1,0:T(8,128)(2,1)S(1)}, bf16[256,512]{1,0:T(8,128)(2,1)S(1)}, u32[]{:S(2)}, u32[]{:S(2)}) collective-permute-start(bf16[256,512]{1,0:T(8,128)(2,1)S(1)} %fusion.26), channel_id=1, source_target_pairs={{8,16},{12,20},{16,8},{20,12},{9,17},{13,21},{17,9},{21,13},{10,18... | collective-permute-start | bytes 786440 | tf_op jit(solution)/shard_map/ppermute | solution.py:132
  135.5 29.4 %copy-start.8 = (f32[512]{0:T(512)S(1)}, f32[512]{0:T(512)}, u32[]{:S(2)}) copy-start(f32[512]{0:T(512)} %get-tuple-element.81) | copy-start | bytes 6148
  135.6 29.7 %collective-permute-start.26 = (bf16[256,512]{1,0:T(8,128)(2,1)S(1)}, bf16[256,512]{1,0:T(8,128)(2,1)S(1)}, u32[]{:S(2)}, u32[]{:S(2)}) collective-permute-start(bf16[256,512]{1,0:T(8,128)(2,1)S(1)} %add_convert_fusion.2), channel_id=1, source_target_pairs={{16,24},{20,28},{8,0},{12,4},{17,25},{21,29},{9,1},{13,5},{18,26},... | collective-permute-start | bytes 786440 | tf_op jit(solution)/shard_map/ppermute | solution.py:135
  154.8 9.0 %collective-permute-start.20 = (bf16[256,512]{1,0:T(8,128)(2,1)S(1)}, bf16[256,512]{1,0:T(8,128)(2,1)S(1)}, u32[]{:S(2)}, u32[]{:S(2)}) collective-permute-start(bf16[256,512]{1,0:T(8,128)(2,1)S(1)} %add_convert_fusion.4), channel_id=1, source_target_pairs={{16,24},{20,28},{8,0},{12,4},{17,25},{21,29},{9,1},{13,5},{18,26},... | collective-permute-start | bytes 786440 | tf_op jit(solution)/shard_map/ppermute | solution.py:135
  156.1 8.6 %collective-permute-start.22 = (bf16[256,512]{1,0:T(8,128)(2,1)S(1)}, bf16[256,512]{1,0:T(8,128)(2,1)S(1)}, u32[]{:S(2)}, u32[]{:S(2)}) collective-permute-start(bf16[256,512]{1,0:T(8,128)(2,1)S(1)} %fusion.22), channel_id=1, source_target_pairs={{8,16},{12,20},{16,8},{20,12},{9,17},{13,21},{17,9},{21,13},{10,18... | collective-permute-start | bytes 786440 | tf_op jit(solution)/shard_map/ppermute | solution.py:132
  157.5 8.2 %copy-start.7 = (f32[512]{0:T(512)S(1)}, f32[512]{0:T(512)}, u32[]{:S(2)}) copy-start(f32[512]{0:T(512)} %get-tuple-element.83) | copy-start | bytes 6148
  163.8 1.6 collective-permute-start.28
  165.3 1.0 copy-start.6
  166.8 19.5 %copy-start.14 = (s32[4]{0:T(128)S(1)}, s32[4]{0:T(128)}, u32[]{:S(2)}) copy-start(s32[4]{0:T(128)} %param.19) | copy-start | bytes 52
  166.8 19.5 %copy-start.4 = (s32[4,128,1]{2,1,0:T(8,128)S(1)}, s32[4,128,1]{2,1,0:T(8,128)}, u32[]{:S(2)}) copy-start(s32[4,128,1]{2,1,0:T(8,128)} %add.361) | copy-start | bytes 6148
  166.8 19.5 %copy-start.11 = (s32[128]{0:T(128)S(1)}, s32[128]{0:T(128)}, u32[]{:S(2)}) copy-start(s32[128]{0:T(128)} %copy-done.10) | copy-start | bytes 1540
  166.8 27.7 %copy-start = (bf16[4,128,1024]{2,1,0:T(8,128)(2,1)S(1)}, bf16[4,128,1024]{2,1,0:T(8,128)(2,1)}, u32[]{:S(2)}) copy-start(bf16[4,128,1024]{2,1,0:T(8,128)(2,1)} %query_ref.1) | copy-start | bytes 3145732
  166.8 27.7 %copy-start.1 = (bf16[4,128,256]{2,1,0:T(8,128)(2,1)S(1)}, bf16[4,128,256]{2,1,0:T(8,128)(2,1)}, u32[]{:S(2)}) copy-start(bf16[4,128,256]{2,1,0:T(8,128)(2,1)} %text_ref.1) | copy-start | bytes 786436
  167.1 2.2 %collective-permute-start.35 = (bf16[2,256,256]{2,1,0:T(8,128)(2,1)S(1)}, bf16[2,256,256]{2,1,0:T(8,128)(2,1)S(1)}, u32[]{:S(2)}, u32[]{:S(2)}) collective-permute-start(bf16[2,256,256]{2,1,0:T(8,128)(2,1)S(1)} %fusion.30), channel_id=1, source_target_pairs={{0,1},{1,0},{2,3},{3,2},{4,5},{5,4},{6,7},{7,6},{8,9},{9,8},{10,11... | collective-permute-start | bytes 786440 | tf_op jit(solution)/shard_map/ppermute | solution.py:24
  167.2 1.5 collective-permute-start.37
  168.7 3.6 %collective-permute-start.38 = (f32[256]{0:T(256)S(1)}, f32[256]{0:T(256)S(1)}, u32[]{:S(2)}, u32[]{:S(2)}) collective-permute-start(f32[256]{0:T(256)S(1)} %add.337), channel_id=1, source_target_pairs={{0,2},{1,3},{2,0},{3,1},{4,6},{5,7},{6,4},{7,5},{8,10},{9,11},{10,... | collective-permute-start | bytes 3080 | tf_op jit(solution)/shard_map/ppermute | solution.py:24
  169.4 5.3 %collective-permute-start.36 = (bf16[1,256,256]{2,1,0:T(8,128)(2,1)S(1)}, bf16[1,256,256]{2,1,0:T(8,128)(2,1)S(1)}, u32[]{:S(2)}, u32[]{:S(2)}) collective-permute-start(bf16[1,256,256]{2,1,0:T(8,128)(2,1)S(1)} %dynamic-slice_convert_fusion.1), channel_id=1, source_target_pairs={{0,2},{1,3},{2,0},{3,1},{4,6},{5,7},{6,4},{7,5},{8,10},{9,11},{10,... | collective-permute-start | bytes 393224 | tf_op jit(solution)/shard_map/ppermute | solution.py:24
  175.8 18.8 %all-to-all-start = ((bf16[8,64,256]{2,1,0:T(8,128)(2,1)}), bf16[8,64,256]{2,1,0:T(8,128)(2,1)S(1)}, u32[]{:S(2)}, u32[]{:S(2)}) async-start(bf16[8,64,256]{2,1,0:T(8,128)(2,1)} %bitcast.25), calls=%async_computation | async-start | bytes 524288 | tf_op jit(solution)/shard_map/all_to_all | solution.py:371

commit v4 on v3

--- a/solution.py
+++ b/solution.py
@@ -24,7 +24,7 @@
     return lax.ppermute(value, axis, [(i, i ^ bit) for i in range(count)])
 
 
-def transpose_panels(local):
+def transpose_panels(local, swap):
     seq_count, tp_count = lax.axis_size("seq"), lax.axis_size("tp")
     width = seq_count // tp_count
     half = tp_count // 2
@@ -32,7 +32,7 @@
     for origin in range(tp_count):
         for inner in range(width):
             for block in range(tp_count):
-                source = (origin * width + inner) * tp_count + block
+                source = (origin * width + inner) * tp_count + (block ^ swap)
                 slot = ((origin ^ block) & 1) * half + origin // 2
                 pairs.append((source, (block * width + inner) * tp_count + slot))
     held = [lax.ppermute(local, ("seq", "tp"), pairs)]
@@ -52,64 +52,67 @@
 ROLE_GROUPS = (3, 0, 2, 1)
 
 
-def partial_kernel(pieces, blocks, roles_ref, *refs):
-    rows_refs = refs[: 4 * pieces]
-    weights_refs = refs[4 * pieces : 4 * pieces + blocks]
-    far_end, near_end, far_mid, near_mid, first, second, held = refs[4 * pieces + blocks :]
-    rows = rows_refs[0].shape[0]
+def order_kernel(pieces, roles_ref, *refs):
+    out_ref = refs[-1]
     for place in range(4):
         for piece in range(pieces):
-            total = None
-            at = 0
-            for weights in weights_refs:
-                depth = weights.shape[0]
-                term = jnp.dot(
-                    rows_refs[place * pieces + piece][:, at : at + depth],
-                    weights[...],
-                    preferred_element_type=jnp.float32,
-                )
-                total = term if total is None else total + term
-                at += depth
-            held[roles_ref[place], piece * rows : (piece + 1) * rows] = total
-    far_end[...] = held[0]
-    near_end[...] = held[1]
-    far_mid[...] = held[2]
-    near_mid[...] = held[3]
-    first[...] = held[0].astype(jnp.bfloat16)
-    second[0] = held[2].astype(jnp.bfloat16)
-    second[1] = held[3].astype(jnp.bfloat16)
-
-
-def partial_products(roles, held, weights):
+            rows_ref = refs[place * pieces + piece]
+            rows = rows_ref.shape[0]
+            out_ref[roles_ref[place], piece * rows : (piece + 1) * rows] = rows_ref[...]
+
+
+def order_rows(roles, held):
     pieces = len(held[0])
     rows, depth = held[0][0].shape
-    columns = weights[0].shape[1]
-    tile = min(columns, 256)
-    block_rows = pieces * rows
-    one = pl.BlockSpec((block_rows, tile), lambda i, roles: (0, i))
     return pl.pallas_call(
-        functools.partial(partial_kernel, pieces, len(weights)),
+        functools.partial(order_kernel, pieces),
         grid_spec=pltpu.PrefetchScalarGridSpec(
             num_scalar_prefetch=1,
-            grid=(columns // tile,),
-            in_specs=[pl.BlockSpec((rows, depth), lambda i, roles: (0, 0))] * (4 * pieces)
-            + [pl.BlockSpec((w.shape[0], tile), lambda i, roles: (0, i)) for w in weights],
-            out_specs=[one] * 5
-            + [pl.BlockSpec((2, block_rows, tile), lambda i, roles: (0, 0, i))],
-            scratch_shapes=[pltpu.VMEM((4, block_rows, tile), jnp.float32)],
-        ),
-        out_shape=[jax.ShapeDtypeStruct((block_rows, columns), jnp.float32)] * 4
-        + [
-            jax.ShapeDtypeStruct((block_rows, columns), jnp.bfloat16),
-            jax.ShapeDtypeStruct((2, block_rows, columns), jnp.bfloat16),
-        ],
+            grid=(1,),
+            in_specs=[pl.BlockSpec((rows, depth), lambda i, roles: (0, 0))] * (4 * pieces),
+            out_specs=pl.BlockSpec((4, pieces * rows, depth), lambda i, roles: (0, 0, 0)),
+        ),
+        out_shape=jax.ShapeDtypeStruct((4, pieces * rows, depth), jnp.bfloat16),
         compiler_params=pltpu.CompilerParams(vmem_limit_bytes=VMEM),
         cost_estimate=pl.CostEstimate(
-            flops=8 * block_rows * depth * columns,
-            bytes_accessed=8 * block_rows * depth + 2 * depth * columns + 22 * block_rows * columns,
+            flops=0, bytes_accessed=16 * pieces * rows * depth, transcendentals=0
+        ),
+    )(roles, *[piece for place in held for piece in place])
+
+
+def partial_kernel(rows_ref, weights_ref, far_end, near_end, middles):
+    _, rows, depth = rows_ref.shape
+    held = rows_ref[...].reshape(4 * rows, depth)
+    total = jnp.dot(held, weights_ref[...], preferred_element_type=jnp.float32)
+    total = total.astype(jnp.bfloat16)
+    far_end[...] = total[:rows]
+    near_end[...] = total[rows : 2 * rows]
+    middles[0] = total[2 * rows : 3 * rows]
+    middles[1] = total[3 * rows :]
+
+
+def partial_products(held, weights):
+    _, rows, depth = held.shape
+    columns = weights.shape[1]
+    tile = min(columns, 256)
+    one = pl.BlockSpec((rows, tile), lambda i: (0, i))
+    return pl.pallas_call(
+        partial_kernel,
+        grid=(columns // tile,),
+        in_specs=[
+            pl.BlockSpec(held.shape, lambda i: (0, 0, 0)),
+            pl.BlockSpec((depth, tile), lambda i: (0, i)),
+        ],
+        out_specs=[one, one, pl.BlockSpec((2, rows, tile), lambda i: (0, 0, i))],
+        out_shape=[jax.ShapeDtypeStruct((rows, columns), jnp.bfloat16)] * 2
+        + [jax.ShapeDtypeStruct((2, rows, columns), jnp.bfloat16)],
+        compiler_params=pltpu.CompilerParams(vmem_limit_bytes=VMEM),
+        cost_estimate=pl.CostEstimate(
+            flops=8 * rows * depth * columns,
+            bytes_accessed=8 * rows * depth + 2 * depth * columns + 8 * rows * columns,
             transcendentals=0,
         ),
-    )(roles, *[piece for place in held for piece in place], *weights)
+    )(held, weights)
 
 
 def along(pairs):
@@ -123,20 +126,22 @@
 
 
 def reduce_groups(parts, is_end):
-    far_end, near_end, far_mid, near_mid, first, second = parts
-    first = lax.ppermute(first, "seq", along(ENDS_IN))
-    second = lax.ppermute(second, "seq", along(ENDS_IN))
-    passed = lax.ppermute(
-        (far_end + first.astype(jnp.float32)).astype(jnp.bfloat16), "seq", along(MIDDLES)
-    )
-    crossed = lax.ppermute(
-        (far_mid + second[0].astype(jnp.float32)).astype(jnp.bfloat16), "seq", along(MIDDLES)
-    )
-    outer = lax.ppermute(
-        (near_end + passed.astype(jnp.float32)).astype(jnp.bfloat16), "seq", along(ENDS_OUT)
-    )
-    end = near_end + outer.astype(jnp.float32)
-    middle = near_mid + second[1].astype(jnp.float32) + crossed.astype(jnp.float32)
+    far_end, near_end, middles = parts
+
+    def add(mine, other):
+        return (mine.astype(jnp.float32) + other.astype(jnp.float32)).astype(jnp.bfloat16)
+
+    first = lax.ppermute(far_end, "seq", along(ENDS_IN))
+    second = lax.ppermute(middles, "seq", along(ENDS_IN))
+    passed = lax.ppermute(add(far_end, first), "seq", along(MIDDLES))
+    crossed = lax.ppermute(add(middles[0], second[0]), "seq", along(MIDDLES))
+    outer = lax.ppermute(add(near_end, passed), "seq", along(ENDS_OUT))
+    end = near_end.astype(jnp.float32) + outer.astype(jnp.float32)
+    middle = (
+        middles[1].astype(jnp.float32)
+        + second[1].astype(jnp.float32)
+        + crossed.astype(jnp.float32)
+    )
     return jnp.where(is_end, end, middle).astype(jnp.bfloat16)
 
 
@@ -145,46 +150,39 @@
     assert tp_count == 4 and seq_count % 4 == 0
     width = seq_count // tp_count
     tiles, panel_rows, depth = panels.shape
-    share = w_merge.shape[0]
     group = lax.axis_index("seq") // width
-    inner = lax.axis_index("seq") % width
     local = panels.reshape(tiles * panel_rows, depth)
-    turned = lax.dynamic_slice_in_dim(
-        jnp.concatenate([local, local], axis=1), inner * share, depth, axis=1
-    )
-    half = turned.shape[0] // 2
-    held_pieces = [transpose_panels(turned[:half]), transpose_panels(turned[half:])]
-    held = list(zip(*held_pieces))
+    half = local.shape[0] // 2
+    held = list(
+        zip(
+            transpose_panels(local[:half], 0),
+            transpose_panels(flip(local[half:], "tp", 2), 2),
+        )
+    )
+    inner_groups = [[g * width + i for i in range(width)] for g in range(tp_count)]
     columns = w_merge.shape[1] // CHUNKS
-    own_chunks = [w_merge[:, c * columns : (c + 1) * columns] for c in range(CHUNKS)]
-    small = jnp.concatenate([small, flip(small, "seq", 1)], axis=0)
-    own_chunks, small = lax.optimization_barrier((own_chunks, small))
+    weights = [
+        lax.all_gather(
+            w_merge[:, c * columns : (c + 1) * columns],
+            "seq",
+            axis=0,
+            tiled=True,
+            axis_index_groups=inner_groups,
+        )
+        for c in range(CHUNKS)
+    ]
+    for bit in bits_of(seq_count):
+        small = jnp.concatenate([small, flip(small, "seq", bit)], axis=0)
     shift = jnp.where(group < 2, 0, 3)
     groups = (panel_base() ^ jnp.arange(4, dtype=jnp.int32)) ^ shift
     roles = jnp.array([ROLE_GROUPS.index(g) for g in range(4)], jnp.int32)[groups]
     is_end = (group == 0) | (group == 3)
-    received = []
-    for own in own_chunks:
-        pieces = []
-        for offset in range(1, width):
-            pairs = [
-                (g * width + (i + offset) % width, g * width + i)
-                for g in range(tp_count)
-                for i in range(width)
-            ]
-            pieces.append(lax.ppermute(own, "seq", pairs))
-        received.append(pieces)
-    _, small = lax.optimization_barrier((held_pieces[1][0], small))
-    for bit in bits_of(seq_count)[1:]:
-        small = jnp.concatenate([small, flip(small, "seq", bit)], axis=0)
+    held = order_rows(roles, held)
     kv = 0.0
     squares = 0.0
     for chunk in range(CHUNKS):
-        weights = [own_chunks[chunk]] + received[chunk]
-        if share % 128:
-            weights = [jnp.concatenate(weights, axis=0)]
-        parts = partial_products(roles, held, weights)
-        merged = reduce_groups(parts, is_end).astype(jnp.float32)
+        merged = reduce_groups(partial_products(held, weights[chunk]), is_end)
+        merged = merged.astype(jnp.float32)
         squares = squares + jnp.sum(merged * merged, axis=1)
         gain = ln_gain[chunk * columns : (chunk + 1) * columns].astype(jnp.float32)
         kv = kv + jnp.dot(

time: 201 us -> 238 us (1.18)
  waiting for transfers between devices: 76 us -> 101 us
  local copies, waits for them, and re-layouts: 8.64 us -> 23.7 us
  between operations: 1.5 us -> 14.8 us
  starting transfers between devices: 75.9 us -> 65.6 us
  Pallas kernels: 23.9 us -> 15.5 us
    ppermute x13 -> x14, waiting for transfers between devices: 11.4 us -> 31.5 us  [flip(): return lax.ppermute(value, axis, [(i, i ^ bit) for i in range(count)])]
    unnamed x32 -> x88, local copies, waits for them, and re-layouts: 0.79 us -> 16.5 us
    all_gather x0 -> x4, waiting for transfers between devices: none -> 14.2 us  [merge_tiles(): lax.all_gather(w_merge[:, c * columns:(c + 1) * columns], 'seq', axis=0,...]
    ppermute x24 -> x20, waiting for transfers between devices: 57.5 us -> 46.8 us  [the longest x4 31.7 us: reduce_groups(): outer = lax.ppermute(add(near_end, passed), 'seq', along(ENDS_OUT))]
    pallas_call x4 -> x5, Pallas kernels: 18.4 us -> 10 us  [the longest x4 9.28 us: partial_products(): pl.pallas_call(partial_kernel, grid=(columns // tile,), in_specs=[pl.Bloc...]
    ppermute x13 -> x14, starting transfers between devices: 28.1 us -> 23.2 us  [flip(): return lax.ppermute(value, axis, [(i, i ^ bit) for i in range(count)])]
    ppermute x24 -> x20, starting transfers between devices: 33.9 us -> 29.2 us  [the longest x4 11.1 us: reduce_groups(): second = lax.ppermute(middles, 'seq', along(ENDS_IN))]
    convert_element_type x12, other arithmetic: 2.81 us -> 5.95 us  [add(): (mine.astype(jnp.float32) + other.astype(jnp.float32)).astype(jnp.bfloat16)]
  transfers between devices with their start and end apart: 40 -> 41, of which waited for: 14 -> 13; matrix products, arithmetic and copies ran while one was open for 9% -> 7% of each run, Pallas kernels for 9% -> 4%
where the time goes in v4:
time: 238 us; the launch traced here: 236 us
  waiting for transfers between devices  101 us (42%)
  starting transfers between devices  65.6 us (28%)
  local copies, waits for them, and re-layouts  23.7 us (10%)
  Pallas kernels  15.5 us (7%)
  between operations  14.8 us (6%)
  other arithmetic  12.4 us (5%)
  matrix products  2.78 us (1%)
    ppermute x4, waiting for transfers between devices, reduce_groups(): outer = lax.ppermute(add(near_end, passed), 'seq', along(ENDS_OUT))  31.7 us
    ppermute x14, waiting for transfers between devices, flip(): return lax.ppermute(value, axis, [(i, i ^ bit) for i in range(count)])  31.5 us
    ppermute x14, starting transfers between devices, flip(): return lax.ppermute(value, axis, [(i, i ^ bit) for i in range(count)])  23.2 us
    unnamed x88, local copies, waits for them, and re-layouts  16.5 us
    all_gather x4, waiting for transfers between devices, merge_tiles(): lax.all_gather(w_merge[:, c * columns:(c + 1) * columns], 'seq', axis=0,...  14.2 us
    ppermute x4, waiting for transfers between devices, reduce_groups(): first = lax.ppermute(far_end, 'seq', along(ENDS_IN))  11.2 us
    ppermute x4, starting transfers between devices, reduce_groups(): second = lax.ppermute(middles, 'seq', along(ENDS_IN))  11.1 us
    all_to_all x1, starting transfers between devices, shards(): lax.all_to_all(outgoing, 'seq', split_axis=0, concat_axis=0, tiled=True)  10.6 us
  transfers between devices with their start and end apart: 41, of which 13 were waited for; matrix products, arithmetic and copies ran while one was open for 7% of the time, Pallas kernels for 4%

profile of v4, /device:TPU:0, one launch (start us, length us, event | category | flops | bytes accessed | tf_op | source)
XLA Modules:
  0.0 236.3 jit_solution(4752637231029190331)
XLA Ops:
  7.3 3.3 %fusion.59 = (bf16[640,512]{1,0:T(8,128)(2,1)}, bf16[640,512]{1,0:T(8,128)(2,1)}, bf16[640,512]{1,0:T(8,128)(2,1)}, bf16[640,512]{1,0:T(8,128)(2,1)}) fusion(bf16[640,2048]{1,0:T(8,128)(2,1)} %param.13), kind=kLoop, calls=%fused_computation.137 | loop fusion | bytes 5242880 | tf_op jit(solution)/shard_map/slice | solution.py:166
  12.2 3.0 %collective-permute-start.4 = (bf16[128,1280]{1,0:T(8,128)(2,1)S(1)}, bf16[128,1280]{1,0:T(8,128)(2,1)S(1)}, u32[]{:S(2)}, u32[]{:S(2)}) collective-permute-start(bf16[128,1280]{1,0:T(8,128)(2,1)S(1)} %get-tuple-element.42), channel_id=1, source_target_pairs={{0,2},{1,3},{2,0},{3,1},{4,6},{5,7},{6,4},{7,5},{8,10},{9,11},{10,... | collective-permute-start | bytes 983048 | tf_op jit(solution)/shard_map/ppermute | solution.py:24
  16.2 1.6 collective-permute-start
  18.8 0.8 gather_fusion.2
  21.7 3.3 %collective-permute-start.1 = (bf16[2,48,256]{2,1,0:T(8,128)(2,1)S(1)}, bf16[2,48,256]{2,1,0:T(8,128)(2,1)S(1)}, u32[]{:S(2)}, u32[]{:S(2)}) collective-permute-start(bf16[2,48,256]{2,1,0:T(8,128)(2,1)S(1)} %pad_maximum_fusion.3), channel_id=1, source_target_pairs={{0,8},{4,12},{8,0},{12,4},{16,24},{20,28},{24,16},{28,20},{1,9},{5... | collective-permute-start | bytes 147464 | tf_op jit(solution)/shard_map/ppermute | solution.py:24
  25.6 3.7 %collective-permute-done.4 = bf16[128,1280]{1,0:T(8,128)(2,1)S(1)} collective-permute-done((bf16[128,1280]{1,0:T(8,128)(2,1)S(1)}, bf16[128,1280]{1,0:T(8,128)(2,1)S(1)}, u32[]{:S(2)}, u32[]{:S(2)}) %collective-permute-start.4) | collective-permute-done | bytes 327712 | tf_op jit(solution)/shard_map/ppermute | solution.py:24
  29.3 1.9 collective-permute-start.5
  31.3 8.5 %collective-permute-done.2 = bf16[4,48,256]{2,1,0:T(8,128)(2,1)S(1)} collective-permute-done((bf16[4,48,256]{2,1,0:T(8,128)(2,1)S(1)}, bf16[4,48,256]{2,1,0:T(8,128)(2,1)S(1)}, u32[]{:S(2)}, u32[]{:S(2)}) %collective-permute-start.2) | collective-permute-done | bytes 98336 | tf_op jit(solution)/shard_map/ppermute | solution.py:24
  40.1 11.9 %collective-permute-start.6 = (bf16[128,1280]{1,0:T(8,128)(2,1)S(1)}, bf16[128,1280]{1,0:T(8,128)(2,1)S(1)}, u32[]{:S(2)}, u32[]{:S(2)}) collective-permute-start(bf16[128,1280]{1,0:T(8,128)(2,1)S(1)} %collective-permute-done.3.refs_0_), channel_id=1, source_target_pairs={{0,2},{1,3},{2,0},{3,1},{4,6},{5,7},{6,4},{7,5},{8,10},{9,11},{10,... | collective-permute-start | bytes 983048 | tf_op jit(solution)/shard_map/ppermute | solution.py:24
  52.7 7.8 %collective-permute-done.6.refs_2_ = bf16[128,1280]{1,0:T(8,128)(2,1)S(1)} collective-permute-done((bf16[128,1280]{1,0:T(8,128)(2,1)S(1)}, bf16[128,1280]{1,0:T(8,128)(2,1)S(1)}, u32[]{:S(2)}, u32[]{:S(2)}) %collective-permute-start.6) | collective-permute-done | bytes 327712 | tf_op jit(solution)/shard_map/ppermute | solution.py:24
  60.5 0.7 copy-done.2
  61.2 5.7 %collective-permute-done.7.refs_3_ = bf16[128,1280]{1,0:T(8,128)(2,1)S(1)} collective-permute-done((bf16[128,1280]{1,0:T(8,128)(2,1)S(1)}, bf16[128,1280]{1,0:T(8,128)(2,1)S(1)}, u32[]{:S(2)}, u32[]{:S(2)}) %collective-permute-start.7) | collective-permute-done | bytes 327712 | tf_op jit(solution)/shard_map/ppermute | solution.py:24
  66.9 0.8 copy-done.4
  69.8 0.8 copy-done.10
  70.5 0.7 copy-done.8
  71.3 0.7 copy-done.12
  72.0 1.0 copy-done.3
  73.0 1.0 copy-done.5
  74.0 1.0 copy-done.7
  75.0 1.0 copy-done.9
  75.9 1.0 copy-done.11
  76.9 1.0 copy-done.13
  78.6 1.3 copy-done.16
  79.9 2.5 %shard_map.135 = (bf16[256,512]{1,0:T(8,128)(2,1)}, bf16[256,512]{1,0:T(8,128)(2,1)S(1)}, bf16[2,256,512]{2,1,0:T(8,128)(2,1)}) custom-call(bf16[4,256,1280]{2,1,0:T(8,128)(2,1)S(1)} %shard_map.131.rows_ref, bf16[1280,512]{1,0:T(8,128)(2,1)S(1)} %copy-done.16), custom_call_target="tpu_custom_call" | custom-call | flops 1342177280 | bytes 4980736 | tf_op jit(solution)/shard_map/pallas_call | solution.py:99
  82.5 2.0 collective-permute-start.27
  84.5 2.1 collective-permute-start.30
  86.6 1.3 copy-done.15
  87.9 2.5 %shard_map.134 = (bf16[256,512]{1,0:T(8,128)(2,1)}, bf16[256,512]{1,0:T(8,128)(2,1)S(1)}, bf16[2,256,512]{2,1,0:T(8,128)(2,1)}) custom-call(bf16[4,256,1280]{2,1,0:T(8,128)(2,1)S(1)} %shard_map.131.rows_ref, bf16[1280,512]{1,0:T(8,128)(2,1)S(1)} %copy-done.15), custom_call_target="tpu_custom_call" | custom-call | flops 1342177280 | bytes 4980736 | tf_op jit(solution)/shard_map/pallas_call | solution.py:99
  90.4 2.0 collective-permute-start.22
  92.4 2.1 collective-permute-start.25
  94.5 1.3 copy-done.14
  95.8 2.3 shard_map.133
  98.1 0.8 copy-done
  98.9 2.0 collective-permute-start.17
  100.9 14.2 %all-gather.5.cloned.1.call-done.weights_ref = bf16[1280,512]{1,0:T(8,128)(2,1)} async-done(((bf16[640,512]{1,0:T(8,128)(2,1)}), bf16[1280,512]{1,0:T(8,128)(2,1)}) %all-gather.5.cloned.1.call-update) | async-done | bytes 1310736 | tf_op jit(solution)/shard_map/all_gather | solution.py:165
  115.1 1.3 copy-done.17
  116.4 1.9 shard_map.132
  118.4 3.4 %collective-permute-start.20 = (bf16[2,256,512]{2,1,0:T(8,128)(2,1)S(1)}, bf16[2,256,512]{2,1,0:T(8,128)(2,1)S(1)}, u32[]{:S(2)}, u32[]{:S(2)}) collective-permute-start(bf16[2,256,512]{2,1,0:T(8,128)(2,1)S(1)} %copy-done.1), channel_id=1, source_target_pairs={{0,8},{4,12},{24,16},{28,20},{1,9},{5,13},{25,17},{29,21},{2,10},{... | collective-permute-start | bytes 1572872 | tf_op jit(solution)/shard_map/ppermute | solution.py:135
  121.8 1.1 add_convert_fusion.1
  122.9 1.3 collective-permute-start.12
  124.2 1.1 add_convert_fusion.3
  125.3 3.5 %collective-permute-start.15 = (bf16[2,256,512]{2,1,0:T(8,128)(2,1)S(1)}, bf16[2,256,512]{2,1,0:T(8,128)(2,1)S(1)}, u32[]{:S(2)}, u32[]{:S(2)}) collective-permute-start(bf16[2,256,512]{2,1,0:T(8,128)(2,1)S(1)} %get-tuple-element.16), channel_id=1, source_target_pairs={{0,8},{4,12},{24,16},{28,20},{1,9},{5,13},{25,17},{29,21},{2,10},{... | collective-permute-start | bytes 1572872 | tf_op jit(solution)/shard_map/ppermute | solution.py:135
  128.9 1.1 add_convert_fusion.5
  130.0 11.2 %collective-permute-done.12 = bf16[256,512]{1,0:T(8,128)(2,1)S(1)} collective-permute-done((bf16[256,512]{1,0:T(8,128)(2,1)S(1)}, bf16[256,512]{1,0:T(8,128)(2,1)S(1)}, u32[]{:S(2)}, u32[]{:S(2)}) %collective-permute-start.12) | collective-permute-done | bytes 262176 | tf_op jit(solution)/shard_map/ppermute | solution.py:134
  142.7 1.1 fusion.28
  144.5 1.1 fusion.27
  146.3 1.3 collective-permute-start.29
  148.5 3.8 %collective-permute-done.15 = bf16[2,256,512]{2,1,0:T(8,128)(2,1)S(1)} collective-permute-done((bf16[2,256,512]{2,1,0:T(8,128)(2,1)S(1)}, bf16[2,256,512]{2,1,0:T(8,128)(2,1)S(1)}, u32[]{:S(2)}, u32[]{:S(2)}) %collective-permute-start.15) | collective-permute-done | bytes 524320 | tf_op jit(solution)/shard_map/ppermute | solution.py:135
  152.3 1.3 collective-permute-start.14
  154.4 1.3 collective-permute-start.24
  155.8 23.9 %collective-permute-done.14 = bf16[256,512]{1,0:T(8,128)(2,1)S(1)} collective-permute-done((bf16[256,512]{1,0:T(8,128)(2,1)S(1)}, bf16[256,512]{1,0:T(8,128)(2,1)S(1)}, u32[]{:S(2)}, u32[]{:S(2)}) %collective-permute-start.14) | collective-permute-done | bytes 262176 | tf_op jit(solution)/shard_map/ppermute | solution.py:138
  179.7 1.3 collective-permute-start.19
  182.4 7.8 %collective-permute-done.19 = bf16[256,512]{1,0:T(8,128)(2,1)S(1)} collective-permute-done((bf16[256,512]{1,0:T(8,128)(2,1)S(1)}, bf16[256,512]{1,0:T(8,128)(2,1)S(1)}, u32[]{:S(2)}, u32[]{:S(2)}) %collective-permute-start.19) | collective-permute-done | bytes 262176 | tf_op jit(solution)/shard_map/ppermute | solution.py:138
  190.2 0.8 collective-permute-start.26
  191.8 1.3 fusion.19
  193.6 1.3 fusion.24
  196.5 0.8 collective-permute-done.34
  197.3 1.7 collective-permute-start.35
  199.5 1.4 collective-permute-done.35
  200.9 3.6 %collective-permute-done.33 = bf16[1,256,256]{2,1,0:T(8,128)(2,1)S(1)} collective-permute-done((bf16[1,256,256]{2,1,0:T(8,128)(2,1)S(1)}, bf16[1,256,256]{2,1,0:T(8,128)(2,1)S(1)}, u32[]{:S(2)}, u32[]{:S(2)}) %collective-permute-start.33) | collective-permute-done | bytes 131104 | tf_op jit(solution)/shard_map/ppermute | solution.py:24
  204.5 1.0 convolution_convert_fusion
  205.5 10.6 %all-to-all-start = ((bf16[8,64,256]{2,1,0:T(8,128)(2,1)}), bf16[8,64,256]{2,1,0:T(8,128)(2,1)S(1)}, u32[]{:S(2)}, u32[]{:S(2)}) async-start(bf16[8,64,256]{2,1,0:T(8,128)(2,1)} %bitcast.26), calls=%async_computation | async-start | bytes 524288 | tf_op jit(solution)/shard_map/all_to_all | solution.py:369
  216.7 7.6 %all-to-all-done = bf16[8,64,256]{2,1,0:T(8,128)(2,1)S(1)} async-done(((bf16[8,64,256]{2,1,0:T(8,128)(2,1)}), bf16[8,64,256]{2,1,0:T(8,128)(2,1)S(1)}, u32[]{:S(2)}, u32[]{:S(2)}) %all-to-all-start) | async-done | bytes 262176 | tf_op jit(solution)/shard_map/all_to_all | solution.py:369
  224.3 5.5 %shard_map.136 = (bf16[4,128,1024]{2,1,0:T(8,128)(2,1)}, bf16[256,256]{1,0:T(8,128)(2,1)}) custom-call(s32[4]{0:T(128)S(1)} %broadcast_xor_fusion.place_ref, bf16[4,128,1024]{2,1,0:T(8,128)(2,1)S(1)} %copy-done.18, bf16[8,32,256]{2,1,0:T(8,128)(2,1)S(1)} %slice.146.prefix_ref, bf16[4,128,256]{2,1,0:T(8,128)(2,1)S(1)} %copy-done.19, ...), custom_call_target="tpu_custom_call" | custom-call | flops 603979776 | bytes 4194304 | tf_op jit(solution)/shard_map/pallas_call | solution.py:272
  (201 shorter events, 19.5 us)
Async XLA Ops:
  7.2 5.0 %copy-start.24 = (bf16[32,8,1280]{2,1,0:T(8,128)(2,1)S(1)}, bf16[32,8,1280]{2,1,0:T(8,128)(2,1)}, u32[]{:S(2)}) copy-start(bf16[32,8,1280]{2,1,0:T(8,128)(2,1)} %param.12) | copy-start | bytes 1966084
  7.2 8.8 %copy-start.40 = (s32[32,1]{0,1:T(1,128)S(1)}, s32[32,1]{0,1:T(1,128)}, u32[]{:S(2)}) copy-start(s32[32,1]{0,1:T(1,128)} %param.16) | copy-start | bytes 388
  7.2 8.9 %copy-start.41 = (s32[32]{0:T(128)S(1)}, s32[32]{0:T(128)}, u32[]{:S(2)}) copy-start(s32[32]{0:T(128)} %param.17) | copy-start | bytes 388
  7.2 9.0 %copy-start.31 = (bf16[1,32,256]{2,1,0:T(8,128)(2,1)S(1)}, bf16[1,32,256]{2,1,0:T(8,128)(2,1)}, u32[]{:S(2)}) copy-start(bf16[1,32,256]{2,1,0:T(8,128)(2,1)} %param.20) | copy-start | bytes 49156
  7.2 10.6 %copy-start.38 = (bf16[2048]{0:T(1024)(128)(2,1)S(1)}, bf16[2048]{0:T(1024)(128)(2,1)}, u32[]{:S(2)}) copy-start(bf16[2048]{0:T(1024)(128)(2,1)} %param.14) | copy-start | bytes 12292
  7.2 11.2 %copy-start.42 = (s32[1,4]{1,0:T(1,128)S(1)}, s32[1,4]{1,0:T(1,128)}, u32[]{:S(2)}) copy-start(s32[1,4]{1,0:T(1,128)} %param.18) | copy-start | bytes 52
  7.2 71.4 %all-gather.11.cloned.1.call-start = ((), (), s32[]{:S(2)}) async-start(), calls=%async_computation.4 | async-start | bytes 1966080 | tf_op jit(solution)/shard_map/all_gather | solution.py:165
  10.6 14.3 %copy-start.20 = (s32[4]{0:T(128)S(1)}, s32[4]{0:T(128)}, u32[]{:S(2)}) copy-start(s32[4]{0:T(128)} %constant.117.clone) | copy-start | bytes 52
  10.6 75.9 %all-gather.9.cloned.1.call-start = ((), (), s32[]{:S(2)}) async-start(), calls=%async_computation.3 | async-start | bytes 1966080 | tf_op jit(solution)/shard_map/all_gather | solution.py:165
  11.4 83.1 %all-gather.7.cloned.1.call-start = ((), (), s32[]{:S(2)}) async-start(), calls=%async_computation.2 | async-start | bytes 1966080 | tf_op jit(solution)/shard_map/all_gather | solution.py:165
  12.1 103.0 %all-gather.5.cloned.1.call-start = ((), (), s32[]{:S(2)}) async-start(), calls=%async_computation.1 | async-start | bytes 1966080 | tf_op jit(solution)/shard_map/all_gather | solution.py:165
  12.2 17.0 %collective-permute-start.4 = (bf16[128,1280]{1,0:T(8,128)(2,1)S(1)}, bf16[128,1280]{1,0:T(8,128)(2,1)S(1)}, u32[]{:S(2)}, u32[]{:S(2)}) collective-permute-start(bf16[128,1280]{1,0:T(8,128)(2,1)S(1)} %get-tuple-element.42), channel_id=1, source_target_pairs={{0,2},{1,3},{2,0},{3,1},{4,6},{5,7},{6,4},{7,5},{8,10},{9,11},{10,... | collective-permute-start | bytes 983048 | tf_op jit(solution)/shard_map/ppermute | solution.py:24
  15.3 24.8 %collective-permute-start.3 = (bf16[128,1280]{1,0:T(8,128)(2,1)S(1)}, bf16[128,1280]{1,0:T(8,128)(2,1)S(1)}, u32[]{:S(2)}, u32[]{:S(2)}) collective-permute-start(bf16[128,1280]{1,0:T(8,128)(2,1)S(1)} %get-tuple-element.43), channel_id=1, source_target_pairs={{0,0},{1,10},{2,16},{3,26},{4,4},{5,14},{6,20},{7,30},{8,2},{9,8},... | collective-permute-start | bytes 983048 | tf_op jit(solution)/shard_map/ppermute | solution.py:38
  16.2 5.4 %collective-permute-start = (bf16[1,48,256]{2,1,0:T(8,128)(2,1)S(1)}, bf16[1,48,256]{2,1,0:T(8,128)(2,1)S(1)}, u32[]{:S(2)}, u32[]{:S(2)}) collective-permute-start(bf16[1,48,256]{2,1,0:T(8,128)(2,1)S(1)} %maximum_bitcast_fusion), channel_id=1, source_target_pairs={{0,4},{4,0},{8,12},{12,8},{16,20},{20,16},{24,28},{28,24},{1,5},{5... | collective-permute-start | bytes 73736 | tf_op jit(solution)/shard_map/ppermute | solution.py:24
  19.9 11.3 %copy-start.25 = (s32[4,16,8]{2,1,0:T(8,128)}, s32[4,16,8]{2,1,0:T(8,128)S(1)}, u32[]{:S(2)}) copy-start(s32[4,16,8]{2,1,0:T(8,128)S(1)} %add.358) | copy-start | bytes 6148
  20.1 11.1 %copy-start.27 = (pred[4,16,8]{2,1,0:T(8,128)(4,1)}, pred[4,16,8]{2,1,0:T(8,128)(4,1)S(1)}, u32[]{:S(2)}) copy-start(pred[4,16,8]{2,1,0:T(8,128)(4,1)S(1)} %broadcast_in_dim.23) | copy-start | bytes 1540
  21.7 9.5 %collective-permute-start.1 = (bf16[2,48,256]{2,1,0:T(8,128)(2,1)S(1)}, bf16[2,48,256]{2,1,0:T(8,128)(2,1)S(1)}, u32[]{:S(2)}, u32[]{:S(2)}) collective-permute-start(bf16[2,48,256]{2,1,0:T(8,128)(2,1)S(1)} %pad_maximum_fusion.3), channel_id=1, source_target_pairs={{0,8},{4,12},{8,0},{12,4},{16,24},{20,28},{24,16},{28,20},{1,9},{5... | collective-permute-start | bytes 147464 | tf_op jit(solution)/shard_map/ppermute | solution.py:24
  29.3 22.7 %collective-permute-start.5 = (bf16[128,1280]{1,0:T(8,128)(2,1)S(1)}, bf16[128,1280]{1,0:T(8,128)(2,1)S(1)}, u32[]{:S(2)}, u32[]{:S(2)}) collective-permute-start(bf16[128,1280]{1,0:T(8,128)(2,1)S(1)} %collective-permute-done.4), channel_id=1, source_target_pairs={{2,0},{3,10},{0,16},{1,26},{6,4},{7,14},{4,20},{5,30},{10,2},{11,8... | collective-permute-start | bytes 983048 | tf_op jit(solution)/shard_map/ppermute | solution.py:38
  31.2 51.3 %copy-start.22 = (bf16[2,48,256]{2,1,0:T(8,128)(2,1)}, bf16[2,48,256]{2,1,0:T(8,128)(2,1)S(1)}, u32[]{:S(2)}) copy-start(bf16[2,48,256]{2,1,0:T(8,128)(2,1)S(1)} %collective-permute-done.1) | copy-start | bytes 147460
  31.2 8.6 %collective-permute-start.2 = (bf16[4,48,256]{2,1,0:T(8,128)(2,1)S(1)}, bf16[4,48,256]{2,1,0:T(8,128)(2,1)S(1)}, u32[]{:S(2)}, u32[]{:S(2)}) collective-permute-start(bf16[4,48,256]{2,1,0:T(8,128)(2,1)S(1)} %pad_maximum_fusion.2), channel_id=1, source_target_pairs={{0,16},{4,20},{8,24},{12,28},{16,0},{20,4},{24,8},{28,12},{1,17},{... | collective-permute-start | bytes 294920 | tf_op jit(solution)/shard_map/ppermute | solution.py:24
  40.1 20.4 %collective-permute-start.6 = (bf16[128,1280]{1,0:T(8,128)(2,1)S(1)}, bf16[128,1280]{1,0:T(8,128)(2,1)S(1)}, u32[]{:S(2)}, u32[]{:S(2)}) collective-permute-start(bf16[128,1280]{1,0:T(8,128)(2,1)S(1)} %collective-permute-done.3.refs_0_), channel_id=1, source_target_pairs={{0,2},{1,3},{2,0},{3,1},{4,6},{5,7},{6,4},{7,5},{8,10},{9,11},{10,... | collective-permute-start | bytes 983048 | tf_op jit(solution)/shard_map/ppermute | solution.py:24
  52.0 14.9 %collective-permute-start.7 = (bf16[128,1280]{1,0:T(8,128)(2,1)S(1)}, bf16[128,1280]{1,0:T(8,128)(2,1)S(1)}, u32[]{:S(2)}, u32[]{:S(2)}) collective-permute-start(bf16[128,1280]{1,0:T(8,128)(2,1)S(1)} %collective-permute-done.5.refs_1_), channel_id=1, source_target_pairs={{0,2},{1,3},{2,0},{3,1},{4,6},{5,7},{6,4},{7,5},{8,10},{9,11},{10,... | collective-permute-start | bytes 983048 | tf_op jit(solution)/shard_map/ppermute | solution.py:24
  52.1 16.9 %collective-permute-start.8 = (bf16[128,1280]{1,0:T(8,128)(2,1)S(1)}, bf16[128,1280]{1,0:T(8,128)(2,1)S(1)}, u32[]{:S(2)}, u32[]{:S(2)}) collective-permute-start(bf16[128,1280]{1,0:T(8,128)(2,1)S(1)} %collective-permute-done.3.refs_0_), channel_id=1, source_target_pairs={{0,1},{1,0},{2,3},{3,2},{4,5},{5,4},{6,7},{7,6},{8,9},{9,8},{10,11... | collective-permute-start | bytes 983048 | tf_op jit(solution)/shard_map/ppermute | solution.py:24
  52.2 18.4 %collective-permute-start.9 = (bf16[128,1280]{1,0:T(8,128)(2,1)S(1)}, bf16[128,1280]{1,0:T(8,128)(2,1)S(1)}, u32[]{:S(2)}, u32[]{:S(2)}) collective-permute-start(bf16[128,1280]{1,0:T(8,128)(2,1)S(1)} %collective-permute-done.5.refs_1_), channel_id=1, source_target_pairs={{0,1},{1,0},{2,3},{3,2},{4,5},{5,4},{6,7},{7,6},{8,9},{9,8},{10,11... | collective-permute-start | bytes 983048 | tf_op jit(solution)/shard_map/ppermute | solution.py:24
  60.5 9.3 %collective-permute-start.10 = (bf16[128,1280]{1,0:T(8,128)(2,1)S(1)}, bf16[128,1280]{1,0:T(8,128)(2,1)S(1)}, u32[]{:S(2)}, u32[]{:S(2)}) collective-permute-start(bf16[128,1280]{1,0:T(8,128)(2,1)S(1)} %collective-permute-done.6.refs_2_), channel_id=1, source_target_pairs={{0,1},{1,0},{2,3},{3,2},{4,5},{5,4},{6,7},{7,6},{8,9},{9,8},{10,11... | collective-permute-start | bytes 983048 | tf_op jit(solution)/shard_map/ppermute | solution.py:24
  66.9 4.4 %collective-permute-start.11 = (bf16[128,1280]{1,0:T(8,128)(2,1)S(1)}, bf16[128,1280]{1,0:T(8,128)(2,1)S(1)}, u32[]{:S(2)}, u32[]{:S(2)}) collective-permute-start(bf16[128,1280]{1,0:T(8,128)(2,1)S(1)} %collective-permute-done.7.refs_3_), channel_id=1, source_target_pairs={{0,1},{1,0},{2,3},{3,2},{4,5},{5,4},{6,7},{7,6},{8,9},{9,8},{10,11... | collective-permute-start | bytes 983048 | tf_op jit(solution)/shard_map/ppermute | solution.py:24
  82.5 35.9 %collective-permute-start.27 = (bf16[256,512]{1,0:T(8,128)(2,1)}, bf16[256,512]{1,0:T(8,128)(2,1)}, u32[]{:S(2)}, u32[]{:S(2)}) collective-permute-start(bf16[256,512]{1,0:T(8,128)(2,1)} %get-tuple-element.24), channel_id=1, source_target_pairs={{0,8},{4,12},{24,16},{28,20},{1,9},{5,13},{25,17},{29,21},{2,10},{... | collective-permute-start | bytes 786440 | tf_op jit(solution)/shard_map/ppermute | solution.py:134
  84.5 57.5 %collective-permute-start.30 = (bf16[2,256,512]{2,1,0:T(8,128)(2,1)}, bf16[2,256,512]{2,1,0:T(8,128)(2,1)}, u32[]{:S(2)}, u32[]{:S(2)}) collective-permute-start(bf16[2,256,512]{2,1,0:T(8,128)(2,1)} %get-tuple-element.25), channel_id=1, source_target_pairs={{0,8},{4,12},{24,16},{28,20},{1,9},{5,13},{25,17},{29,21},{2,10},{... | collective-permute-start | bytes 1572872 | tf_op jit(solution)/shard_map/ppermute | solution.py:135
  90.4 32.5 %collective-permute-start.22 = (bf16[256,512]{1,0:T(8,128)(2,1)}, bf16[256,512]{1,0:T(8,128)(2,1)}, u32[]{:S(2)}, u32[]{:S(2)}) collective-permute-start(bf16[256,512]{1,0:T(8,128)(2,1)} %get-tuple-element.21), channel_id=1, source_target_pairs={{0,8},{4,12},{24,16},{28,20},{1,9},{5,13},{25,17},{29,21},{2,10},{... | collective-permute-start | bytes 786440 | tf_op jit(solution)/shard_map/ppermute | solution.py:134
  92.4 51.3 %collective-permute-start.25 = (bf16[2,256,512]{2,1,0:T(8,128)(2,1)}, bf16[2,256,512]{2,1,0:T(8,128)(2,1)}, u32[]{:S(2)}, u32[]{:S(2)}) collective-permute-start(bf16[2,256,512]{2,1,0:T(8,128)(2,1)} %get-tuple-element.22), channel_id=1, source_target_pairs={{0,8},{4,12},{24,16},{28,20},{1,9},{5,13},{25,17},{29,21},{2,10},{... | collective-permute-start | bytes 1572872 | tf_op jit(solution)/shard_map/ppermute | solution.py:135
  98.9 26.4 %collective-permute-start.17 = (bf16[256,512]{1,0:T(8,128)(2,1)}, bf16[256,512]{1,0:T(8,128)(2,1)}, u32[]{:S(2)}, u32[]{:S(2)}) collective-permute-start(bf16[256,512]{1,0:T(8,128)(2,1)} %get-tuple-element.18), channel_id=1, source_target_pairs={{0,8},{4,12},{24,16},{28,20},{1,9},{5,13},{25,17},{29,21},{2,10},{... | collective-permute-start | bytes 786440 | tf_op jit(solution)/shard_map/ppermute | solution.py:134
  118.4 28.0 %collective-permute-start.20 = (bf16[2,256,512]{2,1,0:T(8,128)(2,1)S(1)}, bf16[2,256,512]{2,1,0:T(8,128)(2,1)S(1)}, u32[]{:S(2)}, u32[]{:S(2)}) collective-permute-start(bf16[2,256,512]{2,1,0:T(8,128)(2,1)S(1)} %copy-done.1), channel_id=1, source_target_pairs={{0,8},{4,12},{24,16},{28,20},{1,9},{5,13},{25,17},{29,21},{2,10},{... | collective-permute-start | bytes 1572872 | tf_op jit(solution)/shard_map/ppermute | solution.py:135
  122.9 18.3 %collective-permute-start.12 = (bf16[256,512]{1,0:T(8,128)(2,1)S(1)}, bf16[256,512]{1,0:T(8,128)(2,1)S(1)}, u32[]{:S(2)}, u32[]{:S(2)}) collective-permute-start(bf16[256,512]{1,0:T(8,128)(2,1)S(1)} %get-tuple-element.15), channel_id=1, source_target_pairs={{0,8},{4,12},{24,16},{28,20},{1,9},{5,13},{25,17},{29,21},{2,10},{... | collective-permute-start | bytes 786440 | tf_op jit(solution)/shard_map/ppermute | solution.py:134
  125.3 26.9 %collective-permute-start.15 = (bf16[2,256,512]{2,1,0:T(8,128)(2,1)S(1)}, bf16[2,256,512]{2,1,0:T(8,128)(2,1)S(1)}, u32[]{:S(2)}, u32[]{:S(2)}) collective-permute-start(bf16[2,256,512]{2,1,0:T(8,128)(2,1)S(1)} %get-tuple-element.16), channel_id=1, source_target_pairs={{0,8},{4,12},{24,16},{28,20},{1,9},{5,13},{25,17},{29,21},{2,10},{... | collective-permute-start | bytes 1572872 | tf_op jit(solution)/shard_map/ppermute | solution.py:135
  130.0 52.0 %copy-start.21 = (bf16[2048,1024]{1,0:T(8,128)(2,1)S(1)}, bf16[2048,1024]{1,0:T(8,128)(2,1)}, u32[]{:S(2)}) copy-start(bf16[2048,1024]{1,0:T(8,128)(2,1)} %param.15) | copy-start | bytes 12582916
  130.0 52.0 %copy-start.35 = (f32[512]{0:T(512)S(1)}, f32[512]{0:T(512)}, u32[]{:S(2)}) copy-start(f32[512]{0:T(512)} %get-tuple-element.46) | copy-start | bytes 6148
  141.2 4.3 %collective-permute-start.28 = (bf16[256,512]{1,0:T(8,128)(2,1)S(1)}, bf16[256,512]{1,0:T(8,128)(2,1)S(1)}, u32[]{:S(2)}, u32[]{:S(2)}) collective-permute-start(bf16[256,512]{1,0:T(8,128)(2,1)S(1)} %add_convert_fusion.1), channel_id=1, source_target_pairs={{8,16},{12,20},{16,8},{20,12},{9,17},{13,21},{17,9},{21,13},{10,18... | collective-permute-start | bytes 786440 | tf_op jit(solution)/shard_map/ppermute | solution.py:136
  142.0 11.7 %collective-permute-start.23 = (bf16[256,512]{1,0:T(8,128)(2,1)S(1)}, bf16[256,512]{1,0:T(8,128)(2,1)S(1)}, u32[]{:S(2)}, u32[]{:S(2)}) collective-permute-start(bf16[256,512]{1,0:T(8,128)(2,1)S(1)} %add_convert_fusion.3), channel_id=1, source_target_pairs={{8,16},{12,20},{16,8},{20,12},{9,17},{13,21},{17,9},{21,13},{10,18... | collective-permute-start | bytes 786440 | tf_op jit(solution)/shard_map/ppermute | solution.py:136
  143.8 10.6 %collective-permute-start.18 = (bf16[256,512]{1,0:T(8,128)(2,1)S(1)}, bf16[256,512]{1,0:T(8,128)(2,1)S(1)}, u32[]{:S(2)}, u32[]{:S(2)}) collective-permute-start(bf16[256,512]{1,0:T(8,128)(2,1)S(1)} %add_convert_fusion.5), channel_id=1, source_target_pairs={{8,16},{12,20},{16,8},{20,12},{9,17},{13,21},{17,9},{21,13},{10,18... | collective-permute-start | bytes 786440 | tf_op jit(solution)/shard_map/ppermute | solution.py:136
  145.6 2.1 collective-permute-start.13
  146.3 47.3 %collective-permute-start.29 = (bf16[256,512]{1,0:T(8,128)(2,1)S(1)}, bf16[256,512]{1,0:T(8,128)(2,1)S(1)}, u32[]{:S(2)}, u32[]{:S(2)}) collective-permute-start(bf16[256,512]{1,0:T(8,128)(2,1)S(1)} %fusion.20), channel_id=1, source_target_pairs={{16,24},{20,28},{8,0},{12,4},{17,25},{21,29},{9,1},{13,5},{18,26},... | collective-permute-start | bytes 786440 | tf_op jit(solution)/shard_map/ppermute | solution.py:138
  147.7 45.9 %collective-permute-start.31 = (bf16[256,512]{1,0:T(8,128)(2,1)S(1)}, bf16[256,512]{1,0:T(8,128)(2,1)S(1)}, u32[]{:S(2)}, u32[]{:S(2)}) collective-permute-start(bf16[256,512]{1,0:T(8,128)(2,1)S(1)} %fusion.28), channel_id=1, source_target_pairs={{8,16},{12,20},{16,8},{20,12},{9,17},{13,21},{17,9},{21,13},{10,18... | collective-permute-start | bytes 786440 | tf_op jit(solution)/shard_map/ppermute | solution.py:137
  148.4 43.0 %copy-start.34 = (f32[512]{0:T(512)S(1)}, f32[512]{0:T(512)}, u32[]{:S(2)}) copy-start(f32[512]{0:T(512)} %get-tuple-element.45) | copy-start | bytes 6148
  152.3 27.4 %collective-permute-start.14 = (bf16[256,512]{1,0:T(8,128)(2,1)S(1)}, bf16[256,512]{1,0:T(8,128)(2,1)S(1)}, u32[]{:S(2)}, u32[]{:S(2)}) collective-permute-start(bf16[256,512]{1,0:T(8,128)(2,1)S(1)} %fusion.5), channel_id=1, source_target_pairs={{16,24},{20,28},{8,0},{12,4},{17,25},{21,29},{9,1},{13,5},{18,26},... | collective-permute-start | bytes 786440 | tf_op jit(solution)/shard_map/ppermute | solution.py:138
  153.6 27.3 %collective-permute-start.16 = (bf16[256,512]{1,0:T(8,128)(2,1)S(1)}, bf16[256,512]{1,0:T(8,128)(2,1)S(1)}, u32[]{:S(2)}, u32[]{:S(2)}) collective-permute-start(bf16[256,512]{1,0:T(8,128)(2,1)S(1)} %fusion.25), channel_id=1, source_target_pairs={{8,16},{12,20},{16,8},{20,12},{9,17},{13,21},{17,9},{21,13},{10,18... | collective-permute-start | bytes 786440 | tf_op jit(solution)/shard_map/ppermute | solution.py:137
  154.4 37.4 %collective-permute-start.24 = (bf16[256,512]{1,0:T(8,128)(2,1)S(1)}, bf16[256,512]{1,0:T(8,128)(2,1)S(1)}, u32[]{:S(2)}, u32[]{:S(2)}) collective-permute-start(bf16[256,512]{1,0:T(8,128)(2,1)S(1)} %fusion.15), channel_id=1, source_target_pairs={{16,24},{20,28},{8,0},{12,4},{17,25},{21,29},{9,1},{13,5},{18,26},... | collective-permute-start | bytes 786440 | tf_op jit(solution)/shard_map/ppermute | solution.py:138
  179.7 10.5 %collective-permute-start.19 = (bf16[256,512]{1,0:T(8,128)(2,1)S(1)}, bf16[256,512]{1,0:T(8,128)(2,1)S(1)}, u32[]{:S(2)}, u32[]{:S(2)}) collective-permute-start(bf16[256,512]{1,0:T(8,128)(2,1)S(1)} %fusion.10), channel_id=1, source_target_pairs={{16,24},{20,28},{8,0},{12,4},{17,25},{21,29},{9,1},{13,5},{18,26},... | collective-permute-start | bytes 786440 | tf_op jit(solution)/shard_map/ppermute | solution.py:138
  181.0 10.1 %collective-permute-start.21 = (bf16[256,512]{1,0:T(8,128)(2,1)S(1)}, bf16[256,512]{1,0:T(8,128)(2,1)S(1)}, u32[]{:S(2)}, u32[]{:S(2)}) collective-permute-start(bf16[256,512]{1,0:T(8,128)(2,1)S(1)} %fusion.26), channel_id=1, source_target_pairs={{8,16},{12,20},{16,8},{20,12},{9,17},{13,21},{17,9},{21,13},{10,18... | collective-permute-start | bytes 786440 | tf_op jit(solution)/shard_map/ppermute | solution.py:137
  182.0 11.2 %copy-start.33 = (f32[512]{0:T(512)S(1)}, f32[512]{0:T(512)}, u32[]{:S(2)}) copy-start(f32[512]{0:T(512)} %get-tuple-element.47) | copy-start | bytes 6148
  190.2 1.6 collective-permute-start.26
  195.4 20.7 %copy-start.43 = (s32[4]{0:T(128)S(1)}, s32[4]{0:T(128)}, u32[]{:S(2)}) copy-start(s32[4]{0:T(128)} %param.19) | copy-start | bytes 52
  195.4 20.7 %copy-start.26 = (s32[4,16,8]{2,1,0:T(8,128)S(1)}, s32[4,16,8]{2,1,0:T(8,128)}, u32[]{:S(2)}) copy-start(s32[4,16,8]{2,1,0:T(8,128)} %copy-done.25) | copy-start | bytes 6148
  195.4 20.8 %copy-start.28 = (pred[4,16,8]{2,1,0:T(8,128)(4,1)S(1)}, pred[4,16,8]{2,1,0:T(8,128)(4,1)}, u32[]{:S(2)}) copy-start(pred[4,16,8]{2,1,0:T(8,128)(4,1)} %copy-done.27) | copy-start | bytes 1540
  195.4 21.0 %copy-start.30 = (s32[4,288]{1,0:T(4,128)S(1)}, s32[4,288]{1,0:T(4,128)}, u32[]{:S(2)}) copy-start(s32[4,288]{1,0:T(4,128)} %add_add_fusion) | copy-start | bytes 13828
  195.4 21.0 %copy-start.29 = (s32[32,8]{1,0:T(8,128)S(1)}, s32[32,8]{1,0:T(8,128)}, u32[]{:S(2)}) copy-start(s32[32,8]{1,0:T(8,128)} %iota_add_fusion.1) | copy-start | bytes 3076
  195.4 21.1 %copy-start.37 = (s32[128]{0:T(128)S(1)}, s32[128]{0:T(128)}, u32[]{:S(2)}) copy-start(s32[128]{0:T(128)} %copy-done.36) | copy-start | bytes 1540
  195.5 21.2 %copy-start.23 = (bf16[2,48,256]{2,1,0:T(8,128)(2,1)S(1)}, bf16[2,48,256]{2,1,0:T(8,128)(2,1)}, u32[]{:S(2)}) copy-start(bf16[2,48,256]{2,1,0:T(8,128)(2,1)} %copy-done.22) | copy-start | bytes 147460
  195.5 28.8 %copy-start.18 = (bf16[4,128,1024]{2,1,0:T(8,128)(2,1)S(1)}, bf16[4,128,1024]{2,1,0:T(8,128)(2,1)}, u32[]{:S(2)}) copy-start(bf16[4,128,1024]{2,1,0:T(8,128)(2,1)} %query_ref.1) | copy-start | bytes 3145732
  195.5 28.8 %copy-start.19 = (bf16[4,128,256]{2,1,0:T(8,128)(2,1)S(1)}, bf16[4,128,256]{2,1,0:T(8,128)(2,1)}, u32[]{:S(2)}) copy-start(bf16[4,128,256]{2,1,0:T(8,128)(2,1)} %text_ref.1) | copy-start | bytes 786436
  195.7 3.3 %collective-permute-start.32 = (bf16[2,256,256]{2,1,0:T(8,128)(2,1)S(1)}, bf16[2,256,256]{2,1,0:T(8,128)(2,1)S(1)}, u32[]{:S(2)}, u32[]{:S(2)}) collective-permute-start(bf16[2,256,256]{2,1,0:T(8,128)(2,1)S(1)} %fusion.29), channel_id=1, source_target_pairs={{0,1},{1,0},{2,3},{3,2},{4,5},{5,4},{6,7},{7,6},{8,9},{9,8},{10,11... | collective-permute-start | bytes 786440 | tf_op jit(solution)/shard_map/ppermute | solution.py:24
  195.8 1.5 collective-permute-start.34
  197.3 3.6 %collective-permute-start.35 = (f32[256]{0:T(256)S(1)}, f32[256]{0:T(256)S(1)}, u32[]{:S(2)}, u32[]{:S(2)}) collective-permute-start(f32[256]{0:T(256)S(1)} %add.349), channel_id=1, source_target_pairs={{0,2},{1,3},{2,0},{3,1},{4,6},{5,7},{6,4},{7,5},{8,10},{9,11},{10,... | collective-permute-start | bytes 3080 | tf_op jit(solution)/shard_map/ppermute | solution.py:24
  199.1 5.3 %collective-permute-start.33 = (bf16[1,256,256]{2,1,0:T(8,128)(2,1)S(1)}, bf16[1,256,256]{2,1,0:T(8,128)(2,1)S(1)}, u32[]{:S(2)}, u32[]{:S(2)}) collective-permute-start(bf16[1,256,256]{2,1,0:T(8,128)(2,1)S(1)} %dynamic-slice_convert_fusion.1), channel_id=1, source_target_pairs={{0,2},{1,3},{2,0},{3,1},{4,6},{5,7},{6,4},{7,5},{8,10},{9,11},{10,... | collective-permute-start | bytes 393224 | tf_op jit(solution)/shard_map/ppermute | solution.py:24
  205.5 18.8 %all-to-all-start = ((bf16[8,64,256]{2,1,0:T(8,128)(2,1)}), bf16[8,64,256]{2,1,0:T(8,128)(2,1)S(1)}, u32[]{:S(2)}, u32[]{:S(2)}) async-start(bf16[8,64,256]{2,1,0:T(8,128)(2,1)} %bitcast.26), calls=%async_computation | async-start | bytes 524288 | tf_op jit(solution)/shard_map/all_to_all | solution.py:369
  (21 other events, 25.1 us)
Sparse Core Ops, SparseCore 0:
  10.8 26.9 all-gather.10
  39.3 24.2 all-gather.8
  65.1 24.2 all-gather.6
  90.8 24.2 all-gather.4

commit v5 on v4

--- a/solution.py
+++ b/solution.py
@@ -49,70 +49,83 @@
     return 2 * (place % half) + ((place // half) ^ (group & 1))
 
 
-ROLE_GROUPS = (3, 0, 2, 1)
-
-
-def order_kernel(pieces, roles_ref, *refs):
+ROLE_GROUPS = (3, 2, 0, 1)
+
+
+def order_kernel(share, scalars_ref, *refs):
     out_ref = refs[-1]
+    rows, depth = refs[0].shape
+    members = depth // share
     for place in range(4):
-        for piece in range(pieces):
-            rows_ref = refs[place * pieces + piece]
-            rows = rows_ref.shape[0]
-            out_ref[roles_ref[place], piece * rows : (piece + 1) * rows] = rows_ref[...]
-
-
-def order_rows(roles, held):
-    pieces = len(held[0])
-    rows, depth = held[0][0].shape
+        at = pl.ds(pl.multiple_of(scalars_ref[place] * rows, rows), rows)
+        for member in range(members):
+            if members == 1:
+                out_ref[at, :] = refs[place][...]
+            else:
+                source = lax.rem(scalars_ref[4] + member, members)
+                columns = pl.ds(pl.multiple_of(source * share, share), share)
+                out_ref[at, member * share : (member + 1) * share] = refs[place][:, columns]
+
+
+def order_rows(scalars, held, share):
+    rows, depth = held[0].shape
     return pl.pallas_call(
-        functools.partial(order_kernel, pieces),
+        functools.partial(order_kernel, share),
         grid_spec=pltpu.PrefetchScalarGridSpec(
             num_scalar_prefetch=1,
             grid=(1,),
-            in_specs=[pl.BlockSpec((rows, depth), lambda i, roles: (0, 0))] * (4 * pieces),
-            out_specs=pl.BlockSpec((4, pieces * rows, depth), lambda i, roles: (0, 0, 0)),
-        ),
-        out_shape=jax.ShapeDtypeStruct((4, pieces * rows, depth), jnp.bfloat16),
+            in_specs=[pl.BlockSpec((rows, depth), lambda i, scalars: (0, 0))] * 4,
+            out_specs=pl.BlockSpec((4 * rows, depth), lambda i, scalars: (0, 0)),
+        ),
+        out_shape=jax.ShapeDtypeStruct((4 * rows, depth), jnp.bfloat16),
         compiler_params=pltpu.CompilerParams(vmem_limit_bytes=VMEM),
         cost_estimate=pl.CostEstimate(
-            flops=0, bytes_accessed=16 * pieces * rows * depth, transcendentals=0
-        ),
-    )(roles, *[piece for place in held for piece in place])
-
-
-def partial_kernel(rows_ref, weights_ref, far_end, near_end, middles):
-    _, rows, depth = rows_ref.shape
-    held = rows_ref[...].reshape(4 * rows, depth)
-    total = jnp.dot(held, weights_ref[...], preferred_element_type=jnp.float32)
-    total = total.astype(jnp.bfloat16)
-    far_end[...] = total[:rows]
-    near_end[...] = total[rows : 2 * rows]
-    middles[0] = total[2 * rows : 3 * rows]
-    middles[1] = total[3 * rows :]
-
-
-def partial_products(held, weights):
-    _, rows, depth = held.shape
-    columns = weights.shape[1]
-    tile = min(columns, 256)
-    one = pl.BlockSpec((rows, tile), lambda i: (0, i))
+            flops=0, bytes_accessed=16 * rows * depth, transcendentals=0
+        ),
+    )(scalars, *held)
+
+
+def partial_kernel(halves, *refs):
+    rows_refs, weights_refs = refs[:halves], refs[halves:-2]
+    far_ref, near_ref = refs[-2:]
+    for half, rows_ref in enumerate(rows_refs):
+        total = None
+        at = 0
+        for weights_ref in weights_refs:
+            depth = weights_ref.shape[0]
+            term = jnp.dot(
+                rows_ref[:, at : at + depth],
+                weights_ref[...],
+                preferred_element_type=jnp.float32,
+            )
+            total = term if total is None else total + term
+            at += depth
+        total = total.astype(jnp.bfloat16)
+        rows = total.shape[0] // 2
+        far_ref[half * rows : (half + 1) * rows] = total[:rows]
+        near_ref[half * rows : (half + 1) * rows] = total[rows:]
+
+
+def partial_products(held, weights, first, count):
+    rows, depth = held[0].shape
+    out_rows = len(held) * rows // 2
+    tile = min(count, 256)
+    offset = first // tile
+    out = pl.BlockSpec((out_rows, tile), lambda i: (0, i))
     return pl.pallas_call(
-        partial_kernel,
-        grid=(columns // tile,),
-        in_specs=[
-            pl.BlockSpec(held.shape, lambda i: (0, 0, 0)),
-            pl.BlockSpec((depth, tile), lambda i: (0, i)),
-        ],
-        out_specs=[one, one, pl.BlockSpec((2, rows, tile), lambda i: (0, 0, i))],
-        out_shape=[jax.ShapeDtypeStruct((rows, columns), jnp.bfloat16)] * 2
-        + [jax.ShapeDtypeStruct((2, rows, columns), jnp.bfloat16)],
+        functools.partial(partial_kernel, len(held)),
+        grid=(count // tile,),
+        in_specs=[pl.BlockSpec((rows, depth), lambda i: (0, 0))] * len(held)
+        + [pl.BlockSpec((w.shape[0], tile), lambda i: (0, i + offset)) for w in weights],
+        out_specs=[out, out],
+        out_shape=[jax.ShapeDtypeStruct((out_rows, count), jnp.bfloat16)] * 2,
         compiler_params=pltpu.CompilerParams(vmem_limit_bytes=VMEM),
         cost_estimate=pl.CostEstimate(
-            flops=8 * rows * depth * columns,
-            bytes_accessed=8 * rows * depth + 2 * depth * columns + 8 * rows * columns,
+            flops=4 * out_rows * depth * count,
+            bytes_accessed=4 * out_rows * depth + 2 * depth * count + 4 * out_rows * count,
             transcendentals=0,
         ),
-    )(held, weights)
+    )(*held, *weights)
 
 
 def along(pairs):
@@ -125,24 +138,19 @@
 ENDS_OUT = ((2, 3), (1, 0))
 
 
-def reduce_groups(parts, is_end):
-    far_end, near_end, middles = parts
+def reduce_groups(parts):
+    far, near = parts
 
     def add(mine, other):
         return (mine.astype(jnp.float32) + other.astype(jnp.float32)).astype(jnp.bfloat16)
 
-    first = lax.ppermute(far_end, "seq", along(ENDS_IN))
-    second = lax.ppermute(middles, "seq", along(ENDS_IN))
-    passed = lax.ppermute(add(far_end, first), "seq", along(MIDDLES))
-    crossed = lax.ppermute(add(middles[0], second[0]), "seq", along(MIDDLES))
-    outer = lax.ppermute(add(near_end, passed), "seq", along(ENDS_OUT))
-    end = near_end.astype(jnp.float32) + outer.astype(jnp.float32)
-    middle = (
-        middles[1].astype(jnp.float32)
-        + second[1].astype(jnp.float32)
-        + crossed.astype(jnp.float32)
-    )
-    return jnp.where(is_end, end, middle).astype(jnp.bfloat16)
+    inward = lax.ppermute(far, "seq", along(ENDS_IN))
+    across = lax.ppermute(add(far, inward), "seq", along(MIDDLES))
+    outward = lax.ppermute(add(near, across), "seq", along(ENDS_OUT))
+    return add(near, outward)
+
+
+PLAN = (((0,), 0, 1), ((0,), 1, 1), ((1,), 0, 1), ((1,), 1, 1), ((0, 1), 2, 1), ((0,), 3, 1), ((1,), 3, 1))
 
 
 def merge_tiles(panels, w_merge, ln_gain, w_kv, small):
@@ -150,47 +158,71 @@
     assert tp_count == 4 and seq_count % 4 == 0
     width = seq_count // tp_count
     tiles, panel_rows, depth = panels.shape
+    share = w_merge.shape[0]
     group = lax.axis_index("seq") // width
+    inner = lax.axis_index("seq") % width
     local = panels.reshape(tiles * panel_rows, depth)
     half = local.shape[0] // 2
-    held = list(
-        zip(
-            transpose_panels(local[:half], 0),
-            transpose_panels(flip(local[half:], "tp", 2), 2),
-        )
-    )
-    inner_groups = [[g * width + i for i in range(width)] for g in range(tp_count)]
+    pieces = [
+        transpose_panels(local[:half], 0),
+        transpose_panels(flip(local[half:], "tp", 2), 2),
+    ]
     columns = w_merge.shape[1] // CHUNKS
-    weights = [
-        lax.all_gather(
-            w_merge[:, c * columns : (c + 1) * columns],
-            "seq",
-            axis=0,
-            tiled=True,
-            axis_index_groups=inner_groups,
-        )
-        for c in range(CHUNKS)
-    ]
-    for bit in bits_of(seq_count):
-        small = jnp.concatenate([small, flip(small, "seq", bit)], axis=0)
+    weights = []
+    for chunk in range(CHUNKS):
+        own = w_merge[:, chunk * columns : (chunk + 1) * columns]
+        if chunk >= 2:
+            own, _ = lax.optimization_barrier((own, weights[chunk - 2][1]))
+        parts = [own]
+        for offset in range(1, width):
+            pairs = [
+                (g * width + (i + offset) % width, g * width + i)
+                for g in range(tp_count)
+                for i in range(width)
+            ]
+            parts.append(lax.ppermute(own, "seq", pairs))
+        weights.append(parts)
+    turn = inner
+    if share % 128:
+        weights = [
+            [parts[0], jnp.roll(jnp.concatenate(parts, axis=0), inner * share, axis=0)]
+            for parts in weights
+        ]
+        weights = [parts[1:] for parts in weights]
+        share = depth
     shift = jnp.where(group < 2, 0, 3)
     groups = (panel_base() ^ jnp.arange(4, dtype=jnp.int32)) ^ shift
     roles = jnp.array([ROLE_GROUPS.index(g) for g in range(4)], jnp.int32)[groups]
-    is_end = (group == 0) | (group == 3)
-    held = order_rows(roles, held)
-    kv = 0.0
-    squares = 0.0
-    for chunk in range(CHUNKS):
-        merged = reduce_groups(partial_products(held, weights[chunk]), is_end)
+    scalars = jnp.concatenate([roles, jnp.full((4,), turn, jnp.int32)])
+    held = [order_rows(scalars, piece, share) for piece in pieces]
+    kv = [0.0, 0.0]
+    squares = [0.0, 0.0]
+    for step, (halves, first, count) in enumerate(PLAN):
+        chunk_rows = [held[h] for h in halves]
+        merged = reduce_groups(partial_products(chunk_rows, weights[first], 0, columns * count))
         merged = merged.astype(jnp.float32)
-        squares = squares + jnp.sum(merged * merged, axis=1)
-        gain = ln_gain[chunk * columns : (chunk + 1) * columns].astype(jnp.float32)
-        kv = kv + jnp.dot(
-            (merged * gain[None, :]).astype(jnp.bfloat16),
-            w_kv[chunk * columns : (chunk + 1) * columns],
-            preferred_element_type=jnp.float32,
-        )
-    return kv, squares, small
+        at = slice(first * columns, (first + count) * columns)
+        gained = (merged * ln_gain[at].astype(jnp.float32)[None, :]).astype(jnp.bfloat16)
+        for i, h in enumerate(halves):
+            rows = slice(i * 2 * half, (i + 1) * 2 * half)
+            squares[h] = squares[h] + jnp.sum(merged[rows] * merged[rows], axis=1)
+            kv[h] = kv[h] + jnp.dot(gained[rows], w_kv[at], preferred_element_type=jnp.float32)
+        if step == len(PLAN) - 2:
+            small, kv[0] = lax.optimization_barrier((small, kv[0]))
+    for bit in bits_of(seq_count):
+        small = jnp.concatenate([small, flip(small, "seq", bit)], axis=0)
+    def arrange(parts):
+        return jnp.concatenate([part[:half] for part in parts] + [part[half:] for part in parts])
+
+    return arrange(kv), arrange(squares), small
+
+
+def return_rows(tile_kv):
+    width = lax.axis_size("seq") // lax.axis_size("tp")
+    group = lax.axis_index("seq") // width
+    rows = tile_kv.shape[0] // 2
+    returned = lax.ppermute(tile_kv[rows:], "seq", along(ENDS_IN))
+    return jnp.where((group == 0) | (group == 3), tile_kv[:rows], returned)
 
 
 def scatter_heads(kv, squares):
@@ -364,7 +396,7 @@
 
     kv, squares = scatter_heads(kv, squares)
     row_scale = lax.rsqrt(squares / D + 1e-06)
-    tile_kv = (kv * row_scale[:, None]).astype(jnp.bfloat16)
+    tile_kv = return_rows((kv * row_scale[:, None]).astype(jnp.bfloat16))
     outgoing = jnp.dot(chooser, tile_kv, preferred_element_type=jnp.float32).astype(jnp.bfloat16)
     pages = lax.all_to_all(outgoing, "seq", split_axis=0, concat_axis=0, tiled=True)
     attended, vision_kv = attend(

time: 238 us -> 204 us (0.86)
  waiting for transfers between devices: 101 us -> 69.3 us
  between operations: 14.8 us -> 1.73 us
  starting transfers between devices: 65.6 us -> 76.2 us
  Pallas kernels: 15.5 us -> 24.5 us
  local copies, waits for them, and re-layouts: 23.7 us -> 16.2 us
    ppermute x14, waiting for transfers between devices: 31.5 us -> 15.8 us  [flip(): return lax.ppermute(value, axis, [(i, i ^ bit) for i in range(count)])]
    all_gather x4 -> x0, waiting for transfers between devices: 14.2 us -> none  [merge_tiles(): lax.all_gather(w_merge[:, c * columns:(c + 1) * columns], 'seq', axis=0,...]
    unnamed x88 -> x61, local copies, waits for them, and re-layouts: 16.5 us -> 4.41 us
    ppermute x20 -> x26, starting transfers between devices: 29.2 us -> 41.1 us  [the longest x7 21.5 us: reduce_groups(): inward = lax.ppermute(far, 'seq', along(ENDS_IN))]
    pallas_call x5 -> x9, Pallas kernels: 10 us -> 19 us  [the longest x7 16.6 us: partial_products(): pl.pallas_call(functools.partial(partial_kernel, len(held)), grid=(count...]
    all_to_all x1, starting transfers between devices: 10.6 us -> 4.81 us  [shards(): lax.all_to_all(outgoing, 'seq', split_axis=0, concat_axis=0, tiled=True)]
    convert_element_type x12 -> x14, other arithmetic: 5.95 us -> 3.13 us  [add(): (mine.astype(jnp.float32) + other.astype(jnp.float32)).astype(jnp.bfloat16)]
    ppermute x2, starting transfers between devices: 2.58 us -> 4.99 us  [transpose_panels(): held = [lax.ppermute(local, ('seq', 'tp'), pairs)]]
  transfers between devices with their start and end apart: 41 -> 43, of which waited for: 13 -> 14; matrix products, arithmetic and copies ran while one was open for 7% -> 10% of each run, Pallas kernels for 4% -> 9%
where the time goes in v5:
time: 204 us; the launch traced here: 203 us
  starting transfers between devices  76.2 us (37%)
  waiting for transfers between devices  69.3 us (34%)
  Pallas kernels  24.5 us (12%)
  local copies, waits for them, and re-layouts  16.2 us (8%)
  other arithmetic  10.4 us (5%)
  matrix products  4.51 us (2%)
    ppermute x7, waiting for transfers between devices, reduce_groups(): outward = lax.ppermute(add(near, across), 'seq', along(ENDS_OUT))  37.2 us
    ppermute x14, starting transfers between devices, flip(): return lax.ppermute(value, axis, [(i, i ^ bit) for i in range(count)])  25.3 us
    ppermute x7, starting transfers between devices, reduce_groups(): inward = lax.ppermute(far, 'seq', along(ENDS_IN))  21.5 us
    pallas_call x7, Pallas kernels, partial_products(): pl.pallas_call(functools.partial(partial_kernel, len(held)), grid=(count...  16.6 us
    ppermute x14, waiting for transfers between devices, flip(): return lax.ppermute(value, axis, [(i, i ^ bit) for i in range(count)])  15.8 us
    ppermute x7, starting transfers between devices, reduce_groups(): outward = lax.ppermute(add(near, across), 'seq', along(ENDS_OUT))  9.23 us
    all_to_all x1, waiting for transfers between devices, shards(): lax.all_to_all(outgoing, 'seq', split_axis=0, concat_axis=0, tiled=True)  8.04 us
    pallas_call x1, Pallas kernels, attend(): pl.pallas_call(attend_kernel, grid_spec=pltpu.PrefetchScalarGridSpec(num_...  5.51 us
  transfers between devices with their start and end apart: 43, of which 14 were waited for; matrix products, arithmetic and copies ran while one was open for 10% of the time, Pallas kernels for 9%

profile of v5, /device:TPU:0, one launch (start us, length us, event | category | flops | bytes accessed | tf_op | source)
XLA Modules:
  0.0 202.8 jit_solution(13717163351550466690)
XLA Ops:
  0.6 1.1 slice_bitcast_fusion.4
  1.7 3.0 %collective-permute-start.12 = (bf16[128,1280]{1,0:T(8,128)(2,1)S(1)}, bf16[128,1280]{1,0:T(8,128)(2,1)}, u32[]{:S(2)}, u32[]{:S(2)}) collective-permute-start(bf16[128,1280]{1,0:T(8,128)(2,1)S(1)} %get-tuple-element.54), channel_id=1, source_target_pairs={{0,2},{1,3},{2,0},{3,1},{4,6},{5,7},{6,4},{7,5},{8,10},{9,11},{10,... | collective-permute-start | bytes 983048 | tf_op jit(solution)/shard_map/ppermute | solution.py:24
  4.8 0.8 collective-permute-start
  5.6 2.7 %fusion.76 = (bf16[640,512]{1,0:T(8,128)(2,1)S(1)}, bf16[640,512]{1,0:T(8,128)(2,1)S(1)}, bf16[640,512]{1,0:T(8,128)(2,1)S(1)}, bf16[640,512]{1,0:T(8,128)(2,1)}) fusion(bf16[640,2048]{1,0:T(8,128)(2,1)} %param.13), kind=kLoop, calls=%fused_computation.169 | loop fusion | bytes 5242880 | tf_op jit(solution)/shard_map/slice | solution.py:173
  8.3 1.6 collective-permute-start.8
  11.0 0.8 gather_fusion.2
  13.8 5.3 %collective-permute-start.1 = (bf16[128,1280]{1,0:T(8,128)(2,1)S(1)}, bf16[128,1280]{1,0:T(8,128)(2,1)S(1)}, u32[]{:S(2)}, u32[]{:S(2)}) collective-permute-start(bf16[128,1280]{1,0:T(8,128)(2,1)S(1)} %collective-permute-done.refs_0_), channel_id=1, source_target_pairs={{0,2},{1,3},{2,0},{3,1},{4,6},{5,7},{6,4},{7,5},{8,10},{9,11},{10,... | collective-permute-start | bytes 983048 | tf_op jit(solution)/shard_map/ppermute | solution.py:24
  19.8 4.7 %collective-permute-start.2 = (bf16[128,1280]{1,0:T(8,128)(2,1)S(1)}, bf16[128,1280]{1,0:T(8,128)(2,1)S(1)}, u32[]{:S(2)}, u32[]{:S(2)}) collective-permute-start(bf16[128,1280]{1,0:T(8,128)(2,1)S(1)} %collective-permute-done.refs_0_), channel_id=1, source_target_pairs={{0,1},{1,0},{2,3},{3,2},{4,5},{5,4},{6,7},{7,6},{8,9},{9,8},{10,11... | collective-permute-start | bytes 983048 | tf_op jit(solution)/shard_map/ppermute | solution.py:24
  24.5 4.2 %collective-permute-start.13 = (bf16[128,1280]{1,0:T(8,128)(2,1)}, bf16[128,1280]{1,0:T(8,128)(2,1)}, u32[]{:S(2)}, u32[]{:S(2)}) collective-permute-start(bf16[128,1280]{1,0:T(8,128)(2,1)} %collective-permute-done.12), channel_id=1, source_target_pairs={{2,0},{3,10},{0,16},{1,26},{6,4},{7,14},{4,20},{5,30},{10,2},{11,8... | collective-permute-start | bytes 983048 | tf_op jit(solution)/shard_map/ppermute | solution.py:38
  28.8 3.5 %collective-permute-start.3 = (bf16[128,1280]{1,0:T(8,128)(2,1)S(1)}, bf16[128,1280]{1,0:T(8,128)(2,1)S(1)}, u32[]{:S(2)}, u32[]{:S(2)}) collective-permute-start(bf16[128,1280]{1,0:T(8,128)(2,1)S(1)} %collective-permute-done.1.refs_1_), channel_id=1, source_target_pairs={{0,1},{1,0},{2,3},{3,2},{4,5},{5,4},{6,7},{7,6},{8,9},{9,8},{10,11... | collective-permute-start | bytes 983048 | tf_op jit(solution)/shard_map/ppermute | solution.py:24
  32.3 0.7 copy-done.5
  34.8 3.7 %collective-permute-start.14 = (bf16[128,1280]{1,0:T(8,128)(2,1)}, bf16[128,1280]{1,0:T(8,128)(2,1)}, u32[]{:S(2)}, u32[]{:S(2)}) collective-permute-start(bf16[128,1280]{1,0:T(8,128)(2,1)} %collective-permute-done.13.refs_0_), channel_id=1, source_target_pairs={{0,2},{1,3},{2,0},{3,1},{4,6},{5,7},{6,4},{7,5},{8,10},{9,11},{10,... | collective-permute-start | bytes 983048 | tf_op jit(solution)/shard_map/ppermute | solution.py:24
  38.5 1.0 copy-done.4
  39.5 1.0 copy-done.6
  41.1 2.8 %shard_map.133 = (bf16[256,512]{1,0:T(8,128)(2,1)}, bf16[256,512]{1,0:T(8,128)(2,1)S(1)}) custom-call(bf16[512,1280]{1,0:T(8,128)(2,1)S(1)} %shard_map.131.refs_0_, bf16[640,512]{1,0:T(8,128)(2,1)S(1)} %get-tuple-element.41.refs_1_, bf16[640,512]{1,0:T(8,128)(2,1)} %collective-permute-done.8.refs_2_), custom_call_target="tpu_custom_call" | custom-call | flops 671088640 | bytes 3145728 | tf_op jit(solution)/shard_map/pallas_call | solution.py:115
  44.0 6.7 %collective-permute-start.9 = (bf16[256,512]{1,0:T(8,128)(2,1)}, bf16[256,512]{1,0:T(8,128)(2,1)}, u32[]{:S(2)}, u32[]{:S(2)}) collective-permute-start(bf16[256,512]{1,0:T(8,128)(2,1)} %get-tuple-element.23), channel_id=1, source_target_pairs={{0,8},{4,12},{24,16},{28,20},{1,9},{5,13},{25,17},{29,21},{2,10},{... | collective-permute-start | bytes 786440 | tf_op jit(solution)/shard_map/ppermute | solution.py:147
  50.7 1.5 collective-permute-start.21
  52.2 2.8 %shard_map.132 = (bf16[256,512]{1,0:T(8,128)(2,1)}, bf16[256,512]{1,0:T(8,128)(2,1)S(1)}) custom-call(bf16[512,1280]{1,0:T(8,128)(2,1)S(1)} %shard_map.131.refs_0_, bf16[640,512]{1,0:T(8,128)(2,1)S(1)} %get-tuple-element.42.refs_1_, bf16[640,512]{1,0:T(8,128)(2,1)} %collective-permute-done.4.refs_2_), custom_call_target="tpu_custom_call" | custom-call | flops 671088640 | bytes 3145728 | tf_op jit(solution)/shard_map/pallas_call | solution.py:115
  55.0 0.7 copy-done
  55.7 2.0 collective-permute-start.5
  58.3 0.8 broadcast_in_dim.31
  59.1 1.6 add.371
  60.7 0.7 broadcast_in_dim.30.seen_ref
  61.4 1.5 add.372.all_ref
  63.4 0.9 collective-permute-start.15
  64.3 1.1 add_convert_fusion.5
  66.1 1.1 add_convert_fusion.6
  67.9 1.7 shard_map.134.refs_1_.refs_0_
  69.6 2.2 %shard_map.138 = (bf16[256,512]{1,0:T(8,128)(2,1)S(1)}, bf16[256,512]{1,0:T(8,128)(2,1)S(1)}) custom-call(bf16[512,1280]{1,0:T(8,128)(2,1)S(1)} %shard_map.134.refs_1_.refs_0_, bf16[640,512]{1,0:T(8,128)(2,1)S(1)} %get-tuple-element.41.refs_1_, bf16[640,512]{1,0:T(8,128)(2,1)} %collective-permute-done.8.refs_2_), custom_call_target="tpu_custom_call" | custom-call | flops 671088640 | bytes 3145728 | tf_op jit(solution)/shard_map/pallas_call | solution.py:115
  71.9 7.1 %collective-permute-start.31 = (bf16[256,512]{1,0:T(8,128)(2,1)S(1)}, bf16[256,512]{1,0:T(8,128)(2,1)S(1)}, u32[]{:S(2)}, u32[]{:S(2)}) collective-permute-start(bf16[256,512]{1,0:T(8,128)(2,1)S(1)} %get-tuple-element.35), channel_id=1, source_target_pairs={{0,8},{4,12},{24,16},{28,20},{1,9},{5,13},{25,17},{29,21},{2,10},{... | collective-permute-start | bytes 786440 | tf_op jit(solution)/shard_map/ppermute | solution.py:147
  79.0 2.2 %shard_map.139 = (bf16[256,512]{1,0:T(8,128)(2,1)S(1)}, bf16[256,512]{1,0:T(8,128)(2,1)S(1)}) custom-call(bf16[512,1280]{1,0:T(8,128)(2,1)S(1)} %shard_map.134.refs_1_.refs_0_, bf16[640,512]{1,0:T(8,128)(2,1)S(1)} %get-tuple-element.27.refs_1_, bf16[640,512]{1,0:T(8,128)(2,1)} %collective-permute-done.21.refs_2_), custom_call_target="tpu_custom_call" | custom-call | flops 671088640 | bytes 3145728 | tf_op jit(solution)/shard_map/pallas_call | solution.py:115
  81.2 1.3 collective-permute-start.34
  82.5 2.2 %shard_map.136 = (bf16[256,512]{1,0:T(8,128)(2,1)S(1)}, bf16[256,512]{1,0:T(8,128)(2,1)S(1)}) custom-call(bf16[512,1280]{1,0:T(8,128)(2,1)S(1)} %shard_map.131.refs_0_, bf16[640,512]{1,0:T(8,128)(2,1)S(1)} %get-tuple-element.27.refs_1_, bf16[640,512]{1,0:T(8,128)(2,1)} %collective-permute-done.21.refs_2_), custom_call_target="tpu_custom_call" | custom-call | flops 671088640 | bytes 3145728 | tf_op jit(solution)/shard_map/pallas_call | solution.py:115
  84.8 1.3 collective-permute-start.22
  86.1 2.2 %shard_map.135 = (bf16[512,512]{1,0:T(8,128)(2,1)S(1)}, bf16[512,512]{1,0:T(8,128)(2,1)S(1)}) custom-call(bf16[512,1280]{1,0:T(8,128)(2,1)S(1)} %shard_map.131.refs_0_, bf16[512,1280]{1,0:T(8,128)(2,1)S(1)} %shard_map.134.refs_1_.refs_0_, bf16[640,512]{1,0:T(8,128)(2,1)S(1)} %copy-done.2, bf16[640,512]{1,0:T(8,128)(2,1)S(1)} %collective-permute-done.17.refs_3_), custom_call_target="tpu_custom_call" | custom-call | flops 1342177280 | bytes 4980736 | tf_op jit(solution)/shard_map/pallas_call | solution.py:115
  88.3 2.2 %shard_map.137 = (bf16[256,512]{1,0:T(8,128)(2,1)S(1)}, bf16[256,512]{1,0:T(8,128)(2,1)S(1)}) custom-call(bf16[512,1280]{1,0:T(8,128)(2,1)S(1)} %shard_map.134.refs_1_.refs_0_, bf16[640,512]{1,0:T(8,128)(2,1)S(1)} %get-tuple-element.42.refs_1_, bf16[640,512]{1,0:T(8,128)(2,1)} %collective-permute-done.4.refs_2_), custom_call_target="tpu_custom_call" | custom-call | flops 671088640 | bytes 3145728 | tf_op jit(solution)/shard_map/pallas_call | solution.py:115
  90.5 1.3 collective-permute-start.28
  91.9 1.7 collective-permute-start.18
  93.7 1.3 collective-permute-start.11
  95.1 1.3 collective-permute-start.7
  97.7 4.9 %collective-permute-done.28 = bf16[256,512]{1,0:T(8,128)(2,1)S(1)} collective-permute-done((bf16[256,512]{1,0:T(8,128)(2,1)S(1)}, bf16[256,512]{1,0:T(8,128)(2,1)S(1)}, u32[]{:S(2)}, u32[]{:S(2)}) %collective-permute-start.28) | collective-permute-done | bytes 262176 | tf_op jit(solution)/shard_map/ppermute | solution.py:147
  103.3 5.8 %collective-permute-done.7 = bf16[256,512]{1,0:T(8,128)(2,1)S(1)} collective-permute-done((bf16[256,512]{1,0:T(8,128)(2,1)S(1)}, bf16[256,512]{1,0:T(8,128)(2,1)S(1)}, u32[]{:S(2)}, u32[]{:S(2)}) %collective-permute-start.7) | collective-permute-done | bytes 262176 | tf_op jit(solution)/shard_map/ppermute | solution.py:149
  111.8 1.3 collective-permute-start.33
  113.2 1.3 collective-permute-start.36
  114.6 1.3 collective-permute-start.24
  116.0 1.3 collective-permute-start.30
  117.4 0.7 collective-permute-start.19
  118.1 6.2 %collective-permute-done.33 = bf16[256,512]{1,0:T(8,128)(2,1)S(1)} collective-permute-done((bf16[256,512]{1,0:T(8,128)(2,1)S(1)}, bf16[256,512]{1,0:T(8,128)(2,1)S(1)}, u32[]{:S(2)}, u32[]{:S(2)}) %collective-permute-start.33) | collective-permute-done | bytes 262176 | tf_op jit(solution)/shard_map/ppermute | solution.py:149
  124.5 14.1 %collective-permute-done.30 = bf16[256,512]{1,0:T(8,128)(2,1)S(1)} collective-permute-done((bf16[256,512]{1,0:T(8,128)(2,1)S(1)}, bf16[256,512]{1,0:T(8,128)(2,1)S(1)}, u32[]{:S(2)}, u32[]{:S(2)}) %collective-permute-start.30) | collective-permute-done | bytes 262176 | tf_op jit(solution)/shard_map/ppermute | solution.py:149
  139.4 1.5 collective-permute-start.20
  141.7 11.0 %collective-permute-done.20 = bf16[512,512]{1,0:T(8,128)(2,1)S(1)} collective-permute-done((bf16[512,512]{1,0:T(8,128)(2,1)S(1)}, bf16[512,512]{1,0:T(8,128)(2,1)S(1)}, u32[]{:S(2)}, u32[]{:S(2)}) %collective-permute-start.20) | collective-permute-done | bytes 524320 | tf_op jit(solution)/shard_map/ppermute | solution.py:149
  156.7 1.7 collective-permute-start.40
  158.4 1.9 collective-permute-done.40
  160.4 4.1 %collective-permute-done.26 = bf16[2,48,256]{2,1,0:T(8,128)(2,1)S(1)} collective-permute-done((bf16[2,48,256]{2,1,0:T(8,128)(2,1)S(1)}, bf16[2,48,256]{2,1,0:T(8,128)(2,1)S(1)}, u32[]{:S(2)}, u32[]{:S(2)}) %collective-permute-start.26) | collective-permute-done | bytes 49184 | tf_op jit(solution)/shard_map/ppermute | solution.py:24
  164.7 5.9 %collective-permute-done.27 = bf16[4,48,256]{2,1,0:T(8,128)(2,1)S(1)} collective-permute-done((bf16[4,48,256]{2,1,0:T(8,128)(2,1)S(1)}, bf16[4,48,256]{2,1,0:T(8,128)(2,1)S(1)}, u32[]{:S(2)}, u32[]{:S(2)}) %collective-permute-start.27) | collective-permute-done | bytes 98336 | tf_op jit(solution)/shard_map/ppermute | solution.py:24
  171.3 1.1 bitcast_add_fusion
  172.6 1.7 collective-permute-start.38
  175.3 3.7 %collective-permute-done.38 = bf16[1,512,256]{2,1,0:T(8,128)(2,1)S(1)} collective-permute-done((bf16[1,512,256]{2,1,0:T(8,128)(2,1)S(1)}, bf16[1,512,256]{2,1,0:T(8,128)(2,1)S(1)}, u32[]{:S(2)}, u32[]{:S(2)}) %collective-permute-start.38) | collective-permute-done | bytes 262176 | tf_op jit(solution)/shard_map/ppermute | solution.py:24
  179.2 1.6 collective-permute-start.41
  180.9 2.3 %collective-permute-done.41 = bf16[256,256]{1,0:T(8,128)(2,1)S(1)} collective-permute-done((bf16[256,256]{1,0:T(8,128)(2,1)S(1)}, bf16[256,256]{1,0:T(8,128)(2,1)S(1)}, u32[]{:S(2)}, u32[]{:S(2)}) %collective-permute-start.41) | collective-permute-done | bytes 131104 | tf_op jit(solution)/shard_map/ppermute | solution.py:224
  183.3 1.0 convolution_convert_fusion
  184.3 4.8 %all-to-all-start = ((bf16[8,64,256]{2,1,0:T(8,128)(2,1)}), bf16[8,64,256]{2,1,0:T(8,128)(2,1)S(1)}, u32[]{:S(2)}, u32[]{:S(2)}) async-start(bf16[8,64,256]{2,1,0:T(8,128)(2,1)} %bitcast.18), calls=%async_computation | async-start | bytes 524288 | tf_op jit(solution)/shard_map/all_to_all | solution.py:401
  189.2 8.0 %all-to-all-done = bf16[8,64,256]{2,1,0:T(8,128)(2,1)S(1)} async-done(((bf16[8,64,256]{2,1,0:T(8,128)(2,1)}), bf16[8,64,256]{2,1,0:T(8,128)(2,1)S(1)}, u32[]{:S(2)}, u32[]{:S(2)}) %all-to-all-start) | async-done | bytes 262176 | tf_op jit(solution)/shard_map/all_to_all | solution.py:401
  197.3 5.5 %shard_map.140 = (bf16[4,128,1024]{2,1,0:T(8,128)(2,1)}, bf16[256,256]{1,0:T(8,128)(2,1)}) custom-call(s32[4]{0:T(128)S(1)} %broadcast_xor_fusion.place_ref, bf16[4,128,1024]{2,1,0:T(8,128)(2,1)S(1)} %copy-done.8, bf16[8,32,256]{2,1,0:T(8,128)(2,1)S(1)} %slice.148.prefix_ref, bf16[4,128,256]{2,1,0:T(8,128)(2,1)S(1)} %copy-done.9, ...), custom_call_target="tpu_custom_call" | custom-call | flops 603979776 | bytes 4194304 | tf_op jit(solution)/shard_map/pallas_call | solution.py:304
  (197 shorter events, 21.9 us)
Async XLA Ops:
  1.7 22.8 %collective-permute-start.12 = (bf16[128,1280]{1,0:T(8,128)(2,1)S(1)}, bf16[128,1280]{1,0:T(8,128)(2,1)}, u32[]{:S(2)}, u32[]{:S(2)}) collective-permute-start(bf16[128,1280]{1,0:T(8,128)(2,1)S(1)} %get-tuple-element.54), channel_id=1, source_target_pairs={{0,2},{1,3},{2,0},{3,1},{4,6},{5,7},{6,4},{7,5},{8,10},{9,11},{10,... | collective-permute-start | bytes 983048 | tf_op jit(solution)/shard_map/ppermute | solution.py:24
  4.8 5.6 %copy-start.25 = (s32[32,1]{0,1:T(1,128)S(1)}, s32[32,1]{0,1:T(1,128)}, u32[]{:S(2)}) copy-start(s32[32,1]{0,1:T(1,128)} %param.16) | copy-start | bytes 388
  4.8 5.8 %copy-start.26 = (s32[1,4]{1,0:T(1,128)S(1)}, s32[1,4]{1,0:T(1,128)}, u32[]{:S(2)}) copy-start(s32[1,4]{1,0:T(1,128)} %param.18) | copy-start | bytes 52
  4.8 9.0 %collective-permute-start = (bf16[128,1280]{1,0:T(8,128)(2,1)S(1)}, bf16[128,1280]{1,0:T(8,128)(2,1)S(1)}, u32[]{:S(2)}, u32[]{:S(2)}) collective-permute-start(bf16[128,1280]{1,0:T(8,128)(2,1)S(1)} %get-tuple-element.55), channel_id=1, source_target_pairs={{0,0},{1,10},{2,16},{3,26},{4,4},{5,14},{6,20},{7,30},{8,2},{9,8},... | collective-permute-start | bytes 983048 | tf_op jit(solution)/shard_map/ppermute | solution.py:38
  8.3 10.8 %copy-start.27 = (s32[32]{0:T(128)S(1)}, s32[32]{0:T(128)}, u32[]{:S(2)}) copy-start(s32[32]{0:T(128)} %param.17) | copy-start | bytes 388
  8.3 10.8 %copy-start.10 = (s32[4]{0:T(128)S(1)}, s32[4]{0:T(128)}, u32[]{:S(2)}) copy-start(s32[4]{0:T(128)} %constant.123.clone) | copy-start | bytes 52
  8.3 24.7 %copy-start.20 = (bf16[1,32,256]{2,1,0:T(8,128)(2,1)S(1)}, bf16[1,32,256]{2,1,0:T(8,128)(2,1)}, u32[]{:S(2)}) copy-start(bf16[1,32,256]{2,1,0:T(8,128)(2,1)} %param.20) | copy-start | bytes 49156
  8.3 32.8 %collective-permute-start.8 = (bf16[640,512]{1,0:T(8,128)(2,1)S(1)}, bf16[640,512]{1,0:T(8,128)(2,1)}, u32[]{:S(2)}, u32[]{:S(2)}) collective-permute-start(bf16[640,512]{1,0:T(8,128)(2,1)S(1)} %get-tuple-element.41.refs_1_), channel_id=1, source_target_pairs={{4,0},{0,4},{12,8},{8,12},{20,16},{16,20},{28,24},{24,28},{5,1},{1... | collective-permute-start | bytes 1966088 | tf_op jit(solution)/shard_map/ppermute | solution.py:183
  9.9 42.3 %collective-permute-start.4 = (bf16[640,512]{1,0:T(8,128)(2,1)S(1)}, bf16[640,512]{1,0:T(8,128)(2,1)}, u32[]{:S(2)}, u32[]{:S(2)}) collective-permute-start(bf16[640,512]{1,0:T(8,128)(2,1)S(1)} %get-tuple-element.42.refs_1_), channel_id=1, source_target_pairs={{4,0},{0,4},{12,8},{8,12},{20,16},{16,20},{28,24},{24,28},{5,1},{1... | collective-permute-start | bytes 1966088 | tf_op jit(solution)/shard_map/ppermute | solution.py:183
  12.2 26.3 %copy-start.22 = (s32[128]{0:T(128)}, s32[128]{0:T(128)S(1)}, u32[]{:S(2)}) copy-start(s32[128]{0:T(128)S(1)} %add.359) | copy-start | bytes 1540
  13.8 24.7 %copy-start.3 = (bf16[128,1280]{1,0:T(8,128)(2,1)}, bf16[128,1280]{1,0:T(8,128)(2,1)S(1)}, u32[]{:S(2)}) copy-start(bf16[128,1280]{1,0:T(8,128)(2,1)S(1)} %collective-permute-done.refs_0_) | copy-start | bytes 983044
  13.8 15.0 %collective-permute-start.1 = (bf16[128,1280]{1,0:T(8,128)(2,1)S(1)}, bf16[128,1280]{1,0:T(8,128)(2,1)S(1)}, u32[]{:S(2)}, u32[]{:S(2)}) collective-permute-start(bf16[128,1280]{1,0:T(8,128)(2,1)S(1)} %collective-permute-done.refs_0_), channel_id=1, source_target_pairs={{0,2},{1,3},{2,0},{3,1},{4,6},{5,7},{6,4},{7,5},{8,10},{9,11},{10,... | collective-permute-start | bytes 983048 | tf_op jit(solution)/shard_map/ppermute | solution.py:24
  19.8 18.7 %collective-permute-start.2 = (bf16[128,1280]{1,0:T(8,128)(2,1)S(1)}, bf16[128,1280]{1,0:T(8,128)(2,1)S(1)}, u32[]{:S(2)}, u32[]{:S(2)}) collective-permute-start(bf16[128,1280]{1,0:T(8,128)(2,1)S(1)} %collective-permute-done.refs_0_), channel_id=1, source_target_pairs={{0,1},{1,0},{2,3},{3,2},{4,5},{5,4},{6,7},{7,6},{8,9},{9,8},{10,11... | collective-permute-start | bytes 983048 | tf_op jit(solution)/shard_map/ppermute | solution.py:24
  24.5 10.3 %collective-permute-start.13 = (bf16[128,1280]{1,0:T(8,128)(2,1)}, bf16[128,1280]{1,0:T(8,128)(2,1)}, u32[]{:S(2)}, u32[]{:S(2)}) collective-permute-start(bf16[128,1280]{1,0:T(8,128)(2,1)} %collective-permute-done.12), channel_id=1, source_target_pairs={{2,0},{3,10},{0,16},{1,26},{6,4},{7,14},{4,20},{5,30},{10,2},{11,8... | collective-permute-start | bytes 983048 | tf_op jit(solution)/shard_map/ppermute | solution.py:38
  28.8 9.7 %collective-permute-start.3 = (bf16[128,1280]{1,0:T(8,128)(2,1)S(1)}, bf16[128,1280]{1,0:T(8,128)(2,1)S(1)}, u32[]{:S(2)}, u32[]{:S(2)}) collective-permute-start(bf16[128,1280]{1,0:T(8,128)(2,1)S(1)} %collective-permute-done.1.refs_1_), channel_id=1, source_target_pairs={{0,1},{1,0},{2,3},{3,2},{4,5},{5,4},{6,7},{7,6},{8,9},{9,8},{10,11... | collective-permute-start | bytes 983048 | tf_op jit(solution)/shard_map/ppermute | solution.py:24
  34.8 28.5 %collective-permute-start.14 = (bf16[128,1280]{1,0:T(8,128)(2,1)}, bf16[128,1280]{1,0:T(8,128)(2,1)}, u32[]{:S(2)}, u32[]{:S(2)}) collective-permute-start(bf16[128,1280]{1,0:T(8,128)(2,1)} %collective-permute-done.13.refs_0_), channel_id=1, source_target_pairs={{0,2},{1,3},{2,0},{3,1},{4,6},{5,7},{6,4},{7,5},{8,10},{9,11},{10,... | collective-permute-start | bytes 983048 | tf_op jit(solution)/shard_map/ppermute | solution.py:24
  44.0 20.3 %collective-permute-start.9 = (bf16[256,512]{1,0:T(8,128)(2,1)}, bf16[256,512]{1,0:T(8,128)(2,1)}, u32[]{:S(2)}, u32[]{:S(2)}) collective-permute-start(bf16[256,512]{1,0:T(8,128)(2,1)} %get-tuple-element.23), channel_id=1, source_target_pairs={{0,8},{4,12},{24,16},{28,20},{1,9},{5,13},{25,17},{29,21},{2,10},{... | collective-permute-start | bytes 786440 | tf_op jit(solution)/shard_map/ppermute | solution.py:147
  50.7 28.3 %collective-permute-start.21 = (bf16[640,512]{1,0:T(8,128)(2,1)S(1)}, bf16[640,512]{1,0:T(8,128)(2,1)}, u32[]{:S(2)}, u32[]{:S(2)}) collective-permute-start(bf16[640,512]{1,0:T(8,128)(2,1)S(1)} %get-tuple-element.27.refs_1_), channel_id=1, source_target_pairs={{4,0},{0,4},{12,8},{8,12},{20,16},{16,20},{28,24},{24,28},{5,1},{1... | collective-permute-start | bytes 1966088 | tf_op jit(solution)/shard_map/ppermute | solution.py:183
  55.7 9.7 %collective-permute-start.5 = (bf16[256,512]{1,0:T(8,128)(2,1)}, bf16[256,512]{1,0:T(8,128)(2,1)}, u32[]{:S(2)}, u32[]{:S(2)}) collective-permute-start(bf16[256,512]{1,0:T(8,128)(2,1)} %get-tuple-element.21), channel_id=1, source_target_pairs={{0,8},{4,12},{24,16},{28,20},{1,9},{5,13},{25,17},{29,21},{2,10},{... | collective-permute-start | bytes 786440 | tf_op jit(solution)/shard_map/ppermute | solution.py:147
  62.8 21.9 %collective-permute-start.17 = (bf16[640,512]{1,0:T(8,128)(2,1)}, bf16[640,512]{1,0:T(8,128)(2,1)S(1)}, u32[]{:S(2)}, u32[]{:S(2)}) collective-permute-start(bf16[640,512]{1,0:T(8,128)(2,1)} %get-tuple-element.24.refs_2_), channel_id=1, source_target_pairs={{4,0},{0,4},{12,8},{8,12},{20,16},{16,20},{28,24},{24,28},{5,1},{1... | collective-permute-start | bytes 1966088 | tf_op jit(solution)/shard_map/ppermute | solution.py:183
  63.4 3.8 %collective-permute-start.15 = (bf16[128,1280]{1,0:T(8,128)(2,1)}, bf16[128,1280]{1,0:T(8,128)(2,1)S(1)}, u32[]{:S(2)}, u32[]{:S(2)}) collective-permute-start(bf16[128,1280]{1,0:T(8,128)(2,1)} %collective-permute-done.13.refs_0_), channel_id=1, source_target_pairs={{0,1},{1,0},{2,3},{3,2},{4,5},{5,4},{6,7},{7,6},{8,9},{9,8},{10,11... | collective-permute-start | bytes 983048 | tf_op jit(solution)/shard_map/ppermute | solution.py:24
  64.3 3.7 %collective-permute-start.16 = (bf16[128,1280]{1,0:T(8,128)(2,1)}, bf16[128,1280]{1,0:T(8,128)(2,1)S(1)}, u32[]{:S(2)}, u32[]{:S(2)}) collective-permute-start(bf16[128,1280]{1,0:T(8,128)(2,1)} %collective-permute-done.14.refs_1_), channel_id=1, source_target_pairs={{0,1},{1,0},{2,3},{3,2},{4,5},{5,4},{6,7},{7,6},{8,9},{9,8},{10,11... | collective-permute-start | bytes 983048 | tf_op jit(solution)/shard_map/ppermute | solution.py:24
  65.4 25.1 %collective-permute-start.10 = (bf16[256,512]{1,0:T(8,128)(2,1)S(1)}, bf16[256,512]{1,0:T(8,128)(2,1)S(1)}, u32[]{:S(2)}, u32[]{:S(2)}) collective-permute-start(bf16[256,512]{1,0:T(8,128)(2,1)S(1)} %add_convert_fusion.5), channel_id=1, source_target_pairs={{8,16},{12,20},{16,8},{20,12},{9,17},{13,21},{17,9},{21,13},{10,18... | collective-permute-start | bytes 786440 | tf_op jit(solution)/shard_map/ppermute | solution.py:148
  67.2 24.7 %collective-permute-start.6 = (bf16[256,512]{1,0:T(8,128)(2,1)S(1)}, bf16[256,512]{1,0:T(8,128)(2,1)S(1)}, u32[]{:S(2)}, u32[]{:S(2)}) collective-permute-start(bf16[256,512]{1,0:T(8,128)(2,1)S(1)} %add_convert_fusion.6), channel_id=1, source_target_pairs={{8,16},{12,20},{16,8},{20,12},{9,17},{13,21},{17,9},{21,13},{10,18... | collective-permute-start | bytes 786440 | tf_op jit(solution)/shard_map/ppermute | solution.py:148
  71.8 14.2 %copy-start.2 = (bf16[640,512]{1,0:T(8,128)(2,1)S(1)}, bf16[640,512]{1,0:T(8,128)(2,1)}, u32[]{:S(2)}) copy-start(bf16[640,512]{1,0:T(8,128)(2,1)} %get-tuple-element.24.refs_2_) | copy-start | bytes 1966084
  71.9 21.8 %collective-permute-start.31 = (bf16[256,512]{1,0:T(8,128)(2,1)S(1)}, bf16[256,512]{1,0:T(8,128)(2,1)S(1)}, u32[]{:S(2)}, u32[]{:S(2)}) collective-permute-start(bf16[256,512]{1,0:T(8,128)(2,1)S(1)} %get-tuple-element.35), channel_id=1, source_target_pairs={{0,8},{4,12},{24,16},{28,20},{1,9},{5,13},{25,17},{29,21},{2,10},{... | collective-permute-start | bytes 786440 | tf_op jit(solution)/shard_map/ppermute | solution.py:147
  81.2 13.8 %collective-permute-start.34 = (bf16[256,512]{1,0:T(8,128)(2,1)S(1)}, bf16[256,512]{1,0:T(8,128)(2,1)S(1)}, u32[]{:S(2)}, u32[]{:S(2)}) collective-permute-start(bf16[256,512]{1,0:T(8,128)(2,1)S(1)} %get-tuple-element.37), channel_id=1, source_target_pairs={{0,8},{4,12},{24,16},{28,20},{1,9},{5,13},{25,17},{29,21},{2,10},{... | collective-permute-start | bytes 786440 | tf_op jit(solution)/shard_map/ppermute | solution.py:147
  84.8 12.1 %collective-permute-start.22 = (bf16[256,512]{1,0:T(8,128)(2,1)S(1)}, bf16[256,512]{1,0:T(8,128)(2,1)S(1)}, u32[]{:S(2)}, u32[]{:S(2)}) collective-permute-start(bf16[256,512]{1,0:T(8,128)(2,1)S(1)} %get-tuple-element.29), channel_id=1, source_target_pairs={{0,8},{4,12},{24,16},{28,20},{1,9},{5,13},{25,17},{29,21},{2,10},{... | collective-permute-start | bytes 786440 | tf_op jit(solution)/shard_map/ppermute | solution.py:147
  88.3 5.4 %copy-start.1 = (bf16[256,512]{1,0:T(8,128)(2,1)S(1)}, bf16[256,512]{1,0:T(8,128)(2,1)}, u32[]{:S(2)}) copy-start(bf16[256,512]{1,0:T(8,128)(2,1)} %copy-done) | copy-start | bytes 786436
  90.5 12.0 %collective-permute-start.28 = (bf16[256,512]{1,0:T(8,128)(2,1)S(1)}, bf16[256,512]{1,0:T(8,128)(2,1)S(1)}, u32[]{:S(2)}, u32[]{:S(2)}) collective-permute-start(bf16[256,512]{1,0:T(8,128)(2,1)S(1)} %get-tuple-element.33), channel_id=1, source_target_pairs={{0,8},{4,12},{24,16},{28,20},{1,9},{5,13},{25,17},{29,21},{2,10},{... | collective-permute-start | bytes 786440 | tf_op jit(solution)/shard_map/ppermute | solution.py:147
  91.8 17.9 %copy-start.11 = (bf16[2048,1024]{1,0:T(8,128)(2,1)S(1)}, bf16[2048,1024]{1,0:T(8,128)(2,1)}, u32[]{:S(2)}) copy-start(bf16[2048,1024]{1,0:T(8,128)(2,1)} %param.15) | copy-start | bytes 12582916
  91.9 17.9 %copy-start.19 = (f32[512]{0:T(512)S(1)}, f32[512]{0:T(512)}, u32[]{:S(2)}) copy-start(f32[512]{0:T(512)} %get-tuple-element.58) | copy-start | bytes 6148
  91.9 25.3 %collective-permute-start.18 = (bf16[512,512]{1,0:T(8,128)(2,1)S(1)}, bf16[512,512]{1,0:T(8,128)(2,1)S(1)}, u32[]{:S(2)}, u32[]{:S(2)}) collective-permute-start(bf16[512,512]{1,0:T(8,128)(2,1)S(1)} %get-tuple-element.26), channel_id=1, source_target_pairs={{0,8},{4,12},{24,16},{28,20},{1,9},{5,13},{25,17},{29,21},{2,10},{... | collective-permute-start | bytes 1572872 | tf_op jit(solution)/shard_map/ppermute | solution.py:147
  93.7 16.5 %collective-permute-start.11 = (bf16[256,512]{1,0:T(8,128)(2,1)S(1)}, bf16[256,512]{1,0:T(8,128)(2,1)S(1)}, u32[]{:S(2)}, u32[]{:S(2)}) collective-permute-start(bf16[256,512]{1,0:T(8,128)(2,1)S(1)} %fusion.16), channel_id=1, source_target_pairs={{16,24},{20,28},{8,0},{12,4},{17,25},{21,29},{9,1},{13,5},{18,26},... | collective-permute-start | bytes 786440 | tf_op jit(solution)/shard_map/ppermute | solution.py:149
  95.1 14.0 %collective-permute-start.7 = (bf16[256,512]{1,0:T(8,128)(2,1)S(1)}, bf16[256,512]{1,0:T(8,128)(2,1)S(1)}, u32[]{:S(2)}, u32[]{:S(2)}) collective-permute-start(bf16[256,512]{1,0:T(8,128)(2,1)S(1)} %fusion.12), channel_id=1, source_target_pairs={{16,24},{20,28},{8,0},{12,4},{17,25},{21,29},{9,1},{13,5},{18,26},... | collective-permute-start | bytes 786440 | tf_op jit(solution)/shard_map/ppermute | solution.py:149
  96.5 14.5 %copy-start.18 = (f32[512]{0:T(512)S(1)}, f32[512]{0:T(512)}, u32[]{:S(2)}) copy-start(f32[512]{0:T(512)} %get-tuple-element.57) | copy-start | bytes 6148
  96.9 14.8 %collective-permute-start.32 = (bf16[256,512]{1,0:T(8,128)(2,1)S(1)}, bf16[256,512]{1,0:T(8,128)(2,1)S(1)}, u32[]{:S(2)}, u32[]{:S(2)}) collective-permute-start(bf16[256,512]{1,0:T(8,128)(2,1)S(1)} %add_convert_fusion.2), channel_id=1, source_target_pairs={{8,16},{12,20},{16,8},{20,12},{9,17},{13,21},{17,9},{21,13},{10,18... | collective-permute-start | bytes 786440 | tf_op jit(solution)/shard_map/ppermute | solution.py:148
  102.5 10.6 %collective-permute-start.35 = (bf16[256,512]{1,0:T(8,128)(2,1)S(1)}, bf16[256,512]{1,0:T(8,128)(2,1)S(1)}, u32[]{:S(2)}, u32[]{:S(2)}) collective-permute-start(bf16[256,512]{1,0:T(8,128)(2,1)S(1)} %add_convert_fusion.1), channel_id=1, source_target_pairs={{8,16},{12,20},{16,8},{20,12},{9,17},{13,21},{17,9},{21,13},{10,18... | collective-permute-start | bytes 786440 | tf_op jit(solution)/shard_map/ppermute | solution.py:148
  109.1 5.4 %collective-permute-start.23 = (bf16[256,512]{1,0:T(8,128)(2,1)S(1)}, bf16[256,512]{1,0:T(8,128)(2,1)S(1)}, u32[]{:S(2)}, u32[]{:S(2)}) collective-permute-start(bf16[256,512]{1,0:T(8,128)(2,1)S(1)} %add_convert_fusion.4), channel_id=1, source_target_pairs={{8,16},{12,20},{16,8},{20,12},{9,17},{13,21},{17,9},{21,13},{10,18... | collective-permute-start | bytes 786440 | tf_op jit(solution)/shard_map/ppermute | solution.py:148
  110.2 5.6 %collective-permute-start.29 = (bf16[256,512]{1,0:T(8,128)(2,1)S(1)}, bf16[256,512]{1,0:T(8,128)(2,1)S(1)}, u32[]{:S(2)}, u32[]{:S(2)}) collective-permute-start(bf16[256,512]{1,0:T(8,128)(2,1)S(1)} %add_convert_fusion.3), channel_id=1, source_target_pairs={{8,16},{12,20},{16,8},{20,12},{9,17},{13,21},{17,9},{21,13},{10,18... | collective-permute-start | bytes 786440 | tf_op jit(solution)/shard_map/ppermute | solution.py:148
  111.8 12.5 %collective-permute-start.33 = (bf16[256,512]{1,0:T(8,128)(2,1)S(1)}, bf16[256,512]{1,0:T(8,128)(2,1)S(1)}, u32[]{:S(2)}, u32[]{:S(2)}) collective-permute-start(bf16[256,512]{1,0:T(8,128)(2,1)S(1)} %fusion.28), channel_id=1, source_target_pairs={{16,24},{20,28},{8,0},{12,4},{17,25},{21,29},{9,1},{13,5},{18,26},... | collective-permute-start | bytes 786440 | tf_op jit(solution)/shard_map/ppermute | solution.py:149
  113.2 27.7 %collective-permute-start.36 = (bf16[256,512]{1,0:T(8,128)(2,1)S(1)}, bf16[256,512]{1,0:T(8,128)(2,1)S(1)}, u32[]{:S(2)}, u32[]{:S(2)}) collective-permute-start(bf16[256,512]{1,0:T(8,128)(2,1)S(1)} %fusion.32), channel_id=1, source_target_pairs={{16,24},{20,28},{8,0},{12,4},{17,25},{21,29},{9,1},{13,5},{18,26},... | collective-permute-start | bytes 786440 | tf_op jit(solution)/shard_map/ppermute | solution.py:149
  114.6 26.5 %collective-permute-start.24 = (bf16[256,512]{1,0:T(8,128)(2,1)S(1)}, bf16[256,512]{1,0:T(8,128)(2,1)S(1)}, u32[]{:S(2)}, u32[]{:S(2)}) collective-permute-start(bf16[256,512]{1,0:T(8,128)(2,1)S(1)} %fusion.20), channel_id=1, source_target_pairs={{16,24},{20,28},{8,0},{12,4},{17,25},{21,29},{9,1},{13,5},{18,26},... | collective-permute-start | bytes 786440 | tf_op jit(solution)/shard_map/ppermute | solution.py:149
  116.0 22.7 %collective-permute-start.30 = (bf16[256,512]{1,0:T(8,128)(2,1)S(1)}, bf16[256,512]{1,0:T(8,128)(2,1)S(1)}, u32[]{:S(2)}, u32[]{:S(2)}) collective-permute-start(bf16[256,512]{1,0:T(8,128)(2,1)S(1)} %fusion.24), channel_id=1, source_target_pairs={{16,24},{20,28},{8,0},{12,4},{17,25},{21,29},{9,1},{13,5},{18,26},... | collective-permute-start | bytes 786440 | tf_op jit(solution)/shard_map/ppermute | solution.py:149
  117.4 21.8 %collective-permute-start.19 = (bf16[512,512]{1,0:T(8,128)(2,1)S(1)}, bf16[512,512]{1,0:T(8,128)(2,1)S(1)}, u32[]{:S(2)}, u32[]{:S(2)}) collective-permute-start(bf16[512,512]{1,0:T(8,128)(2,1)S(1)} %add_convert_fusion), channel_id=1, source_target_pairs={{8,16},{12,20},{16,8},{20,12},{9,17},{13,21},{17,9},{21,13},{10,18... | collective-permute-start | bytes 1572872 | tf_op jit(solution)/shard_map/ppermute | solution.py:148
  139.4 13.3 %collective-permute-start.20 = (bf16[512,512]{1,0:T(8,128)(2,1)S(1)}, bf16[512,512]{1,0:T(8,128)(2,1)S(1)}, u32[]{:S(2)}, u32[]{:S(2)}) collective-permute-start(bf16[512,512]{1,0:T(8,128)(2,1)S(1)} %fusion), channel_id=1, source_target_pairs={{16,24},{20,28},{8,0},{12,4},{17,25},{21,29},{9,1},{13,5},{18,26},... | collective-permute-start | bytes 1572872 | tf_op jit(solution)/shard_map/ppermute | solution.py:149
  141.1 11.6 %copy-start.21 = (f32[512]{0:T(512)S(1)}, f32[512]{0:T(512)}, u32[]{:S(2)}) copy-start(f32[512]{0:T(512)} %get-tuple-element.59) | copy-start | bytes 6148
  155.4 1.2 collective-permute-start.39
  156.0 4.3 %collective-permute-start.25 = (bf16[1,48,256]{2,1,0:T(8,128)(2,1)S(1)}, bf16[1,48,256]{2,1,0:T(8,128)(2,1)S(1)}, u32[]{:S(2)}, u32[]{:S(2)}) collective-permute-start(bf16[1,48,256]{2,1,0:T(8,128)(2,1)S(1)} %copy-done.13), channel_id=1, source_target_pairs={{0,4},{4,0},{8,12},{12,8},{16,20},{20,16},{24,28},{28,24},{1,5},{5... | collective-permute-start | bytes 73736 | tf_op jit(solution)/shard_map/ppermute | solution.py:24
  156.7 3.7 %collective-permute-start.40 = (f32[512]{0:T(512)S(1)}, f32[512]{0:T(512)S(1)}, u32[]{:S(2)}, u32[]{:S(2)}) collective-permute-start(f32[512]{0:T(512)S(1)} %fusion.75), channel_id=1, source_target_pairs={{0,2},{1,3},{2,0},{3,1},{4,6},{5,7},{6,4},{7,5},{8,10},{9,11},{10,... | collective-permute-start | bytes 6152 | tf_op jit(solution)/shard_map/ppermute | solution.py:24
  158.4 12.4 %collective-permute-start.37 = (bf16[2,512,256]{2,1,0:T(8,128)(2,1)S(1)}, bf16[2,512,256]{2,1,0:T(8,128)(2,1)}, u32[]{:S(2)}, u32[]{:S(2)}) collective-permute-start(bf16[2,512,256]{2,1,0:T(8,128)(2,1)S(1)} %fusion.36), channel_id=1, source_target_pairs={{0,1},{1,0},{2,3},{3,2},{4,5},{5,4},{6,7},{7,6},{8,9},{9,8},{10,11... | collective-permute-start | bytes 1572872 | tf_op jit(solution)/shard_map/ppermute | solution.py:24
  160.3 4.2 %collective-permute-start.26 = (bf16[2,48,256]{2,1,0:T(8,128)(2,1)S(1)}, bf16[2,48,256]{2,1,0:T(8,128)(2,1)S(1)}, u32[]{:S(2)}, u32[]{:S(2)}) collective-permute-start(bf16[2,48,256]{2,1,0:T(8,128)(2,1)S(1)} %pad_maximum_fusion.3), channel_id=1, source_target_pairs={{0,8},{4,12},{8,0},{12,4},{16,24},{20,28},{24,16},{28,20},{1,9},{5... | collective-permute-start | bytes 147464 | tf_op jit(solution)/shard_map/ppermute | solution.py:24
  164.5 6.1 %collective-permute-start.27 = (bf16[4,48,256]{2,1,0:T(8,128)(2,1)S(1)}, bf16[4,48,256]{2,1,0:T(8,128)(2,1)S(1)}, u32[]{:S(2)}, u32[]{:S(2)}) collective-permute-start(bf16[4,48,256]{2,1,0:T(8,128)(2,1)S(1)} %pad_maximum_fusion.2), channel_id=1, source_target_pairs={{0,16},{4,20},{8,24},{12,28},{16,0},{20,4},{24,8},{28,12},{1,17},{... | collective-permute-start | bytes 294920 | tf_op jit(solution)/shard_map/ppermute | solution.py:24
  172.4 16.6 %copy-start.28 = (s32[4]{0:T(128)S(1)}, s32[4]{0:T(128)}, u32[]{:S(2)}) copy-start(s32[4]{0:T(128)} %param.19) | copy-start | bytes 52
  172.4 16.6 %copy-start.12 = (s32[4,128,1]{2,1,0:T(8,128)S(1)}, s32[4,128,1]{2,1,0:T(8,128)}, u32[]{:S(2)}) copy-start(s32[4,128,1]{2,1,0:T(8,128)} %add.371) | copy-start | bytes 6148
  172.5 16.6 %copy-start.15 = (pred[4,128,1]{2,1,0:T(8,128)(4,1)S(1)}, pred[4,128,1]{2,1,0:T(8,128)(4,1)}, u32[]{:S(2)}) copy-start(pred[4,128,1]{2,1,0:T(8,128)(4,1)} %broadcast_in_dim.31) | copy-start | bytes 1540
  172.5 16.6 %copy-start.23 = (s32[128]{0:T(128)S(1)}, s32[128]{0:T(128)}, u32[]{:S(2)}) copy-start(s32[128]{0:T(128)} %copy-done.22) | copy-start | bytes 1540
  172.5 24.8 %copy-start.7 = (s32[256,1]{1,0:T(8,128)S(1)}, s32[256,1]{1,0:T(8,128)}, u32[]{:S(2)}) copy-start(s32[256,1]{1,0:T(8,128)} %add.372.all_ref) | copy-start | bytes 3076
  172.5 24.8 %copy-start.8 = (bf16[4,128,1024]{2,1,0:T(8,128)(2,1)S(1)}, bf16[4,128,1024]{2,1,0:T(8,128)(2,1)}, u32[]{:S(2)}) copy-start(bf16[4,128,1024]{2,1,0:T(8,128)(2,1)} %query_ref.1) | copy-start | bytes 3145732
  172.5 24.8 %copy-start.9 = (bf16[4,128,256]{2,1,0:T(8,128)(2,1)S(1)}, bf16[4,128,256]{2,1,0:T(8,128)(2,1)}, u32[]{:S(2)}) copy-start(bf16[4,128,256]{2,1,0:T(8,128)(2,1)} %text_ref.1) | copy-start | bytes 786436
  172.6 6.4 %collective-permute-start.38 = (bf16[1,512,256]{2,1,0:T(8,128)(2,1)S(1)}, bf16[1,512,256]{2,1,0:T(8,128)(2,1)S(1)}, u32[]{:S(2)}, u32[]{:S(2)}) collective-permute-start(bf16[1,512,256]{2,1,0:T(8,128)(2,1)S(1)} %dynamic-slice_convert_fusion.1), channel_id=1, source_target_pairs={{0,2},{1,3},{2,0},{3,1},{4,6},{5,7},{6,4},{7,5},{8,10},{9,11},{10,... | collective-permute-start | bytes 786440 | tf_op jit(solution)/shard_map/ppermute | solution.py:24
  179.1 10.1 %copy-start.17 = (bf16[8,48,256]{2,1,0:T(8,128)(2,1)S(1)}, bf16[8,48,256]{2,1,0:T(8,128)(2,1)}, u32[]{:S(2)}) copy-start(bf16[8,48,256]{2,1,0:T(8,128)(2,1)} %copy-done.16) | copy-start | bytes 589828
  179.2 4.1 %collective-permute-start.41 = (bf16[256,256]{1,0:T(8,128)(2,1)S(1)}, bf16[256,256]{1,0:T(8,128)(2,1)S(1)}, u32[]{:S(2)}, u32[]{:S(2)}) collective-permute-start(bf16[256,256]{1,0:T(8,128)(2,1)S(1)} %slice.157), channel_id=1, source_target_pairs={{0,8},{4,12},{24,16},{28,20},{1,9},{5,13},{25,17},{29,21},{2,10},{... | collective-permute-start | bytes 393224 | tf_op jit(solution)/shard_map/ppermute | solution.py:224
  184.3 13.0 %all-to-all-start = ((bf16[8,64,256]{2,1,0:T(8,128)(2,1)}), bf16[8,64,256]{2,1,0:T(8,128)(2,1)S(1)}, u32[]{:S(2)}, u32[]{:S(2)}) async-start(bf16[8,64,256]{2,1,0:T(8,128)(2,1)} %bitcast.18), calls=%async_computation | async-start | bytes 524288 | tf_op jit(solution)/shard_map/all_to_all | solution.py:401
  (8 other events, 9.6 us)

commit v6 on v5

--- a/solution.py
+++ b/solution.py
@@ -11,7 +11,6 @@
 HD = 128
 GROUP = 8
 MOST_PAGES = 16
-CHUNKS = 4
 VMEM = 48 * 1024 * 1024
 
 
@@ -52,80 +51,83 @@
 ROLE_GROUPS = (3, 2, 0, 1)
 
 
-def order_kernel(share, scalars_ref, *refs):
+def order_kernel(share, pieces, scalars_ref, *refs):
     out_ref = refs[-1]
     rows, depth = refs[0].shape
     members = depth // share
     for place in range(4):
-        at = pl.ds(pl.multiple_of(scalars_ref[place] * rows, rows), rows)
-        for member in range(members):
-            if members == 1:
-                out_ref[at, :] = refs[place][...]
-            else:
-                source = lax.rem(scalars_ref[4] + member, members)
-                columns = pl.ds(pl.multiple_of(source * share, share), share)
-                out_ref[at, member * share : (member + 1) * share] = refs[place][:, columns]
+        for piece in range(pieces):
+            row = (scalars_ref[place] * pieces + piece) * rows
+            at = pl.ds(pl.multiple_of(row, rows), rows)
+            rows_ref = refs[place * pieces + piece]
+            for member in range(members):
+                if members == 1:
+                    out_ref[at, :] = rows_ref[...]
+                else:
+                    source = lax.rem(scalars_ref[4] + member, members)
+                    columns = pl.ds(pl.multiple_of(source * share, share), share)
+                    out_ref[at, member * share : (member + 1) * share] = rows_ref[:, columns]
 
 
 def order_rows(scalars, held, share):
-    rows, depth = held[0].shape
+    pieces = len(held[0])
+    rows, depth = held[0][0].shape
     return pl.pallas_call(
-        functools.partial(order_kernel, share),
+        functools.partial(order_kernel, share, pieces),
         grid_spec=pltpu.PrefetchScalarGridSpec(
             num_scalar_prefetch=1,
             grid=(1,),
-            in_specs=[pl.BlockSpec((rows, depth), lambda i, scalars: (0, 0))] * 4,
-            out_specs=pl.BlockSpec((4 * rows, depth), lambda i, scalars: (0, 0)),
-        ),
-        out_shape=jax.ShapeDtypeStruct((4 * rows, depth), jnp.bfloat16),
+            in_specs=[pl.BlockSpec((rows, depth), lambda i, scalars: (0, 0))] * (4 * pieces),
+            out_specs=pl.BlockSpec((4 * pieces * rows, depth), lambda i, scalars: (0, 0)),
+        ),
+        out_shape=jax.ShapeDtypeStruct((4 * pieces * rows, depth), jnp.bfloat16),
         compiler_params=pltpu.CompilerParams(vmem_limit_bytes=VMEM),
         cost_estimate=pl.CostEstimate(
-            flops=0, bytes_accessed=16 * rows * depth, transcendentals=0
-        ),
-    )(scalars, *held)
-
-
-def partial_kernel(halves, *refs):
-    rows_refs, weights_refs = refs[:halves], refs[halves:-2]
+            flops=0, bytes_accessed=16 * pieces * rows * depth, transcendentals=0
+        ),
+    )(scalars, *[piece for place in held for piece in place])
+
+
+def partial_kernel(rows_ref, *refs):
+    weights_refs = refs[:-2]
     far_ref, near_ref = refs[-2:]
-    for half, rows_ref in enumerate(rows_refs):
-        total = None
-        at = 0
-        for weights_ref in weights_refs:
-            depth = weights_ref.shape[0]
-            term = jnp.dot(
-                rows_ref[:, at : at + depth],
-                weights_ref[...],
-                preferred_element_type=jnp.float32,
-            )
-            total = term if total is None else total + term
-            at += depth
-        total = total.astype(jnp.bfloat16)
-        rows = total.shape[0] // 2
-        far_ref[half * rows : (half + 1) * rows] = total[:rows]
-        near_ref[half * rows : (half + 1) * rows] = total[rows:]
-
-
-def partial_products(held, weights, first, count):
-    rows, depth = held[0].shape
-    out_rows = len(held) * rows // 2
+    total = None
+    at = 0
+    for weights_ref in weights_refs:
+        depth = weights_ref.shape[0]
+        term = jnp.dot(
+            rows_ref[:, at : at + depth], weights_ref[...], preferred_element_type=jnp.float32
+        )
+        total = term if total is None else total + term
+        at += depth
+    total = total.astype(jnp.bfloat16)
+    rows = total.shape[0] // 2
+    far_ref[...] = total[:rows]
+    near_ref[...] = total[rows:]
+
+
+def partial_products(held, weights, count):
+    rows, depth = held.shape
     tile = min(count, 256)
-    offset = first // tile
-    out = pl.BlockSpec((out_rows, tile), lambda i: (0, i))
+
+    def block(used, first):
+        return pl.BlockSpec((used, tile), lambda i: (0, i + first // tile))
+
+    out = pl.BlockSpec((rows // 2, tile), lambda i: (0, i))
     return pl.pallas_call(
-        functools.partial(partial_kernel, len(held)),
+        partial_kernel,
         grid=(count // tile,),
-        in_specs=[pl.BlockSpec((rows, depth), lambda i: (0, 0))] * len(held)
-        + [pl.BlockSpec((w.shape[0], tile), lambda i: (0, i + offset)) for w in weights],
+        in_specs=[pl.BlockSpec((rows, depth), lambda i: (0, 0))]
+        + [block(used, first) for _, used, first in weights],
         out_specs=[out, out],
-        out_shape=[jax.ShapeDtypeStruct((out_rows, count), jnp.bfloat16)] * 2,
+        out_shape=[jax.ShapeDtypeStruct((rows // 2, count), jnp.bfloat16)] * 2,
         compiler_params=pltpu.CompilerParams(vmem_limit_bytes=VMEM),
         cost_estimate=pl.CostEstimate(
-            flops=4 * out_rows * depth * count,
-            bytes_accessed=4 * out_rows * depth + 2 * depth * count + 4 * out_rows * count,
+            flops=2 * rows * depth * count,
+            bytes_accessed=2 * rows * depth + 2 * depth * count + 2 * rows * count,
             transcendentals=0,
         ),
-    )(*held, *weights)
+    )(held, *[array for array, _, _ in weights])
 
 
 def along(pairs):
@@ -138,19 +140,37 @@
 ENDS_OUT = ((2, 3), (1, 0))
 
 
-def reduce_groups(parts):
+def reduce_groups(parts, is_end, small):
     far, near = parts
+    rows = far.shape[0]
 
     def add(mine, other):
-        return (mine.astype(jnp.float32) + other.astype(jnp.float32)).astype(jnp.bfloat16)
-
-    inward = lax.ppermute(far, "seq", along(ENDS_IN))
-    across = lax.ppermute(add(far, inward), "seq", along(MIDDLES))
-    outward = lax.ppermute(add(near, across), "seq", along(ENDS_OUT))
-    return add(near, outward)
-
-
-PLAN = (((0,), 0, 1), ((0,), 1, 1), ((1,), 0, 1), ((1,), 1, 1), ((0, 1), 2, 1), ((0,), 3, 1), ((1,), 3, 1))
+        return (mine.astype(jnp.float32) + other[:rows].astype(jnp.float32)).astype(jnp.bfloat16)
+
+    def send(value, extra, pairs):
+        if small is not None:
+            value = jnp.concatenate([value] + extra, axis=0)
+        return lax.ppermute(value, "seq", along(pairs))
+
+    def part(value, index):
+        count = small.shape[0]
+        return value[rows + index * count : rows + (index + 1) * count]
+
+    message = far if small is None else jnp.concatenate([far, small], axis=0)
+    inward = lax.ppermute(message, "seq", along(ENDS_IN))
+    extra = [] if small is None else [part(inward, 0), small]
+    across = send(add(far, inward), extra, MIDDLES)
+    extra = [] if small is None else [small, part(across, 1), part(across, 0)]
+    outward = send(add(near, across), extra, ENDS_OUT)
+    shared = None
+    if small is not None:
+        at_end = [part(outward, 0), part(outward, 1), part(outward, 2)]
+        at_middle = [part(inward, 0), part(across, 0), part(across, 1)]
+        shared = [small] + [jnp.where(is_end, e, m) for e, m in zip(at_end, at_middle)]
+    return add(near, outward), message, inward, shared
+
+
+PLAN = (2, 2, 2, 1, 1)
 
 
 def merge_tiles(panels, w_merge, ln_gain, w_kv, small):
@@ -161,60 +181,74 @@
     share = w_merge.shape[0]
     group = lax.axis_index("seq") // width
     inner = lax.axis_index("seq") % width
+    is_end = (group == 0) | (group == 3)
     local = panels.reshape(tiles * panel_rows, depth)
     half = local.shape[0] // 2
-    pieces = [
-        transpose_panels(local[:half], 0),
-        transpose_panels(flip(local[half:], "tp", 2), 2),
-    ]
-    columns = w_merge.shape[1] // CHUNKS
-    weights = []
-    for chunk in range(CHUNKS):
-        own = w_merge[:, chunk * columns : (chunk + 1) * columns]
-        if chunk >= 2:
-            own, _ = lax.optimization_barrier((own, weights[chunk - 2][1]))
-        parts = [own]
+    swapped = flip(local[half:], "tp", 2)
+    pieces = [transpose_panels(local[:half], 0), transpose_panels(swapped, 2)]
+    columns = w_merge.shape[1] // 2
+    small = small.reshape(-1, columns)
+    extra = small.shape[0]
+    received = []
+    for side in range(2):
+        own = w_merge[:, side * columns : (side + 1) * columns]
+        if side == 0:
+            own = jnp.concatenate([own, small], axis=0)
+        else:
+            own, _ = lax.optimization_barrier((own, swapped))
+        others = []
         for offset in range(1, width):
             pairs = [
                 (g * width + (i + offset) % width, g * width + i)
                 for g in range(tp_count)
                 for i in range(width)
             ]
-            parts.append(lax.ppermute(own, "seq", pairs))
-        weights.append(parts)
-    turn = inner
-    if share % 128:
-        weights = [
-            [parts[0], jnp.roll(jnp.concatenate(parts, axis=0), inner * share, axis=0)]
-            for parts in weights
-        ]
-        weights = [parts[1:] for parts in weights]
+            others.append(lax.ppermute(own, "seq", pairs))
+        received.append(others)
+    small = jnp.stack([small] + [other[share : share + extra] for other in received[0]])
+    small_shape = small.shape
+    if width > 2 or share % 128:
+        weights = []
+        for side in range(2):
+            own = w_merge[:, side * columns : (side + 1) * columns]
+            parts = [own] + [other[:share] for other in received[side]]
+            weights.append(jnp.roll(jnp.concatenate(parts, axis=0), inner * share, axis=0))
         share = depth
     shift = jnp.where(group < 2, 0, 3)
     groups = (panel_base() ^ jnp.arange(4, dtype=jnp.int32)) ^ shift
     roles = jnp.array([ROLE_GROUPS.index(g) for g in range(4)], jnp.int32)[groups]
-    scalars = jnp.concatenate([roles, jnp.full((4,), turn, jnp.int32)])
-    held = [order_rows(scalars, piece, share) for piece in pieces]
-    kv = [0.0, 0.0]
-    squares = [0.0, 0.0]
-    for step, (halves, first, count) in enumerate(PLAN):
-        chunk_rows = [held[h] for h in halves]
-        merged = reduce_groups(partial_products(chunk_rows, weights[first], 0, columns * count))
+    scalars = jnp.concatenate([roles, jnp.full((4,), inner, jnp.int32)])
+    held = order_rows(scalars, list(zip(*pieces)), share)
+    kv = 0.0
+    squares = 0.0
+    inwards = []
+    first = 0
+    for step, part in enumerate(PLAN):
+        count = part * w_merge.shape[1] // sum(PLAN)
+        side = first // columns
+        inside = first - side * columns
+        if share == depth:
+            operands = [(weights[side], depth, inside)]
+        else:
+            operands = [(w_merge, share, first), (received[side][0], share, inside)]
+        rows = held
+        if step >= 1:
+            before = (message,) + tuple(inwards[step - 2 : step - 1] if step >= 2 else ())
+            rows, _ = lax.optimization_barrier((held, before))
+        riding = small.reshape(-1, count) if step == 0 else None
+        merged, message, inward, shared = reduce_groups(
+            partial_products(rows, operands, count), is_end, riding
+        )
+        inwards.append(inward)
+        if step == 0:
+            everyone = jnp.stack(shared).reshape((4,) + small_shape)
         merged = merged.astype(jnp.float32)
-        at = slice(first * columns, (first + count) * columns)
+        at = slice(first, first + count)
         gained = (merged * ln_gain[at].astype(jnp.float32)[None, :]).astype(jnp.bfloat16)
-        for i, h in enumerate(halves):
-            rows = slice(i * 2 * half, (i + 1) * 2 * half)
-            squares[h] = squares[h] + jnp.sum(merged[rows] * merged[rows], axis=1)
-            kv[h] = kv[h] + jnp.dot(gained[rows], w_kv[at], preferred_element_type=jnp.float32)
-        if step == len(PLAN) - 2:
-            small, kv[0] = lax.optimization_barrier((small, kv[0]))
-    for bit in bits_of(seq_count):
-        small = jnp.concatenate([small, flip(small, "seq", bit)], axis=0)
-    def arrange(parts):
-        return jnp.concatenate([part[:half] for part in parts] + [part[half:] for part in parts])
-
-    return arrange(kv), arrange(squares), small
+        squares = squares + jnp.sum(merged * merged, axis=1)
+        kv = kv + jnp.dot(gained, w_kv[at], preferred_element_type=jnp.float32)
+        first += count
+    return kv, squares, everyone
 
 
 def return_rows(tile_kv):
@@ -240,11 +274,15 @@
     return blocks[0], squares
 
 
+SMALL_ROWS = 64
+
+
 def pack_small(prefix_cache, sources, tiles):
     width = prefix_cache.shape[2]
     asks = jnp.stack([sources, tiles]).astype(jnp.bfloat16)
-    asks = jnp.pad(asks, ((0, 14), (0, width - asks.shape[1])))
-    return jnp.concatenate([prefix_cache[0], asks], axis=0)[None]
+    rows = SMALL_ROWS - prefix_cache.shape[1]
+    asks = jnp.pad(asks, ((0, rows - 2), (0, width - asks.shape[1])))
+    return jnp.concatenate([prefix_cache[0], asks], axis=0)
 
 
 def attend_kernel(
@@ -356,16 +394,23 @@
     kv, squares, small = merge_tiles(
         panels, w_merge, ln_gain, w_kv, pack_small(prefix_cache, sources, page_tile)
     )
+    width = seq_count // lax.axis_size("tp")
+    small = small.reshape(seq_count, SMALL_ROWS, -1)
+
+    def place_of(index):
+        group = (index // width) ^ (holder // width)
+        return group * width + (index - holder) % width
+
     prefix_rows = prefix_cache.shape[1]
     prefixes = small[:, :prefix_rows]
-    asked_sources = small[:, prefix_rows, :page_count].astype(jnp.int32)
-    asked_tiles = small[:, prefix_rows + 1, :page_count].astype(jnp.int32)
+    place = place_of(jnp.arange(seq_count, dtype=jnp.int32))
+    asked_sources = small[:, prefix_rows, :page_count].astype(jnp.int32)[place]
+    asked_tiles = small[:, prefix_rows + 1, :page_count].astype(jnp.int32)[place]
     asked = (asked_sources == holder).astype(jnp.int32)
     order = jnp.cumsum(asked, axis=1) - 1
     slots = jnp.arange(capacity, dtype=jnp.int32)
     picked = asked[:, None, :] * (order[:, None, :] == slots[None, :, None]).astype(jnp.int32)
     wanted = jnp.sum(picked * asked_tiles[:, None, :], axis=2)
-    wanted = wanted[jnp.arange(seq_count, dtype=jnp.int32) ^ holder]
     within = jnp.arange(panel_rows, dtype=jnp.int32)
     wanted_rows = (wanted.reshape(-1, 1) * panel_rows + within[None, :]).reshape(-1)
     chooser = wanted_rows[:, None] == jnp.arange(tile_count * panel_rows, dtype=jnp.int32)[None, :]
@@ -400,7 +445,7 @@
     outgoing = jnp.dot(chooser, tile_kv, preferred_element_type=jnp.float32).astype(jnp.bfloat16)
     pages = lax.all_to_all(outgoing, "seq", split_axis=0, concat_axis=0, tiled=True)
     attended, vision_kv = attend(
-        prefix_id ^ holder, queries, prefixes, text_kv, pages, picks, seen, all_rows
+        place_of(prefix_id), queries, prefixes, text_kv, pages, picks, seen, all_rows
     )
     return (attended, vision_kv)
 

time: 204 us -> 222 us (1.088)
  local copies, waits for them, and re-layouts: 16.2 us -> 26.7 us
  starting transfers between devices: 76.2 us -> 65.9 us
  other arithmetic: 10.4 us -> 18.7 us
  matrix products: 4.51 us -> 11.9 us
  waiting for transfers between devices: 69.3 us -> 74.6 us
  Pallas kernels: 24.5 us -> 20.5 us
    unnamed x61 -> x99, local copies, waits for them, and re-layouts: 4.41 us -> 12.5 us
    dot_general x8 -> x5, matrix products: 3.53 us -> 11 us  [merge_tiles(): kv = kv + jnp.dot(gained, w_kv[at], preferred_element_type=jnp.float32)]
    ppermute x14 -> x11, starting transfers between devices: 25.3 us -> 17.9 us  [flip(): return lax.ppermute(value, axis, [(i, i ^ bit) for i in range(count)])]
    ppermute x2, waiting for transfers between devices: 0.54 us -> 6.39 us  [transpose_panels(): held = [lax.ppermute(local, ('seq', 'tp'), pairs)]]
    pallas_call x9 -> x6, Pallas kernels: 19 us -> 15 us  [the longest x5 14.2 us: partial_products(): pl.pallas_call(partial_kernel, grid=(count // tile,), in_specs=[pl.BlockS...]
    reduce_sum x7 -> x5, other arithmetic: 1.13 us -> 3.88 us  [merge_tiles(): squares = squares + jnp.sum(merged * merged, axis=1)]
    ppermute x14 -> x11, waiting for transfers between devices: 15.8 us -> 13.4 us  [flip(): return lax.ppermute(value, axis, [(i, i ^ bit) for i in range(count)])]
    ppermute x25 -> x17, waiting for transfers between devices: 42.5 us -> 44.4 us  [the longest x5 27.7 us: reduce_groups(): inward = lax.ppermute(message, 'seq', along(ENDS_IN))]
  transfers between devices with their start and end apart: 43 -> 32, of which waited for: 14 -> 13; matrix products, arithmetic and copies ran while one was open for 10% -> 17% of each run, Pallas kernels for 9% -> 7%
where the time goes in v6:
time: 222 us; the launch traced here: 220 us
  waiting for transfers between devices  74.6 us (34%)
  starting transfers between devices  65.9 us (30%)
  local copies, waits for them, and re-layouts  26.7 us (12%)
  Pallas kernels  20.5 us (9%)
  other arithmetic  18.7 us (8%)
  matrix products  11.9 us (5%)
    ppermute x5, waiting for transfers between devices, reduce_groups(): inward = lax.ppermute(message, 'seq', along(ENDS_IN))  27.7 us
    ppermute x5, starting transfers between devices, reduce_groups(): inward = lax.ppermute(message, 'seq', along(ENDS_IN))  25.2 us
    ppermute x11, starting transfers between devices, flip(): return lax.ppermute(value, axis, [(i, i ^ bit) for i in range(count)])  17.9 us
    ppermute x10, waiting for transfers between devices, send(): return lax.ppermute(value, 'seq', along(pairs))  16.8 us
    pallas_call x5, Pallas kernels, partial_products(): pl.pallas_call(partial_kernel, grid=(count // tile,), in_specs=[pl.BlockS...  14.2 us
    ppermute x11, waiting for transfers between devices, flip(): return lax.ppermute(value, axis, [(i, i ^ bit) for i in range(count)])  13.4 us
    unnamed x99, local copies, waits for them, and re-layouts  12.5 us
    dot_general x5, matrix products, merge_tiles(): kv = kv + jnp.dot(gained, w_kv[at], preferred_element_type=jnp.float32)  11 us
  transfers between devices with their start and end apart: 32, of which 13 were waited for; matrix products, arithmetic and copies ran while one was open for 17% of the time, Pallas kernels for 7%

profile of v6, /device:TPU:0, one launch (start us, length us, event | category | flops | bytes accessed | tf_op | source)
XLA Modules:
  0.0 219.9 jit_solution(4724276604286801968)
XLA Ops:
  0.6 1.1 slice_bitcast_fusion.4
  1.7 3.0 %collective-permute-start.2 = (bf16[128,1280]{1,0:T(8,128)(2,1)S(1)}, bf16[128,1280]{1,0:T(8,128)(2,1)S(1)}, u32[]{:S(2)}, u32[]{:S(2)}) collective-permute-start(bf16[128,1280]{1,0:T(8,128)(2,1)S(1)} %get-tuple-element.43), channel_id=1, source_target_pairs={{0,2},{1,3},{2,0},{3,1},{4,6},{5,7},{6,4},{7,5},{8,10},{9,11},{10,... | collective-permute-start | bytes 983048 | tf_op jit(solution)/shard_map/ppermute | solution.py:23
  5.5 0.9 convert_reduce_fusion
  8.5 3.0 %fusion.69 = (bf16[640,1024]{1,0:T(8,128)(2,1)}, bf16[640,1024]{1,0:T(8,128)(2,1)S(1)}) fusion(bf16[640,2048]{1,0:T(8,128)(2,1)} %refs_0_.9), kind=kLoop, calls=%fused_computation.165 | loop fusion | bytes 5242880 | tf_op jit(solution)/shard_map/slice | solution.py:194
  11.6 1.2 pad_maximum_fusion.1
  12.8 1.5 collective-permute-start
  15.4 3.3 %collective-permute-done.2 = bf16[128,1280]{1,0:T(8,128)(2,1)S(1)} collective-permute-done((bf16[128,1280]{1,0:T(8,128)(2,1)S(1)}, bf16[128,1280]{1,0:T(8,128)(2,1)S(1)}, u32[]{:S(2)}, u32[]{:S(2)}) %collective-permute-start.2) | collective-permute-done | bytes 327712 | tf_op jit(solution)/shard_map/ppermute | solution.py:23
  18.8 2.4 %collective-permute-start.3 = (bf16[128,1280]{1,0:T(8,128)(2,1)S(1)}, bf16[128,1280]{1,0:T(8,128)(2,1)S(1)}, u32[]{:S(2)}, u32[]{:S(2)}) collective-permute-start(bf16[128,1280]{1,0:T(8,128)(2,1)S(1)} %collective-permute-done.2), channel_id=1, source_target_pairs={{2,0},{3,10},{0,16},{1,26},{6,4},{7,14},{4,20},{5,30},{10,2},{11,8... | collective-permute-start | bytes 983048 | tf_op jit(solution)/shard_map/ppermute | solution.py:37
  21.8 2.1 collective-permute-start.4
  23.9 6.4 %collective-permute-done.3.refs_1_ = bf16[128,1280]{1,0:T(8,128)(2,1)S(1)} collective-permute-done((bf16[128,1280]{1,0:T(8,128)(2,1)S(1)}, bf16[128,1280]{1,0:T(8,128)(2,1)S(1)}, u32[]{:S(2)}, u32[]{:S(2)}) %collective-permute-start.3) | collective-permute-done | bytes 327712 | tf_op jit(solution)/shard_map/ppermute | solution.py:37
  30.3 5.3 %collective-permute-start.5 = (bf16[128,1280]{1,0:T(8,128)(2,1)S(1)}, bf16[128,1280]{1,0:T(8,128)(2,1)S(1)}, u32[]{:S(2)}, u32[]{:S(2)}) collective-permute-start(bf16[128,1280]{1,0:T(8,128)(2,1)S(1)} %collective-permute-done.3.refs_1_), channel_id=1, source_target_pairs={{0,2},{1,3},{2,0},{3,1},{4,6},{5,7},{6,4},{7,5},{8,10},{9,11},{10,... | collective-permute-start | bytes 983048 | tf_op jit(solution)/shard_map/ppermute | solution.py:23
  38.0 2.6 %collective-permute-start.6 = (bf16[128,1280]{1,0:T(8,128)(2,1)S(1)}, bf16[128,1280]{1,0:T(8,128)(2,1)S(1)}, u32[]{:S(2)}, u32[]{:S(2)}) collective-permute-start(bf16[128,1280]{1,0:T(8,128)(2,1)S(1)} %collective-permute-done.1.refs_0_), channel_id=1, source_target_pairs={{0,1},{1,0},{2,3},{3,2},{4,5},{5,4},{6,7},{7,6},{8,9},{9,8},{10,11... | collective-permute-start | bytes 983048 | tf_op jit(solution)/shard_map/ppermute | solution.py:23
  41.1 2.7 %collective-permute-done.5.refs_3_ = bf16[128,1280]{1,0:T(8,128)(2,1)S(1)} collective-permute-done((bf16[128,1280]{1,0:T(8,128)(2,1)S(1)}, bf16[128,1280]{1,0:T(8,128)(2,1)S(1)}, u32[]{:S(2)}, u32[]{:S(2)}) %collective-permute-start.5) | collective-permute-done | bytes 327712 | tf_op jit(solution)/shard_map/ppermute | solution.py:23
  43.8 1.8 collective-permute-start.9
  47.2 1.5 collective-permute-start.16
  50.9 1.0 copy-done.7
  51.8 1.0 copy-done.9
  52.8 1.0 copy-done.11
  53.8 1.0 copy-done.13
  54.8 1.0 copy-done.15
  55.7 1.0 copy-done.17
  58.3 3.2 %shard_map.132 = (bf16[512,512]{1,0:T(8,128)(2,1)S(1)}, bf16[512,512]{1,0:T(8,128)(2,1)S(1)}) custom-call(bf16[1024,1280]{1,0:T(8,128)(2,1)S(1)} %shard_map.131.rows_ref, bf16[640,2048]{1,0:T(8,128)(2,1)} %refs_0_.9, bf16[656,1024]{1,0:T(8,128)(2,1)} %collective-permute-done.refs_1_), custom_call_target="tpu_custom_call" | custom-call | flops 1342177280 | bytes 4980736 | tf_op jit(solution)/shard_map/pallas_call | solution.py:117
  61.5 0.9 constant_dynamic-update-slice_fusion.1
  63.1 3.8 %shard_map.133 = (bf16[512,512]{1,0:T(8,128)(2,1)}, bf16[512,512]{1,0:T(8,128)(2,1)S(1)}) custom-call(bf16[1024,1280]{1,0:T(8,128)(2,1)S(1)} %shard_map.131.rows_ref, bf16[640,2048]{1,0:T(8,128)(2,1)} %refs_0_.9, bf16[656,1024]{1,0:T(8,128)(2,1)} %collective-permute-done.refs_1_), custom_call_target="tpu_custom_call" | custom-call | flops 1342177280 | bytes 4980736 | tf_op jit(solution)/shard_map/pallas_call | solution.py:117
  67.7 3.7 %collective-permute-start.13 = (bf16[512,512]{1,0:T(8,128)(2,1)}, bf16[512,512]{1,0:T(8,128)(2,1)}, u32[]{:S(2)}, u32[]{:S(2)}) collective-permute-start(bf16[512,512]{1,0:T(8,128)(2,1)} %get-tuple-element.21), channel_id=1, source_target_pairs={{0,8},{4,12},{24,16},{28,20},{1,9},{5,13},{25,17},{29,21},{2,10},{... | collective-permute-start | bytes 1572872 | tf_op jit(solution)/shard_map/ppermute | solution.py:160
  71.9 2.1 collective-permute-start.10
  75.3 7.8 %collective-permute-done.13 = bf16[512,512]{1,0:T(8,128)(2,1)} collective-permute-done((bf16[512,512]{1,0:T(8,128)(2,1)}, bf16[512,512]{1,0:T(8,128)(2,1)}, u32[]{:S(2)}, u32[]{:S(2)}) %collective-permute-start.13) | collective-permute-done | bytes 524320 | tf_op jit(solution)/shard_map/ppermute | solution.py:160
  83.1 1.3 add_convert_fusion.1
  85.2 9.9 %collective-permute-done.10 = bf16[576,512]{1,0:T(8,128)(2,1)} collective-permute-done((bf16[576,512]{1,0:T(8,128)(2,1)}, bf16[576,512]{1,0:T(8,128)(2,1)}, u32[]{:S(2)}, u32[]{:S(2)}) %collective-permute-start.10) | collective-permute-done | bytes 589856 | tf_op jit(solution)/shard_map/ppermute | solution.py:160
  95.1 3.1 %shard_map.134 = (bf16[512,512]{1,0:T(8,128)(2,1)S(1)}, bf16[512,512]{1,0:T(8,128)(2,1)S(1)}) custom-call(bf16[1024,1280]{1,0:T(8,128)(2,1)S(1)} %shard_map.131.rows_ref, bf16[640,2048]{1,0:T(8,128)(2,1)} %refs_0_.9, bf16[640,1024]{1,0:T(8,128)(2,1)} %collective-permute-done.16.refs_1_), custom_call_target="tpu_custom_call" | custom-call | flops 1342177280 | bytes 4980736 | tf_op jit(solution)/shard_map/pallas_call | solution.py:117
  98.2 4.5 %collective-permute-start.17 = (bf16[512,512]{1,0:T(8,128)(2,1)S(1)}, bf16[512,512]{1,0:T(8,128)(2,1)S(1)}, u32[]{:S(2)}, u32[]{:S(2)}) collective-permute-start(bf16[512,512]{1,0:T(8,128)(2,1)S(1)} %get-tuple-element.25), channel_id=1, source_target_pairs={{0,8},{4,12},{24,16},{28,20},{1,9},{5,13},{25,17},{29,21},{2,10},{... | collective-permute-start | bytes 1572872 | tf_op jit(solution)/shard_map/ppermute | solution.py:160
  102.8 2.1 shard_map.135
  104.9 1.4 collective-permute-start.20
  107.2 1.2 add_convert_fusion.2
  109.1 10.0 %collective-permute-done.20 = bf16[512,256]{1,0:T(8,128)(2,1)S(1)} collective-permute-done((bf16[512,256]{1,0:T(8,128)(2,1)S(1)}, bf16[512,256]{1,0:T(8,128)(2,1)S(1)}, u32[]{:S(2)}, u32[]{:S(2)}) %collective-permute-start.20) | collective-permute-done | bytes 262176 | tf_op jit(solution)/shard_map/ppermute | solution.py:160
  120.0 1.3 collective-permute-start.15
  121.4 1.3 collective-permute-start.22
  123.6 2.1 shard_map.136
  125.6 13.4 %collective-permute-start.23 = (bf16[512,256]{1,0:T(8,128)(2,1)S(1)}, bf16[512,256]{1,0:T(8,128)(2,1)S(1)}, u32[]{:S(2)}, u32[]{:S(2)}) collective-permute-start(bf16[512,256]{1,0:T(8,128)(2,1)S(1)} %get-tuple-element.31), channel_id=1, source_target_pairs={{0,8},{4,12},{24,16},{28,20},{1,9},{5,13},{25,17},{29,21},{2,10},{... | collective-permute-start | bytes 786440 | tf_op jit(solution)/shard_map/ppermute | solution.py:160
  139.3 1.3 collective-permute-start.12
  142.0 1.5 fusion.32
  144.2 3.3 %fusion.14 = f32[512,1024]{1,0:T(8,128)} fusion(bf16[2048,1024]{1,0:T(8,128)(2,1)} %param.15, f32[512]{0:T(512)S(1)} %get-tuple-element.49, bf16[512,512]{1,0:T(8,128)(2,1)S(1)} %copy-done.3, bf16[512,512]{1,0:T(8,128)(2,1)S(1)} %collective-permute-done.15), kind=kOutput, calls=%fused_computation.37 | convolution fusion | flops 538705920 | bytes 4196352 | tf_op jit(solution)/shard_map/dot_general | solution.py:249
  148.5 1.3 collective-permute-start.25
  149.8 0.9 fusion.8
  150.7 1.5 collective-permute-start.19
  152.2 13.7 %collective-permute-done.25 = bf16[512,256]{1,0:T(8,128)(2,1)S(1)} collective-permute-done((bf16[512,256]{1,0:T(8,128)(2,1)S(1)}, bf16[512,256]{1,0:T(8,128)(2,1)S(1)}, u32[]{:S(2)}, u32[]{:S(2)}) %collective-permute-start.25) | collective-permute-done | bytes 262176 | tf_op jit(solution)/shard_map/ppermute | solution.py:153
  167.5 0.9 fusion.49
  169.9 2.2 fusion.16
  172.1 2.4 %collective-permute-done.19 = bf16[512,512]{1,0:T(8,128)(2,1)} collective-permute-done((bf16[512,512]{1,0:T(8,128)(2,1)}, bf16[512,512]{1,0:T(8,128)(2,1)}, u32[]{:S(2)}, u32[]{:S(2)}) %collective-permute-start.19) | collective-permute-done | bytes 524320 | tf_op jit(solution)/shard_map/ppermute | solution.py:153
  174.5 2.3 %fusion.12 = f32[512,1024]{1,0:T(8,128)S(1)} fusion(bf16[2048,1024]{1,0:T(8,128)(2,1)} %param.15, f32[512]{0:T(512)S(1)} %copy-done.36, bf16[512,512]{1,0:T(8,128)(2,1)S(1)} %copy-done.1, bf16[512,512]{1,0:T(8,128)(2,1)} %collective-permute-done.19), kind=kOutput, calls=%fused_computation.34 | convolution fusion | flops 538705920 | bytes 4196352 | tf_op jit(solution)/shard_map/dot_general | solution.py:249
  176.9 1.7 add_add_fusion
  179.0 0.9 fusion.26
  180.8 1.3 fusion.11
  184.1 1.2 bitcast_add_fusion
  185.3 1.0 copy-done.22
  186.3 1.5 collective-permute-start.27
  187.9 6.7 %collective-permute-done.27 = bf16[1,512,256]{2,1,0:T(8,128)(2,1)S(1)} collective-permute-done((bf16[1,512,256]{2,1,0:T(8,128)(2,1)S(1)}, bf16[1,512,256]{2,1,0:T(8,128)(2,1)S(1)}, u32[]{:S(2)}, u32[]{:S(2)}) %collective-permute-start.27) | collective-permute-done | bytes 262176 | tf_op jit(solution)/shard_map/ppermute | solution.py:23
  194.7 1.2 fusion.30
  195.9 1.5 collective-permute-start.30
  197.5 2.3 %collective-permute-done.30 = bf16[256,256]{1,0:T(8,128)(2,1)S(1)} collective-permute-done((bf16[256,256]{1,0:T(8,128)(2,1)S(1)}, bf16[256,256]{1,0:T(8,128)(2,1)S(1)}, u32[]{:S(2)}, u32[]{:S(2)}) %collective-permute-start.30) | collective-permute-done | bytes 131104 | tf_op jit(solution)/shard_map/ppermute | solution.py:258
  199.8 1.0 convolution_convert_fusion
  200.8 5.3 %all-to-all-start = ((bf16[8,64,256]{2,1,0:T(8,128)(2,1)}), bf16[8,64,256]{2,1,0:T(8,128)(2,1)S(1)}, u32[]{:S(2)}, u32[]{:S(2)}) async-start(bf16[8,64,256]{2,1,0:T(8,128)(2,1)} %bitcast.21), calls=%async_computation | async-start | bytes 524288 | tf_op jit(solution)/shard_map/all_to_all | solution.py:446
  206.3 8.0 %all-to-all-done = bf16[8,64,256]{2,1,0:T(8,128)(2,1)S(1)} async-done(((bf16[8,64,256]{2,1,0:T(8,128)(2,1)}), bf16[8,64,256]{2,1,0:T(8,128)(2,1)S(1)}, u32[]{:S(2)}, u32[]{:S(2)}) %all-to-all-start) | async-done | bytes 262176 | tf_op jit(solution)/shard_map/all_to_all | solution.py:446
  214.4 5.5 %shard_map.137 = (bf16[4,128,1024]{2,1,0:T(8,128)(2,1)}, bf16[256,256]{1,0:T(8,128)(2,1)}) custom-call(s32[4]{0:T(128)S(1)} %fusion.59.place_ref, bf16[4,128,1024]{2,1,0:T(8,128)(2,1)S(1)} %copy-done.18, bf16[8,32,256]{2,1,0:T(8,128)(2,1)S(1)} %slice.144.prefix_ref, bf16[4,128,256]{2,1,0:T(8,128)(2,1)S(1)} %copy-done.19, bf16[512,256]{1,0:T(8,128)(2,1)S(1)} %bitcast.59, ...), custom_call_target="tpu_custom_call" | custom-call | flops 603979776 | bytes 4194304 | tf_op jit(solution)/shard_map/pallas_call | solution.py:342
  (207 shorter events, 30.4 us)
Async XLA Ops:
  1.7 17.0 %collective-permute-start.2 = (bf16[128,1280]{1,0:T(8,128)(2,1)S(1)}, bf16[128,1280]{1,0:T(8,128)(2,1)S(1)}, u32[]{:S(2)}, u32[]{:S(2)}) collective-permute-start(bf16[128,1280]{1,0:T(8,128)(2,1)S(1)} %get-tuple-element.43), channel_id=1, source_target_pairs={{0,2},{1,3},{2,0},{3,1},{4,6},{5,7},{6,4},{7,5},{8,10},{9,11},{10,... | collective-permute-start | bytes 983048 | tf_op jit(solution)/shard_map/ppermute | solution.py:23
  4.8 17.0 %collective-permute-start.1 = (bf16[128,1280]{1,0:T(8,128)(2,1)S(1)}, bf16[128,1280]{1,0:T(8,128)(2,1)S(1)}, u32[]{:S(2)}, u32[]{:S(2)}) collective-permute-start(bf16[128,1280]{1,0:T(8,128)(2,1)S(1)} %get-tuple-element.44), channel_id=1, source_target_pairs={{0,0},{1,10},{2,16},{3,26},{4,4},{5,14},{6,20},{7,30},{8,2},{9,8},... | collective-permute-start | bytes 983048 | tf_op jit(solution)/shard_map/ppermute | solution.py:37
  11.6 2.7 %copy-start.48 = (s32[1,4]{1,0:T(1,128)S(1)}, s32[1,4]{1,0:T(1,128)}, u32[]{:S(2)}) copy-start(s32[1,4]{1,0:T(1,128)} %param.18) | copy-start | bytes 52
  11.6 3.1 %copy-start.46 = (s32[32,1]{0,1:T(1,128)S(1)}, s32[32,1]{0,1:T(1,128)}, u32[]{:S(2)}) copy-start(s32[32,1]{0,1:T(1,128)} %param.16) | copy-start | bytes 388
  12.8 33.0 %copy-start.20 = (s32[4]{0:T(128)S(1)}, s32[4]{0:T(128)}, u32[]{:S(2)}) copy-start(s32[4]{0:T(128)} %constant.165.clone) | copy-start | bytes 52
  12.8 44.7 %collective-permute-start = (bf16[656,1024]{1,0:T(8,128)(2,1)}, bf16[656,1024]{1,0:T(8,128)(2,1)}, u32[]{:S(2)}, u32[]{:S(2)}) collective-permute-start(bf16[656,1024]{1,0:T(8,128)(2,1)} %pad_maximum_fusion.1), channel_id=1, source_target_pairs={{4,0},{0,4},{12,8},{8,12},{20,16},{16,20},{28,24},{24,28},{5,1},{1... | collective-permute-start | bytes 4030472 | tf_op jit(solution)/shard_map/ppermute | solution.py:206
  18.8 11.5 %collective-permute-start.3 = (bf16[128,1280]{1,0:T(8,128)(2,1)S(1)}, bf16[128,1280]{1,0:T(8,128)(2,1)S(1)}, u32[]{:S(2)}, u32[]{:S(2)}) collective-permute-start(bf16[128,1280]{1,0:T(8,128)(2,1)S(1)} %collective-permute-done.2), channel_id=1, source_target_pairs={{2,0},{3,10},{0,16},{1,26},{6,4},{7,14},{4,20},{5,30},{10,2},{11,8... | collective-permute-start | bytes 983048 | tf_op jit(solution)/shard_map/ppermute | solution.py:37
  21.4 24.2 %copy-start.41 = (s32[128]{0:T(128)}, s32[128]{0:T(128)S(1)}, u32[]{:S(2)}) copy-start(s32[128]{0:T(128)S(1)} %add.365) | copy-start | bytes 1540
  21.8 18.8 %collective-permute-start.4 = (bf16[128,1280]{1,0:T(8,128)(2,1)S(1)}, bf16[128,1280]{1,0:T(8,128)(2,1)S(1)}, u32[]{:S(2)}, u32[]{:S(2)}) collective-permute-start(bf16[128,1280]{1,0:T(8,128)(2,1)S(1)} %collective-permute-done.1.refs_0_), channel_id=1, source_target_pairs={{0,2},{1,3},{2,0},{3,1},{4,6},{5,7},{6,4},{7,5},{8,10},{9,11},{10,... | collective-permute-start | bytes 983048 | tf_op jit(solution)/shard_map/ppermute | solution.py:23
  30.3 13.5 %collective-permute-start.5 = (bf16[128,1280]{1,0:T(8,128)(2,1)S(1)}, bf16[128,1280]{1,0:T(8,128)(2,1)S(1)}, u32[]{:S(2)}, u32[]{:S(2)}) collective-permute-start(bf16[128,1280]{1,0:T(8,128)(2,1)S(1)} %collective-permute-done.3.refs_1_), channel_id=1, source_target_pairs={{0,2},{1,3},{2,0},{3,1},{4,6},{5,7},{6,4},{7,5},{8,10},{9,11},{10,... | collective-permute-start | bytes 983048 | tf_op jit(solution)/shard_map/ppermute | solution.py:23
  38.0 8.5 %collective-permute-start.6 = (bf16[128,1280]{1,0:T(8,128)(2,1)S(1)}, bf16[128,1280]{1,0:T(8,128)(2,1)S(1)}, u32[]{:S(2)}, u32[]{:S(2)}) collective-permute-start(bf16[128,1280]{1,0:T(8,128)(2,1)S(1)} %collective-permute-done.1.refs_0_), channel_id=1, source_target_pairs={{0,1},{1,0},{2,3},{3,2},{4,5},{5,4},{6,7},{7,6},{8,9},{9,8},{10,11... | collective-permute-start | bytes 983048 | tf_op jit(solution)/shard_map/ppermute | solution.py:23
  40.6 8.1 %collective-permute-start.7 = (bf16[128,1280]{1,0:T(8,128)(2,1)S(1)}, bf16[128,1280]{1,0:T(8,128)(2,1)S(1)}, u32[]{:S(2)}, u32[]{:S(2)}) collective-permute-start(bf16[128,1280]{1,0:T(8,128)(2,1)S(1)} %collective-permute-done.3.refs_1_), channel_id=1, source_target_pairs={{0,1},{1,0},{2,3},{3,2},{4,5},{5,4},{6,7},{7,6},{8,9},{9,8},{10,11... | collective-permute-start | bytes 983048 | tf_op jit(solution)/shard_map/ppermute | solution.py:23
  40.6 8.8 %copy-start.6 = (bf16[128,1280]{1,0:T(8,128)(2,1)}, bf16[128,1280]{1,0:T(8,128)(2,1)S(1)}, u32[]{:S(2)}) copy-start(bf16[128,1280]{1,0:T(8,128)(2,1)S(1)} %collective-permute-done.4.refs_2_) | copy-start | bytes 983044
  40.6 8.8 %collective-permute-start.8 = (bf16[128,1280]{1,0:T(8,128)(2,1)S(1)}, bf16[128,1280]{1,0:T(8,128)(2,1)S(1)}, u32[]{:S(2)}, u32[]{:S(2)}) collective-permute-start(bf16[128,1280]{1,0:T(8,128)(2,1)S(1)} %collective-permute-done.4.refs_2_), channel_id=1, source_target_pairs={{0,1},{1,0},{2,3},{3,2},{4,5},{5,4},{6,7},{7,6},{8,9},{9,8},{10,11... | collective-permute-start | bytes 983048 | tf_op jit(solution)/shard_map/ppermute | solution.py:23
  43.8 5.6 %copy-start.8 = (bf16[128,1280]{1,0:T(8,128)(2,1)}, bf16[128,1280]{1,0:T(8,128)(2,1)S(1)}, u32[]{:S(2)}) copy-start(bf16[128,1280]{1,0:T(8,128)(2,1)S(1)} %collective-permute-done.5.refs_3_) | copy-start | bytes 983044
  43.8 6.3 %collective-permute-start.9 = (bf16[128,1280]{1,0:T(8,128)(2,1)S(1)}, bf16[128,1280]{1,0:T(8,128)(2,1)S(1)}, u32[]{:S(2)}, u32[]{:S(2)}) collective-permute-start(bf16[128,1280]{1,0:T(8,128)(2,1)S(1)} %collective-permute-done.5.refs_3_), channel_id=1, source_target_pairs={{0,1},{1,0},{2,3},{3,2},{4,5},{5,4},{6,7},{7,6},{8,9},{9,8},{10,11... | collective-permute-start | bytes 983048 | tf_op jit(solution)/shard_map/ppermute | solution.py:23
  47.2 47.9 %collective-permute-start.16 = (bf16[640,1024]{1,0:T(8,128)(2,1)}, bf16[640,1024]{1,0:T(8,128)(2,1)}, u32[]{:S(2)}, u32[]{:S(2)}) collective-permute-start(bf16[640,1024]{1,0:T(8,128)(2,1)} %get-tuple-element.23), channel_id=1, source_target_pairs={{4,0},{0,4},{12,8},{8,12},{20,16},{16,20},{28,24},{24,28},{5,1},{1... | collective-permute-start | bytes 3932168 | tf_op jit(solution)/shard_map/ppermute | solution.py:206
  58.3 4.1 %copy-start.27 = (bf16[64,512]{1,0:T(8,128)(2,1)}, bf16[64,512]{1,0:T(8,128)(2,1)S(1)}, u32[]{:S(2)}) copy-start(bf16[64,512]{1,0:T(8,128)(2,1)S(1)} %reshape.362) | copy-start | bytes 196612
  63.1 8.3 %copy-start.45 = (bf16[2048]{0:T(1024)(128)(2,1)S(1)}, bf16[2048]{0:T(1024)(128)(2,1)}, u32[]{:S(2)}) copy-start(bf16[2048]{0:T(1024)(128)(2,1)} %param.14) | copy-start | bytes 12292
  67.7 15.5 %collective-permute-start.13 = (bf16[512,512]{1,0:T(8,128)(2,1)}, bf16[512,512]{1,0:T(8,128)(2,1)}, u32[]{:S(2)}, u32[]{:S(2)}) collective-permute-start(bf16[512,512]{1,0:T(8,128)(2,1)} %get-tuple-element.21), channel_id=1, source_target_pairs={{0,8},{4,12},{24,16},{28,20},{1,9},{5,13},{25,17},{29,21},{2,10},{... | collective-permute-start | bytes 1572872 | tf_op jit(solution)/shard_map/ppermute | solution.py:160
  71.9 23.1 %collective-permute-start.10 = (bf16[576,512]{1,0:T(8,128)(2,1)}, bf16[576,512]{1,0:T(8,128)(2,1)}, u32[]{:S(2)}, u32[]{:S(2)}) collective-permute-start(bf16[576,512]{1,0:T(8,128)(2,1)} %constant_dynamic-update-slice_fusion), channel_id=1, source_target_pairs={{0,8},{4,12},{24,16},{28,20},{1,9},{5,13},{25,17},{29,21},{2,10},{... | collective-permute-start | bytes 1769480 | tf_op jit(solution)/shard_map/ppermute | solution.py:160
  74.1 94.5 %copy-start.40 = (s32[1024]{0:T(1024)}, s32[1024]{0:T(1024)S(1)}, u32[]{:S(2)}) copy-start(s32[1024]{0:T(1024)S(1)} %pad_clamp_fusion.1) | copy-start | bytes 12292
  84.5 35.4 %collective-permute-start.14 = (bf16[512,512]{1,0:T(8,128)(2,1)S(1)}, bf16[512,512]{1,0:T(8,128)(2,1)S(1)}, u32[]{:S(2)}, u32[]{:S(2)}) collective-permute-start(bf16[512,512]{1,0:T(8,128)(2,1)S(1)} %add_convert_fusion.1), channel_id=1, source_target_pairs={{8,16},{12,20},{16,8},{20,12},{9,17},{13,21},{17,9},{21,13},{10,18... | collective-permute-start | bytes 1572872 | tf_op jit(solution)/shard_map/ppermute | solution.py:153
  98.2 51.6 %copy-start = (bf16[512,512]{1,0:T(8,128)(2,1)}, bf16[512,512]{1,0:T(8,128)(2,1)S(1)}, u32[]{:S(2)}) copy-start(bf16[512,512]{1,0:T(8,128)(2,1)S(1)} %get-tuple-element.24) | copy-start | bytes 1572868
  98.2 9.0 %copy-start.5 = (bf16[512,512]{1,0:T(8,128)(2,1)S(1)}, bf16[512,512]{1,0:T(8,128)(2,1)}, u32[]{:S(2)}) copy-start(bf16[512,512]{1,0:T(8,128)(2,1)} %copy-done.4) | copy-start | bytes 1572868
  98.2 10.1 %copy-start.28 = (bf16[64,512]{1,0:T(8,128)(2,1)S(1)}, bf16[64,512]{1,0:T(8,128)(2,1)}, u32[]{:S(2)}) copy-start(bf16[64,512]{1,0:T(8,128)(2,1)} %copy-done.27) | copy-start | bytes 196612
  98.2 24.5 %collective-permute-start.17 = (bf16[512,512]{1,0:T(8,128)(2,1)S(1)}, bf16[512,512]{1,0:T(8,128)(2,1)S(1)}, u32[]{:S(2)}, u32[]{:S(2)}) collective-permute-start(bf16[512,512]{1,0:T(8,128)(2,1)S(1)} %get-tuple-element.25), channel_id=1, source_target_pairs={{0,8},{4,12},{24,16},{28,20},{1,9},{5,13},{25,17},{29,21},{2,10},{... | collective-permute-start | bytes 1572872 | tf_op jit(solution)/shard_map/ppermute | solution.py:160
  104.9 15.0 %copy-start.3 = (bf16[512,512]{1,0:T(8,128)(2,1)S(1)}, bf16[512,512]{1,0:T(8,128)(2,1)}, u32[]{:S(2)}) copy-start(bf16[512,512]{1,0:T(8,128)(2,1)} %copy-done.2) | copy-start | bytes 1572868
  104.9 14.2 %collective-permute-start.20 = (bf16[512,256]{1,0:T(8,128)(2,1)S(1)}, bf16[512,256]{1,0:T(8,128)(2,1)S(1)}, u32[]{:S(2)}, u32[]{:S(2)}) collective-permute-start(bf16[512,256]{1,0:T(8,128)(2,1)S(1)} %get-tuple-element.28), channel_id=1, source_target_pairs={{0,8},{4,12},{24,16},{28,20},{1,9},{5,13},{25,17},{29,21},{2,10},{... | collective-permute-start | bytes 786440 | tf_op jit(solution)/shard_map/ppermute | solution.py:160
  108.4 30.6 %collective-permute-start.11 = (bf16[640,512]{1,0:T(8,128)(2,1)S(1)}, bf16[640,512]{1,0:T(8,128)(2,1)S(1)}, u32[]{:S(2)}, u32[]{:S(2)}) collective-permute-start(bf16[640,512]{1,0:T(8,128)(2,1)S(1)} %pad_maximum_fusion.3), channel_id=1, source_target_pairs={{8,16},{12,20},{16,8},{20,12},{9,17},{13,21},{17,9},{21,13},{10,18... | collective-permute-start | bytes 1966088 | tf_op jit(solution)/shard_map/ppermute | solution.py:153
  119.2 2.2 collective-permute-start.21
  120.0 24.2 %collective-permute-start.15 = (bf16[512,512]{1,0:T(8,128)(2,1)S(1)}, bf16[512,512]{1,0:T(8,128)(2,1)S(1)}, u32[]{:S(2)}, u32[]{:S(2)}) collective-permute-start(bf16[512,512]{1,0:T(8,128)(2,1)S(1)} %fusion.4), channel_id=1, source_target_pairs={{16,24},{20,28},{8,0},{12,4},{17,25},{21,29},{9,1},{13,5},{18,26},... | collective-permute-start | bytes 1572872 | tf_op jit(solution)/shard_map/ppermute | solution.py:153
  121.4 19.8 %collective-permute-start.22 = (bf16[512,256]{1,0:T(8,128)(2,1)S(1)}, bf16[512,256]{1,0:T(8,128)(2,1)S(1)}, u32[]{:S(2)}, u32[]{:S(2)}) collective-permute-start(bf16[512,256]{1,0:T(8,128)(2,1)S(1)} %fusion.18), channel_id=1, source_target_pairs={{16,24},{20,28},{8,0},{12,4},{17,25},{21,29},{9,1},{13,5},{18,26},... | collective-permute-start | bytes 786440 | tf_op jit(solution)/shard_map/ppermute | solution.py:153
  122.9 26.9 %collective-permute-start.18 = (bf16[512,512]{1,0:T(8,128)(2,1)S(1)}, bf16[512,512]{1,0:T(8,128)(2,1)S(1)}, u32[]{:S(2)}, u32[]{:S(2)}) collective-permute-start(bf16[512,512]{1,0:T(8,128)(2,1)S(1)} %add_convert_fusion), channel_id=1, source_target_pairs={{8,16},{12,20},{16,8},{20,12},{9,17},{13,21},{17,9},{21,13},{10,18... | collective-permute-start | bytes 1572872 | tf_op jit(solution)/shard_map/ppermute | solution.py:153
  125.6 16.3 %copy-start.44 = (f32[256]{0:T(256)S(1)}, f32[256]{0:T(256)}, u32[]{:S(2)}) copy-start(f32[256]{0:T(256)} %get-tuple-element.48) | copy-start | bytes 3076
  125.6 17.8 %collective-permute-start.23 = (bf16[512,256]{1,0:T(8,128)(2,1)S(1)}, bf16[512,256]{1,0:T(8,128)(2,1)S(1)}, u32[]{:S(2)}, u32[]{:S(2)}) collective-permute-start(bf16[512,256]{1,0:T(8,128)(2,1)S(1)} %get-tuple-element.31), channel_id=1, source_target_pairs={{0,8},{4,12},{24,16},{28,20},{1,9},{5,13},{25,17},{29,21},{2,10},{... | collective-permute-start | bytes 786440 | tf_op jit(solution)/shard_map/ppermute | solution.py:160
  139.3 27.3 %collective-permute-start.12 = (bf16[704,512]{1,0:T(8,128)(2,1)S(1)}, bf16[704,512]{1,0:T(8,128)(2,1)S(1)}, u32[]{:S(2)}, u32[]{:S(2)}) collective-permute-start(bf16[704,512]{1,0:T(8,128)(2,1)S(1)} %pad_maximum_fusion.2), channel_id=1, source_target_pairs={{16,24},{20,28},{8,0},{12,4},{17,25},{21,29},{9,1},{13,5},{18,26},... | collective-permute-start | bytes 2162696 | tf_op jit(solution)/shard_map/ppermute | solution.py:153
  143.5 4.8 %collective-permute-start.24 = (bf16[512,256]{1,0:T(8,128)(2,1)S(1)}, bf16[512,256]{1,0:T(8,128)(2,1)S(1)}, u32[]{:S(2)}, u32[]{:S(2)}) collective-permute-start(bf16[512,256]{1,0:T(8,128)(2,1)S(1)} %add_convert_fusion.3), channel_id=1, source_target_pairs={{8,16},{12,20},{16,8},{20,12},{9,17},{13,21},{17,9},{21,13},{10,18... | collective-permute-start | bytes 786440 | tf_op jit(solution)/shard_map/ppermute | solution.py:153
  147.5 20.8 %copy-start.33 = (bf16[1,64,512]{2,1,0:T(8,128)(2,1)S(1)}, bf16[1,64,512]{2,1,0:T(8,128)(2,1)}, u32[]{:S(2)}) copy-start(bf16[1,64,512]{2,1,0:T(8,128)(2,1)} %stack_reshape.7) | copy-start | bytes 196612
  148.5 17.4 %collective-permute-start.25 = (bf16[512,256]{1,0:T(8,128)(2,1)S(1)}, bf16[512,256]{1,0:T(8,128)(2,1)S(1)}, u32[]{:S(2)}, u32[]{:S(2)}) collective-permute-start(bf16[512,256]{1,0:T(8,128)(2,1)S(1)} %fusion.22), channel_id=1, source_target_pairs={{16,24},{20,28},{8,0},{12,4},{17,25},{21,29},{9,1},{13,5},{18,26},... | collective-permute-start | bytes 786440 | tf_op jit(solution)/shard_map/ppermute | solution.py:153
  150.7 23.8 %collective-permute-start.19 = (bf16[512,512]{1,0:T(8,128)(2,1)}, bf16[512,512]{1,0:T(8,128)(2,1)}, u32[]{:S(2)}, u32[]{:S(2)}) collective-permute-start(bf16[512,512]{1,0:T(8,128)(2,1)} %fusion.8), channel_id=1, source_target_pairs={{16,24},{20,28},{8,0},{12,4},{17,25},{21,29},{9,1},{13,5},{18,26},... | collective-permute-start | bytes 1572872 | tf_op jit(solution)/shard_map/ppermute | solution.py:153
  165.9 2.5 %copy-start.25 = (bf16[512,256]{1,0:T(8,128)(2,1)}, bf16[512,256]{1,0:T(8,128)(2,1)S(1)}, u32[]{:S(2)}) copy-start(bf16[512,256]{1,0:T(8,128)(2,1)S(1)} %collective-permute-done.25) | copy-start | bytes 786436
  169.9 4.6 %copy-start.1 = (bf16[512,512]{1,0:T(8,128)(2,1)S(1)}, bf16[512,512]{1,0:T(8,128)(2,1)}, u32[]{:S(2)}) copy-start(bf16[512,512]{1,0:T(8,128)(2,1)} %copy-done) | copy-start | bytes 1572868
  169.9 4.6 %copy-start.36 = (f32[512]{0:T(512)S(1)}, f32[512]{0:T(512)}, u32[]{:S(2)}) copy-start(f32[512]{0:T(512)} %get-tuple-element.50) | copy-start | bytes 6148
  174.5 2.3 %copy-start.21 = (f32[512,1024]{1,0:T(8,128)S(1)}, f32[512,1024]{1,0:T(8,128)}, u32[]{:S(2)}) copy-start(f32[512,1024]{1,0:T(8,128)} %fusion.14) | copy-start | bytes 6291460
  174.5 2.3 %copy-start.26 = (bf16[512,256]{1,0:T(8,128)(2,1)S(1)}, bf16[512,256]{1,0:T(8,128)(2,1)}, u32[]{:S(2)}) copy-start(bf16[512,256]{1,0:T(8,128)(2,1)} %copy-done.25) | copy-start | bytes 786436
  174.5 2.3 %copy-start.43 = (f32[256]{0:T(256)S(1)}, f32[256]{0:T(256)}, u32[]{:S(2)}) copy-start(f32[256]{0:T(256)} %get-tuple-element.47) | copy-start | bytes 3076
  178.9 3.2 %copy-start.37 = (f32[512]{0:T(512)S(1)}, f32[512]{0:T(512)}, u32[]{:S(2)}) copy-start(f32[512]{0:T(512)} %fusion.21) | copy-start | bytes 6148
  178.9 3.2 %copy-start.38 = (f32[512]{0:T(512)S(1)}, f32[512]{0:T(512)}, u32[]{:S(2)}) copy-start(f32[512]{0:T(512)} %fusion.7) | copy-start | bytes 6148
  178.9 3.2 %copy-start.39 = (f32[512]{0:T(512)S(1)}, f32[512]{0:T(512)}, u32[]{:S(2)}) copy-start(f32[512]{0:T(512)} %fusion.25) | copy-start | bytes 6148
  178.9 3.7 %copy-start.35 = (s32[8,32]{1,0:T(8,128)S(1)}, s32[8,32]{1,0:T(8,128)}, u32[]{:S(2)}) copy-start(s32[8,32]{1,0:T(8,128)} %broadcast_add_fusion) | copy-start | bytes 3076
  179.8 4.3 %collective-permute-start.26 = (bf16[2,512,256]{2,1,0:T(8,128)(2,1)}, bf16[2,512,256]{2,1,0:T(8,128)(2,1)}, u32[]{:S(2)}, u32[]{:S(2)}) collective-permute-start(bf16[2,512,256]{2,1,0:T(8,128)(2,1)} %fusion.26), channel_id=1, source_target_pairs={{0,1},{1,0},{2,3},{3,2},{4,5},{5,4},{6,7},{7,6},{8,9},{9,8},{10,11... | collective-permute-start | bytes 1572872 | tf_op jit(solution)/shard_map/ppermute | solution.py:23
  182.1 1.3 collective-permute-start.28
  183.5 4.4 %collective-permute-start.29 = (f32[512]{0:T(512)S(1)}, f32[512]{0:T(512)S(1)}, u32[]{:S(2)}, u32[]{:S(2)}) collective-permute-start(f32[512]{0:T(512)S(1)} %add.353), channel_id=1, source_target_pairs={{0,2},{1,3},{2,0},{3,1},{4,6},{5,7},{6,4},{7,5},{8,10},{9,11},{10,... | collective-permute-start | bytes 6152 | tf_op jit(solution)/shard_map/ppermute | solution.py:23
  186.2 19.9 %copy-start.47 = (s32[4]{0:T(128)S(1)}, s32[4]{0:T(128)}, u32[]{:S(2)}) copy-start(s32[4]{0:T(128)} %param.19) | copy-start | bytes 52
  186.3 19.9 %copy-start.29 = (s32[4,128,1]{2,1,0:T(8,128)S(1)}, s32[4,128,1]{2,1,0:T(8,128)}, u32[]{:S(2)}) copy-start(s32[4,128,1]{2,1,0:T(8,128)} %add.377) | copy-start | bytes 6148
  186.3 19.9 %copy-start.32 = (pred[4,128,1]{2,1,0:T(8,128)(4,1)S(1)}, pred[4,128,1]{2,1,0:T(8,128)(4,1)}, u32[]{:S(2)}) copy-start(pred[4,128,1]{2,1,0:T(8,128)(4,1)} %broadcast_in_dim.28) | copy-start | bytes 1540
  186.3 19.9 %copy-start.42 = (s32[128]{0:T(128)S(1)}, s32[128]{0:T(128)}, u32[]{:S(2)}) copy-start(s32[128]{0:T(128)} %copy-done.41) | copy-start | bytes 1540
  186.3 20.0 %copy-start.31 = (bf16[8,64,256]{2,1,0:T(8,128)(2,1)S(1)}, bf16[8,64,256]{2,1,0:T(8,128)(2,1)}, u32[]{:S(2)}) copy-start(bf16[8,64,256]{2,1,0:T(8,128)(2,1)} %copy-done.30) | copy-start | bytes 786436
  186.3 28.1 %copy-start.18 = (bf16[4,128,1024]{2,1,0:T(8,128)(2,1)S(1)}, bf16[4,128,1024]{2,1,0:T(8,128)(2,1)}, u32[]{:S(2)}) copy-start(bf16[4,128,1024]{2,1,0:T(8,128)(2,1)} %query_ref.1) | copy-start | bytes 3145732
  186.3 28.1 %copy-start.19 = (bf16[4,128,256]{2,1,0:T(8,128)(2,1)S(1)}, bf16[4,128,256]{2,1,0:T(8,128)(2,1)}, u32[]{:S(2)}) copy-start(bf16[4,128,256]{2,1,0:T(8,128)(2,1)} %text_ref.1) | copy-start | bytes 786436
  186.3 8.3 %collective-permute-start.27 = (bf16[1,512,256]{2,1,0:T(8,128)(2,1)S(1)}, bf16[1,512,256]{2,1,0:T(8,128)(2,1)S(1)}, u32[]{:S(2)}, u32[]{:S(2)}) collective-permute-start(bf16[1,512,256]{2,1,0:T(8,128)(2,1)S(1)} %dynamic-slice_convert_fusion.1), channel_id=1, source_target_pairs={{0,2},{1,3},{2,0},{3,1},{4,6},{5,7},{6,4},{7,5},{8,10},{9,11},{10,... | collective-permute-start | bytes 786440 | tf_op jit(solution)/shard_map/ppermute | solution.py:23
  195.9 4.0 %collective-permute-start.30 = (bf16[256,256]{1,0:T(8,128)(2,1)S(1)}, bf16[256,256]{1,0:T(8,128)(2,1)S(1)}, u32[]{:S(2)}, u32[]{:S(2)}) collective-permute-start(bf16[256,256]{1,0:T(8,128)(2,1)S(1)} %slice.149), channel_id=1, source_target_pairs={{0,8},{4,12},{24,16},{28,20},{1,9},{5,13},{25,17},{29,21},{2,10},{... | collective-permute-start | bytes 393224 | tf_op jit(solution)/shard_map/ppermute | solution.py:258
  200.8 13.5 %all-to-all-start = ((bf16[8,64,256]{2,1,0:T(8,128)(2,1)}), bf16[8,64,256]{2,1,0:T(8,128)(2,1)S(1)}, u32[]{:S(2)}, u32[]{:S(2)}) async-start(bf16[8,64,256]{2,1,0:T(8,128)(2,1)} %bitcast.21), calls=%async_computation | async-start | bytes 524288 | tf_op jit(solution)/shard_map/all_to_all | solution.py:446
  (17 other events, 16.4 us)

commit v7 on v6

--- a/solution.py
+++ b/solution.py
@@ -11,7 +11,7 @@
 HD = 128
 GROUP = 8
 MOST_PAGES = 16
-VMEM = 48 * 1024 * 1024
+VMEM = 16 * 1024 * 1024
 
 
 def bits_of(count):
@@ -233,14 +233,14 @@
             operands = [(w_merge, share, first), (received[side][0], share, inside)]
         rows = held
         if step >= 1:
-            before = (message,) + tuple(inwards[step - 2 : step - 1] if step >= 2 else ())
+            before = inwards[step - 2] if step >= 2 else message
             rows, _ = lax.optimization_barrier((held, before))
-        riding = small.reshape(-1, count) if step == 0 else None
+        riding = small.reshape(-1, count) if step == 2 else None
         merged, message, inward, shared = reduce_groups(
             partial_products(rows, operands, count), is_end, riding
         )
         inwards.append(inward)
-        if step == 0:
+        if step == 2:
             everyone = jnp.stack(shared).reshape((4,) + small_shape)
         merged = merged.astype(jnp.float32)
         at = slice(first, first + count)

time: 222 us -> 208 us (0.937)
  local copies, waits for them, and re-layouts: 26.7 us -> 21.2 us
  starting transfers between devices: 65.9 us -> 63 us
  matrix products: 11.9 us -> 9.53 us
    ppermute x10, waiting for transfers between devices: 16.8 us -> 25.9 us  [send(): return lax.ppermute(value, 'seq', along(pairs))]
    ppermute x5, waiting for transfers between devices: 27.7 us -> 21.6 us  [reduce_groups(): inward = lax.ppermute(message, 'seq', along(ENDS_IN))]
    unnamed x99 -> x64, local copies, waits for them, and re-layouts: 12.5 us -> 7.31 us
    ppermute x11, waiting for transfers between devices: 13.4 us -> 9.97 us  [flip(): return lax.ppermute(value, axis, [(i, i ^ bit) for i in range(count)])]
    dot_general x5, matrix products: 11 us -> 8.54 us  [merge_tiles(): kv = kv + jnp.dot(gained, w_kv[at], preferred_element_type=jnp.float32)]
  transfers between devices with their start and end apart: 32 -> 32, of which waited for: 13 -> 15; matrix products, arithmetic and copies ran while one was open for 17% -> 15% of each run, Pallas kernels for 7% -> 8%
where the time goes in v7:
time: 208 us; the launch traced here: 207 us
  waiting for transfers between devices  73.2 us (35%)
  starting transfers between devices  63 us (30%)
  Pallas kernels  21.6 us (10%)
  local copies, waits for them, and re-layouts  21.2 us (10%)
  other arithmetic  17.2 us (8%)
  matrix products  9.53 us (5%)
    ppermute x10, waiting for transfers between devices, send(): return lax.ppermute(value, 'seq', along(pairs))  25.9 us
    ppermute x5, starting transfers between devices, reduce_groups(): inward = lax.ppermute(message, 'seq', along(ENDS_IN))  24.4 us
    ppermute x5, waiting for transfers between devices, reduce_groups(): inward = lax.ppermute(message, 'seq', along(ENDS_IN))  21.6 us
    ppermute x11, starting transfers between devices, flip(): return lax.ppermute(value, axis, [(i, i ^ bit) for i in range(count)])  16.2 us
    pallas_call x5, Pallas kernels, partial_products(): pl.pallas_call(partial_kernel, grid=(count // tile,), in_specs=[pl.BlockS...  14.2 us
    ppermute x10, starting transfers between devices, send(): return lax.ppermute(value, 'seq', along(pairs))  10.2 us
    ppermute x11, waiting for transfers between devices, flip(): return lax.ppermute(value, axis, [(i, i ^ bit) for i in range(count)])  9.97 us
    dot_general x5, matrix products, merge_tiles(): kv = kv + jnp.dot(gained, w_kv[at], preferred_element_type=jnp.float32)  8.54 us
  transfers between devices with their start and end apart: 32, of which 15 were waited for; matrix products, arithmetic and copies ran while one was open for 15% of the time, Pallas kernels for 8%

profile of v7, /device:TPU:0, one launch (start us, length us, event | category | flops | bytes accessed | tf_op | source)
XLA Modules:
  0.0 207.1 jit_solution(841547084612816687)
XLA Ops:
  0.6 1.1 slice_bitcast_fusion.4
  1.7 3.0 %collective-permute-start.2 = (bf16[128,1280]{1,0:T(8,128)(2,1)S(1)}, bf16[128,1280]{1,0:T(8,128)(2,1)S(1)}, u32[]{:S(2)}, u32[]{:S(2)}) collective-permute-start(bf16[128,1280]{1,0:T(8,128)(2,1)S(1)} %get-tuple-element.43), channel_id=1, source_target_pairs={{0,2},{1,3},{2,0},{3,1},{4,6},{5,7},{6,4},{7,5},{8,10},{9,11},{10,... | collective-permute-start | bytes 983048 | tf_op jit(solution)/shard_map/ppermute | solution.py:23
  5.5 0.9 convert_reduce_fusion
  8.5 3.0 %fusion.69 = (bf16[640,1024]{1,0:T(8,128)(2,1)}, bf16[640,1024]{1,0:T(8,128)(2,1)S(1)}) fusion(bf16[640,2048]{1,0:T(8,128)(2,1)} %refs_0_.9), kind=kLoop, calls=%fused_computation.164 | loop fusion | bytes 5242880 | tf_op jit(solution)/shard_map/slice | solution.py:194
  11.6 1.2 pad_maximum_fusion.1
  12.8 1.5 collective-permute-start
  16.2 2.6 %collective-permute-done.2 = bf16[128,1280]{1,0:T(8,128)(2,1)S(1)} collective-permute-done((bf16[128,1280]{1,0:T(8,128)(2,1)S(1)}, bf16[128,1280]{1,0:T(8,128)(2,1)S(1)}, u32[]{:S(2)}, u32[]{:S(2)}) %collective-permute-start.2) | collective-permute-done | bytes 327712 | tf_op jit(solution)/shard_map/ppermute | solution.py:23
  18.8 3.5 %collective-permute-start.3 = (bf16[128,1280]{1,0:T(8,128)(2,1)S(1)}, bf16[128,1280]{1,0:T(8,128)(2,1)S(1)}, u32[]{:S(2)}, u32[]{:S(2)}) collective-permute-start(bf16[128,1280]{1,0:T(8,128)(2,1)S(1)} %collective-permute-done.2), channel_id=1, source_target_pairs={{2,0},{3,10},{0,16},{1,26},{6,4},{7,14},{4,20},{5,30},{10,2},{11,8... | collective-permute-start | bytes 983048 | tf_op jit(solution)/shard_map/ppermute | solution.py:37
  22.4 1.2 collective-permute-start.6
  23.9 7.4 %collective-permute-done.3.refs_1_ = bf16[128,1280]{1,0:T(8,128)(2,1)S(1)} collective-permute-done((bf16[128,1280]{1,0:T(8,128)(2,1)S(1)}, bf16[128,1280]{1,0:T(8,128)(2,1)S(1)}, u32[]{:S(2)}, u32[]{:S(2)}) %collective-permute-start.3) | collective-permute-done | bytes 327712 | tf_op jit(solution)/shard_map/ppermute | solution.py:37
  31.3 4.2 %collective-permute-start.5 = (bf16[128,1280]{1,0:T(8,128)(2,1)S(1)}, bf16[128,1280]{1,0:T(8,128)(2,1)}, u32[]{:S(2)}, u32[]{:S(2)}) collective-permute-start(bf16[128,1280]{1,0:T(8,128)(2,1)S(1)} %collective-permute-done.3.refs_1_), channel_id=1, source_target_pairs={{0,2},{1,3},{2,0},{3,1},{4,6},{5,7},{6,4},{7,5},{8,10},{9,11},{10,... | collective-permute-start | bytes 983048 | tf_op jit(solution)/shard_map/ppermute | solution.py:23
  35.6 1.4 collective-permute-start.11
  38.4 0.8 add.377
  40.7 2.5 %collective-permute-start.7 = (bf16[128,1280]{1,0:T(8,128)(2,1)S(1)}, bf16[128,1280]{1,0:T(8,128)(2,1)S(1)}, u32[]{:S(2)}, u32[]{:S(2)}) collective-permute-start(bf16[128,1280]{1,0:T(8,128)(2,1)S(1)} %collective-permute-done.3.refs_1_), channel_id=1, source_target_pairs={{0,1},{1,0},{2,3},{3,2},{4,5},{5,4},{6,7},{7,6},{8,9},{9,8},{10,11... | collective-permute-start | bytes 983048 | tf_op jit(solution)/shard_map/ppermute | solution.py:23
  43.9 2.6 %collective-permute-start.9 = (bf16[128,1280]{1,0:T(8,128)(2,1)}, bf16[128,1280]{1,0:T(8,128)(2,1)S(1)}, u32[]{:S(2)}, u32[]{:S(2)}) collective-permute-start(bf16[128,1280]{1,0:T(8,128)(2,1)} %collective-permute-done.5.refs_3_), channel_id=1, source_target_pairs={{0,1},{1,0},{2,3},{3,2},{4,5},{5,4},{6,7},{7,6},{8,9},{9,8},{10,11... | collective-permute-start | bytes 983048 | tf_op jit(solution)/shard_map/ppermute | solution.py:23
  48.0 1.1 copy-done.8
  49.1 1.8 shard_map.131.rows_ref
  50.9 3.3 %shard_map.132 = (bf16[512,512]{1,0:T(8,128)(2,1)S(1)}, bf16[512,512]{1,0:T(8,128)(2,1)S(1)}) custom-call(bf16[1024,1280]{1,0:T(8,128)(2,1)S(1)} %shard_map.131.rows_ref, bf16[640,2048]{1,0:T(8,128)(2,1)S(1)} %copy-done, bf16[656,1024]{1,0:T(8,128)(2,1)} %collective-permute-done.refs_1_), custom_call_target="tpu_custom_call" | custom-call | flops 1342177280 | bytes 4980736 | tf_op jit(solution)/shard_map/pallas_call | solution.py:117
  54.3 0.8 copy-done.5
  55.1 3.7 %shard_map.134 = (bf16[512,512]{1,0:T(8,128)(2,1)}, bf16[512,512]{1,0:T(8,128)(2,1)S(1)}) custom-call(bf16[1024,1280]{1,0:T(8,128)(2,1)S(1)} %shard_map.131.rows_ref, bf16[640,2048]{1,0:T(8,128)(2,1)S(1)} %copy-done, bf16[656,1024]{1,0:T(8,128)(2,1)} %collective-permute-done.refs_1_), custom_call_target="tpu_custom_call" | custom-call | flops 1342177280 | bytes 4980736 | tf_op jit(solution)/shard_map/pallas_call | solution.py:117
  58.8 0.8 copy-done.3
  59.6 5.3 %collective-permute-start.17 = (bf16[512,512]{1,0:T(8,128)(2,1)}, bf16[512,512]{1,0:T(8,128)(2,1)}, u32[]{:S(2)}, u32[]{:S(2)}) collective-permute-start(bf16[512,512]{1,0:T(8,128)(2,1)} %get-tuple-element.25), channel_id=1, source_target_pairs={{0,8},{4,12},{24,16},{28,20},{1,9},{5,13},{25,17},{29,21},{2,10},{... | collective-permute-start | bytes 1572872 | tf_op jit(solution)/shard_map/ppermute | solution.py:160
  64.8 1.4 slice_convert_fusion.5
  68.3 1.3 collective-permute-start.10
  69.6 7.0 %collective-permute-done.17 = bf16[512,512]{1,0:T(8,128)(2,1)} collective-permute-done((bf16[512,512]{1,0:T(8,128)(2,1)}, bf16[512,512]{1,0:T(8,128)(2,1)}, u32[]{:S(2)}, u32[]{:S(2)}) %collective-permute-start.17) | collective-permute-done | bytes 524320 | tf_op jit(solution)/shard_map/ppermute | solution.py:160
  76.6 1.7 copy-done.2
  78.3 2.0 shard_map.135
  80.3 4.4 %collective-permute-start.20 = (bf16[512,256]{1,0:T(8,128)(2,1)S(1)}, bf16[512,256]{1,0:T(8,128)(2,1)S(1)}, u32[]{:S(2)}, u32[]{:S(2)}) collective-permute-start(bf16[512,256]{1,0:T(8,128)(2,1)S(1)} %get-tuple-element.28), channel_id=1, source_target_pairs={{0,8},{4,12},{24,16},{28,20},{1,9},{5,13},{25,17},{29,21},{2,10},{... | collective-permute-start | bytes 786440 | tf_op jit(solution)/shard_map/ppermute | solution.py:160
  84.7 1.3 add_convert_fusion
  86.7 5.8 %collective-permute-done.20 = bf16[512,256]{1,0:T(8,128)(2,1)S(1)} collective-permute-done((bf16[512,256]{1,0:T(8,128)(2,1)S(1)}, bf16[512,256]{1,0:T(8,128)(2,1)S(1)}, u32[]{:S(2)}, u32[]{:S(2)}) %collective-permute-start.20) | collective-permute-done | bytes 262176 | tf_op jit(solution)/shard_map/ppermute | solution.py:160
  93.5 0.8 collective-permute-start.15
  94.3 3.1 %shard_map.133 = (bf16[512,512]{1,0:T(8,128)(2,1)S(1)}, bf16[512,512]{1,0:T(8,128)(2,1)S(1)}) custom-call(bf16[1024,1280]{1,0:T(8,128)(2,1)S(1)} %copy-done.2, bf16[640,2048]{1,0:T(8,128)(2,1)S(1)} %copy-done, bf16[640,1024]{1,0:T(8,128)(2,1)} %collective-permute-done.11.refs_1_), custom_call_target="tpu_custom_call" | custom-call | flops 1342177280 | bytes 4980736 | tf_op jit(solution)/shard_map/pallas_call | solution.py:117
  97.5 9.0 %collective-permute-start.12 = (bf16[576,512]{1,0:T(8,128)(2,1)S(1)}, bf16[576,512]{1,0:T(8,128)(2,1)S(1)}, u32[]{:S(2)}, u32[]{:S(2)}) collective-permute-start(bf16[576,512]{1,0:T(8,128)(2,1)S(1)} %pad_maximum_fusion.4), channel_id=1, source_target_pairs={{0,8},{4,12},{24,16},{28,20},{1,9},{5,13},{25,17},{29,21},{2,10},{... | collective-permute-start | bytes 1769480 | tf_op jit(solution)/shard_map/ppermute | solution.py:160
  106.6 1.3 collective-permute-start.22
  108.1 1.3 collective-permute-start.19
  109.5 1.3 collective-permute-start.16
  110.8 7.2 %collective-permute-done.12 = bf16[576,512]{1,0:T(8,128)(2,1)S(1)} collective-permute-done((bf16[576,512]{1,0:T(8,128)(2,1)S(1)}, bf16[576,512]{1,0:T(8,128)(2,1)S(1)}, u32[]{:S(2)}, u32[]{:S(2)}) %collective-permute-start.12) | collective-permute-done | bytes 589856 | tf_op jit(solution)/shard_map/ppermute | solution.py:160
  118.0 2.1 %shard_map.136 = (bf16[512,256]{1,0:T(8,128)(2,1)S(1)}, bf16[512,256]{1,0:T(8,128)(2,1)S(1)}) custom-call(bf16[1024,1280]{1,0:T(8,128)(2,1)S(1)} %copy-done.2, bf16[640,2048]{1,0:T(8,128)(2,1)S(1)} %copy-done, bf16[640,1024]{1,0:T(8,128)(2,1)} %collective-permute-done.11.refs_1_), custom_call_target="tpu_custom_call" | custom-call | flops 671088640 | bytes 3801088 | tf_op jit(solution)/shard_map/pallas_call | solution.py:117
  120.1 4.4 %collective-permute-start.23 = (bf16[512,256]{1,0:T(8,128)(2,1)S(1)}, bf16[512,256]{1,0:T(8,128)(2,1)S(1)}, u32[]{:S(2)}, u32[]{:S(2)}) collective-permute-start(bf16[512,256]{1,0:T(8,128)(2,1)S(1)} %get-tuple-element.31), channel_id=1, source_target_pairs={{0,8},{4,12},{24,16},{28,20},{1,9},{5,13},{25,17},{29,21},{2,10},{... | collective-permute-start | bytes 786440 | tf_op jit(solution)/shard_map/ppermute | solution.py:160
  126.7 1.7 collective-permute-done.23
  129.2 8.5 %collective-permute-done.16 = bf16[512,512]{1,0:T(8,128)(2,1)S(1)} collective-permute-done((bf16[512,512]{1,0:T(8,128)(2,1)S(1)}, bf16[512,512]{1,0:T(8,128)(2,1)S(1)}, u32[]{:S(2)}, u32[]{:S(2)}) %collective-permute-start.16) | collective-permute-done | bytes 524320 | tf_op jit(solution)/shard_map/ppermute | solution.py:153
  137.7 0.8 fusion.5
  138.5 2.1 fusion.16
  140.8 1.3 collective-permute-start.14
  142.1 0.8 fusion.9
  143.0 1.5 collective-permute-start.25
  144.5 2.1 fusion.14
  146.5 17.4 %collective-permute-done.25 = bf16[512,256]{1,0:T(8,128)(2,1)S(1)} collective-permute-done((bf16[512,256]{1,0:T(8,128)(2,1)S(1)}, bf16[512,256]{1,0:T(8,128)(2,1)S(1)}, u32[]{:S(2)}, u32[]{:S(2)}) %collective-permute-start.25) | collective-permute-done | bytes 262176 | tf_op jit(solution)/shard_map/ppermute | solution.py:153
  164.1 0.8 copy-done.15
  165.0 0.8 reshape_reshape.3
  165.8 0.8 slice_convert_fusion.1
  168.2 2.3 %fusion.12 = f32[512,1024]{1,0:T(8,128)S(1)} fusion(bf16[2048,1024]{1,0:T(8,128)(2,1)} %param.15, f32[512]{0:T(512)S(1)} %get-tuple-element.50, bf16[512,512]{1,0:T(8,128)(2,1)S(1)} %get-tuple-element.20, bf16[704,512]{1,0:T(8,128)(2,1)} %copy-done.15), kind=kOutput, calls=%fused_computation.34 | convolution fusion | flops 538705920 | bytes 4196352 | tf_op jit(solution)/shard_map/dot_general | solution.py:249
  170.9 1.7 add_add_fusion
  174.5 0.9 collective-permute-done.28
  176.3 1.4 collective-permute-start.27
  178.3 0.8 collective-permute-done.29
  179.8 4.7 %collective-permute-done.27 = bf16[1,512,256]{2,1,0:T(8,128)(2,1)S(1)} collective-permute-done((bf16[1,512,256]{2,1,0:T(8,128)(2,1)S(1)}, bf16[1,512,256]{2,1,0:T(8,128)(2,1)S(1)}, u32[]{:S(2)}, u32[]{:S(2)}) %collective-permute-start.27) | collective-permute-done | bytes 262176 | tf_op jit(solution)/shard_map/ppermute | solution.py:23
  184.7 1.5 collective-permute-start.30
  186.9 1.7 collective-permute-done.30
  188.6 1.0 convolution_convert_fusion
  189.6 3.7 %all-to-all-start = ((bf16[8,64,256]{2,1,0:T(8,128)(2,1)}), bf16[8,64,256]{2,1,0:T(8,128)(2,1)S(1)}, u32[]{:S(2)}, u32[]{:S(2)}) async-start(bf16[8,64,256]{2,1,0:T(8,128)(2,1)} %bitcast.21), calls=%async_computation | async-start | bytes 524288 | tf_op jit(solution)/shard_map/all_to_all | solution.py:446
  194.0 0.9 add_select_fusion.pick_ref
  195.0 6.6 %all-to-all-done = bf16[8,64,256]{2,1,0:T(8,128)(2,1)S(1)} async-done(((bf16[8,64,256]{2,1,0:T(8,128)(2,1)}), bf16[8,64,256]{2,1,0:T(8,128)(2,1)S(1)}, u32[]{:S(2)}, u32[]{:S(2)}) %all-to-all-start) | async-done | bytes 262176 | tf_op jit(solution)/shard_map/all_to_all | solution.py:446
  201.6 5.5 %shard_map.137 = (bf16[4,128,1024]{2,1,0:T(8,128)(2,1)}, bf16[256,256]{1,0:T(8,128)(2,1)}) custom-call(s32[4]{0:T(128)S(1)} %fusion.59.place_ref, bf16[4,128,1024]{2,1,0:T(8,128)(2,1)S(1)} %copy-done.9, bf16[8,32,256]{2,1,0:T(8,128)(2,1)S(1)} %slice.144.prefix_ref, bf16[4,128,256]{2,1,0:T(8,128)(2,1)S(1)} %copy-done.10, bf16[512,256]{1,0:T(8,128)(2,1)S(1)} %bitcast.59, ...), custom_call_target="tpu_custom_call" | custom-call | flops 603979776 | bytes 4194304 | tf_op jit(solution)/shard_map/pallas_call | solution.py:342
  (173 shorter events, 25.1 us)
Async XLA Ops:
  1.7 17.0 %collective-permute-start.2 = (bf16[128,1280]{1,0:T(8,128)(2,1)S(1)}, bf16[128,1280]{1,0:T(8,128)(2,1)S(1)}, u32[]{:S(2)}, u32[]{:S(2)}) collective-permute-start(bf16[128,1280]{1,0:T(8,128)(2,1)S(1)} %get-tuple-element.43), channel_id=1, source_target_pairs={{0,2},{1,3},{2,0},{3,1},{4,6},{5,7},{6,4},{7,5},{8,10},{9,11},{10,... | collective-permute-start | bytes 983048 | tf_op jit(solution)/shard_map/ppermute | solution.py:23
  4.8 17.6 %collective-permute-start.1 = (bf16[128,1280]{1,0:T(8,128)(2,1)S(1)}, bf16[128,1280]{1,0:T(8,128)(2,1)S(1)}, u32[]{:S(2)}, u32[]{:S(2)}) collective-permute-start(bf16[128,1280]{1,0:T(8,128)(2,1)S(1)} %get-tuple-element.44), channel_id=1, source_target_pairs={{0,0},{1,10},{2,16},{3,26},{4,4},{5,14},{6,20},{7,30},{8,2},{9,8},... | collective-permute-start | bytes 983048 | tf_op jit(solution)/shard_map/ppermute | solution.py:37
  11.6 2.7 %copy-start.30 = (s32[32,1]{0,1:T(1,128)S(1)}, s32[32,1]{0,1:T(1,128)}, u32[]{:S(2)}) copy-start(s32[32,1]{0,1:T(1,128)} %param.16) | copy-start | bytes 388
  11.6 2.7 %copy-start.31 = (s32[1,4]{1,0:T(1,128)S(1)}, s32[1,4]{1,0:T(1,128)}, u32[]{:S(2)}) copy-start(s32[1,4]{1,0:T(1,128)} %param.18) | copy-start | bytes 52
  12.8 26.6 %copy-start.11 = (s32[4]{0:T(128)S(1)}, s32[4]{0:T(128)}, u32[]{:S(2)}) copy-start(s32[4]{0:T(128)} %constant.165.clone) | copy-start | bytes 52
  12.8 34.3 %copy-start.29 = (bf16[2048]{0:T(1024)(128)(2,1)S(1)}, bf16[2048]{0:T(1024)(128)(2,1)}, u32[]{:S(2)}) copy-start(bf16[2048]{0:T(1024)(128)(2,1)} %param.14) | copy-start | bytes 12292
  12.8 38.1 %collective-permute-start = (bf16[656,1024]{1,0:T(8,128)(2,1)}, bf16[656,1024]{1,0:T(8,128)(2,1)}, u32[]{:S(2)}, u32[]{:S(2)}) collective-permute-start(bf16[656,1024]{1,0:T(8,128)(2,1)} %pad_maximum_fusion.1), channel_id=1, source_target_pairs={{4,0},{0,4},{12,8},{8,12},{20,16},{16,20},{28,24},{24,28},{5,1},{1... | collective-permute-start | bytes 4030472 | tf_op jit(solution)/shard_map/ppermute | solution.py:206
  16.0 2.8 %copy-start.26 = (s32[128]{0:T(128)}, s32[128]{0:T(128)S(1)}, u32[]{:S(2)}) copy-start(s32[128]{0:T(128)S(1)} %add.365) | copy-start | bytes 1540
  18.8 12.6 %collective-permute-start.3 = (bf16[128,1280]{1,0:T(8,128)(2,1)S(1)}, bf16[128,1280]{1,0:T(8,128)(2,1)S(1)}, u32[]{:S(2)}, u32[]{:S(2)}) collective-permute-start(bf16[128,1280]{1,0:T(8,128)(2,1)S(1)} %collective-permute-done.2), channel_id=1, source_target_pairs={{2,0},{3,10},{0,16},{1,26},{6,4},{7,14},{4,20},{5,30},{10,2},{11,8... | collective-permute-start | bytes 983048 | tf_op jit(solution)/shard_map/ppermute | solution.py:37
  22.4 17.6 %collective-permute-start.6 = (bf16[128,1280]{1,0:T(8,128)(2,1)S(1)}, bf16[128,1280]{1,0:T(8,128)(2,1)S(1)}, u32[]{:S(2)}, u32[]{:S(2)}) collective-permute-start(bf16[128,1280]{1,0:T(8,128)(2,1)S(1)} %collective-permute-done.1.refs_0_), channel_id=1, source_target_pairs={{0,1},{1,0},{2,3},{3,2},{4,5},{5,4},{6,7},{7,6},{8,9},{9,8},{10,11... | collective-permute-start | bytes 983048 | tf_op jit(solution)/shard_map/ppermute | solution.py:23
  23.6 19.6 %collective-permute-start.4 = (bf16[128,1280]{1,0:T(8,128)(2,1)S(1)}, bf16[128,1280]{1,0:T(8,128)(2,1)}, u32[]{:S(2)}, u32[]{:S(2)}) collective-permute-start(bf16[128,1280]{1,0:T(8,128)(2,1)S(1)} %collective-permute-done.1.refs_0_), channel_id=1, source_target_pairs={{0,2},{1,3},{2,0},{3,1},{4,6},{5,7},{6,4},{7,5},{8,10},{9,11},{10,... | collective-permute-start | bytes 983048 | tf_op jit(solution)/shard_map/ppermute | solution.py:23
  31.3 12.6 %collective-permute-start.5 = (bf16[128,1280]{1,0:T(8,128)(2,1)S(1)}, bf16[128,1280]{1,0:T(8,128)(2,1)}, u32[]{:S(2)}, u32[]{:S(2)}) collective-permute-start(bf16[128,1280]{1,0:T(8,128)(2,1)S(1)} %collective-permute-done.3.refs_1_), channel_id=1, source_target_pairs={{0,2},{1,3},{2,0},{3,1},{4,6},{5,7},{6,4},{7,5},{8,10},{9,11},{10,... | collective-permute-start | bytes 983048 | tf_op jit(solution)/shard_map/ppermute | solution.py:23
  35.6 41.0 %collective-permute-start.11 = (bf16[640,1024]{1,0:T(8,128)(2,1)}, bf16[640,1024]{1,0:T(8,128)(2,1)}, u32[]{:S(2)}, u32[]{:S(2)}) collective-permute-start(bf16[640,1024]{1,0:T(8,128)(2,1)} %get-tuple-element.19), channel_id=1, source_target_pairs={{4,0},{0,4},{12,8},{8,12},{20,16},{16,20},{28,24},{24,28},{5,1},{1... | collective-permute-start | bytes 3932168 | tf_op jit(solution)/shard_map/ppermute | solution.py:206
  40.0 0.7 copy-start.7
  40.7 6.9 %collective-permute-start.7 = (bf16[128,1280]{1,0:T(8,128)(2,1)S(1)}, bf16[128,1280]{1,0:T(8,128)(2,1)S(1)}, u32[]{:S(2)}, u32[]{:S(2)}) collective-permute-start(bf16[128,1280]{1,0:T(8,128)(2,1)S(1)} %collective-permute-done.3.refs_1_), channel_id=1, source_target_pairs={{0,1},{1,0},{2,3},{3,2},{4,5},{5,4},{6,7},{7,6},{8,9},{9,8},{10,11... | collective-permute-start | bytes 983048 | tf_op jit(solution)/shard_map/ppermute | solution.py:23
  43.3 4.4 %collective-permute-start.8 = (bf16[128,1280]{1,0:T(8,128)(2,1)}, bf16[128,1280]{1,0:T(8,128)(2,1)S(1)}, u32[]{:S(2)}, u32[]{:S(2)}) collective-permute-start(bf16[128,1280]{1,0:T(8,128)(2,1)} %collective-permute-done.4.refs_2_), channel_id=1, source_target_pairs={{0,1},{1,0},{2,3},{3,2},{4,5},{5,4},{6,7},{7,6},{8,9},{9,8},{10,11... | collective-permute-start | bytes 983048 | tf_op jit(solution)/shard_map/ppermute | solution.py:23
  43.9 4.1 %collective-permute-start.9 = (bf16[128,1280]{1,0:T(8,128)(2,1)}, bf16[128,1280]{1,0:T(8,128)(2,1)S(1)}, u32[]{:S(2)}, u32[]{:S(2)}) collective-permute-start(bf16[128,1280]{1,0:T(8,128)(2,1)} %collective-permute-done.5.refs_3_), channel_id=1, source_target_pairs={{0,1},{1,0},{2,3},{3,2},{4,5},{5,4},{6,7},{7,6},{8,9},{9,8},{10,11... | collective-permute-start | bytes 983048 | tf_op jit(solution)/shard_map/ppermute | solution.py:23
  47.7 3.3 %copy-start = (bf16[640,2048]{1,0:T(8,128)(2,1)S(1)}, bf16[640,2048]{1,0:T(8,128)(2,1)}, u32[]{:S(2)}) copy-start(bf16[640,2048]{1,0:T(8,128)(2,1)} %refs_0_.9) | copy-start | bytes 7864324
  48.0 1.1 copy-start.8
  50.9 4.2 %copy-start.1 = (bf16[1024,1280]{1,0:T(8,128)(2,1)}, bf16[1024,1280]{1,0:T(8,128)(2,1)S(1)}, u32[]{:S(2)}) copy-start(bf16[1024,1280]{1,0:T(8,128)(2,1)S(1)} %shard_map.131.rows_ref) | copy-start | bytes 7864324
  54.3 0.8 copy-start.5
  55.1 11.9 %copy-start.21 = (bf16[1,16,1024]{2,1,0:T(8,128)(2,1)S(1)}, bf16[1,16,1024]{2,1,0:T(8,128)(2,1)}, u32[]{:S(2)}) copy-start(bf16[1,16,1024]{2,1,0:T(8,128)(2,1)} %stack_reshape.6) | copy-start | bytes 98308
  58.8 0.8 copy-start.3
  59.6 17.0 %collective-permute-start.17 = (bf16[512,512]{1,0:T(8,128)(2,1)}, bf16[512,512]{1,0:T(8,128)(2,1)}, u32[]{:S(2)}, u32[]{:S(2)}) collective-permute-start(bf16[512,512]{1,0:T(8,128)(2,1)} %get-tuple-element.25), channel_id=1, source_target_pairs={{0,8},{4,12},{24,16},{28,20},{1,9},{5,13},{25,17},{29,21},{2,10},{... | collective-permute-start | bytes 1572872 | tf_op jit(solution)/shard_map/ppermute | solution.py:160
  68.3 25.0 %collective-permute-start.10 = (bf16[512,512]{1,0:T(8,128)(2,1)S(1)}, bf16[512,512]{1,0:T(8,128)(2,1)S(1)}, u32[]{:S(2)}, u32[]{:S(2)}) collective-permute-start(bf16[512,512]{1,0:T(8,128)(2,1)S(1)} %get-tuple-element.17), channel_id=1, source_target_pairs={{0,8},{4,12},{24,16},{28,20},{1,9},{5,13},{25,17},{29,21},{2,10},{... | collective-permute-start | bytes 1572872 | tf_op jit(solution)/shard_map/ppermute | solution.py:160
  76.6 1.7 copy-start.2
  80.3 12.2 %collective-permute-start.20 = (bf16[512,256]{1,0:T(8,128)(2,1)S(1)}, bf16[512,256]{1,0:T(8,128)(2,1)S(1)}, u32[]{:S(2)}, u32[]{:S(2)}) collective-permute-start(bf16[512,256]{1,0:T(8,128)(2,1)S(1)} %get-tuple-element.28), channel_id=1, source_target_pairs={{0,8},{4,12},{24,16},{28,20},{1,9},{5,13},{25,17},{29,21},{2,10},{... | collective-permute-start | bytes 786440 | tf_op jit(solution)/shard_map/ppermute | solution.py:160
  86.0 21.8 %collective-permute-start.18 = (bf16[512,512]{1,0:T(8,128)(2,1)S(1)}, bf16[512,512]{1,0:T(8,128)(2,1)S(1)}, u32[]{:S(2)}, u32[]{:S(2)}) collective-permute-start(bf16[512,512]{1,0:T(8,128)(2,1)S(1)} %add_convert_fusion), channel_id=1, source_target_pairs={{8,16},{12,20},{16,8},{20,12},{9,17},{13,21},{17,9},{21,13},{10,18... | collective-permute-start | bytes 1572872 | tf_op jit(solution)/shard_map/ppermute | solution.py:153
  92.6 13.9 %collective-permute-start.21 = (bf16[512,256]{1,0:T(8,128)(2,1)S(1)}, bf16[512,256]{1,0:T(8,128)(2,1)S(1)}, u32[]{:S(2)}, u32[]{:S(2)}) collective-permute-start(bf16[512,256]{1,0:T(8,128)(2,1)S(1)} %add_convert_fusion.4), channel_id=1, source_target_pairs={{8,16},{12,20},{16,8},{20,12},{9,17},{13,21},{17,9},{21,13},{10,18... | collective-permute-start | bytes 786440 | tf_op jit(solution)/shard_map/ppermute | solution.py:153
  93.5 4.0 %copy-start.17 = (bf16[64,512]{1,0:T(8,128)(2,1)S(1)}, bf16[64,512]{1,0:T(8,128)(2,1)}, u32[]{:S(2)}) copy-start(bf16[64,512]{1,0:T(8,128)(2,1)} %reshape.362) | copy-start | bytes 196612
  93.5 15.9 %collective-permute-start.15 = (bf16[512,512]{1,0:T(8,128)(2,1)S(1)}, bf16[512,512]{1,0:T(8,128)(2,1)S(1)}, u32[]{:S(2)}, u32[]{:S(2)}) collective-permute-start(bf16[512,512]{1,0:T(8,128)(2,1)S(1)} %add_convert_fusion.1), channel_id=1, source_target_pairs={{8,16},{12,20},{16,8},{20,12},{9,17},{13,21},{17,9},{21,13},{10,18... | collective-permute-start | bytes 1572872 | tf_op jit(solution)/shard_map/ppermute | solution.py:153
  97.4 10.5 %copy-start.4 = (bf16[512,512]{1,0:T(8,128)(2,1)S(1)}, bf16[512,512]{1,0:T(8,128)(2,1)}, u32[]{:S(2)}) copy-start(bf16[512,512]{1,0:T(8,128)(2,1)} %copy-done.3) | copy-start | bytes 1572868
  97.4 12.0 %copy-start.6 = (bf16[512,512]{1,0:T(8,128)(2,1)S(1)}, bf16[512,512]{1,0:T(8,128)(2,1)}, u32[]{:S(2)}) copy-start(bf16[512,512]{1,0:T(8,128)(2,1)} %copy-done.5) | copy-start | bytes 1572868
  97.5 20.5 %collective-permute-start.12 = (bf16[576,512]{1,0:T(8,128)(2,1)S(1)}, bf16[576,512]{1,0:T(8,128)(2,1)S(1)}, u32[]{:S(2)}, u32[]{:S(2)}) collective-permute-start(bf16[576,512]{1,0:T(8,128)(2,1)S(1)} %pad_maximum_fusion.4), channel_id=1, source_target_pairs={{0,8},{4,12},{24,16},{28,20},{1,9},{5,13},{25,17},{29,21},{2,10},{... | collective-permute-start | bytes 1769480 | tf_op jit(solution)/shard_map/ppermute | solution.py:160
  106.6 18.9 %collective-permute-start.22 = (bf16[512,256]{1,0:T(8,128)(2,1)S(1)}, bf16[512,256]{1,0:T(8,128)(2,1)S(1)}, u32[]{:S(2)}, u32[]{:S(2)}) collective-permute-start(bf16[512,256]{1,0:T(8,128)(2,1)S(1)} %fusion.18), channel_id=1, source_target_pairs={{16,24},{20,28},{8,0},{12,4},{17,25},{21,29},{9,1},{13,5},{18,26},... | collective-permute-start | bytes 786440 | tf_op jit(solution)/shard_map/ppermute | solution.py:153
  108.1 34.0 %collective-permute-start.19 = (bf16[512,512]{1,0:T(8,128)(2,1)S(1)}, bf16[512,512]{1,0:T(8,128)(2,1)S(1)}, u32[]{:S(2)}, u32[]{:S(2)}) collective-permute-start(bf16[512,512]{1,0:T(8,128)(2,1)S(1)} %fusion.6), channel_id=1, source_target_pairs={{16,24},{20,28},{8,0},{12,4},{17,25},{21,29},{9,1},{13,5},{18,26},... | collective-permute-start | bytes 1572872 | tf_op jit(solution)/shard_map/ppermute | solution.py:153
  109.5 28.2 %collective-permute-start.16 = (bf16[512,512]{1,0:T(8,128)(2,1)S(1)}, bf16[512,512]{1,0:T(8,128)(2,1)S(1)}, u32[]{:S(2)}, u32[]{:S(2)}) collective-permute-start(bf16[512,512]{1,0:T(8,128)(2,1)S(1)} %fusion.2), channel_id=1, source_target_pairs={{16,24},{20,28},{8,0},{12,4},{17,25},{21,29},{9,1},{13,5},{18,26},... | collective-permute-start | bytes 1572872 | tf_op jit(solution)/shard_map/ppermute | solution.py:153
  118.0 8.2 %copy-start.14 = (bf16[2048,1024]{1,0:T(8,128)(2,1)S(1)}, bf16[2048,1024]{1,0:T(8,128)(2,1)}, u32[]{:S(2)}) copy-start(bf16[2048,1024]{1,0:T(8,128)(2,1)} %param.15) | copy-start | bytes 12582916
  120.1 6.1 %copy-start.28 = (f32[256]{0:T(256)S(1)}, f32[256]{0:T(256)}, u32[]{:S(2)}) copy-start(f32[256]{0:T(256)} %get-tuple-element.48) | copy-start | bytes 3076
  120.1 8.3 %collective-permute-start.23 = (bf16[512,256]{1,0:T(8,128)(2,1)S(1)}, bf16[512,256]{1,0:T(8,128)(2,1)S(1)}, u32[]{:S(2)}, u32[]{:S(2)}) collective-permute-start(bf16[512,256]{1,0:T(8,128)(2,1)S(1)} %get-tuple-element.31), channel_id=1, source_target_pairs={{0,8},{4,12},{24,16},{28,20},{1,9},{5,13},{25,17},{29,21},{2,10},{... | collective-permute-start | bytes 786440 | tf_op jit(solution)/shard_map/ppermute | solution.py:160
  124.8 15.8 %collective-permute-start.13 = (bf16[640,512]{1,0:T(8,128)(2,1)S(1)}, bf16[640,512]{1,0:T(8,128)(2,1)S(1)}, u32[]{:S(2)}, u32[]{:S(2)}) collective-permute-start(bf16[640,512]{1,0:T(8,128)(2,1)S(1)} %pad_maximum_fusion.3), channel_id=1, source_target_pairs={{8,16},{12,20},{16,8},{20,12},{9,17},{13,21},{17,9},{21,13},{10,18... | collective-permute-start | bytes 1966088 | tf_op jit(solution)/shard_map/ppermute | solution.py:153
  126.2 12.3 %copy-start.22 = (f32[512]{0:T(512)S(1)}, f32[512]{0:T(512)}, u32[]{:S(2)}) copy-start(f32[512]{0:T(512)} %get-tuple-element.51) | copy-start | bytes 6148
  128.5 14.4 %collective-permute-start.24 = (bf16[512,256]{1,0:T(8,128)(2,1)S(1)}, bf16[512,256]{1,0:T(8,128)(2,1)S(1)}, u32[]{:S(2)}, u32[]{:S(2)}) collective-permute-start(bf16[512,256]{1,0:T(8,128)(2,1)S(1)} %add_convert_fusion.3), channel_id=1, source_target_pairs={{8,16},{12,20},{16,8},{20,12},{9,17},{13,21},{17,9},{21,13},{10,18... | collective-permute-start | bytes 786440 | tf_op jit(solution)/shard_map/ppermute | solution.py:153
  140.8 23.3 %collective-permute-start.14 = (bf16[704,512]{1,0:T(8,128)(2,1)S(1)}, bf16[704,512]{1,0:T(8,128)(2,1)S(1)}, u32[]{:S(2)}, u32[]{:S(2)}) collective-permute-start(bf16[704,512]{1,0:T(8,128)(2,1)S(1)} %pad_maximum_fusion.2), channel_id=1, source_target_pairs={{16,24},{20,28},{8,0},{12,4},{17,25},{21,29},{9,1},{13,5},{18,26},... | collective-permute-start | bytes 2162696 | tf_op jit(solution)/shard_map/ppermute | solution.py:153
  143.0 20.9 %collective-permute-start.25 = (bf16[512,256]{1,0:T(8,128)(2,1)S(1)}, bf16[512,256]{1,0:T(8,128)(2,1)S(1)}, u32[]{:S(2)}, u32[]{:S(2)}) collective-permute-start(bf16[512,256]{1,0:T(8,128)(2,1)S(1)} %fusion.22), channel_id=1, source_target_pairs={{16,24},{20,28},{8,0},{12,4},{17,25},{21,29},{9,1},{13,5},{18,26},... | collective-permute-start | bytes 786440 | tf_op jit(solution)/shard_map/ppermute | solution.py:153
  144.5 20.5 %copy-start.20 = (bf16[1,64,512]{2,1,0:T(8,128)(2,1)S(1)}, bf16[1,64,512]{2,1,0:T(8,128)(2,1)}, u32[]{:S(2)}) copy-start(bf16[1,64,512]{2,1,0:T(8,128)(2,1)} %stack_reshape.7) | copy-start | bytes 196612
  164.1 0.9 copy-start.15
  168.2 2.3 %copy-start.12 = (f32[512,1024]{1,0:T(8,128)S(1)}, f32[512,1024]{1,0:T(8,128)}, u32[]{:S(2)}) copy-start(f32[512,1024]{1,0:T(8,128)} %fusion.16) | copy-start | bytes 6291460
  168.2 2.7 %copy-start.13 = (f32[512,1024]{1,0:T(8,128)S(1)}, f32[512,1024]{1,0:T(8,128)}, u32[]{:S(2)}) copy-start(f32[512,1024]{1,0:T(8,128)} %fusion.14) | copy-start | bytes 6291460
  168.2 2.7 %copy-start.27 = (f32[256]{0:T(256)S(1)}, f32[256]{0:T(256)}, u32[]{:S(2)}) copy-start(f32[256]{0:T(256)} %get-tuple-element.47) | copy-start | bytes 3076
  172.8 1.1 copy-start.16
  172.9 1.2 copy-start.23
  173.0 1.2 copy-start.24
  173.0 1.2 copy-start.25
  173.0 3.1 %collective-permute-start.26 = (bf16[2,512,256]{2,1,0:T(8,128)(2,1)S(1)}, bf16[2,512,256]{2,1,0:T(8,128)(2,1)S(1)}, u32[]{:S(2)}, u32[]{:S(2)}) collective-permute-start(bf16[2,512,256]{2,1,0:T(8,128)(2,1)S(1)} %fusion.26), channel_id=1, source_target_pairs={{0,1},{1,0},{2,3},{3,2},{4,5},{5,4},{6,7},{7,6},{8,9},{9,8},{10,11... | collective-permute-start | bytes 1572872 | tf_op jit(solution)/shard_map/ppermute | solution.py:23
  174.2 1.2 collective-permute-start.28
  175.4 3.7 %collective-permute-start.29 = (f32[512]{0:T(512)S(1)}, f32[512]{0:T(512)}, u32[]{:S(2)}, u32[]{:S(2)}) collective-permute-start(f32[512]{0:T(512)S(1)} %add.353), channel_id=1, source_target_pairs={{0,2},{1,3},{2,0},{3,1},{4,6},{5,7},{6,4},{7,5},{8,10},{9,11},{10,... | collective-permute-start | bytes 6152 | tf_op jit(solution)/shard_map/ppermute | solution.py:23
  176.2 17.8 %copy-start.18 = (s32[4,128,1]{2,1,0:T(8,128)S(1)}, s32[4,128,1]{2,1,0:T(8,128)}, u32[]{:S(2)}) copy-start(s32[4,128,1]{2,1,0:T(8,128)} %add.377) | copy-start | bytes 6148
  176.2 18.7 %copy-start.19 = (bf16[8,64,256]{2,1,0:T(8,128)(2,1)S(1)}, bf16[8,64,256]{2,1,0:T(8,128)(2,1)}, u32[]{:S(2)}) copy-start(bf16[8,64,256]{2,1,0:T(8,128)(2,1)} %reshape_reshape.3) | copy-start | bytes 786436
  176.2 25.3 %copy-start.9 = (bf16[4,128,1024]{2,1,0:T(8,128)(2,1)S(1)}, bf16[4,128,1024]{2,1,0:T(8,128)(2,1)}, u32[]{:S(2)}) copy-start(bf16[4,128,1024]{2,1,0:T(8,128)(2,1)} %query_ref.1) | copy-start | bytes 3145732
  176.3 25.3 %copy-start.10 = (bf16[4,128,256]{2,1,0:T(8,128)(2,1)S(1)}, bf16[4,128,256]{2,1,0:T(8,128)(2,1)}, u32[]{:S(2)}) copy-start(bf16[4,128,256]{2,1,0:T(8,128)(2,1)} %text_ref.1) | copy-start | bytes 786436
  176.3 8.2 %collective-permute-start.27 = (bf16[1,512,256]{2,1,0:T(8,128)(2,1)S(1)}, bf16[1,512,256]{2,1,0:T(8,128)(2,1)S(1)}, u32[]{:S(2)}, u32[]{:S(2)}) collective-permute-start(bf16[1,512,256]{2,1,0:T(8,128)(2,1)S(1)} %dynamic-slice_convert_fusion.1), channel_id=1, source_target_pairs={{0,2},{1,3},{2,0},{3,1},{4,6},{5,7},{6,4},{7,5},{8,10},{9,11},{10,... | collective-permute-start | bytes 786440 | tf_op jit(solution)/shard_map/ppermute | solution.py:23
  184.7 4.0 %collective-permute-start.30 = (bf16[256,256]{1,0:T(8,128)(2,1)S(1)}, bf16[256,256]{1,0:T(8,128)(2,1)S(1)}, u32[]{:S(2)}, u32[]{:S(2)}) collective-permute-start(bf16[256,256]{1,0:T(8,128)(2,1)S(1)} %slice.149), channel_id=1, source_target_pairs={{0,8},{4,12},{24,16},{28,20},{1,9},{5,13},{25,17},{29,21},{2,10},{... | collective-permute-start | bytes 393224 | tf_op jit(solution)/shard_map/ppermute | solution.py:258
  189.6 11.9 %all-to-all-start = ((bf16[8,64,256]{2,1,0:T(8,128)(2,1)}), bf16[8,64,256]{2,1,0:T(8,128)(2,1)S(1)}, u32[]{:S(2)}, u32[]{:S(2)}) async-start(bf16[8,64,256]{2,1,0:T(8,128)(2,1)} %bitcast.21), calls=%async_computation | async-start | bytes 524288 | tf_op jit(solution)/shard_map/all_to_all | solution.py:446
